TPU v7x, 32 devices: a whole 2x2x4 slice. The times are simulated.
32 devices in a mesh: dp: 8 (over z, core), mp: 4 (over y, x).
Axes of the slice: x: 2, y: 2, z: 4, core: 2. Of those that a mesh axis runs over, the one named last changes fastest.
Arguments:
- block_in: bfloat16 [16, 1024, 2048], P('dp', 'mp'), may hold values from -6 to 6
- norm1_gain: float32 [2048], replicated, may hold values from 0.25 to 1.75
- w_branch: bfloat16 [2048, 2560], P(None, 'mp'), may hold values from -0.125 to 0.125
- w_input: bfloat16 [2048, 2560], P(None, 'mp'), may hold values from -0.125 to 0.125
- conv_weight: float32 [4, 2560], P(None, 'mp'), may hold values from -3 to 3
- conv_bias: float32 [2560], P('mp'), may hold values from -3 to 3
- gate_a_weight: bfloat16 [16, 160, 160], P('mp'), may hold values from -0.5 to 0.5
- gate_a_bias: float32 [2560], P('mp'), may hold values from -4 to 4
- gate_i_weight: bfloat16 [16, 160, 160], P('mp'), may hold values from -0.5 to 0.5
- gate_i_bias: float32 [2560], P('mp'), may hold values from -4 to 4
- decay_param: float32 [2560], P('mp'), may hold values from 4 to 9
- w_out: bfloat16 [2560, 2048], P('mp'), may hold values from -0.3125 to 0.3125
- norm2_gain: float32 [2048], replicated, may hold values from 0.25 to 1.75
- w_gate: bfloat16 [2048, 6144], P(None, 'mp'), may hold values from -0.125 to 0.125
- w_up: bfloat16 [2048, 6144], P(None, 'mp'), may hold values from -0.125 to 0.125
- w_down: bfloat16 [6144, 2048], P('mp'), may hold values from -0.109375 to 0.109375
- lengths: int32 [16], P('dp'), may hold values from 256 to 1024, as said below
- cotangent: bfloat16 [16, 1024, 2048], P('dp', 'mp'), may hold values from -6 to 6
Outputs:
- block_out: bfloat16 [16, 1024, 2048], P('dp', 'mp')
- input_grad: bfloat16 [16, 1024, 2048], P('dp', 'mp')
- grad_norm1_gain: float32 [2048], replicated
- grad_w_branch: float32 [2048, 2560], P(None, 'mp')
- grad_w_input: float32 [2048, 2560], P(None, 'mp')
- grad_conv_weight: float32 [4, 2560], P(None, 'mp')
- grad_conv_bias: float32 [2560], P('mp')
- grad_gate_a_weight: float32 [16, 160, 160], P('mp')
- grad_gate_a_bias: float32 [2560], P('mp')
- grad_gate_i_weight: float32 [16, 160, 160], P('mp')
- grad_gate_i_bias: float32 [2560], P('mp')
- grad_decay_param: float32 [2560], P('mp')
- grad_w_out: float32 [2560, 2048], P('mp')
- grad_norm2_gain: float32 [2048], replicated
- grad_w_gate: float32 [2048, 6144], P(None, 'mp')
- grad_w_up: float32 [2048, 6144], P(None, 'mp')
- grad_w_down: float32 [6144, 2048], P('mp')
- final_state: float32 [16, 2560], P('dp', 'mp')
Inputs may be any that keep to these rules, and one draw needn't show every extreme that they name: `lengths`: in each aligned block of 2 sequences, one sequence drawn from the seed has length 1024; every length is at least 256.
All inputs are finite; a program needn't handle non-finite values.
Results may differ from a plain program's by a relative error of at most 0.019.
Values may be sent and summed in bfloat16 or wider, within the bound.
A program may use at most 448 MiB of HBM per device.

v0:
```python
import jax
import jax.numpy as jnp
from jax import lax
from jax.sharding import PartitionSpec as P

DECAY_EXP = 8


eps = 1e-06


def normalize(values, gain):
    return values * lax.rsqrt(jnp.mean(values * values, axis=-1, keepdims=True) + eps) * gain


def project(left, right):
    return jnp.einsum("rtd,dc->rtc", left, right, preferred_element_type=jnp.float32)


def project_back(left, right):
    return jnp.einsum("rtc,dc->rtd", left, right, preferred_element_type=jnp.float32)


def weight_grad(left, right):
    return jnp.einsum("rtd,rtc->dc", left, right, preferred_element_type=jnp.float32)


def causal_conv(seq, conv_weight, conv_bias):
    span = seq.shape[1]
    total = conv_bias + conv_weight[0] * seq
    for shift in range(1, conv_weight.shape[0]):
        moved = jnp.pad(seq, ((0, 0), (shift, 0), (0, 0)))[:, :span]
        total = total + conv_weight[shift] * moved
    return total


def conv_taps_grad(grad, seq, taps):
    span = seq.shape[1]
    rows_out = []
    for shift in range(taps):
        moved = jnp.pad(seq, ((0, 0), (shift, 0), (0, 0)))[:, :span]
        rows_out.append(jnp.sum(grad * moved, axis=(0, 1)))
    return jnp.stack(rows_out, axis=0)


def conv_back(grad, conv_weight):
    total = conv_weight[0] * grad
    for shift in range(1, conv_weight.shape[0]):
        moved = jnp.pad(grad, ((0, 0), (0, shift), (0, 0)))[:, shift:]
        total = total + conv_weight[shift] * moved
    return total


def combine(earlier, later):
    return (earlier[0] * later[0], later[0] * earlier[1] + later[1])


def block_product(values, weight):
    count, span, width = values.shape
    blocks = values.reshape(count, span, weight.shape[0], weight.shape[1])
    return jnp.einsum("rtnb,nbc->rtnc", blocks, weight, preferred_element_type=jnp.float32).reshape(
        count, span, width
    )


def block_product_back(grad, weight):
    count, span, width = grad.shape
    blocks = grad.reshape(count, span, weight.shape[0], weight.shape[2])
    return jnp.einsum("rtnc,nbc->rtnb", blocks, weight, preferred_element_type=jnp.float32).reshape(
        count, span, width
    )


def block_weight_grad(values, grad, nblocks):
    count, span, width = values.shape
    left = values.reshape(count, span, nblocks, width // nblocks)
    right = grad.reshape(count, span, nblocks, width // nblocks)
    return jnp.einsum("rtnb,rtnc->nbc", left, right, preferred_element_type=jnp.float32)


def per_device(
    block_in,
    norm1_gain,
    w_branch,
    w_input,
    conv_weight,
    conv_bias,
    gate_a_weight,
    gate_a_bias,
    gate_i_weight,
    gate_i_bias,
    decay_param,
    w_out,
    norm2_gain,
    w_gate,
    w_up,
    w_down,
    lengths,
    cotangent,
):
    count, piece, width = block_in.shape
    span = piece * lax.axis_size("mp")
    nblocks = gate_a_weight.shape[0]
    live = (jnp.arange(span, dtype=jnp.int32)[None, :] < lengths[:, None])[..., None]

    def core(conv_vals, gate_a_pre, gate_i_pre, decay_vals, branch_pre):
        gate_a = jax.nn.sigmoid(gate_a_pre)
        gate_i = jax.nn.sigmoid(gate_i_pre)
        log_a = -DECAY_EXP * jax.nn.softplus(-decay_vals) * gate_a
        decay = jnp.exp(log_a)
        scaled = jnp.sqrt(-jnp.expm1(2.0 * log_a)) * gate_i * conv_vals
        gated_a = jnp.where(live, decay, 1.0)
        gated_in = jnp.where(live, scaled, 0.0)
        carried, states = lax.associative_scan(combine, (gated_a, gated_in), axis=1)
        return (states * jax.nn.gelu(branch_pre), states[:, -1])

    resid = block_in.astype(jnp.float32)
    normed_in = normalize(resid, norm1_gain).astype(jnp.bfloat16)
    seq_in = lax.all_gather(normed_in, "mp", axis=1, tiled=True)
    branch_pre = project(seq_in, w_branch)
    input_pre = project(seq_in, w_input)
    conv_out = causal_conv(input_pre, conv_weight, conv_bias).astype(jnp.bfloat16)
    gate_a_pre = block_product(conv_out, gate_a_weight) + gate_a_bias
    gate_i_pre = block_product(conv_out, gate_i_weight) + gate_i_bias
    mixed, pull_core, final_state = jax.vjp(
        core,
        conv_out.astype(jnp.float32),
        gate_a_pre,
        gate_i_pre,
        decay_param,
        branch_pre,
        has_aux=True,
    )
    mixed_low = mixed.astype(jnp.bfloat16)
    branch = lax.psum_scatter(project(mixed_low, w_out), "mp", scatter_dimension=1, tiled=True)
    resid_mid = resid + branch
    normed_mid = normalize(resid_mid, norm2_gain).astype(jnp.bfloat16)
    seq_mid = lax.all_gather(normed_mid, "mp", axis=1, tiled=True)
    mlp_gate = project(seq_mid, w_gate)
    mlp_up = project(seq_mid, w_up)
    activated, pull_gelu = jax.vjp(jax.nn.gelu, mlp_gate)
    hidden = (activated * mlp_up).astype(jnp.bfloat16)
    mlp_total = lax.psum_scatter(
        project(hidden, w_down).astype(jnp.bfloat16), "mp", scatter_dimension=1, tiled=True
    ).astype(jnp.float32)
    block_out = (resid_mid + mlp_total).astype(jnp.bfloat16)
    cot_seq = lax.all_gather(cotangent, "mp", axis=1, tiled=True)
    grad_w_down = weight_grad(hidden, cot_seq)
    d_hidden = project_back(cot_seq, w_down)
    d_gate = pull_gelu(d_hidden * mlp_up)[0].astype(jnp.bfloat16)
    d_up = (d_hidden * activated).astype(jnp.bfloat16)
    grad_w_gate = weight_grad(seq_mid, d_gate)
    grad_w_up = weight_grad(seq_mid, d_up)
    d_mid_part = project_back(d_gate, w_gate) + project_back(d_up, w_up)
    d_mid = lax.psum_scatter(d_mid_part, "mp", scatter_dimension=1, tiled=True)
    norm_mid_out, pull_norm_mid = jax.vjp(normalize, resid_mid, norm2_gain)
    d_resid_norm, grad_norm2_gain = pull_norm_mid(d_mid)
    d_resid = cotangent.astype(jnp.float32) + d_resid_norm
    d_resid_seq = lax.all_gather(d_resid.astype(jnp.bfloat16), "mp", axis=1, tiled=True)
    grad_w_out = weight_grad(mixed_low, d_resid_seq)
    d_mixed = project_back(d_resid_seq, w_out)
    d_conv_rec, d_gate_a, d_gate_i, grad_decay_param, d_branch = pull_core(d_mixed)
    d_gate_a_low = d_gate_a.astype(jnp.bfloat16)
    d_gate_i_low = d_gate_i.astype(jnp.bfloat16)
    grad_gate_a_bias = jnp.sum(d_gate_a_low.astype(jnp.float32), axis=(0, 1))
    grad_gate_i_bias = jnp.sum(d_gate_i_low.astype(jnp.float32), axis=(0, 1))
    grad_gate_a_weight = block_weight_grad(conv_out, d_gate_a_low, nblocks)
    grad_gate_i_weight = block_weight_grad(conv_out, d_gate_i_low, nblocks)
    d_conv = (
        d_conv_rec
        + block_product_back(d_gate_a_low, gate_a_weight)
        + block_product_back(d_gate_i_low, gate_i_weight)
    )
    grad_conv_bias = jnp.sum(d_conv, axis=(0, 1))
    grad_conv_weight = conv_taps_grad(d_conv, input_pre, conv_weight.shape[0])
    d_input = conv_back(d_conv, conv_weight).astype(jnp.bfloat16)
    d_branch_low = d_branch.astype(jnp.bfloat16)
    grad_w_branch = weight_grad(seq_in, d_branch_low)
    grad_w_input = weight_grad(seq_in, d_input)
    d_in_part = project_back(d_branch_low, w_branch) + project_back(d_input, w_input)
    d_in = lax.psum_scatter(
        d_in_part.astype(jnp.bfloat16), "mp", scatter_dimension=1, tiled=True
    ).astype(jnp.float32)
    norm_in_out, pull_norm_in = jax.vjp(normalize, resid, norm1_gain)
    d_resid_in, grad_norm1_gain = pull_norm_in(d_in)
    input_grad = (d_resid + d_resid_in).astype(jnp.bfloat16)
    grad_norm1_gain, grad_norm2_gain = lax.psum((grad_norm1_gain, grad_norm2_gain), ("dp", "mp"))
    (
        grad_w_branch,
        grad_w_input,
        grad_conv_weight,
        grad_conv_bias,
        grad_gate_a_weight,
        grad_gate_a_bias,
        grad_gate_i_weight,
        grad_gate_i_bias,
        grad_decay_param,
        grad_w_out,
        grad_w_gate,
        grad_w_up,
        grad_w_down,
    ) = (
        lax.psum(grad_w_branch.astype(jnp.bfloat16), "dp").astype(jnp.float32),
        lax.psum(grad_w_input.astype(jnp.bfloat16), "dp").astype(jnp.float32),
        lax.psum(grad_conv_weight.astype(jnp.bfloat16), "dp").astype(jnp.float32),
        lax.psum(grad_conv_bias.astype(jnp.bfloat16), "dp").astype(jnp.float32),
        lax.psum(grad_gate_a_weight.astype(jnp.bfloat16), "dp").astype(jnp.float32),
        lax.psum(grad_gate_a_bias.astype(jnp.bfloat16), "dp").astype(jnp.float32),
        lax.psum(grad_gate_i_weight.astype(jnp.bfloat16), "dp").astype(jnp.float32),
        lax.psum(grad_gate_i_bias.astype(jnp.bfloat16), "dp").astype(jnp.float32),
        lax.psum(grad_decay_param.astype(jnp.bfloat16), "dp").astype(jnp.float32),
        lax.psum(grad_w_out.astype(jnp.bfloat16), "dp").astype(jnp.float32),
        lax.psum(grad_w_gate.astype(jnp.bfloat16), "dp").astype(jnp.float32),
        lax.psum(grad_w_up.astype(jnp.bfloat16), "dp").astype(jnp.float32),
        lax.psum(grad_w_down.astype(jnp.bfloat16), "dp").astype(jnp.float32),
    )
    return (
        block_out,
        input_grad,
        grad_norm1_gain,
        grad_w_branch,
        grad_w_input,
        grad_conv_weight,
        grad_conv_bias,
        grad_gate_a_weight,
        grad_gate_a_bias,
        grad_gate_i_weight,
        grad_gate_i_bias,
        grad_decay_param,
        grad_w_out,
        grad_norm2_gain,
        grad_w_gate,
        grad_w_up,
        grad_w_down,
        final_state,
    )


def solution(mesh):
    placed = (
        P("dp", "mp", None),
        P(),
        P(None, "mp"),
        P(None, "mp"),
        P(None, "mp"),
        P("mp"),
        P("mp", None, None),
        P("mp"),
        P("mp", None, None),
        P("mp"),
        P("mp"),
        P("mp", None),
        P(),
        P(None, "mp"),
        P(None, "mp"),
        P("mp", None),
        P("dp"),
        P("dp", "mp", None),
    )
    return jax.shard_map(
        per_device,
        mesh=mesh,
        in_specs=placed,
        out_specs=(
            P("dp", "mp", None),
            P("dp", "mp", None),
            P(),
            P(None, "mp"),
            P(None, "mp"),
            P(None, "mp"),
            P("mp"),
            P("mp", None, None),
            P("mp"),
            P("mp", None, None),
            P("mp"),
            P("mp"),
            P("mp", None),
            P(),
            P(None, "mp"),
            P(None, "mp"),
            P("mp", None),
            P("dp", "mp"),
        ),
        check_vma=False,
    )
```

profile of v0, /device:TPU:9, one launch (start us, length us, event | category | flops | bytes accessed | tf_op | source)
XLA Modules:
  0.0 2367.3 jit_solution(16019323715120458884)
XLA Ops:
  14.5 88.6 %all-gather.5.cloned.1.call-done = bf16[2,1024,2048]{2,1,0:T(8,128)(2,1)} async-done(((bf16[2,256,2048]{2,1,0:T(8,128)(2,1)}), bf16[2,1024,2048]{2,1,0:T(8,128)(2,1)}) %all-gather.5.cloned.1.call-update) | async-done | bytes 8388624 | tf_op jit(solution)/shard_map/all_gather | solution.py:119
  103.1 9.9 fusion.59
  146.6 18.7 exponential_select_fusion
  165.3 13.0 slice.355
  178.3 13.0 slice.359
  191.3 13.2 slice.354
  205.2 13.0 slice.356
  218.2 13.1 slice.427
  231.3 13.0 slice.357
  244.4 6.9 fusion.120
  251.3 7.5 slice.361
  258.8 7.5 slice.365
  266.2 7.5 slice.360
  275.1 7.5 slice.362
  282.6 7.5 slice.425
  290.1 7.7 slice.363
  442.1 10.7 pad.418
  452.9 11.0 pad.419
  463.8 14.0 multiply_convert_fusion.2
  479.3 9.6 fusion.52
  489.4 153.5 %reduce-scatter.5.cloned.1.call-done = f32[2,256,2048]{2,1,0:T(8,128)} async-done(((f32[2,1024,2048]{2,1,0:T(8,128)}), f32[2,256,2048]{2,1,0:T(8,128)}) %reduce-scatter.5.cloned.1.call-update) | async-done | bytes 4194320 | tf_op jit(solution)/shard_map/reduce_scatter | solution.py:135
  650.7 87.2 %all-gather.7.cloned.1.call-done = bf16[2,1024,2048]{2,1,0:T(8,128)(2,1)} async-done(((bf16[2,256,2048]{2,1,0:T(8,128)(2,1)}), bf16[2,1024,2048]{2,1,0:T(8,128)(2,1)}) %all-gather.7.cloned.1.call-update) | async-done | bytes 8388624 | tf_op jit(solution)/shard_map/all_gather | solution.py:138
  737.9 19.4 fusion.12
  757.3 17.3 fusion.16
  774.6 52.6 %all-gather.9.cloned.1.call-done = bf16[2,1024,2048]{2,1,0:T(8,128)(2,1)} async-done(((bf16[2,256,2048]{2,1,0:T(8,128)(2,1)}), bf16[2,1024,2048]{2,1,0:T(8,128)(2,1)}) %all-gather.9.cloned.1.call-update) | async-done | bytes 8388624 | tf_op jit(solution)/shard_map/all_gather | solution.py:147
  827.3 34.0 %multiply_convert_fusion = (bf16[2,1024,1536]{2,1,0:T(8,128)(2,1)}, bf16[2,1024,1536]{2,1,0:T(8,128)(2,1)}, bf16[2,1024,1536]{2,1,0:T(8,128)(2,1)}) fusion(f32[2,1024,1536]{2,1,0:T(8,128)} %fusion.16, f32[2,1024,1536]{2,1,0:T(8,128)} %fusion.12, bf16[2,1024,2048]{2,1,0:T(8,128)(2,1)} %all-gather.9.cloned.1.call-done, bf16[1536,2048]{1,0:T(8,128)(2,1)} %param.33), kind=kOutput, calls=%fused_computation.13 | convolution fusion | flops 12966690816 | bytes 58720256 | tf_op jit(solution)/shard_map/rtc,dc->rtd/dot_general | solution.py:21
  861.2 19.5 fusion.14
  880.7 23.2 convolution_add_fusion
  904.0 153.9 %reduce-scatter.9.cloned.1.call-done = f32[2,256,2048]{2,1,0:T(8,128)} async-done(((f32[2,1024,2048]{2,1,0:T(8,128)}), f32[2,256,2048]{2,1,0:T(8,128)}) %reduce-scatter.9.cloned.1.call-update) | async-done | bytes 4194320 | tf_op jit(solution)/shard_map/reduce_scatter | solution.py:155
  1068.0 19.7 bitcast_convert_fusion
  1087.7 19.2 bitcast_convert_fusion.1
  1107.0 15.8 bitcast_convert_fusion.2
  1122.8 32.9 %all-gather.11.cloned.1.call-done = bf16[2,1024,2048]{2,1,0:T(8,128)(2,1)} async-done(((bf16[2,256,2048]{2,1,0:T(8,128)(2,1)}), bf16[2,1024,2048]{2,1,0:T(8,128)(2,1)}) %all-gather.11.cloned.1.call-update) | async-done | bytes 8388624 | tf_op jit(solution)/shard_map/all_gather | solution.py:159
  1155.7 15.3 fusion.65
  1175.7 13.0 slice.428
  1188.7 7.6 fusion.118
  1197.7 13.0 slice.429
  1216.3 7.5 slice.430
  1229.8 7.5 slice.431
  1365.1 6.5 multiply_add_fusion.4
  1408.5 12.7 multiply_add_fusion.1
  1425.6 10.9 pad.485
  1436.4 11.1 pad.422
  1447.5 11.0 pad.513
  1458.5 11.0 pad.486
  1469.5 11.1 pad.514
  1480.7 11.0 pad.487
  1491.8 29.8 %multiply_reduce_fusion = (f32[640]{0:T(1024)S(1)}, f32[2,1024,640]{2,1,0:T(8,128)S(1)}, f32[2,1024,640]{2,1,0:T(8,128)S(1)}) fusion(f32[2,1024,640]{2,1,0:T(8,128)} %copy.60, f32[640]{0:T(1024)S(1)} %copy-done.77, f32[2,1024,640]{2,1,0:T(8,128)} %pad.514, f32[2,1024,640]{2,1,0:T(8,128)} %pad.487, f32[2,1024,640]{2,1,0:T(8,128)} %pad.513, ...), kind=kLoop, calls=%fused_computation.72 | loop fusion | flops 51117440 | bytes 57701888 | tf_op jit(solution)/shard_map/transpose(jvp())/reduce_sum | solution.py:109
  1521.5 18.8 fusion.113
  1584.9 18.6 multiply_reduce_fusion.4
  1605.9 10.2 bitcast_convert_fusion.3
  1616.2 8.3 bitcast_convert_fusion.5
  1624.5 8.5 bitcast_convert_fusion.4
  1633.1 12.2 fusion.54
  1645.3 12.5 add_convert_fusion
  1657.9 19.5 fusion.18
  1678.9 22.9 all-reduce.102
  1704.8 466.2 %all-reduce.106.cloned.1.call-done = (bf16[2048,640]{1,0:T(8,128)(2,1)}, bf16[2048,640]{1,0:T(8,128)(2,1)}, bf16[4,160,160]{2,1,0:T(8,128)(2,1)}, bf16[4,160,160...) async-done(((bf16[2048,640]{1,0:T(8,128)(2,1)}, ...) | async-done | bytes 27148304 | tf_op jit(solution)/shard_map/psum | solution.py:203
  2185.5 9.8 convert_element_type.191
  2195.3 6.6 convert_element_type.193
  2208.2 52.6 %reduce-scatter.11.cloned.1.call-done = bf16[2,256,2048]{2,1,0:T(8,128)(2,1)} async-done(((bf16[2,1024,2048]{2,1,0:T(8,128)(2,1)}), bf16[2,256,2048]{2,1,0:T(8,128)(2,1)}) %reduce-scatter.11.cloned.1.call-update) | async-done | bytes 2097168 | tf_op jit(solution)/shard_map/reduce_scatter | solution.py:181
  2264.7 40.6 %all-reduce.101 = (f32[2048]{0:T(1024)}, f32[2048]{0:T(1024)}) all-reduce(f32[2048]{0:T(1024)S(1)} %get-tuple-element.25, f32[2048]{0:T(1024)S(1)} %copy-done.88), channel_id=1, replica_groups=mesh['dp'=8,'mp'=4] {'dp','mp'}, use_global_device_ids=true, to_apply=%region_9.10 | all-reduce | flops 4096 | bytes 32768 | tf_op jit(solution)/shard_map/psum | solution.py:187
  2305.4 46.3 %reduce-scatter.7.cloned.1.call-done = bf16[2,256,2048]{2,1,0:T(8,128)(2,1)} async-done(((bf16[2,1024,2048]{2,1,0:T(8,128)(2,1)}), bf16[2,256,2048]{2,1,0:T(8,128)(2,1)}) %reduce-scatter.7.cloned.1.call-update) | async-done | bytes 2097168 | tf_op jit(solution)/shard_map/reduce_scatter | solution.py:143
  2351.7 8.6 fusion.47
  (533 shorter events, 469.4 us)
Async XLA Ops:
  7.2 456.6 %copy-start = (bf16[2048,640]{1,0:T(8,128)(2,1)S(1)}, bf16[2048,640]{1,0:T(8,128)(2,1)}, u32[]{:S(2)}) copy-start(bf16[2048,640]{1,0:T(8,128)(2,1)} %param.20) | copy-start | bytes 7864324
  7.2 95.9 %all-gather.5.cloned.1.call-start = ((), (), s32[]{:S(2)}) async-start(), calls=%async_computation.4 | async-start | bytes 10485760 | tf_op jit(solution)/shard_map/all_gather | solution.py:119
  14.2 628.7 %reduce-scatter.5.cloned.1.call-start = ((), (), s32[]{:S(2)}) async-start(), calls=%async_computation.5 | async-start | bytes 20971520 | tf_op jit(solution)/shard_map/reduce_scatter | solution.py:135
  14.3 132.3 %copy-start.55 = (f32[640]{0:T(1024)}, f32[640]{0:T(1024)S(1)}, u32[]{:S(2)}) copy-start(f32[640]{0:T(1024)S(1)} %get-tuple-element.27) | copy-start | bytes 7684
  14.3 132.3 %copy-start.57 = (f32[640]{0:T(1024)}, f32[640]{0:T(1024)S(1)}, u32[]{:S(2)}) copy-start(f32[640]{0:T(1024)S(1)} %get-tuple-element.28) | copy-start | bytes 7684
  14.3 132.2 %copy-start.59 = (f32[640]{0:T(1024)}, f32[640]{0:T(1024)S(1)}, u32[]{:S(2)}) copy-start(f32[640]{0:T(1024)S(1)} %get-tuple-element.29) | copy-start | bytes 7684
  14.3 132.2 %copy-start.61 = (f32[640]{0:T(1024)}, f32[640]{0:T(1024)S(1)}, u32[]{:S(2)}) copy-start(f32[640]{0:T(1024)S(1)} %get-tuple-element.30) | copy-start | bytes 7684
  14.4 132.2 %copy-start.84 = (pred[2,1024]{1,0:T(4,128)(4,1)}, pred[2,1024]{1,0:T(4,128)(4,1)S(1)}, u32[]{:S(2)}) copy-start(pred[2,1024]{1,0:T(4,128)(4,1)S(1)} %iota_compare_fusion) | copy-start | bytes 6148
  14.4 132.1 %copy-start.67 = (f32[640]{0:T(1024)}, f32[640]{0:T(1024)S(1)}, u32[]{:S(2)}) copy-start(f32[640]{0:T(1024)S(1)} %fusion.98) | copy-start | bytes 7684
  14.4 100.8 %copy-start.74 = (f32[640]{0:T(1024)S(1)}, f32[640]{0:T(1024)}, u32[]{:S(2)}) copy-start(f32[640]{0:T(1024)} %param.23) | copy-start | bytes 7684
  305.2 25.6 %copy-start.15 = (f32[2,128,640]{2,1,0:T(8,128)}, f32[2,128,640]{2,1,0:T(8,128)S(1)}, u32[]{:S(2)}) copy-start(f32[2,128,640]{2,1,0:T(8,128)S(1)} %slice.367) | copy-start | bytes 1966084
  331.9 49.0 %copy-start.18 = (f32[2,64,640]{2,1,0:T(8,128)}, f32[2,64,640]{2,1,0:T(8,128)S(1)}, u32[]{:S(2)}) copy-start(f32[2,64,640]{2,1,0:T(8,128)S(1)} %slice.373) | copy-start | bytes 983044
  333.2 54.8 %copy-start.24 = (f32[2,64,640]{2,1,0:T(8,128)}, f32[2,64,640]{2,1,0:T(8,128)S(1)}, u32[]{:S(2)}) copy-start(f32[2,64,640]{2,1,0:T(8,128)S(1)} %slice.377) | copy-start | bytes 983044
  344.8 51.0 %copy-start.26 = (f32[2,32,640]{2,1,0:T(8,128)}, f32[2,32,640]{2,1,0:T(8,128)S(1)}, u32[]{:S(2)}) copy-start(f32[2,32,640]{2,1,0:T(8,128)S(1)} %slice.379) | copy-start | bytes 491524
  357.4 42.0 %copy-start.41 = (f32[2,16,640]{2,1,0:T(8,128)}, f32[2,16,640]{2,1,0:T(8,128)S(1)}, u32[]{:S(2)}) copy-start(f32[2,16,640]{2,1,0:T(8,128)S(1)} %slice.385) | copy-start | bytes 245764
  380.9 22.2 copy-start.50
  400.4 13.6 copy-start.13
  463.8 15.5 copy-start.106
  488.9 159.4 %copy-start.63 = (f32[2048]{0:T(1024)S(1)}, f32[2048]{0:T(1024)}, u32[]{:S(2)}) copy-start(f32[2048]{0:T(1024)} %param.30) | copy-start | bytes 24580
  488.9 249.0 %all-gather.7.cloned.1.call-start = ((), (), s32[]{:S(2)}) async-start(), calls=%async_computation.6 | async-start | bytes 10485760 | tf_op jit(solution)/shard_map/all_gather | solution.py:138
  650.1 177.1 %all-gather.9.cloned.1.call-start = ((), (), s32[]{:S(2)}) async-start(), calls=%async_computation.8 | async-start | bytes 10485760 | tf_op jit(solution)/shard_map/all_gather | solution.py:147
  650.7 407.2 %reduce-scatter.9.cloned.1.call-start = ((), (), s32[]{:S(2)}) async-start(), calls=%async_computation.9 | async-start | bytes 20971520 | tf_op jit(solution)/shard_map/reduce_scatter | solution.py:155
  737.9 19.4 copy-start.105
  903.9 154.0 %copy-start.64 = (f32[2048]{0:T(1024)S(1)}, f32[2048]{0:T(1024)}, u32[]{:S(2)}) copy-start(f32[2048]{0:T(1024)} %param.30) | copy-start | bytes 24580
  903.9 154.0 %copy-start.82 = (f32[2,256]{1,0:T(2,128)S(1)}, f32[2,256]{1,0:T(2,128)}, u32[]{:S(2)}) copy-start(f32[2,256]{1,0:T(2,128)} %copy-done.81) | copy-start | bytes 6148
  903.9 159.2 %copy-start.100 = (f32[2,256]{1,0:T(2,128)S(1)}, f32[2,256]{1,0:T(2,128)}, u32[]{:S(2)}) copy-start(f32[2,256]{1,0:T(2,128)} %copy-done.99) | copy-start | bytes 6148
  904.0 251.8 %all-gather.11.cloned.1.call-start = ((), (), s32[]{:S(2)}) async-start(), calls=%async_computation.10 | async-start | bytes 10485760 | tf_op jit(solution)/shard_map/all_gather | solution.py:159
  1067.9 1103.1 %all-reduce.106.cloned.1.call-start = ((), (), s32[]{:S(2)}) async-start(), calls=%async_computation.12 | async-start | bytes 54788096 | tf_op jit(solution)/shard_map/psum | solution.py:203
  1068.0 38.9 %slice-start.8 = ((s8[8388608]{0:T(1024)(128)(4,1)}), s8[4194304]{0:T(1024)(128)(4,1)S(1)}, s32[]{:S(2)}) async-start(s8[8388608]{0:T(1024)(128)(4,1)} %bitcast.162), calls=%async_computation.21 | async-start | bytes 8388608
  1068.0 38.9 %slice-start.10 = ((s8[6291456]{0:T(1024)(128)(4,1)}), s8[4194304]{0:T(1024)(128)(4,1)S(1)}, s32[]{:S(2)}) async-start(s8[6291456]{0:T(1024)(128)(4,1)} %bitcast.164), calls=%async_computation.23 | async-start | bytes 8388608
  1087.7 19.2 slice-start.9
  1087.7 19.2 slice-start.11
  1253.8 11.4 copy-start.29
  1258.1 20.0 copy-start.48
  1258.1 22.3 copy-start.54
  1262.7 31.3 %copy-start.42 = (f32[2,16,640]{2,1,0:T(8,128)S(1)}, f32[2,16,640]{2,1,0:T(8,128)}, u32[]{:S(2)}) copy-start(f32[2,16,640]{2,1,0:T(8,128)} %copy-done.41) | copy-start | bytes 245764
  1265.2 41.1 %copy-start.27 = (f32[2,32,640]{2,1,0:T(8,128)S(1)}, f32[2,32,640]{2,1,0:T(8,128)}, u32[]{:S(2)}) copy-start(f32[2,32,640]{2,1,0:T(8,128)} %copy-done.26) | copy-start | bytes 491524
  1265.2 41.1 %copy-start.39 = (f32[2,32,640]{2,1,0:T(8,128)S(1)}, f32[2,32,640]{2,1,0:T(8,128)}, u32[]{:S(2)}) copy-start(f32[2,32,640]{2,1,0:T(8,128)} %slice.383) | copy-start | bytes 491524
  1265.3 41.1 %copy-start.40 = (f32[2,32,640]{2,1,0:T(8,128)S(1)}, f32[2,32,640]{2,1,0:T(8,128)}, u32[]{:S(2)}) copy-start(f32[2,32,640]{2,1,0:T(8,128)} %slice.380) | copy-start | bytes 491524
  1320.0 21.2 copy-start.16
  1320.0 21.2 copy-start.91
  1346.8 16.1 copy-start.25
  1350.0 15.1 copy-start.90
  1391.2 17.3 copy-start.89
  1480.6 11.1 copy-start.62
  1480.6 11.1 copy-start.68
  1480.6 11.1 copy-start.75
  1480.7 11.1 copy-start.77
  1521.5 18.8 copy-start.4
  1603.5 12.7 slice-start.6
  1605.9 18.6 copy-start.33
  1633.0 627.8 %reduce-scatter.11.cloned.1.call-start = ((), (), s32[]{:S(2)}) async-start(), calls=%async_computation.11 | async-start | bytes 10485760 | tf_op jit(solution)/shard_map/reduce_scatter | solution.py:181
  1633.1 12.2 copy-start.34
  1633.1 12.2 copy-start.107
  1657.8 693.8 %reduce-scatter.7.cloned.1.call-start = ((), (), s32[]{:S(2)}) async-start(), calls=%async_computation.7 | async-start | bytes 10485760 | tf_op jit(solution)/shard_map/reduce_scatter | solution.py:143
  2182.4 12.9 slice-start.4
  2185.5 16.3 slice-start.2
  2201.9 59.0 %copy-start.73 = (f32[2048]{0:T(1024)S(1)}, f32[2048]{0:T(1024)}, u32[]{:S(2)}) copy-start(f32[2048]{0:T(1024)} %param.19) | copy-start | bytes 24580
  2201.9 59.0 %copy-start.87 = (f32[2,256]{1,0:T(2,128)S(1)}, f32[2,256]{1,0:T(2,128)}, u32[]{:S(2)}) copy-start(f32[2,256]{1,0:T(2,128)} %copy-done.86) | copy-start | bytes 6148
  2201.9 62.9 %copy-start.88 = (f32[2048]{0:T(1024)S(1)}, f32[2048]{0:T(1024)}, u32[]{:S(2)}) copy-start(f32[2048]{0:T(1024)} %get-tuple-element.22) | copy-start | bytes 24580
  2201.9 103.4 %copy-start.98 = (f32[2,256]{1,0:T(2,128)S(1)}, f32[2,256]{1,0:T(2,128)}, u32[]{:S(2)}) copy-start(f32[2,256]{1,0:T(2,128)} %copy-done.97) | copy-start | bytes 6148
  2201.9 149.8 %copy-start.65 = (f32[2048]{0:T(1024)S(1)}, f32[2048]{0:T(1024)}, u32[]{:S(2)}) copy-start(f32[2048]{0:T(1024)} %param.30) | copy-start | bytes 24580
  2201.9 149.8 %copy-start.83 = (f32[2,256]{1,0:T(2,128)S(1)}, f32[2,256]{1,0:T(2,128)}, u32[]{:S(2)}) copy-start(f32[2,256]{1,0:T(2,128)} %copy-done.81) | copy-start | bytes 6148
  2201.9 149.8 %copy-start.96 = (f32[2,256]{1,0:T(2,128)S(1)}, f32[2,256]{1,0:T(2,128)}, u32[]{:S(2)}) copy-start(f32[2,256]{1,0:T(2,128)} %copy-done.95) | copy-start | bytes 6148
  (68 other events, 321.4 us)
Sparse Core Ops, SparseCore 0:
  14.3 88.7 all-gather.4
  489.0 153.7 reduce-scatter.4
  650.2 87.6 all-gather.6
  739.6 87.6 all-gather.8
  904.1 153.7 reduce-scatter.8
  1068.1 87.6 all-gather.10
  1633.1 537.8 all-reduce.105
  2174.1 86.7 reduce-scatter.10
  2264.2 87.4 reduce-scatter.6
where the time goes:
time: 2390 us; the launch traced here: 2370 us
  waiting for transfers between devices  1130 us (47%)
  local copies, waits for them, and re-layouts  552 us (23%)
  matrix products  308 us (13%)
  other arithmetic  292 us (12%)
  blocking collectives  63.5 us (3%)
    psum x1, waiting for transfers between devices, per_device(): lax.psum(grad_w_branch.astype(jnp.bfloat16), 'dp').astype(jnp.float32)  466 us
    slice x78, local copies, waits for them, and re-layouts, core(): carried, states = lax.associative_scan(combine, (gated_a, gated_in), axis=1)  256 us
    pad x79, local copies, waits for them, and re-layouts, core(): carried, states = lax.associative_scan(combine, (gated_a, gated_in), axis=1)  222 us
    reduce_scatter x1, waiting for transfers between devices, per_device(): d_mid = lax.psum_scatter(d_mid_part, 'mp', scatter_dimension=1, tiled=True)  154 us
    reduce_scatter x1, waiting for transfers between devices, per_device(): lax.psum_scatter(project(mixed_low, w_out), 'mp', scatter_dimension=1, ti...  153 us
    dot_general x6, matrix products, project_back(): jnp.einsum('rtc,dc->rtd', left, right, preferred_element_type=jnp.float32)  117 us
    dot_general x6, matrix products, project(): jnp.einsum('rtd,dc->rtc', left, right, preferred_element_type=jnp.float32)  89.6 us
    all_gather x1, waiting for transfers between devices, per_device(): seq_in = lax.all_gather(normed_in, 'mp', axis=1, tiled=True)  88.6 us
  transfers between devices with their start and end apart: 9, of which 9 were waited for; matrix products, arithmetic and copies ran while one was open for 8% of the time, Pallas kernels for 0%

commit v1 on v0

v1 whole, which is shorter than its diff:
```python
import functools
import math

import jax
import jax.numpy as jnp
from jax import lax
from jax.experimental import pallas as pl
from jax.experimental.pallas import tpu as pltpu
from jax.sharding import PartitionSpec as P

DECAY_EXP = 8.0
EPS = 1e-06
GELU_C = math.sqrt(2.0 / math.pi)
GELU_K = 0.044715
LANES = 128
SUB = 8
VMEM_BYTES = 56 * 1024 * 1024

f32 = jnp.float32
bf16 = jnp.bfloat16


def dot_nn(left, right):
    return lax.dot_general(left, right, (((1,), (0,)), ((), ())), preferred_element_type=f32)


def dot_nt(left, right):
    return lax.dot_general(left, right, (((1,), (1,)), ((), ())), preferred_element_type=f32)


def one_minus_square(log_a, decay):
    x = 2.0 * log_a
    tail = 1.0 + x * (1.0 / 7.0)
    for k in (6.0, 5.0, 4.0, 3.0, 2.0):
        tail = 1.0 + x * (1.0 / k) * tail
    return jnp.where(x > -0.4, -x * tail, 1.0 - decay * decay)


def gelu_parts(x):
    square = x * x
    th = jnp.tanh(GELU_C * x * (1.0 + GELU_K * square))
    half = 0.5 * (1.0 + th)
    value = x * half
    slope = half + 0.5 * x * (1.0 - th * th) * (GELU_C * (1.0 + 3.0 * GELU_K * square))
    return value, slope


def row_index(shape):
    return lax.broadcasted_iota(jnp.int32, shape, 0)


def shift_down(prev, cur, k, row):
    return jnp.where(row < k, pltpu.roll(prev, k, 0), pltpu.roll(cur, k, 0))


def shift_up(cur, following, k, row):
    return jnp.where(row < SUB - k, pltpu.roll(cur, SUB - k, 0), pltpu.roll(following, SUB - k, 0))


def rec_forward_kernel(
    info, x, w_branch, w_input, taps, conv_bias, w_ga, w_gi, ga_bias, gi_bias, decay_param,
    mixed, pre, branch, conv, ga, gi, prev_state, final,
    ga_pre, gi_pre, tail, carry,
):
    step = pl.program_id(0)
    rows, width = mixed.shape[1:]
    pieces = rows // 16
    lanes = [pl.ds(at, LANES) for at in range(0, width, LANES)]
    row = row_index((SUB, LANES))

    @pl.when(step == 0)
    def _():
        tail[...] = jnp.zeros_like(tail)
        carry[...] = jnp.zeros_like(carry)

    pre[0] = dot_nn(x[0], w_input[...])

    def conv_piece(i, _):
        base = pl.multiple_of(i * 16, 16)
        for lane in lanes:
            bias = conv_bias[:, lane]
            before = tail[:, lane]
            parts = []
            for half in range(2):
                cur = pre[0, pl.ds(base + SUB * half, SUB), lane]
                total = bias + taps[0:1, lane] * cur
                for k in range(1, 4):
                    total = total + taps[k : k + 1, lane] * shift_down(before, cur, k, row)
                parts.append(total)
                before = cur
            tail[:, lane] = before
            conv[0, pl.ds(base, 16), lane] = jnp.concatenate(parts, axis=0).astype(bf16)
        return 0

    lax.fori_loop(0, pieces, conv_piece, 0)
    ga_pre[...] = dot_nn(conv[0], w_ga[...])
    gi_pre[...] = dot_nn(conv[0], w_gi[...])
    branch[0] = dot_nn(x[0], w_branch[...])
    length = info[1]

    def scan_piece(i, _):
        base = pl.multiple_of(i * 16, 16)
        start = step * rows + base
        for lane in lanes:
            rate = -DECAY_EXP * jax.nn.softplus(-decay_param[:, lane])
            conv_two = conv[0, pl.ds(base, 16), lane].astype(f32)
            state = carry[:, lane]
            outs = []
            for half in range(2):
                at = pl.ds(base + SUB * half, SUB)
                live = (row + (start + SUB * half)) < length
                gate_a = jax.nn.sigmoid(ga_pre[at, lane] + ga_bias[:, lane])
                gate_i = jax.nn.sigmoid(gi_pre[at, lane] + gi_bias[:, lane])
                ga[0, at, lane] = gate_a
                gi[0, at, lane] = gate_i
                log_a = rate * gate_a
                decay = jnp.exp(log_a)
                scaled = jnp.sqrt(one_minus_square(log_a, decay)) * gate_i * conv_two[SUB * half : SUB * half + SUB]
                mul = jnp.where(live, decay, 1.0)
                add = jnp.where(live, scaled, 0.0)
                for shift in (1, 2, 4):
                    inside = row >= shift
                    add = add + mul * jnp.where(inside, pltpu.roll(add, shift, 0), 0.0)
                    mul = mul * jnp.where(inside, pltpu.roll(mul, shift, 0), 1.0)
                states = mul * state + add
                prev_state[0, at, lane] = jnp.where(row == 0, state, pltpu.roll(states, 1, 0))
                state = jnp.broadcast_to(states[SUB - 1 : SUB], (SUB, LANES))
                value, _ = gelu_parts(branch[0, at, lane])
                outs.append(states * value)
            carry[:, lane] = state
            mixed[0, pl.ds(base, 16), lane] = jnp.concatenate(outs, axis=0).astype(bf16)
        return 0

    lax.fori_loop(0, pieces, scan_piece, 0)
    final[...] = carry[...]


def rec_backward_kernel(
    info, d_resid, w_out, w_branch, w_input, taps, w_ga, w_gi, decay_param,
    pre, branch, conv, ga, gi, prev_state,
    d_in, d_branch, d_input, d_ga, d_gi, sums,
    d_mixed, d_conv, flow, later,
):
    step = pl.program_id(0)
    rows, width = d_branch.shape[1:]
    pieces = rows // 16
    lanes = [pl.ds(at, LANES) for at in range(0, width, LANES)]
    row = row_index((SUB, LANES))
    first = (pl.num_programs(0) - 1 - step) * rows
    length = info[1]

    @pl.when(step == 0)
    def _():
        flow[...] = jnp.zeros_like(flow)
        later[...] = jnp.zeros_like(later)
        sums[...] = jnp.zeros_like(sums)

    d_mixed[...] = dot_nt(d_resid[0], w_out[...])

    def scan_piece(j, _):
        base = pl.multiple_of((pieces - 1 - j) * 16, 16)
        for lane in lanes:
            rate = -DECAY_EXP * jax.nn.softplus(-decay_param[:, lane])
            conv_two = conv[0, pl.ds(base, 16), lane].astype(f32)
            carried = flow[:, lane]
            outs = [None, None]
            sum_log = sums[0, :, lane]
            for half in (1, 0):
                at = pl.ds(base + SUB * half, SUB)
                live = (row + (first + base + SUB * half)) < length
                conv_val = conv_two[SUB * half : SUB * half + SUB]
                gate_a = ga[0, at, lane]
                gate_i = gi[0, at, lane]
                before = prev_state[0, at, lane]
                d_mix = d_mixed[at, lane]
                log_a = rate * gate_a
                decay = jnp.exp(log_a)
                space = one_minus_square(log_a, decay)
                inverse = lax.rsqrt(jnp.maximum(space, 1e-37))
                root = space * inverse
                gated = gate_i * conv_val
                mul = jnp.where(live, decay, 1.0)
                states = mul * before + jnp.where(live, root * gated, 0.0)
                value, slope = gelu_parts(branch[0, at, lane])
                d_br = d_mix * states * slope
                direct = d_mix * value
                add = mul * direct
                for shift in (1, 2, 4):
                    inside = row < SUB - shift
                    add = add + mul * jnp.where(inside, pltpu.roll(add, SUB - shift, 0), 0.0)
                    mul = mul * jnp.where(inside, pltpu.roll(mul, SUB - shift, 0), 1.0)
                moved = add + mul * carried
                d_state = direct + jnp.where(row == SUB - 1, carried, pltpu.roll(moved, SUB - 1, 0))
                carried = jnp.broadcast_to(moved[0:1], (SUB, LANES))
                d_state = jnp.where(live, d_state, 0.0)
                d_log = d_state * decay * (before - gated * decay * inverse)
                sum_log = sum_log + d_log * gate_a
                d_gate_a = d_log * rate * gate_a * (1.0 - gate_a)
                d_rooted = d_state * root
                d_conv_rec = d_rooted * gate_i
                d_gate_i = d_rooted * conv_val * gate_i * (1.0 - gate_i)
                d_conv[at, lane] = d_conv_rec
                outs[half] = (d_br, d_gate_a, d_gate_i)
            flow[:, lane] = carried
            sums[0, :, lane] = sum_log
            for target, which in ((d_branch, 0), (d_ga, 1), (d_gi, 2)):
                both = jnp.concatenate([outs[0][which], outs[1][which]], axis=0).astype(bf16)
                target[0, pl.ds(base, 16), lane] = both
                if which > 0:
                    wide = both.astype(f32)
                    sums[which, :, lane] += wide[:SUB] + wide[SUB:]
        return 0

    lax.fori_loop(0, pieces, scan_piece, 0)
    d_conv[...] += dot_nt(d_ga[0], w_ga[...]) + dot_nt(d_gi[0], w_gi[...])

    def conv_piece(j, _):
        base = pl.multiple_of((pieces - 1 - j) * 16, 16)
        for lane in lanes:
            following = later[:, lane]
            totals = [None, None]
            tap_sums = [sums[3 + k, :, lane] for k in range(5)]
            for half in (1, 0):
                at = pl.ds(base + SUB * half, SUB)
                cur = d_conv[at, lane]
                seen = pre[0, at, lane]
                tap_sums[0] = tap_sums[0] + cur
                tap_sums[1] = tap_sums[1] + cur * seen
                total = taps[0:1, lane] * cur
                for k in range(1, 4):
                    ahead = shift_up(cur, following, k, row)
                    tap_sums[1 + k] = tap_sums[1 + k] + ahead * seen
                    total = total + taps[k : k + 1, lane] * ahead
                totals[half] = total
                following = cur
            later[:, lane] = following
            for k in range(5):
                sums[3 + k, :, lane] = tap_sums[k]
            d_input[0, pl.ds(base, 16), lane] = jnp.concatenate(totals, axis=0).astype(bf16)
        return 0

    lax.fori_loop(0, pieces, conv_piece, 0)
    d_in[0] = (dot_nt(d_branch[0], w_branch[...]) + dot_nt(d_input[0], w_input[...])).astype(bf16)


def mlp_kernel(x, cot, w_gate, w_up, w_down, hidden, d_gate, d_up, gate_pre, up_pre, d_hidden):
    rows = x.shape[1]
    gate_pre[...] = dot_nn(x[0], w_gate[...])
    up_pre[...] = dot_nn(x[0], w_up[...])
    d_hidden[...] = dot_nt(cot[0], w_down[...])

    def piece(i, _):
        at = pl.ds(pl.multiple_of(i * 16, 16), 16)
        for lane in range(0, hidden.shape[2], LANES):
            lane = pl.ds(lane, LANES)
            up = up_pre[at, lane]
            back = d_hidden[at, lane]
            value, slope = gelu_parts(gate_pre[at, lane])
            hidden[0, at, lane] = (value * up).astype(bf16)
            d_gate[0, at, lane] = (back * up * slope).astype(bf16)
            d_up[0, at, lane] = (back * value).astype(bf16)
        return 0

    lax.fori_loop(0, rows // 16, piece, 0)


def whole(array):
    zeros = (0,) * array.ndim
    return pl.BlockSpec(array.shape, lambda *_: zeros, pipeline_mode=pl.Buffered(1))


def rec_forward(info, x, params):
    blocks, rows, model = x.shape
    width = params[0].shape[1]

    def at(step, info):
        return (step ^ info[0], 0, 0)

    wide = pl.BlockSpec((1, rows, width), at)
    out = jax.ShapeDtypeStruct((blocks, rows, width), f32)
    low = jax.ShapeDtypeStruct((blocks, rows, width), bf16)
    return pl.pallas_call(
        rec_forward_kernel,
        out_shape=(low, out, out, low, out, out, out, jax.ShapeDtypeStruct((SUB, width), f32)),
        grid_spec=pltpu.PrefetchScalarGridSpec(
            num_scalar_prefetch=1,
            grid=(blocks,),
            in_specs=[pl.BlockSpec((1, rows, model), at)] + [whole(p) for p in params],
            out_specs=(wide,) * 7 + (pl.BlockSpec((SUB, width), lambda *_: (0, 0)),),
            scratch_shapes=[
                pltpu.VMEM((rows, width), f32),
                pltpu.VMEM((rows, width), f32),
                pltpu.VMEM((SUB, width), f32),
                pltpu.VMEM((SUB, width), f32),
            ],
        ),
        compiler_params=pltpu.CompilerParams(vmem_limit_bytes=VMEM_BYTES),
        cost_estimate=pl.CostEstimate(
            flops=20 * blocks * rows * model * width, bytes_accessed=blocks * rows * (2 * model + 24 * width), transcendentals=0
        ),
        name="rec_forward",
    )(info, x, *params)


def rec_backward(info, d_resid, params, saved):
    blocks, rows, model = d_resid.shape
    width = saved[0].shape[2]

    def at(step, info):
        return ((blocks - 1 - step) ^ info[0], 0, 0)

    wide = pl.BlockSpec((1, rows, width), at)
    long = pl.BlockSpec((1, rows, model), at)
    low = jax.ShapeDtypeStruct((blocks, rows, width), bf16)
    return pl.pallas_call(
        rec_backward_kernel,
        out_shape=(
            jax.ShapeDtypeStruct((blocks, rows, model), bf16),
            low,
            low,
            low,
            low,
            jax.ShapeDtypeStruct((8, SUB, width), f32),
        ),
        grid_spec=pltpu.PrefetchScalarGridSpec(
            num_scalar_prefetch=1,
            grid=(blocks,),
            in_specs=[long] + [whole(p) for p in params] + [wide] * len(saved),
            out_specs=(long, wide, wide, wide, wide, pl.BlockSpec((8, SUB, width), lambda *_: (0, 0, 0))),
            scratch_shapes=[
                pltpu.VMEM((rows, width), f32),
                pltpu.VMEM((rows, width), f32),
                pltpu.VMEM((SUB, width), f32),
                pltpu.VMEM((SUB, width), f32),
            ],
        ),
        compiler_params=pltpu.CompilerParams(vmem_limit_bytes=VMEM_BYTES),
        cost_estimate=pl.CostEstimate(
            flops=30 * blocks * rows * model * width, bytes_accessed=blocks * rows * (4 * model + 32 * width), transcendentals=0
        ),
        name="rec_backward",
    )(info, d_resid, *params, *saved)


def mlp_core(x, cot, w_gate, w_up, w_down):
    blocks, rows, model = x.shape
    units = w_gate.shape[1]
    tile = max(t for t in range(LANES, 512 + 1, LANES) if units % t == 0)
    low = jax.ShapeDtypeStruct((blocks, rows, units), bf16)
    long = pl.BlockSpec((1, rows, model), lambda j, r: (r, 0, 0))
    column = pl.BlockSpec((model, tile), lambda j, r: (0, j))
    part = pl.BlockSpec((1, rows, tile), lambda j, r: (r, 0, j))
    return pl.pallas_call(
        mlp_kernel,
        out_shape=(low, low, low),
        grid=(units // tile, blocks),
        in_specs=[long, long, column, column, pl.BlockSpec((tile, model), lambda j, r: (j, 0))],
        out_specs=(part, part, part),
        scratch_shapes=[pltpu.VMEM((rows, tile), f32)] * 3,
        compiler_params=pltpu.CompilerParams(vmem_limit_bytes=VMEM_BYTES),
        cost_estimate=pl.CostEstimate(
            flops=9 * blocks * rows * model * units, bytes_accessed=blocks * rows * 16 * model, transcendentals=0
        ),
        name="mlp_core",
    )(x, cot, w_gate, w_up, w_down)


def swap(value, axis, bit):
    size = lax.axis_size(axis)
    return lax.ppermute(value, axis, [(i, i ^ bit) for i in range(size)])


def gather(shard):
    size = lax.axis_size("mp")
    if size != 4:
        return jnp.stack([shard] + [swap(shard, "mp", r) for r in range(1, size)])
    half = shard.shape[0] // 2
    by_x = swap(shard, "mp", 1)
    by_y = swap(shard, "mp", 2)
    far = jnp.concatenate([swap(by_x[:half], "mp", 2), swap(by_y[half:], "mp", 1)], axis=0)
    return jnp.stack([shard, by_x, by_y, far])


def scatter(parts):
    size = lax.axis_size("mp")
    if size != 4:
        total = parts[0].astype(f32)
        for r in range(1, size):
            total = total + swap(parts[r], "mp", r).astype(f32)
        return total
    half = parts.shape[1] // 2
    from_x = swap(parts[3, :half], "mp", 1)
    from_y = swap(parts[3, half:], "mp", 2)
    for_y = jnp.concatenate(
        [(parts[2, :half].astype(f32) + from_x.astype(f32)).astype(bf16), parts[2, half:]], axis=0
    )
    for_x = jnp.concatenate(
        [parts[1, :half], (parts[1, half:].astype(f32) + from_y.astype(f32)).astype(bf16)], axis=0
    )
    return parts[0].astype(f32) + swap(for_y, "mp", 2).astype(f32) + swap(for_x, "mp", 1).astype(f32)


def add_low(left, right):
    return (left.astype(f32) + right.astype(f32)).astype(bf16)


def sum_over_dp(part):
    size = lax.axis_size("dp")
    rows = part.shape[0]
    if size != 8 or rows % 64 != 0:
        return lax.psum(part, "dp").astype(f32)
    me = lax.axis_index("dp")
    core = me % 2
    chip = me // 2
    outer = jnp.where((chip == 0) | (chip == 3), 0, 1)

    def split(value, mine):
        half = value.shape[0] // 2
        keep = lax.dynamic_slice_in_dim(value, mine * half, half, 0)
        give = lax.dynamic_slice_in_dim(value, (1 - mine) * half, half, 0)
        return keep, give

    def join(kept, other, mine):
        return jnp.concatenate(
            [jnp.where(mine == 0, kept, other), jnp.where(mine == 0, other, kept)], axis=0
        )

    keep, give = split(part, core)
    total = add_low(keep, swap(give, "dp", 1))
    keep, give = split(total, outer)
    total = add_low(keep, swap(give, "dp", 2))
    total = add_low(total, lax.ppermute(total, "dp", [(i, (3 - i // 2) * 2 + i % 2) for i in range(8)]))
    total = join(total, swap(total, "dp", 2), outer)
    return join(total, swap(total, "dp", 1), core).astype(f32)


def normalize(values, gain):
    return values * lax.rsqrt(jnp.mean(values * values, axis=-1, keepdims=True) + EPS) * gain


def normalize_back(values, gain, grad):
    inverse = lax.rsqrt(jnp.mean(values * values, axis=-1, keepdims=True) + EPS)
    scaled = grad * gain
    unit = values * inverse
    return inverse * (scaled - unit * jnp.mean(scaled * unit, axis=-1, keepdims=True))


def dense_blocks(weight):
    blocks, inner, outer = weight.shape
    rows = [
        jnp.pad(weight[n], ((0, 0), (n * outer, (blocks - 1 - n) * outer))) for n in range(blocks)
    ]
    return jnp.concatenate(rows, axis=0)


def diagonal_blocks(full, blocks):
    inner = full.shape[0] // blocks
    return jnp.stack([full[n * inner : (n + 1) * inner, n * inner : (n + 1) * inner] for n in range(blocks)])


def weight_grad(lefts, rights):
    total = None
    for left, right in zip(lefts, rights):
        term = jnp.einsum("rtd,rtc->dc", left, right, preferred_element_type=f32)
        total = term if total is None else total + term
    return total


def per_device(
    block_in,
    norm1_gain,
    w_branch,
    w_input,
    conv_weight,
    conv_bias,
    gate_a_weight,
    gate_a_bias,
    gate_i_weight,
    gate_i_bias,
    decay_param,
    w_out,
    norm2_gain,
    w_gate,
    w_up,
    w_down,
    lengths,
    cotangent,
):
    count = block_in.shape[0]
    nblocks = gate_a_weight.shape[0]
    true_width = w_branch.shape[1]
    extra = -true_width % LANES
    me = lax.axis_index("mp")

    def pad_last(value):
        return jnp.pad(value, [(0, 0)] * (value.ndim - 1) + [(0, extra)]) if extra else value

    def line(value):
        return pad_last(value)[None, :]

    wb, wi = pad_last(w_branch), pad_last(w_input)
    wo = jnp.pad(w_out, ((0, extra), (0, 0))) if extra else w_out
    w_ga, w_gi = dense_blocks(gate_a_weight), dense_blocks(gate_i_weight)
    if extra:
        w_ga, w_gi = (jnp.pad(v, ((0, extra), (0, extra))) for v in (w_ga, w_gi))
    taps = pad_last(conv_weight)
    decay_line = line(decay_param)
    forward_params = (
        wb, wi, taps, line(conv_bias), w_ga, w_gi, line(gate_a_bias), line(gate_i_bias), decay_line
    )
    backward_params = (wo, wb, wi, taps, w_ga, w_gi, decay_line)
    seqs = range(count)
    infos = [jnp.stack([me.astype(jnp.int32), lengths[s]]) for s in seqs]

    resid = [block_in[s].astype(f32) for s in seqs]
    seq_in = [gather(normalize(resid[s], norm1_gain).astype(bf16)) for s in seqs]
    cot_seq = [gather(cotangent[s]) for s in seqs]

    mixed, saved, finals, resid_mid, seq_mid = [], [], [], [], []
    for s in seqs:
        out = rec_forward(infos[s], seq_in[s], forward_params)
        mixed.append(out[0])
        saved.append(out[1:7])
        finals.append(out[7][:1, :true_width])
        part = jnp.einsum("rtc,cd->rtd", out[0], wo, preferred_element_type=f32).astype(bf16)
        resid_mid.append(resid[s] + scatter(part))
        seq_mid.append(gather(normalize(resid_mid[s], norm2_gain).astype(bf16)))

    hidden, d_gate, d_up, d_resid, d_resid_seq, mlp_part = [], [], [], [], [], []
    for s in seqs:
        low_hidden, low_gate, low_up = mlp_core(seq_mid[s], cot_seq[s], w_gate, w_up, w_down)
        hidden.append(low_hidden)
        d_gate.append(low_gate)
        d_up.append(low_up)
        part = jnp.einsum("rtc,dc->rtd", low_gate, w_gate, preferred_element_type=f32)
        part = (part + jnp.einsum("rtc,dc->rtd", low_up, w_up, preferred_element_type=f32)).astype(bf16)
        d_mid = scatter(part)
        d_resid.append(cotangent[s].astype(f32) + normalize_back(resid_mid[s], norm2_gain, d_mid))
        d_resid_seq.append(gather(d_resid[s].astype(bf16)))
        mlp_part.append(jnp.einsum("rtc,cd->rtd", low_hidden, w_down, preferred_element_type=f32).astype(bf16))

    block_out = jnp.stack([(resid_mid[s] + scatter(mlp_part[s])).astype(bf16) for s in seqs])

    grad_w_down = sum_over_dp(weight_grad(hidden, cot_seq).astype(bf16))
    grad_w_gate = sum_over_dp(weight_grad(seq_mid, d_gate).astype(bf16))
    grad_w_up = sum_over_dp(weight_grad(seq_mid, d_up).astype(bf16))

    d_branch, d_input, d_ga, d_gi, sums, input_grad = [], [], [], [], [], []
    for s in seqs:
        out = rec_backward(infos[s], d_resid_seq[s], backward_params, saved[s])
        d_branch.append(out[1])
        d_input.append(out[2])
        d_ga.append(out[3])
        d_gi.append(out[4])
        sums.append(out[5])
        d_in = scatter(out[0])
        input_grad.append((d_resid[s] + normalize_back(resid[s], norm1_gain, d_in)).astype(bf16))
    input_grad = jnp.stack(input_grad)

    grad_w_out = sum_over_dp(weight_grad(mixed, d_resid_seq).astype(bf16)[:true_width])
    grad_w_branch = sum_over_dp(weight_grad(seq_in, d_branch).astype(bf16)[:, :true_width])
    grad_w_input = sum_over_dp(weight_grad(seq_in, d_input).astype(bf16)[:, :true_width])

    conv = [part[2] for part in saved]
    full_ga = diagonal_blocks(weight_grad(conv, d_ga)[:true_width, :true_width], nblocks)
    full_gi = diagonal_blocks(weight_grad(conv, d_gi)[:true_width, :true_width], nblocks)
    vectors = jnp.sum(sum(sums), axis=1)[:, :true_width]
    decay_grad = vectors[0] * DECAY_EXP * jax.nn.sigmoid(-decay_param)
    vectors = jnp.concatenate([decay_grad[None, :], vectors[1:]], axis=0)
    small = jnp.concatenate([full_ga.reshape(-1), full_gi.reshape(-1), vectors.reshape(-1)]).astype(bf16)
    used = small.shape[0]
    columns = 640
    padded = -(-used // (64 * columns)) * 64 * columns
    small = sum_over_dp(jnp.pad(small, (0, padded - used)).reshape(-1, columns)).reshape(-1)[:used]
    many = full_ga.size
    grad_gate_a_weight = small[:many].reshape(full_ga.shape)
    grad_gate_i_weight = small[many : 2 * many].reshape(full_gi.shape)
    vectors = small[2 * many :].reshape(8, true_width)

    gain1 = jnp.sum(w_branch.astype(f32) * grad_w_branch + w_input.astype(f32) * grad_w_input, axis=1) / norm1_gain
    gain2 = jnp.sum(w_gate.astype(f32) * grad_w_gate + w_up.astype(f32) * grad_w_up, axis=1) / norm2_gain
    gains = jnp.stack([gain1, gain2])
    if lax.axis_size("mp") == 4:
        gains = gains + swap(gains, "mp", 1)
        gains = gains + swap(gains, "mp", 2)
    else:
        gains = lax.psum(gains, "mp")

    return (
        block_out,
        input_grad,
        gains[0],
        grad_w_branch,
        grad_w_input,
        vectors[4:8],
        vectors[3],
        grad_gate_a_weight,
        vectors[1],
        grad_gate_i_weight,
        vectors[2],
        vectors[0],
        grad_w_out,
        gains[1],
        grad_w_gate,
        grad_w_up,
        grad_w_down,
        jnp.concatenate(finals, axis=0),
    )


def solution(mesh):
    placed = (
        P("dp", "mp", None),
        P(),
        P(None, "mp"),
        P(None, "mp"),
        P(None, "mp"),
        P("mp"),
        P("mp", None, None),
        P("mp"),
        P("mp", None, None),
        P("mp"),
        P("mp"),
        P("mp", None),
        P(),
        P(None, "mp"),
        P(None, "mp"),
        P("mp", None),
        P("dp"),
        P("dp", "mp", None),
    )
    return jax.shard_map(
        per_device,
        mesh=mesh,
        in_specs=placed,
        out_specs=(
            P("dp", "mp", None),
            P("dp", "mp", None),
            P(),
            P(None, "mp"),
            P(None, "mp"),
            P(None, "mp"),
            P("mp"),
            P("mp", None, None),
            P("mp"),
            P("mp", None, None),
            P("mp"),
            P("mp"),
            P("mp", None),
            P(),
            P(None, "mp"),
            P(None, "mp"),
            P("mp", None),
            P("dp", "mp"),
        ),
        check_vma=False,
    )
```

time: 2390 us -> 1420 us (0.59)
  waiting for transfers between devices: 1130 us -> 588 us
  local copies, waits for them, and re-layouts: 552 us -> 61.8 us
  Pallas kernels: 0 us -> 211 us
  starting transfers between devices: 0.77 us -> 186 us
  matrix products: 308 us -> 186 us
  other arithmetic: 292 us -> 171 us
  blocking collectives: 63.5 us -> 0 us
    ppermute x0 -> x101, waiting for transfers between devices: none -> 588 us  [the longest x94 407 us: swap(): return lax.ppermute(value, axis, [(i, i ^ bit) for i in range(size)])]
    psum x1 -> x0, waiting for transfers between devices: 466 us -> none  [per_device(): lax.psum(grad_w_branch.astype(jnp.bfloat16), 'dp').astype(jnp.float32)]
    reduce_scatter x4 -> x0, waiting for transfers between devices: 406 us -> none  [the longest x1 154 us: per_device(): d_mid = lax.psum_scatter(d_mid_part, 'mp', scatter_dimension=1, tiled=True)]
    all_gather x4 -> x0, waiting for transfers between devices: 261 us -> none  [the longest x1 88.6 us: per_device(): seq_in = lax.all_gather(normed_in, 'mp', axis=1, tiled=True)]
    slice x79 -> x23, local copies, waits for them, and re-layouts: 256 us -> 15.4 us  [the longest x8 6.35 us: gather(): by_x[:half]]
    pad x79 -> x0, local copies, waits for them, and re-layouts: 222 us -> none  [core(): carried, states = lax.associative_scan(combine, (gated_a, gated_in), axis=1)]
    pallas_call x0 -> x6, Pallas kernels: none -> 211 us  [the longest x2 81.1 us: rec_backward(): pl.pallas_call(rec_backward_kernel, out_shape=(jax.ShapeDtypeStruct((bloc...]
    ppermute x0 -> x101, starting transfers between devices: none -> 186 us  [the longest x94 173 us: swap(): return lax.ppermute(value, axis, [(i, i ^ bit) for i in range(size)])]
  transfers between devices with their start and end apart: 9 -> 101, of which waited for: 9 -> 41; matrix products, arithmetic and copies ran while one was open for 8% -> 29% of each run, Pallas kernels for 0% -> 15%
where the time goes in v1:
time: 1420 us; the launch traced here: 1410 us
  waiting for transfers between devices  588 us (41%)
  Pallas kernels  211 us (15%)
  starting transfers between devices  186 us (13%)
  matrix products  186 us (13%)
  other arithmetic  171 us (12%)
  local copies, waits for them, and re-layouts  61.8 us (4%)
    ppermute x94, waiting for transfers between devices, swap(): return lax.ppermute(value, axis, [(i, i ^ bit) for i in range(size)])  407 us
    ppermute x7, waiting for transfers between devices, sum_over_dp(): lax.ppermute(total, 'dp', [(i, (3 - i // 2) * 2 + i % 2) for i in range(8)])  181 us
    ppermute x94, starting transfers between devices, swap(): return lax.ppermute(value, axis, [(i, i ^ bit) for i in range(size)])  173 us
    dot_general x16, matrix products, weight_grad(): term = jnp.einsum('rtd,rtc->dc', left, right, preferred_element_type=f32)  114 us
    pallas_call x2, Pallas kernels, rec_backward(): pl.pallas_call(rec_backward_kernel, out_shape=(jax.ShapeDtypeStruct((bloc...  81.1 us
    pallas_call x2, Pallas kernels, mlp_core(): pl.pallas_call(mlp_kernel, out_shape=(low, low, low), grid=(units // tile...  72.8 us
    pallas_call x2, Pallas kernels, rec_forward(): pl.pallas_call(rec_forward_kernel, out_shape=(low, out, out, low, out, ou...  57.2 us
    another operation x16, other arithmetic, gather(): return jnp.stack([shard, by_x, by_y, far])  29.3 us
  transfers between devices with their start and end apart: 101, of which 41 were waited for; matrix products, arithmetic and copies ran while one was open for 29% of the time, Pallas kernels for 15%

profile of v1, /device:TPU:9, one launch (start us, length us, event | category | flops | bytes accessed | tf_op | source)
XLA Modules:
  0.0 1407.4 jit_solution(1422887779533056052)
XLA Ops:
  20.4 9.6 collective-permute-done.1
  34.2 18.2 %collective-permute-done.21 = bf16[256,2048]{1,0:T(8,128)(2,1)} collective-permute-done((bf16[256,2048]{1,0:T(8,128)(2,1)}, bf16[256,2048]{1,0:T(8,128)(2,1)}, u32[]{:S(2)}, u32[]{:S(2)}) %collective-permute-start.21) | collective-permute-done | bytes 1048608 | tf_op jit(solution)/shard_map/ppermute | solution.py:370
  57.9 6.6 collective-permute-done.3
  67.9 28.5 %rec_forward.2 = (bf16[4,256,640]{2,1,0:T(8,128)(2,1)}, f32[4,256,640]{2,1,0:T(8,128)}, f32[4,256,640]{2,1,0:T(8,128)}, bf16[4,256,640]{2,1,0:T(8,128)(2,1)}, f3...) custom-call(s32[2]{0:T(128)} %pad_add_fusion.info, ...), custom_call_target="tpu_custom_call" | custom-call | flops 26843545600 | bytes 19922944 | tf_op jit(solution)/shard_map/rec_forward/pallas_call | solution.py:282
  96.4 5.6 convolution_convert_fusion.1
  110.7 28.7 %rec_forward.3 = (bf16[4,256,640]{2,1,0:T(8,128)(2,1)}, f32[4,256,640]{2,1,0:T(8,128)}, f32[4,256,640]{2,1,0:T(8,128)}, bf16[4,256,640]{2,1,0:T(8,128)(2,1)}, f3...) custom-call(s32[2]{0:T(128)} %pad_add_fusion.1.info, ...), custom_call_target="tpu_custom_call" | custom-call | flops 26843545600 | bytes 19922944 | tf_op jit(solution)/shard_map/rec_forward/pallas_call | solution.py:282
  160.2 17.1 %collective-permute-done.7 = bf16[256,2048]{1,0:T(8,128)(2,1)S(1)} collective-permute-done((bf16[256,2048]{1,0:T(8,128)(2,1)S(1)}, bf16[256,2048]{1,0:T(8,128)(2,1)S(1)}, u32[]{:S(2)}, u32[]{:S(2)}) %collective-permute-start.7) | collective-permute-done | bytes 1048608 | tf_op jit(solution)/shard_map/ppermute | solution.py:370
  178.6 21.3 %collective-permute-done.27 = bf16[256,2048]{1,0:T(8,128)(2,1)S(1)} collective-permute-done((bf16[256,2048]{1,0:T(8,128)(2,1)S(1)}, bf16[256,2048]{1,0:T(8,128)(2,1)S(1)}, u32[]{:S(2)}, u32[]{:S(2)}) %collective-permute-start.27) | collective-permute-done | bytes 1048608 | tf_op jit(solution)/shard_map/ppermute | solution.py:370
  205.0 17.3 %collective-permute-done.13 = bf16[256,2048]{1,0:T(8,128)(2,1)S(1)} collective-permute-done((bf16[256,2048]{1,0:T(8,128)(2,1)S(1)}, bf16[256,2048]{1,0:T(8,128)(2,1)S(1)}, u32[]{:S(2)}, u32[]{:S(2)}) %collective-permute-start.13) | collective-permute-done | bytes 1048608 | tf_op jit(solution)/shard_map/ppermute | solution.py:370
  224.7 20.2 %collective-permute-done.33 = bf16[256,2048]{1,0:T(8,128)(2,1)S(1)} collective-permute-done((bf16[256,2048]{1,0:T(8,128)(2,1)}, bf16[256,2048]{1,0:T(8,128)(2,1)S(1)}, u32[]{:S(2)}, u32[]{:S(2)}) %collective-permute-start.33) | collective-permute-done | bytes 1048608 | tf_op jit(solution)/shard_map/ppermute | solution.py:370
  247.9 8.3 collective-permute-done.15
  257.1 21.5 %collective-permute-done.14 = bf16[128,2048]{1,0:T(8,128)(2,1)} collective-permute-done((bf16[128,2048]{1,0:T(8,128)(2,1)S(1)}, bf16[128,2048]{1,0:T(8,128)(2,1)}, u32[]{:S(2)}, u32[]{:S(2)}) %collective-permute-start.14) | collective-permute-done | bytes 524320 | tf_op jit(solution)/shard_map/ppermute | solution.py:370
  296.2 16.1 %collective-permute-done.29 = bf16[256,2048]{1,0:T(8,128)(2,1)S(1)} collective-permute-done((bf16[256,2048]{1,0:T(8,128)(2,1)S(1)}, bf16[256,2048]{1,0:T(8,128)(2,1)S(1)}, u32[]{:S(2)}, u32[]{:S(2)}) %collective-permute-start.29) | collective-permute-done | bytes 1048608 | tf_op jit(solution)/shard_map/ppermute | solution.py:370
  316.2 7.3 collective-permute-done.11
  328.3 36.5 %mlp_core.2 = (bf16[4,256,1536]{2,1,0:T(8,128)(2,1)}, bf16[4,256,1536]{2,1,0:T(8,128)(2,1)}, bf16[4,256,1536]{2,1,0:T(8,128)(2,1)}) custom-call(bf16[4,256,2048]{2,1,0:T(8,128)(2,1)} %pad_maximum_fusion.1.x, bf16[4,256,2048]{2,1,0:T(8,128)(2,1)} %pad_maximum_fusion.2.cot, bf16[2048,1536]{1,0:T(8,128)(2,1)} %w_gate.3, bf16[2048,1536]{1,0:T(8,128)(2,1)} %w_up.3, ...), custom_call_target="tpu_custom_call" | custom-call | flops 28991029248 | bytes 33554432 | tf_op jit(solution)/shard_map/mlp_core/pallas_call | solution.py:353
  364.8 11.0 fusion.5
  375.8 12.0 fusion.122
  387.8 12.0 fusion.123
  399.8 10.3 add_convert_fusion.1
  410.1 11.9 fusion.121
  422.0 8.2 fusion.18
  437.3 36.4 %mlp_core.3 = (bf16[4,256,1536]{2,1,0:T(8,128)(2,1)}, bf16[4,256,1536]{2,1,0:T(8,128)(2,1)}, bf16[4,256,1536]{2,1,0:T(8,128)(2,1)}) custom-call(bf16[4,256,2048]{2,1,0:T(8,128)(2,1)} %pad_maximum_fusion.4.x, bf16[4,256,2048]{2,1,0:T(8,128)(2,1)} %pad_maximum_fusion.5.cot, bf16[2048,1536]{1,0:T(8,128)(2,1)} %w_gate.3, bf16[2048,1536]{1,0:T(8,128)(2,1)} %w_up.3, ...), custom_call_target="tpu_custom_call" | custom-call | flops 28991029248 | bytes 33554432 | tf_op jit(solution)/shard_map/mlp_core/pallas_call | solution.py:353
  473.6 9.9 fusion.3
  483.6 8.9 add_convert_fusion
  497.0 12.5 fusion.2
  509.5 10.7 fusion.1
  520.3 12.4 fusion.21
  550.3 8.8 collective-permute-done.43
  562.2 7.6 collective-permute-done.41
  569.8 23.5 %collective-permute-start.74 = (bf16[1024,1536]{1,0:T(8,128)(2,1)}, bf16[1024,1536]{1,0:T(8,128)(2,1)}, u32[]{:S(2)}, u32[]{:S(2)}) collective-permute-start(bf16[1024,1536]{1,0:T(8,128)(2,1)} %constant_dynamic-slice_fusion.9), channel_id=1, source_target_pairs={{0,4},{4,0},{8,12},{12,8},{16,20},{20,16},{24,28},{28,24},{1,5},{5... | collective-permute-start | bytes 9437192 | tf_op jit(solution)/shard_map/ppermute | solution.py:370
  594.7 9.4 collective-permute-done.19
  604.1 10.7 collective-permute-done.17
  619.2 7.4 collective-permute-done.39
  627.5 9.8 collective-permute-done.37
  637.3 5.9 fusion.124
  646.1 11.8 fusion
  665.4 15.9 %collective-permute-done.57 = bf16[256,2048]{1,0:T(8,128)(2,1)S(1)} collective-permute-done((bf16[256,2048]{1,0:T(8,128)(2,1)S(1)}, bf16[256,2048]{1,0:T(8,128)(2,1)S(1)}, u32[]{:S(2)}, u32[]{:S(2)}) %collective-permute-start.57) | collective-permute-done | bytes 1048608 | tf_op jit(solution)/shard_map/ppermute | solution.py:370
  681.3 18.4 %collective-permute-start.79 = (bf16[1024,1536]{1,0:T(8,128)(2,1)}, bf16[1024,1536]{1,0:T(8,128)(2,1)}, u32[]{:S(2)}, u32[]{:S(2)}) collective-permute-start(bf16[1024,1536]{1,0:T(8,128)(2,1)} %constant_dynamic-slice_fusion.7), channel_id=1, source_target_pairs={{0,4},{4,0},{8,12},{12,8},{16,20},{20,16},{24,28},{28,24},{1,5},{5... | collective-permute-start | bytes 9437192 | tf_op jit(solution)/shard_map/ppermute | solution.py:370
  704.9 40.3 %rec_backward.2 = (bf16[4,256,2048]{2,1,0:T(8,128)(2,1)}, bf16[4,256,640]{2,1,0:T(8,128)(2,1)}, bf16[4,256,640]{2,1,0:T(8,128)(2,1)}, bf16[4,256,640]{2,1,0:T(8,...) custom-call(s32[2]{0:T(128)} %pad_add_fusion.info, bf16[4,256,2048]{2,1,0:T(8,128)(2,1)} %pad_maximum_fusion.6.d_resid, ...), custom_call_target="tpu_custom_call" | custom-call | flops 40265318400 | bytes 29360128 | tf_op jit(solution)/shard_map/rec_backward/pallas_call | solution.py:315
  752.2 40.7 %rec_backward.3 = (bf16[4,256,2048]{2,1,0:T(8,128)(2,1)}, bf16[4,256,640]{2,1,0:T(8,128)(2,1)}, bf16[4,256,640]{2,1,0:T(8,128)(2,1)}, bf16[4,256,640]{2,1,0:T(8,...) custom-call(s32[2]{0:T(128)} %pad_add_fusion.1.info, bf16[4,256,2048]{2,1,0:T(8,128)(2,1)} %pad_maximum_fusion.7.d_resid, ...), custom_call_target="tpu_custom_call" | custom-call | flops 40265318400 | bytes 29360128 | tf_op jit(solution)/shard_map/rec_backward/pallas_call | solution.py:315
  817.3 5.7 fusion.133
  839.8 7.8 fusion.17
  847.7 7.8 fusion.16
  859.0 7.8 collective-permute-start.86
  922.1 15.4 %collective-permute-done.63 = bf16[256,2048]{1,0:T(8,128)(2,1)S(1)} collective-permute-done((bf16[256,2048]{1,0:T(8,128)(2,1)}, bf16[256,2048]{1,0:T(8,128)(2,1)S(1)}, u32[]{:S(2)}, u32[]{:S(2)}) %collective-permute-start.63) | collective-permute-done | bytes 1048608 | tf_op jit(solution)/shard_map/ppermute | solution.py:370
  953.6 26.8 %collective-permute-done.80 = bf16[512,1536]{1,0:T(8,128)(2,1)S(1)} collective-permute-done((bf16[512,1536]{1,0:T(8,128)(2,1)}, bf16[512,1536]{1,0:T(8,128)(2,1)S(1)}, u32[]{:S(2)}, u32[]{:S(2)}) %collective-permute-start.80) | collective-permute-done | bytes 1572896 | tf_op jit(solution)/shard_map/ppermute | solution.py:370
  982.8 31.3 %collective-permute-done.97 = bf16[384,2048]{1,0:T(8,128)(2,1)S(1)} collective-permute-done((bf16[384,2048]{1,0:T(8,128)(2,1)}, bf16[384,2048]{1,0:T(8,128)(2,1)S(1)}, u32[]{:S(2)}, u32[]{:S(2)}) %collective-permute-start.97) | collective-permute-done | bytes 1572896 | tf_op jit(solution)/shard_map/ppermute | solution.py:370
  1016.7 11.4 collective-permute-done.65
  1030.4 11.8 collective-permute-done.70
  1044.5 11.8 collective-permute-done.92
  1060.0 120.4 %collective-permute-done.66 = bf16[512,640]{1,0:T(8,128)(2,1)S(1)} collective-permute-done((bf16[512,640]{1,0:T(8,128)(2,1)S(1)}, bf16[512,640]{1,0:T(8,128)(2,1)S(1)}, u32[]{:S(2)}, u32[]{:S(2)}) %collective-permute-start.66) | collective-permute-done | bytes 655392 | tf_op jit(solution)/shard_map/ppermute | solution.py:432
  1181.8 36.5 %collective-permute-done.71 = bf16[512,640]{1,0:T(8,128)(2,1)S(1)} collective-permute-done((bf16[512,640]{1,0:T(8,128)(2,1)S(1)}, bf16[512,640]{1,0:T(8,128)(2,1)S(1)}, u32[]{:S(2)}, u32[]{:S(2)}) %collective-permute-start.71) | collective-permute-done | bytes 655392 | tf_op jit(solution)/shard_map/ppermute | solution.py:432
  1218.5 13.9 collective-permute-done.93
  1236.8 7.4 collective-permute-done.72
  1244.2 14.5 %collective-permute-start.68 = (bf16[1024,640]{1,0:T(8,128)(2,1)S(1)}, bf16[1024,640]{1,0:T(8,128)(2,1)S(1)}, u32[]{:S(2)}, u32[]{:S(2)}) collective-permute-start(bf16[1024,640]{1,0:T(8,128)(2,1)S(1)} %pad_maximum_fusion.13), channel_id=1, source_target_pairs={{0,4},{4,0},{8,12},{12,8},{16,20},{20,16},{24,28},{28,24},{1,5},{5... | collective-permute-start | bytes 3932168 | tf_op jit(solution)/shard_map/ppermute | solution.py:370
  1258.9 7.2 collective-permute-done.98
  1277.0 14.8 %collective-permute-done.77 = bf16[512,1536]{1,0:T(8,128)(2,1)S(1)} collective-permute-done((bf16[512,1536]{1,0:T(8,128)(2,1)S(1)}, bf16[512,1536]{1,0:T(8,128)(2,1)S(1)}, u32[]{:S(2)}, u32[]{:S(2)}) %collective-permute-start.77) | collective-permute-done | bytes 1572896 | tf_op jit(solution)/shard_map/ppermute | solution.py:370
  1293.9 14.6 %collective-permute-start.78 = (bf16[1024,1536]{1,0:T(8,128)(2,1)}, bf16[1024,1536]{1,0:T(8,128)(2,1)}, u32[]{:S(2)}, u32[]{:S(2)}) collective-permute-start(bf16[1024,1536]{1,0:T(8,128)(2,1)} %pad_maximum_fusion.8), channel_id=1, source_target_pairs={{0,4},{4,0},{8,12},{12,8},{16,20},{20,16},{24,28},{28,24},{1,5},{5... | collective-permute-start | bytes 9437192 | tf_op jit(solution)/shard_map/ppermute | solution.py:370
  1308.5 17.1 %collective-permute-done.82 = bf16[512,1536]{1,0:T(8,128)(2,1)S(1)} collective-permute-done((bf16[512,1536]{1,0:T(8,128)(2,1)S(1)}, bf16[512,1536]{1,0:T(8,128)(2,1)S(1)}, u32[]{:S(2)}, u32[]{:S(2)}) %collective-permute-start.82) | collective-permute-done | bytes 1572896 | tf_op jit(solution)/shard_map/ppermute | solution.py:370
  1327.6 14.6 %collective-permute-start.83 = (bf16[1024,1536]{1,0:T(8,128)(2,1)}, bf16[1024,1536]{1,0:T(8,128)(2,1)}, u32[]{:S(2)}, u32[]{:S(2)}) collective-permute-start(bf16[1024,1536]{1,0:T(8,128)(2,1)} %pad_maximum_fusion.9), channel_id=1, source_target_pairs={{0,4},{4,0},{8,12},{12,8},{16,20},{20,16},{24,28},{28,24},{1,5},{5... | collective-permute-start | bytes 9437192 | tf_op jit(solution)/shard_map/ppermute | solution.py:370
  1344.5 9.4 add_reduce_fusion.1
  1362.8 7.5 collective-permute-start.100
  1380.2 14.5 %add_reduce_fusion = (f32[2048]{0:T(1024)S(1)}, f32[2048,1536]{1,0:T(8,128)}, f32[2048,1536]{1,0:T(8,128)}) fusion(bf16[2048,1536]{1,0:T(8,128)(2,1)} %w_up.3, bf16[2048,1536]{1,0:T(8,128)(2,1)} %w_gate.3, bf16[1024,1536]{1,0:T(8,128)(2,1)S(1)} %get-tuple-element.115, bf16[1024,1536]{1,0:T(8,128)(2,1)S(1)} %get-tuple-element.114, ...), kind=kLoop, calls=%fused_computation.6 | loop fusion | flops 44038144 | bytes 50339840 | tf_op jit(solution)/shard_map/reduce_sum | solution.py:581
  1400.0 6.4 maximum_convert_fusion.2
  (629 shorter events, 339.1 us)
Async XLA Ops:
  8.0 44.4 %collective-permute-start.21 = (bf16[256,2048]{1,0:T(8,128)(2,1)}, bf16[256,2048]{1,0:T(8,128)(2,1)}, u32[]{:S(2)}, u32[]{:S(2)}) collective-permute-start(bf16[256,2048]{1,0:T(8,128)(2,1)} %get-tuple-element.183), channel_id=1, source_target_pairs={{0,2},{1,3},{2,0},{3,1},{4,6},{5,7},{6,4},{7,5},{8,10},{9,11},{10,... | collective-permute-start | bytes 3145736 | tf_op jit(solution)/shard_map/ppermute | solution.py:370
  8.2 46.5 %collective-permute-start.20 = (bf16[256,2048]{1,0:T(8,128)(2,1)}, bf16[256,2048]{1,0:T(8,128)(2,1)}, u32[]{:S(2)}, u32[]{:S(2)}) collective-permute-start(bf16[256,2048]{1,0:T(8,128)(2,1)} %get-tuple-element.183), channel_id=1, source_target_pairs={{0,1},{1,0},{2,3},{3,2},{4,5},{5,4},{6,7},{7,6},{8,9},{9,8},{10,11... | collective-permute-start | bytes 3145736 | tf_op jit(solution)/shard_map/ppermute | solution.py:370
  30.0 34.5 %collective-permute-start.3 = (bf16[128,2048]{1,0:T(8,128)(2,1)S(1)}, bf16[128,2048]{1,0:T(8,128)(2,1)S(1)}, u32[]{:S(2)}, u32[]{:S(2)}) collective-permute-start(bf16[128,2048]{1,0:T(8,128)(2,1)S(1)} %slice.455), channel_id=1, source_target_pairs={{0,1},{1,0},{2,3},{3,2},{4,5},{5,4},{6,7},{7,6},{8,9},{9,8},{10,11... | collective-permute-start | bytes 1572872 | tf_op jit(solution)/shard_map/ppermute | solution.py:370
  53.5 51.4 %collective-permute-start.23 = (bf16[128,2048]{1,0:T(8,128)(2,1)S(1)}, bf16[128,2048]{1,0:T(8,128)(2,1)}, u32[]{:S(2)}, u32[]{:S(2)}) collective-permute-start(bf16[128,2048]{1,0:T(8,128)(2,1)S(1)} %slice.475), channel_id=1, source_target_pairs={{0,1},{1,0},{2,3},{3,2},{4,5},{5,4},{6,7},{7,6},{8,9},{9,8},{10,11... | collective-permute-start | bytes 1572872 | tf_op jit(solution)/shard_map/ppermute | solution.py:370
  56.6 48.3 %collective-permute-start.22 = (bf16[128,2048]{1,0:T(8,128)(2,1)}, bf16[128,2048]{1,0:T(8,128)(2,1)}, u32[]{:S(2)}, u32[]{:S(2)}) collective-permute-start(bf16[128,2048]{1,0:T(8,128)(2,1)} %slice.474), channel_id=1, source_target_pairs={{0,2},{1,3},{2,0},{3,1},{4,6},{5,7},{6,4},{7,5},{8,10},{9,11},{10,... | collective-permute-start | bytes 1572872 | tf_op jit(solution)/shard_map/ppermute | solution.py:370
  103.3 43.3 %collective-permute-start.4 = (bf16[128,2048]{1,0:T(8,128)(2,1)}, bf16[128,2048]{1,0:T(8,128)(2,1)}, u32[]{:S(2)}, u32[]{:S(2)}) collective-permute-start(bf16[128,2048]{1,0:T(8,128)(2,1)} %get-tuple-element.148), channel_id=1, source_target_pairs={{0,1},{1,0},{2,3},{3,2},{4,5},{5,4},{6,7},{7,6},{8,9},{9,8},{10,11... | collective-permute-start | bytes 1572872 | tf_op jit(solution)/shard_map/ppermute | solution.py:370
  104.5 42.1 %collective-permute-start.6 = (bf16[128,2048]{1,0:T(8,128)(2,1)}, bf16[128,2048]{1,0:T(8,128)(2,1)}, u32[]{:S(2)}, u32[]{:S(2)}) collective-permute-start(bf16[128,2048]{1,0:T(8,128)(2,1)} %get-tuple-element.149), channel_id=1, source_target_pairs={{0,2},{1,3},{2,0},{3,1},{4,6},{5,7},{6,4},{7,5},{8,10},{9,11},{10,... | collective-permute-start | bytes 1572872 | tf_op jit(solution)/shard_map/ppermute | solution.py:370
  155.4 44.5 %collective-permute-start.27 = (bf16[256,2048]{1,0:T(8,128)(2,1)S(1)}, bf16[256,2048]{1,0:T(8,128)(2,1)S(1)}, u32[]{:S(2)}, u32[]{:S(2)}) collective-permute-start(bf16[256,2048]{1,0:T(8,128)(2,1)S(1)} %pad_maximum_fusion.21), channel_id=1, source_target_pairs={{0,1},{1,0},{2,3},{3,2},{4,5},{5,4},{6,7},{7,6},{8,9},{9,8},{10,11... | collective-permute-start | bytes 3145736 | tf_op jit(solution)/shard_map/ppermute | solution.py:370
  156.7 43.4 %collective-permute-start.25 = (bf16[256,2048]{1,0:T(8,128)(2,1)S(1)}, bf16[256,2048]{1,0:T(8,128)(2,1)S(1)}, u32[]{:S(2)}, u32[]{:S(2)}) collective-permute-start(bf16[256,2048]{1,0:T(8,128)(2,1)S(1)} %pad_maximum_fusion.20), channel_id=1, source_target_pairs={{0,2},{1,3},{2,0},{3,1},{4,6},{5,7},{6,4},{7,5},{8,10},{9,11},{10,... | collective-permute-start | bytes 3145736 | tf_op jit(solution)/shard_map/ppermute | solution.py:370
  159.7 62.6 %collective-permute-start.13 = (bf16[256,2048]{1,0:T(8,128)(2,1)S(1)}, bf16[256,2048]{1,0:T(8,128)(2,1)S(1)}, u32[]{:S(2)}, u32[]{:S(2)}) collective-permute-start(bf16[256,2048]{1,0:T(8,128)(2,1)S(1)} %get-tuple-element.187), channel_id=1, source_target_pairs={{0,2},{1,3},{2,0},{3,1},{4,6},{5,7},{6,4},{7,5},{8,10},{9,11},{10,... | collective-permute-start | bytes 3145736 | tf_op jit(solution)/shard_map/ppermute | solution.py:370
  177.4 46.2 %collective-permute-start.12 = (bf16[256,2048]{1,0:T(8,128)(2,1)S(1)}, bf16[256,2048]{1,0:T(8,128)(2,1)S(1)}, u32[]{:S(2)}, u32[]{:S(2)}) collective-permute-start(bf16[256,2048]{1,0:T(8,128)(2,1)S(1)} %get-tuple-element.187), channel_id=1, source_target_pairs={{0,1},{1,0},{2,3},{3,2},{4,5},{5,4},{6,7},{7,6},{8,9},{9,8},{10,11... | collective-permute-start | bytes 3145736 | tf_op jit(solution)/shard_map/ppermute | solution.py:370
  177.7 67.2 %collective-permute-start.33 = (bf16[256,2048]{1,0:T(8,128)(2,1)}, bf16[256,2048]{1,0:T(8,128)(2,1)S(1)}, u32[]{:S(2)}, u32[]{:S(2)}) collective-permute-start(bf16[256,2048]{1,0:T(8,128)(2,1)} %get-tuple-element.188), channel_id=1, source_target_pairs={{0,2},{1,3},{2,0},{3,1},{4,6},{5,7},{6,4},{7,5},{8,10},{9,11},{10,... | collective-permute-start | bytes 3145736 | tf_op jit(solution)/shard_map/ppermute | solution.py:370
  199.9 46.3 %collective-permute-start.32 = (bf16[256,2048]{1,0:T(8,128)(2,1)}, bf16[256,2048]{1,0:T(8,128)(2,1)}, u32[]{:S(2)}, u32[]{:S(2)}) collective-permute-start(bf16[256,2048]{1,0:T(8,128)(2,1)} %get-tuple-element.188), channel_id=1, source_target_pairs={{0,1},{1,0},{2,3},{3,2},{4,5},{5,4},{6,7},{7,6},{8,9},{9,8},{10,11... | collective-permute-start | bytes 3145736 | tf_op jit(solution)/shard_map/ppermute | solution.py:370
  204.1 76.7 %collective-permute-start.9 = (bf16[256,2048]{1,0:T(8,128)(2,1)}, bf16[256,2048]{1,0:T(8,128)(2,1)}, u32[]{:S(2)}, u32[]{:S(2)}) collective-permute-start(bf16[256,2048]{1,0:T(8,128)(2,1)} %get-tuple-element.222), channel_id=1, source_target_pairs={{0,2},{1,3},{2,0},{3,1},{4,6},{5,7},{6,4},{7,5},{8,10},{9,11},{10,... | collective-permute-start | bytes 3145736 | tf_op jit(solution)/shard_map/ppermute | solution.py:370
  223.7 55.0 %collective-permute-start.14 = (bf16[128,2048]{1,0:T(8,128)(2,1)S(1)}, bf16[128,2048]{1,0:T(8,128)(2,1)}, u32[]{:S(2)}, u32[]{:S(2)}) collective-permute-start(bf16[128,2048]{1,0:T(8,128)(2,1)S(1)} %slice.465), channel_id=1, source_target_pairs={{0,2},{1,3},{2,0},{3,1},{4,6},{5,7},{6,4},{7,5},{8,10},{9,11},{10,... | collective-permute-start | bytes 1572872 | tf_op jit(solution)/shard_map/ppermute | solution.py:370
  244.9 41.7 %collective-permute-start.8 = (bf16[256,2048]{1,0:T(8,128)(2,1)}, bf16[256,2048]{1,0:T(8,128)(2,1)}, u32[]{:S(2)}, u32[]{:S(2)}) collective-permute-start(bf16[256,2048]{1,0:T(8,128)(2,1)} %get-tuple-element.222), channel_id=1, source_target_pairs={{0,1},{1,0},{2,3},{3,2},{4,5},{5,4},{6,7},{7,6},{8,9},{9,8},{10,11... | collective-permute-start | bytes 3145736 | tf_op jit(solution)/shard_map/ppermute | solution.py:370
  246.2 43.5 %collective-permute-start.35 = (bf16[128,2048]{1,0:T(8,128)(2,1)S(1)}, bf16[128,2048]{1,0:T(8,128)(2,1)S(1)}, u32[]{:S(2)}, u32[]{:S(2)}) collective-permute-start(bf16[128,2048]{1,0:T(8,128)(2,1)S(1)} %slice.486), channel_id=1, source_target_pairs={{0,1},{1,0},{2,3},{3,2},{4,5},{5,4},{6,7},{7,6},{8,9},{9,8},{10,11... | collective-permute-start | bytes 1572872 | tf_op jit(solution)/shard_map/ppermute | solution.py:370
  256.1 34.5 %collective-permute-start.34 = (bf16[128,2048]{1,0:T(8,128)(2,1)S(1)}, bf16[128,2048]{1,0:T(8,128)(2,1)S(1)}, u32[]{:S(2)}, u32[]{:S(2)}) collective-permute-start(bf16[128,2048]{1,0:T(8,128)(2,1)S(1)} %slice.485), channel_id=1, source_target_pairs={{0,2},{1,3},{2,0},{3,1},{4,6},{5,7},{6,4},{7,5},{8,10},{9,11},{10,... | collective-permute-start | bytes 1572872 | tf_op jit(solution)/shard_map/ppermute | solution.py:370
  286.7 36.8 %collective-permute-start.11 = (bf16[128,2048]{1,0:T(8,128)(2,1)S(1)}, bf16[128,2048]{1,0:T(8,128)(2,1)S(1)}, u32[]{:S(2)}, u32[]{:S(2)}) collective-permute-start(bf16[128,2048]{1,0:T(8,128)(2,1)S(1)} %slice.464), channel_id=1, source_target_pairs={{0,1},{1,0},{2,3},{3,2},{4,5},{5,4},{6,7},{7,6},{8,9},{9,8},{10,11... | collective-permute-start | bytes 1572872 | tf_op jit(solution)/shard_map/ppermute | solution.py:370
  313.1 120.5 %collective-permute-start.31 = (bf16[128,2048]{1,0:T(8,128)(2,1)}, bf16[128,2048]{1,0:T(8,128)(2,1)}, u32[]{:S(2)}, u32[]{:S(2)}) collective-permute-start(bf16[128,2048]{1,0:T(8,128)(2,1)} %slice.484), channel_id=1, source_target_pairs={{0,1},{1,0},{2,3},{3,2},{4,5},{5,4},{6,7},{7,6},{8,9},{9,8},{10,11... | collective-permute-start | bytes 1572872 | tf_op jit(solution)/shard_map/ppermute | solution.py:370
  315.2 118.4 %collective-permute-start.30 = (bf16[128,2048]{1,0:T(8,128)(2,1)}, bf16[128,2048]{1,0:T(8,128)(2,1)}, u32[]{:S(2)}, u32[]{:S(2)}) collective-permute-start(bf16[128,2048]{1,0:T(8,128)(2,1)} %slice.483), channel_id=1, source_target_pairs={{0,2},{1,3},{2,0},{3,1},{4,6},{5,7},{6,4},{7,5},{8,10},{9,11},{10,... | collective-permute-start | bytes 1572872 | tf_op jit(solution)/shard_map/ppermute | solution.py:370
  431.5 101.3 %collective-permute-start.40 = (bf16[128,2048]{1,0:T(8,128)(2,1)}, bf16[128,2048]{1,0:T(8,128)(2,1)}, u32[]{:S(2)}, u32[]{:S(2)}) collective-permute-start(bf16[128,2048]{1,0:T(8,128)(2,1)} %get-tuple-element.136), channel_id=1, source_target_pairs={{0,1},{1,0},{2,3},{3,2},{4,5},{5,4},{6,7},{7,6},{8,9},{9,8},{10,11... | collective-permute-start | bytes 1572872 | tf_op jit(solution)/shard_map/ppermute | solution.py:370
  432.7 102.0 %collective-permute-start.42 = (bf16[128,2048]{1,0:T(8,128)(2,1)}, bf16[128,2048]{1,0:T(8,128)(2,1)}, u32[]{:S(2)}, u32[]{:S(2)}) collective-permute-start(bf16[128,2048]{1,0:T(8,128)(2,1)} %get-tuple-element.137), channel_id=1, source_target_pairs={{0,2},{1,3},{2,0},{3,1},{4,6},{5,7},{6,4},{7,5},{8,10},{9,11},{10,... | collective-permute-start | bytes 1572872 | tf_op jit(solution)/shard_map/ppermute | solution.py:370
  493.6 43.3 %collective-permute-start.52 = (bf16[128,2048]{1,0:T(8,128)(2,1)}, bf16[128,2048]{1,0:T(8,128)(2,1)}, u32[]{:S(2)}, u32[]{:S(2)}) collective-permute-start(bf16[128,2048]{1,0:T(8,128)(2,1)} %get-tuple-element.130), channel_id=1, source_target_pairs={{0,1},{1,0},{2,3},{3,2},{4,5},{5,4},{6,7},{7,6},{8,9},{9,8},{10,11... | collective-permute-start | bytes 1572872 | tf_op jit(solution)/shard_map/ppermute | solution.py:370
  493.9 44.1 %collective-permute-start.54 = (bf16[128,2048]{1,0:T(8,128)(2,1)}, bf16[128,2048]{1,0:T(8,128)(2,1)}, u32[]{:S(2)}, u32[]{:S(2)}) collective-permute-start(bf16[128,2048]{1,0:T(8,128)(2,1)} %get-tuple-element.131), channel_id=1, source_target_pairs={{0,2},{1,3},{2,0},{3,1},{4,6},{5,7},{6,4},{7,5},{8,10},{9,11},{10,... | collective-permute-start | bytes 1572872 | tf_op jit(solution)/shard_map/ppermute | solution.py:370
  496.6 45.6 %collective-permute-start.16 = (bf16[128,2048]{1,0:T(8,128)(2,1)}, bf16[128,2048]{1,0:T(8,128)(2,1)}, u32[]{:S(2)}, u32[]{:S(2)}) collective-permute-start(bf16[128,2048]{1,0:T(8,128)(2,1)} %get-tuple-element.142), channel_id=1, source_target_pairs={{0,1},{1,0},{2,3},{3,2},{4,5},{5,4},{6,7},{7,6},{8,9},{9,8},{10,11... | collective-permute-start | bytes 1572872 | tf_op jit(solution)/shard_map/ppermute | solution.py:370
  543.1 50.1 %collective-permute-start.55 = (bf16[256,2048]{1,0:T(8,128)(2,1)}, bf16[256,2048]{1,0:T(8,128)(2,1)S(1)}, u32[]{:S(2)}, u32[]{:S(2)}) collective-permute-start(bf16[256,2048]{1,0:T(8,128)(2,1)} %pad_maximum_fusion.29), channel_id=1, source_target_pairs={{0,1},{1,0},{2,3},{3,2},{4,5},{5,4},{6,7},{7,6},{8,9},{9,8},{10,11... | collective-permute-start | bytes 3145736 | tf_op jit(solution)/shard_map/ppermute | solution.py:370
  548.7 45.2 %collective-permute-start.53 = (bf16[256,2048]{1,0:T(8,128)(2,1)}, bf16[256,2048]{1,0:T(8,128)(2,1)}, u32[]{:S(2)}, u32[]{:S(2)}) collective-permute-start(bf16[256,2048]{1,0:T(8,128)(2,1)} %pad_maximum_fusion.28), channel_id=1, source_target_pairs={{0,2},{1,3},{2,0},{3,1},{4,6},{5,7},{6,4},{7,5},{8,10},{9,11},{10,... | collective-permute-start | bytes 3145736 | tf_op jit(solution)/shard_map/ppermute | solution.py:370
  549.7 54.4 %collective-permute-start.19 = (bf16[256,2048]{1,0:T(8,128)(2,1)}, bf16[256,2048]{1,0:T(8,128)(2,1)}, u32[]{:S(2)}, u32[]{:S(2)}) collective-permute-start(bf16[256,2048]{1,0:T(8,128)(2,1)} %pad_maximum_fusion.19), channel_id=1, source_target_pairs={{0,1},{1,0},{2,3},{3,2},{4,5},{5,4},{6,7},{7,6},{8,9},{9,8},{10,11... | collective-permute-start | bytes 3145736 | tf_op jit(solution)/shard_map/ppermute | solution.py:370
  559.1 55.8 %collective-permute-start.17 = (bf16[256,2048]{1,0:T(8,128)(2,1)}, bf16[256,2048]{1,0:T(8,128)(2,1)}, u32[]{:S(2)}, u32[]{:S(2)}) collective-permute-start(bf16[256,2048]{1,0:T(8,128)(2,1)} %pad_maximum_fusion.18), channel_id=1, source_target_pairs={{0,2},{1,3},{2,0},{3,1},{4,6},{5,7},{6,4},{7,5},{8,10},{9,11},{10,... | collective-permute-start | bytes 3145736 | tf_op jit(solution)/shard_map/ppermute | solution.py:370
  569.8 227.0 %collective-permute-start.74 = (bf16[1024,1536]{1,0:T(8,128)(2,1)}, bf16[1024,1536]{1,0:T(8,128)(2,1)}, u32[]{:S(2)}, u32[]{:S(2)}) collective-permute-start(bf16[1024,1536]{1,0:T(8,128)(2,1)} %constant_dynamic-slice_fusion.9), channel_id=1, source_target_pairs={{0,4},{4,0},{8,12},{12,8},{16,20},{20,16},{24,28},{28,24},{1,5},{5... | collective-permute-start | bytes 9437192 | tf_op jit(solution)/shard_map/ppermute | solution.py:370
  593.9 43.4 %collective-permute-start.37 = (bf16[256,2048]{1,0:T(8,128)(2,1)S(1)}, bf16[256,2048]{1,0:T(8,128)(2,1)}, u32[]{:S(2)}, u32[]{:S(2)}) collective-permute-start(bf16[256,2048]{1,0:T(8,128)(2,1)S(1)} %pad_maximum_fusion.22), channel_id=1, source_target_pairs={{0,2},{1,3},{2,0},{3,1},{4,6},{5,7},{6,4},{7,5},{8,10},{9,11},{10,... | collective-permute-start | bytes 3145736 | tf_op jit(solution)/shard_map/ppermute | solution.py:370
  644.9 36.4 %collective-permute-start.57 = (bf16[256,2048]{1,0:T(8,128)(2,1)S(1)}, bf16[256,2048]{1,0:T(8,128)(2,1)S(1)}, u32[]{:S(2)}, u32[]{:S(2)}) collective-permute-start(bf16[256,2048]{1,0:T(8,128)(2,1)S(1)} %get-tuple-element.178), channel_id=1, source_target_pairs={{0,2},{1,3},{2,0},{3,1},{4,6},{5,7},{6,4},{7,5},{8,10},{9,11},{10,... | collective-permute-start | bytes 3145736 | tf_op jit(solution)/shard_map/ppermute | solution.py:370
  646.1 53.6 %collective-permute-start.56 = (bf16[256,2048]{1,0:T(8,128)(2,1)S(1)}, bf16[256,2048]{1,0:T(8,128)(2,1)S(1)}, u32[]{:S(2)}, u32[]{:S(2)}) collective-permute-start(bf16[256,2048]{1,0:T(8,128)(2,1)S(1)} %get-tuple-element.178), channel_id=1, source_target_pairs={{0,1},{1,0},{2,3},{3,2},{4,5},{5,4},{6,7},{7,6},{8,9},{9,8},{10,11... | collective-permute-start | bytes 3145736 | tf_op jit(solution)/shard_map/ppermute | solution.py:370
  660.1 39.8 %collective-permute-start.47 = (bf16[128,2048]{1,0:T(8,128)(2,1)S(1)}, bf16[128,2048]{1,0:T(8,128)(2,1)S(1)}, u32[]{:S(2)}, u32[]{:S(2)}) collective-permute-start(bf16[128,2048]{1,0:T(8,128)(2,1)S(1)} %slice.502), channel_id=1, source_target_pairs={{0,1},{1,0},{2,3},{3,2},{4,5},{5,4},{6,7},{7,6},{8,9},{9,8},{10,11... | collective-permute-start | bytes 1572872 | tf_op jit(solution)/shard_map/ppermute | solution.py:370
  661.7 39.4 %collective-permute-start.46 = (bf16[128,2048]{1,0:T(8,128)(2,1)S(1)}, bf16[128,2048]{1,0:T(8,128)(2,1)S(1)}, u32[]{:S(2)}, u32[]{:S(2)}) collective-permute-start(bf16[128,2048]{1,0:T(8,128)(2,1)S(1)} %slice.501), channel_id=1, source_target_pairs={{0,2},{1,3},{2,0},{3,1},{4,6},{5,7},{6,4},{7,5},{8,10},{9,11},{10,... | collective-permute-start | bytes 1572872 | tf_op jit(solution)/shard_map/ppermute | solution.py:370
  681.3 125.3 %collective-permute-start.79 = (bf16[1024,1536]{1,0:T(8,128)(2,1)}, bf16[1024,1536]{1,0:T(8,128)(2,1)}, u32[]{:S(2)}, u32[]{:S(2)}) collective-permute-start(bf16[1024,1536]{1,0:T(8,128)(2,1)} %constant_dynamic-slice_fusion.7), channel_id=1, source_target_pairs={{0,4},{4,0},{8,12},{12,8},{16,20},{20,16},{24,28},{28,24},{1,5},{5... | collective-permute-start | bytes 9437192 | tf_op jit(solution)/shard_map/ppermute | solution.py:370
  699.8 159.2 %collective-permute-start.96 = (bf16[768,2048]{1,0:T(8,128)(2,1)}, bf16[768,2048]{1,0:T(8,128)(2,1)}, u32[]{:S(2)}, u32[]{:S(2)}) collective-permute-start(bf16[768,2048]{1,0:T(8,128)(2,1)} %constant_dynamic-slice_fusion.1), channel_id=1, source_target_pairs={{0,4},{4,0},{8,12},{12,8},{16,20},{20,16},{24,28},{28,24},{1,5},{5... | collective-permute-start | bytes 9437192 | tf_op jit(solution)/shard_map/ppermute | solution.py:370
  699.9 48.4 %collective-permute-start.59 = (bf16[128,2048]{1,0:T(8,128)(2,1)S(1)}, bf16[128,2048]{1,0:T(8,128)(2,1)S(1)}, u32[]{:S(2)}, u32[]{:S(2)}) collective-permute-start(bf16[128,2048]{1,0:T(8,128)(2,1)S(1)} %slice.511), channel_id=1, source_target_pairs={{0,1},{1,0},{2,3},{3,2},{4,5},{5,4},{6,7},{7,6},{8,9},{9,8},{10,11... | collective-permute-start | bytes 1572872 | tf_op jit(solution)/shard_map/ppermute | solution.py:370
  701.0 48.1 %collective-permute-start.58 = (bf16[128,2048]{1,0:T(8,128)(2,1)S(1)}, bf16[128,2048]{1,0:T(8,128)(2,1)S(1)}, u32[]{:S(2)}, u32[]{:S(2)}) collective-permute-start(bf16[128,2048]{1,0:T(8,128)(2,1)S(1)} %slice.510), channel_id=1, source_target_pairs={{0,2},{1,3},{2,0},{3,1},{4,6},{5,7},{6,4},{7,5},{8,10},{9,11},{10,... | collective-permute-start | bytes 1572872 | tf_op jit(solution)/shard_map/ppermute | solution.py:370
  748.3 136.7 %collective-permute-start.48 = (bf16[128,2048]{1,0:T(8,128)(2,1)}, bf16[128,2048]{1,0:T(8,128)(2,1)}, u32[]{:S(2)}, u32[]{:S(2)}) collective-permute-start(bf16[128,2048]{1,0:T(8,128)(2,1)} %get-tuple-element.118), channel_id=1, source_target_pairs={{0,1},{1,0},{2,3},{3,2},{4,5},{5,4},{6,7},{7,6},{8,9},{9,8},{10,11... | collective-permute-start | bytes 1572872 | tf_op jit(solution)/shard_map/ppermute | solution.py:370
  749.2 136.0 %collective-permute-start.50 = (bf16[128,2048]{1,0:T(8,128)(2,1)}, bf16[128,2048]{1,0:T(8,128)(2,1)}, u32[]{:S(2)}, u32[]{:S(2)}) collective-permute-start(bf16[128,2048]{1,0:T(8,128)(2,1)} %get-tuple-element.119), channel_id=1, source_target_pairs={{0,2},{1,3},{2,0},{3,1},{4,6},{5,7},{6,4},{7,5},{8,10},{9,11},{10,... | collective-permute-start | bytes 1572872 | tf_op jit(solution)/shard_map/ppermute | solution.py:370
  796.8 92.9 %collective-permute-start.60 = (bf16[128,2048]{1,0:T(8,128)(2,1)}, bf16[128,2048]{1,0:T(8,128)(2,1)}, u32[]{:S(2)}, u32[]{:S(2)}) collective-permute-start(bf16[128,2048]{1,0:T(8,128)(2,1)} %get-tuple-element.124), channel_id=1, source_target_pairs={{0,1},{1,0},{2,3},{3,2},{4,5},{5,4},{6,7},{7,6},{8,9},{9,8},{10,11... | collective-permute-start | bytes 1572872 | tf_op jit(solution)/shard_map/ppermute | solution.py:370
  806.6 83.8 %collective-permute-start.62 = (bf16[128,2048]{1,0:T(8,128)(2,1)}, bf16[128,2048]{1,0:T(8,128)(2,1)}, u32[]{:S(2)}, u32[]{:S(2)}) collective-permute-start(bf16[128,2048]{1,0:T(8,128)(2,1)} %get-tuple-element.125), channel_id=1, source_target_pairs={{0,2},{1,3},{2,0},{3,1},{4,6},{5,7},{6,4},{7,5},{8,10},{9,11},{10,... | collective-permute-start | bytes 1572872 | tf_op jit(solution)/shard_map/ppermute | solution.py:370
  909.7 34.1 %collective-permute-start.61 = (bf16[256,2048]{1,0:T(8,128)(2,1)}, bf16[256,2048]{1,0:T(8,128)(2,1)S(1)}, u32[]{:S(2)}, u32[]{:S(2)}) collective-permute-start(bf16[256,2048]{1,0:T(8,128)(2,1)} %pad_maximum_fusion.30), channel_id=1, source_target_pairs={{0,2},{1,3},{2,0},{3,1},{4,6},{5,7},{6,4},{7,5},{8,10},{9,11},{10,... | collective-permute-start | bytes 3145736 | tf_op jit(solution)/shard_map/ppermute | solution.py:370
  911.7 35.8 %collective-permute-start.75 = (bf16[512,1536]{1,0:T(8,128)(2,1)}, bf16[512,1536]{1,0:T(8,128)(2,1)S(1)}, u32[]{:S(2)}, u32[]{:S(2)}) collective-permute-start(bf16[512,1536]{1,0:T(8,128)(2,1)} %constant_dynamic-slice_fusion.8), channel_id=1, source_target_pairs={{0,8},{4,12},{8,0},{12,4},{16,24},{20,28},{24,16},{28,20},{1,9},{5... | collective-permute-start | bytes 4718600 | tf_op jit(solution)/shard_map/ppermute | solution.py:370
  915.1 65.3 %collective-permute-start.80 = (bf16[512,1536]{1,0:T(8,128)(2,1)}, bf16[512,1536]{1,0:T(8,128)(2,1)S(1)}, u32[]{:S(2)}, u32[]{:S(2)}) collective-permute-start(bf16[512,1536]{1,0:T(8,128)(2,1)} %constant_dynamic-slice_fusion.6), channel_id=1, source_target_pairs={{0,8},{4,12},{8,0},{12,4},{16,24},{20,28},{24,16},{28,20},{1,9},{5... | collective-permute-start | bytes 4718600 | tf_op jit(solution)/shard_map/ppermute | solution.py:370
  921.5 92.6 %collective-permute-start.97 = (bf16[384,2048]{1,0:T(8,128)(2,1)}, bf16[384,2048]{1,0:T(8,128)(2,1)S(1)}, u32[]{:S(2)}, u32[]{:S(2)}) collective-permute-start(bf16[384,2048]{1,0:T(8,128)(2,1)} %constant_dynamic-slice_fusion), channel_id=1, source_target_pairs={{0,8},{4,12},{8,0},{12,4},{16,24},{20,28},{24,16},{28,20},{1,9},{5... | collective-permute-start | bytes 4718600 | tf_op jit(solution)/shard_map/ppermute | solution.py:370
  937.4 90.7 %collective-permute-start.65 = (bf16[512,640]{1,0:T(8,128)(2,1)S(1)}, bf16[512,640]{1,0:T(8,128)(2,1)S(1)}, u32[]{:S(2)}, u32[]{:S(2)}) collective-permute-start(bf16[512,640]{1,0:T(8,128)(2,1)S(1)} %constant_dynamic-slice_fusion.12), channel_id=1, source_target_pairs={{0,8},{4,12},{8,0},{12,4},{16,24},{20,28},{24,16},{28,20},{1,9},{5... | collective-permute-start | bytes 1966088 | tf_op jit(solution)/shard_map/ppermute | solution.py:370
  943.8 98.4 %collective-permute-start.70 = (bf16[512,640]{1,0:T(8,128)(2,1)S(1)}, bf16[512,640]{1,0:T(8,128)(2,1)S(1)}, u32[]{:S(2)}, u32[]{:S(2)}) collective-permute-start(bf16[512,640]{1,0:T(8,128)(2,1)S(1)} %constant_dynamic-slice_fusion.10), channel_id=1, source_target_pairs={{0,8},{4,12},{8,0},{12,4},{16,24},{20,28},{24,16},{28,20},{1,9},{5... | collective-permute-start | bytes 1966088 | tf_op jit(solution)/shard_map/ppermute | solution.py:370
  947.5 108.7 %collective-permute-start.92 = (bf16[160,2048]{1,0:T(8,128)(2,1)S(1)}, bf16[160,2048]{1,0:T(8,128)(2,1)S(1)}, u32[]{:S(2)}, u32[]{:S(2)}) collective-permute-start(bf16[160,2048]{1,0:T(8,128)(2,1)S(1)} %constant_dynamic-slice_fusion.2), channel_id=1, source_target_pairs={{0,8},{4,12},{8,0},{12,4},{16,24},{20,28},{24,16},{28,20},{1,9},{5... | collective-permute-start | bytes 1966088 | tf_op jit(solution)/shard_map/ppermute | solution.py:370
  980.4 252.2 %collective-permute-start.76 = (bf16[512,1536]{1,0:T(8,128)(2,1)S(1)}, bf16[512,1536]{1,0:T(8,128)(2,1)S(1)}, u32[]{:S(2)}, u32[]{:S(2)}) collective-permute-start(bf16[512,1536]{1,0:T(8,128)(2,1)S(1)} %add_convert_fusion.10), channel_id=1, source_target_pairs={{0,24},{4,28},{8,16},{12,20},{16,8},{20,12},{24,0},{28,4},{1,25},{... | collective-permute-start | bytes 4718600 | tf_op jit(solution)/shard_map/ppermute | solution.py:432
  1014.1 220.4 %collective-permute-start.81 = (bf16[512,1536]{1,0:T(8,128)(2,1)S(1)}, bf16[512,1536]{1,0:T(8,128)(2,1)S(1)}, u32[]{:S(2)}, u32[]{:S(2)}) collective-permute-start(bf16[512,1536]{1,0:T(8,128)(2,1)S(1)} %add_convert_fusion.8), channel_id=1, source_target_pairs={{0,24},{4,28},{8,16},{12,20},{16,8},{20,12},{24,0},{28,4},{1,25},{... | collective-permute-start | bytes 4718600 | tf_op jit(solution)/shard_map/ppermute | solution.py:432
  1028.3 152.1 %collective-permute-start.66 = (bf16[512,640]{1,0:T(8,128)(2,1)S(1)}, bf16[512,640]{1,0:T(8,128)(2,1)S(1)}, u32[]{:S(2)}, u32[]{:S(2)}) collective-permute-start(bf16[512,640]{1,0:T(8,128)(2,1)S(1)} %add_convert_fusion.19), channel_id=1, source_target_pairs={{0,24},{4,28},{8,16},{12,20},{16,8},{20,12},{24,0},{28,4},{1,25},{... | collective-permute-start | bytes 1966088 | tf_op jit(solution)/shard_map/ppermute | solution.py:432
  1042.4 176.0 %collective-permute-start.71 = (bf16[512,640]{1,0:T(8,128)(2,1)S(1)}, bf16[512,640]{1,0:T(8,128)(2,1)S(1)}, u32[]{:S(2)}, u32[]{:S(2)}) collective-permute-start(bf16[512,640]{1,0:T(8,128)(2,1)S(1)} %add_convert_fusion.17), channel_id=1, source_target_pairs={{0,24},{4,28},{8,16},{12,20},{16,8},{20,12},{24,0},{28,4},{1,25},{... | collective-permute-start | bytes 1966088 | tf_op jit(solution)/shard_map/ppermute | solution.py:432
  1056.4 175.9 %collective-permute-start.93 = (bf16[160,2048]{1,0:T(8,128)(2,1)S(1)}, bf16[160,2048]{1,0:T(8,128)(2,1)S(1)}, u32[]{:S(2)}, u32[]{:S(2)}) collective-permute-start(bf16[160,2048]{1,0:T(8,128)(2,1)S(1)} %add_convert_fusion.15), channel_id=1, source_target_pairs={{0,24},{4,28},{8,16},{12,20},{16,8},{20,12},{24,0},{28,4},{1,25},{... | collective-permute-start | bytes 1966088 | tf_op jit(solution)/shard_map/ppermute | solution.py:432
  1180.4 85.7 %collective-permute-start.98 = (bf16[384,2048]{1,0:T(8,128)(2,1)S(1)}, bf16[384,2048]{1,0:T(8,128)(2,1)S(1)}, u32[]{:S(2)}, u32[]{:S(2)}) collective-permute-start(bf16[384,2048]{1,0:T(8,128)(2,1)S(1)} %add_convert_fusion.6), channel_id=1, source_target_pairs={{0,24},{4,28},{8,16},{12,20},{16,8},{20,12},{24,0},{28,4},{1,25},{... | collective-permute-start | bytes 4718600 | tf_op jit(solution)/shard_map/ppermute | solution.py:432
  1232.6 38.6 %collective-permute-start.94 = (bf16[160,2048]{1,0:T(8,128)(2,1)S(1)}, bf16[160,2048]{1,0:T(8,128)(2,1)S(1)}, u32[]{:S(2)}, u32[]{:S(2)}) collective-permute-start(bf16[160,2048]{1,0:T(8,128)(2,1)S(1)} %add_convert_fusion.14), channel_id=1, source_target_pairs={{0,8},{4,12},{8,0},{12,4},{16,24},{20,28},{24,16},{28,20},{1,9},{5... | collective-permute-start | bytes 1966088 | tf_op jit(solution)/shard_map/ppermute | solution.py:370
  1234.5 57.3 %collective-permute-start.77 = (bf16[512,1536]{1,0:T(8,128)(2,1)S(1)}, bf16[512,1536]{1,0:T(8,128)(2,1)S(1)}, u32[]{:S(2)}, u32[]{:S(2)}) collective-permute-start(bf16[512,1536]{1,0:T(8,128)(2,1)S(1)} %add_convert_fusion.9), channel_id=1, source_target_pairs={{0,8},{4,12},{8,0},{12,4},{16,24},{20,28},{24,16},{28,20},{1,9},{5... | collective-permute-start | bytes 4718600 | tf_op jit(solution)/shard_map/ppermute | solution.py:370
  1235.0 90.5 %collective-permute-start.82 = (bf16[512,1536]{1,0:T(8,128)(2,1)S(1)}, bf16[512,1536]{1,0:T(8,128)(2,1)S(1)}, u32[]{:S(2)}, u32[]{:S(2)}) collective-permute-start(bf16[512,1536]{1,0:T(8,128)(2,1)S(1)} %add_convert_fusion.7), channel_id=1, source_target_pairs={{0,8},{4,12},{8,0},{12,4},{16,24},{20,28},{24,16},{28,20},{1,9},{5... | collective-permute-start | bytes 4718600 | tf_op jit(solution)/shard_map/ppermute | solution.py:370
  1271.2 88.2 %collective-permute-start.99 = (bf16[384,2048]{1,0:T(8,128)(2,1)S(1)}, bf16[384,2048]{1,0:T(8,128)(2,1)}, u32[]{:S(2)}, u32[]{:S(2)}) collective-permute-start(bf16[384,2048]{1,0:T(8,128)(2,1)S(1)} %add_convert_fusion.5), channel_id=1, source_target_pairs={{0,8},{4,12},{8,0},{12,4},{16,24},{20,28},{24,16},{28,20},{1,9},{5... | collective-permute-start | bytes 4718600 | tf_op jit(solution)/shard_map/ppermute | solution.py:370
  1271.5 70.7 %collective-permute-start.95 = (bf16[320,2048]{1,0:T(8,128)(2,1)S(1)}, bf16[320,2048]{1,0:T(8,128)(2,1)S(1)}, u32[]{:S(2)}, u32[]{:S(2)}) collective-permute-start(bf16[320,2048]{1,0:T(8,128)(2,1)S(1)} %pad_maximum_fusion.15), channel_id=1, source_target_pairs={{0,4},{4,0},{8,12},{12,8},{16,20},{20,16},{24,28},{28,24},{1,5},{5... | collective-permute-start | bytes 3932168 | tf_op jit(solution)/shard_map/ppermute | solution.py:370
  1293.9 79.5 %collective-permute-start.78 = (bf16[1024,1536]{1,0:T(8,128)(2,1)}, bf16[1024,1536]{1,0:T(8,128)(2,1)}, u32[]{:S(2)}, u32[]{:S(2)}) collective-permute-start(bf16[1024,1536]{1,0:T(8,128)(2,1)} %pad_maximum_fusion.8), channel_id=1, source_target_pairs={{0,4},{4,0},{8,12},{12,8},{16,20},{20,16},{24,28},{28,24},{1,5},{5... | collective-permute-start | bytes 9437192 | tf_op jit(solution)/shard_map/ppermute | solution.py:370
  1327.6 48.7 %collective-permute-start.83 = (bf16[1024,1536]{1,0:T(8,128)(2,1)}, bf16[1024,1536]{1,0:T(8,128)(2,1)}, u32[]{:S(2)}, u32[]{:S(2)}) collective-permute-start(bf16[1024,1536]{1,0:T(8,128)(2,1)} %pad_maximum_fusion.9), channel_id=1, source_target_pairs={{0,4},{4,0},{8,12},{12,8},{16,20},{20,16},{24,28},{28,24},{1,5},{5... | collective-permute-start | bytes 9437192 | tf_op jit(solution)/shard_map/ppermute | solution.py:370
  (172 other events, 3129.4 us)

commit v2 on v1

v2 whole, which is shorter than its diff:
```python
import functools
import math

import jax
import jax.numpy as jnp
from jax import lax
from jax.experimental import pallas as pl
from jax.experimental.pallas import tpu as pltpu
from jax.sharding import PartitionSpec as P

DECAY_EXP = 8.0
EPS = 1e-06
GELU_C = math.sqrt(2.0 / math.pi)
GELU_K = 0.044715
LANES = 128
SUB = 8
UNIT_TILE = 256
COST_SCALE = 0.5
MODEL_TILE = 512
VMEM_BYTES = 56 * 1024 * 1024

f32 = jnp.float32
bf16 = jnp.bfloat16


def dot_nn(left, right):
    return lax.dot_general(left, right, (((1,), (0,)), ((), ())), preferred_element_type=f32)


def dot_nt(left, right):
    return lax.dot_general(left, right, (((1,), (1,)), ((), ())), preferred_element_type=f32)


def one_minus_square(log_a, decay):
    x = 2.0 * log_a
    tail = 1.0 + x * (1.0 / 7.0)
    for k in (6.0, 5.0, 4.0, 3.0, 2.0):
        tail = 1.0 + x * (1.0 / k) * tail
    return jnp.where(x > -0.4, -x * tail, 1.0 - decay * decay)


def gelu_parts(x):
    square = x * x
    th = jnp.tanh(GELU_C * x * (1.0 + GELU_K * square))
    half = 0.5 * (1.0 + th)
    value = x * half
    slope = half + 0.5 * x * (1.0 - th * th) * (GELU_C * (1.0 + 3.0 * GELU_K * square))
    return value, slope


def row_index(shape):
    return lax.broadcasted_iota(jnp.int32, shape, 0)


def shift_down(prev, cur, k, row):
    return jnp.where(row < k, pltpu.roll(prev, k, 0), pltpu.roll(cur, k, 0))


def shift_up(cur, following, k, row):
    return jnp.where(row < SUB - k, pltpu.roll(cur, SUB - k, 0), pltpu.roll(following, SUB - k, 0))


def load_block(pieces, layout, block, target):
    for ref, (owner, start, count) in zip(pieces, layout):

        @pl.when(block == owner)
        def _(ref=ref, start=start, count=count):
            target[pl.ds(start, count), :] = ref[...]


def store_block(pieces, layout, block, column, value):
    for ref, (owner, start, count) in zip(pieces, layout):

        @pl.when(block == owner)
        def _(ref=ref, start=start, count=count):
            ref[:, column] = value[start : start + count]


def rec_forward_kernel(layout, length, *refs):
    x_pieces, refs = refs[: len(layout)], refs[len(layout) :]
    w_both, taps, conv_bias, w_gates, ga_bias, gi_bias, decay_param, w_out = refs[:8]
    gates_pre, tail, carry, x = refs[-4:]
    outs = refs[-4 - 8 - len(layout) : -4]
    mixed, pre, branch, conv, ga, gi, prev_state, final = outs[:8]
    parts = outs[8:]
    step = pl.program_id(0)
    block = flip(step, lax.axis_index("mp"), 4 if len(layout) == 5 else len(layout))
    rows, width = mixed.shape[1:]
    load_block(x_pieces, layout, block, x)
    pieces = rows // 16
    lanes = [pl.ds(at, LANES) for at in range(0, width, LANES)]
    row = row_index((SUB, LANES))

    @pl.when(step == 0)
    def _():
        tail[...] = jnp.zeros_like(tail)
        carry[...] = jnp.zeros_like(carry)

    both = dot_nn(x[...], w_both[...])
    branch[0] = both[:, :width]
    pre[0] = both[:, width:]

    def conv_piece(i, _):
        base = pl.multiple_of(i * 16, 16)
        for lane in lanes:
            bias = conv_bias[:, lane]
            before = tail[:, lane]
            parts = []
            for half in range(2):
                cur = pre[0, pl.ds(base + SUB * half, SUB), lane]
                total = bias + taps[0:1, lane] * cur
                for k in range(1, 4):
                    total = total + taps[k : k + 1, lane] * shift_down(before, cur, k, row)
                parts.append(total)
                before = cur
            tail[:, lane] = before
            conv[0, pl.ds(base, 16), lane] = jnp.concatenate(parts, axis=0).astype(bf16)
        return 0

    lax.fori_loop(0, pieces, conv_piece, 0)
    gates_pre[...] = dot_nn(conv[0], w_gates[...])
    limit = length[...]

    def scan_piece(i, _):
        base = pl.multiple_of(i * 16, 16)
        start = step * rows + base
        for lane in lanes:
            second = pl.ds(width + lane.start, LANES)
            rate = -DECAY_EXP * jax.nn.softplus(-decay_param[:, lane])
            conv_two = conv[0, pl.ds(base, 16), lane].astype(f32)
            state = carry[:, lane]
            outs = []
            for half in range(2):
                at = pl.ds(base + SUB * half, SUB)
                live = (row + (start + SUB * half)) < limit
                gate_a = jax.nn.sigmoid(gates_pre[at, lane] + ga_bias[:, lane])
                gate_i = jax.nn.sigmoid(gates_pre[at, second] + gi_bias[:, lane])
                ga[0, at, lane] = gate_a
                gi[0, at, lane] = gate_i
                log_a = rate * gate_a
                decay = jnp.exp(log_a)
                scaled = jnp.sqrt(one_minus_square(log_a, decay)) * gate_i * conv_two[SUB * half : SUB * half + SUB]
                mul = jnp.where(live, decay, 1.0)
                add = jnp.where(live, scaled, 0.0)
                for shift in (1, 2, 4):
                    inside = row >= shift
                    add = add + mul * jnp.where(inside, pltpu.roll(add, shift, 0), 0.0)
                    mul = mul * jnp.where(inside, pltpu.roll(mul, shift, 0), 1.0)
                states = mul * state + add
                prev_state[0, at, lane] = jnp.where(row == 0, state, pltpu.roll(states, 1, 0))
                state = jnp.broadcast_to(states[SUB - 1 : SUB], (SUB, LANES))
                value, _ = gelu_parts(branch[0, at, lane])
                outs.append(states * value)
            carry[:, lane] = state
            mixed[0, pl.ds(base, 16), lane] = jnp.concatenate(outs, axis=0).astype(bf16)
        return 0

    lax.fori_loop(0, pieces, scan_piece, 0)
    final[...] = carry[...]
    for at in range(0, w_out.shape[1], MODEL_TILE):
        column = pl.ds(at, MODEL_TILE)
        x[:, column] = dot_nn(mixed[0], w_out[:, column]).astype(bf16)
    store_block(parts, layout, block, slice(None), x[...])


def rec_backward_kernel(layout, nshared, length, *refs):
    many = len(layout)
    d_resid_pieces, x_pieces, refs = refs[:many], refs[many : 2 * many], refs[2 * many :]
    w_out, w_both, taps, w_gates, decay_param = refs[:5]
    pre, branch, conv, ga, gi, prev_state = refs[5:11]
    d_mixed, d_conv, flow, later, x, d_resid = refs[-6:]
    outs = refs[-6 - 4 - many : -6]
    d_both, d_gates, sums, gain_sums = outs[:4]
    parts = outs[4:]
    step = pl.program_id(0)
    rows, width = pre.shape[1:]
    pieces = rows // 16
    lanes = [pl.ds(at, LANES) for at in range(0, width, LANES)]
    row = row_index((SUB, LANES))
    first = (pl.num_programs(0) - 1 - step) * rows
    limit = length[...]

    @pl.when(step == 0)
    def _():
        flow[...] = jnp.zeros_like(flow)
        later[...] = jnp.zeros_like(later)
        sums[...] = jnp.zeros_like(sums)
        gain_sums[...] = jnp.zeros_like(gain_sums)

    block = flip(pl.num_programs(0) - 1 - step, lax.axis_index("mp"), 4 if len(layout) == 5 else len(layout))
    load_block(d_resid_pieces, layout, block, d_resid)
    load_block(x_pieces, layout, block, x)
    d_mixed[...] = dot_nt(d_resid[...], w_out[...])

    def scan_piece(j, _):
        base = pl.multiple_of((pieces - 1 - j) * 16, 16)
        for lane in lanes:
            rate = -DECAY_EXP * jax.nn.softplus(-decay_param[:, lane])
            conv_two = conv[0, pl.ds(base, 16), lane].astype(f32)
            carried = flow[:, lane]
            outs = [None, None]
            sum_log = sums[0, :, lane]
            for half in (1, 0):
                at = pl.ds(base + SUB * half, SUB)
                live = (row + (first + base + SUB * half)) < limit
                conv_val = conv_two[SUB * half : SUB * half + SUB]
                gate_a = ga[0, at, lane]
                gate_i = gi[0, at, lane]
                before = prev_state[0, at, lane]
                d_mix = d_mixed[at, lane]
                log_a = rate * gate_a
                decay = jnp.exp(log_a)
                space = one_minus_square(log_a, decay)
                inverse = lax.rsqrt(jnp.maximum(space, 1e-37))
                root = space * inverse
                gated = gate_i * conv_val
                mul = jnp.where(live, decay, 1.0)
                states = mul * before + jnp.where(live, root * gated, 0.0)
                value, slope = gelu_parts(branch[0, at, lane])
                d_br = d_mix * states * slope
                direct = d_mix * value
                add = mul * direct
                for shift in (1, 2, 4):
                    inside = row < SUB - shift
                    add = add + mul * jnp.where(inside, pltpu.roll(add, SUB - shift, 0), 0.0)
                    mul = mul * jnp.where(inside, pltpu.roll(mul, SUB - shift, 0), 1.0)
                moved = add + mul * carried
                d_state = direct + jnp.where(row == SUB - 1, carried, pltpu.roll(moved, SUB - 1, 0))
                carried = jnp.broadcast_to(moved[0:1], (SUB, LANES))
                d_state = jnp.where(live, d_state, 0.0)
                d_log = d_state * decay * (before - gated * decay * inverse)
                sum_log = sum_log + d_log * gate_a
                d_gate_a = d_log * rate * gate_a * (1.0 - gate_a)
                d_rooted = d_state * root
                d_conv_rec = d_rooted * gate_i
                d_gate_i = d_rooted * conv_val * gate_i * (1.0 - gate_i)
                d_conv[at, lane] = d_conv_rec
                outs[half] = (d_br, d_gate_a, d_gate_i)
            flow[:, lane] = carried
            sums[0, :, lane] = sum_log
            second = pl.ds(width + lane.start, LANES)
            for target, there, which in ((d_both, lane, 0), (d_gates, lane, 1), (d_gates, second, 2)):
                both = jnp.concatenate([outs[0][which], outs[1][which]], axis=0).astype(bf16)
                target[0, pl.ds(base, 16), there] = both
                if which > 0:
                    wide = both.astype(f32)
                    sums[which, :, lane] += wide[:SUB] + wide[SUB:]
        return 0

    lax.fori_loop(0, pieces, scan_piece, 0)
    d_conv[...] += dot_nt(d_gates[0], w_gates[...])

    def conv_piece(j, _):
        base = pl.multiple_of((pieces - 1 - j) * 16, 16)
        for lane in lanes:
            following = later[:, lane]
            totals = [None, None]
            tap_sums = [sums[3 + k, :, lane] for k in range(5)]
            for half in (1, 0):
                at = pl.ds(base + SUB * half, SUB)
                cur = d_conv[at, lane]
                seen = pre[0, at, lane]
                tap_sums[0] = tap_sums[0] + cur
                tap_sums[1] = tap_sums[1] + cur * seen
                total = taps[0:1, lane] * cur
                for k in range(1, 4):
                    ahead = shift_up(cur, following, k, row)
                    tap_sums[1 + k] = tap_sums[1 + k] + ahead * seen
                    total = total + taps[k : k + 1, lane] * ahead
                totals[half] = total
                following = cur
            later[:, lane] = following
            for k in range(5):
                sums[3 + k, :, lane] = tap_sums[k]
            d_both[0, pl.ds(base, 16), pl.ds(width + lane.start, LANES)] = jnp.concatenate(totals, axis=0).astype(bf16)
        return 0

    lax.fori_loop(0, pieces, conv_piece, 0)
    for at in range(0, x.shape[1], MODEL_TILE):
        column = pl.ds(at, MODEL_TILE)
        part = dot_nt(d_both[0], w_both[column, :])
        seen = part * x[:, column].astype(f32)
        gain_sums[:, column] += jnp.sum(seen.reshape(rows // SUB, SUB, MODEL_TILE), axis=0)
        d_resid[:, column] = part.astype(bf16)
    store_block(parts, layout, block, slice(None), d_resid[...])


def mlp_kernel(layout, *refs):
    many = len(layout)
    x_pieces, cot_pieces, (w_gate, w_up, w_down) = refs[:many], refs[many : 2 * many], refs[2 * many : 2 * many + 3]
    x, cot, mid = refs[-3:]
    hidden, d_gate, d_up, mlp_part = refs[-3 - many - 4 : -3 - many]
    parts = refs[-3 - many : -3]
    r = pl.program_id(0)
    load_block(x_pieces, layout, r, x)
    load_block(cot_pieces, layout, r, cot)
    for at in range(0, hidden.shape[2], UNIT_TILE):
        column = pl.ds(at, UNIT_TILE)
        up = dot_nn(x[...], w_up[:, column])
        back = dot_nt(cot[...], w_down[column, :])
        value, slope = gelu_parts(dot_nn(x[...], w_gate[:, column]))
        hidden[0, :, column] = (value * up).astype(bf16)
        d_gate[0, :, column] = (back * up * slope).astype(bf16)
        d_up[0, :, column] = (back * value).astype(bf16)
    for at in range(0, cot.shape[1], MODEL_TILE):
        column = pl.ds(at, MODEL_TILE)
        mlp_part[0, :, column] = dot_nn(hidden[0], w_down[:, column]).astype(bf16)
        total = dot_nt(d_gate[0], w_gate[column, :]) + dot_nt(d_up[0], w_up[column, :])
        mid[:, column] = total.astype(bf16)
    store_block(parts, layout, r, slice(None), mid[...])


def weight_grad_kernel(by_rows, nlefts, nrights, *refs):
    lefts, rights = refs[:nlefts], refs[nlefts : nlefts + nrights]
    keep, give, left, right = refs[-4:]
    start = (pl.program_id(0) == 0) & (pl.program_id(1) == 0)

    def assemble(target, sources):
        at = 0
        for ref in sources:
            target[at : at + ref.shape[0], :] = ref[...]
            at += ref.shape[0]

    if nlefts == 1:
        left = lefts[0]
    elif by_rows:
        assemble(left, lefts)
    else:
        pl.when(start)(functools.partial(assemble, left, lefts))
    if nrights == 1:
        right = rights[0]
    elif not by_rows:
        assemble(right, rights)
    else:
        pl.when(start)(functools.partial(assemble, right, rights))
    total = lax.dot_general(
        left[...], right[...], (((0,), (0,)), ((), ())), preferred_element_type=f32
    ).astype(bf16)

    @pl.when(pl.program_id(0) == 0)
    def _():
        keep[...] = total

    @pl.when(pl.program_id(0) == 1)
    def _():
        give[...] = total


def join_kernel(info, first, second, third, fourth, *outs):
    for at, ref in enumerate((first, second, third, fourth)):

        @pl.when(pl.program_id(0) == at)
        def _(ref=ref):
            start = 0
            for out in outs:
                out[...] = ref[:, start : start + out.shape[1]].astype(f32)
                start += out.shape[1]


ANY = pl.BlockSpec(memory_space=pl.ANY)
PARAMS = pltpu.CompilerParams(vmem_limit_bytes=VMEM_BYTES)
MESH = pl.DeviceIdType.MESH


def flip(index, mask, size):
    total, bit = 0, 1
    while bit < size:
        total = total + ((index // bit + mask // bit) % 2) * bit
        bit *= 2
    return total


def neighbours():
    me = lax.axis_index("mp")
    return {"mp": flip(me, 1, 4)}, {"mp": flip(me, 2, 4)}


def remote(source, target, send, recv, at, device):
    return pltpu.make_async_remote_copy(
        src_ref=source,
        dst_ref=target,
        send_sem=send.at[at],
        recv_sem=recv.at[at],
        device_id=device,
        device_id_type=MESH,
    )


class GatherHost:
    def __init__(self, shard):
        rows, model = shard.shape
        self.operands = [shard]
        self.outputs = [jax.ShapeDtypeStruct((count, model), bf16) for count in (rows, rows, rows // 2, rows // 2)]
        self.scratch = [pltpu.SemaphoreType.DMA((4,)), pltpu.SemaphoreType.DMA((4,))]

    def copies(self, ins, outs, scratch):
        (shard,), (by_x, by_y, far_a, far_b), (send, recv) = ins, outs, scratch
        half = far_a.shape[0]
        x, y = neighbours()
        return (
            remote(shard, by_x, send, recv, 0, x),
            remote(shard, by_y, send, recv, 1, y),
            remote(by_x.at[pl.ds(0, half)], far_a, send, recv, 2, y),
            remote(by_y.at[pl.ds(half, half)], far_b, send, recv, 3, x),
        )

    def begin(self, *refs):
        for copy in self.copies(*refs)[:2]:
            copy.start()

    def middle(self, *refs):
        copies = self.copies(*refs)
        copies[0].wait_recv()
        copies[1].wait_recv()
        copies[2].start()
        copies[3].start()

    def end(self, *refs):
        copies = self.copies(*refs)
        copies[0].wait_send()
        copies[1].wait_send()
        copies[2].wait()
        copies[3].wait()

    def result(self, outs):
        return (self.operands[0],) + tuple(outs)


class ScatterHost:
    def __init__(self, parts):
        rows, model = parts[1].shape
        half = rows // 2
        self.first = parts[0]
        self.operands = list(parts[1:])
        self.outputs = [jax.ShapeDtypeStruct((rows, model), bf16)] * 2
        self.scratch = [pltpu.VMEM((half, model), bf16)] * 4 + [pltpu.SemaphoreType.DMA((6,))] * 2
        self.scratch += [pltpu.SemaphoreType.DMA((2,))]

    def copies(self, ins, outs, scratch):
        (one, two, far_a, far_b), (from_x, from_y) = ins, outs
        got_x, got_y, own_x, own_y, send, recv, local = scratch
        half = far_a.shape[0]
        low, high = pl.ds(0, half), pl.ds(half, half)
        x, y = neighbours()
        return (
            remote(far_a, got_x, send, recv, 0, x),
            remote(far_b, got_y, send, recv, 1, y),
            remote(one.at[low], from_x.at[low], send, recv, 2, x),
            remote(two.at[high], from_y.at[high], send, recv, 3, y),
            remote(own_x, from_x.at[high], send, recv, 4, x),
            remote(own_y, from_y.at[low], send, recv, 5, y),
        ), (
            pltpu.make_async_copy(one.at[high], own_x, local.at[0]),
            pltpu.make_async_copy(two.at[low], own_y, local.at[1]),
        )

    def begin(self, *refs):
        copies, locals_ = self.copies(*refs)
        for copy in copies[:4] + locals_:
            copy.start()

    def middle(self, ins, outs, scratch):
        copies, locals_ = self.copies(ins, outs, scratch)
        got_x, got_y, own_x, own_y = scratch[:4]
        for copy in locals_:
            copy.wait()
        copies[0].wait_recv()
        copies[1].wait_recv()
        own_x[...] = (own_x[...].astype(f32) + got_y[...].astype(f32)).astype(bf16)
        own_y[...] = (own_y[...].astype(f32) + got_x[...].astype(f32)).astype(bf16)
        copies[4].start()
        copies[5].start()

    def end(self, *refs):
        copies, _ = self.copies(*refs)
        copies[0].wait_send()
        copies[1].wait_send()
        for copy in copies[2:]:
            copy.wait()

    def result(self, outs):
        return self.first.astype(f32) + outs[0].astype(f32) + outs[1].astype(f32)


class SendHost:
    def __init__(self, pairs):
        self.operands = [array for array, _ in pairs]
        self.which = [which for _, which in pairs]
        self.outputs = [jax.ShapeDtypeStruct(array.shape, array.dtype) for array in self.operands]
        self.scratch = [pltpu.SemaphoreType.DMA((len(pairs),))] * 2

    def copies(self, ins, outs, scratch):
        to = neighbours()
        return [
            remote(source, target, scratch[0], scratch[1], at, to[self.which[at]])
            for at, (source, target) in enumerate(zip(ins, outs))
        ]

    def begin(self, *refs):
        for copy in self.copies(*refs):
            copy.start()

    def middle(self, *refs):
        pass

    def end(self, *refs):
        for copy in self.copies(*refs):
            copy.wait()

    def result(self, outs):
        return tuple(outs)


def call(kernel, grid, ins, outs, scratch, name, us, hosts=(), before=(), aliases=None, middle=0, unique=None):
    nins, nouts, nscratch = len(ins), len(outs), len(scratch)
    steps = math.prod(grid)

    def body(*refs):
        refs = list(refs)

        def take(count):
            part = refs[:count]
            del refs[:count]
            return part

        own_ins = take(nins)
        host_ins = [take(len(host.operands)) for host in hosts]
        take(len(before))
        own_outs = take(nouts)
        host_outs = [take(len(host.outputs)) for host in hosts]
        own_scratch = take(nscratch)
        host_refs = [(i, o, take(len(host.scratch))) for host, i, o in zip(hosts, host_ins, host_outs)]
        step = pl.program_id(0)
        if len(grid) == 2:
            step = step * grid[1] + pl.program_id(1)
        if hosts:

            @pl.when(step == 0)
            def _():
                barrier = pltpu.get_barrier_semaphore()
                for device in neighbours():
                    pl.semaphore_signal(barrier, inc=1, device_id=device, device_id_type=MESH)
                pl.semaphore_wait(barrier, 2)
                for host, there in zip(hosts, host_refs):
                    host.begin(*there)

            @pl.when(step == middle)
            def _():
                for host, there in zip(hosts, host_refs):
                    host.middle(*there)

        kernel(*own_ins, *own_outs, *own_scratch)
        if hosts:

            @pl.when(step == steps - 1)
            def _():
                for host, there in zip(hosts, host_refs):
                    host.end(*there)

    host_operands = [v for host in hosts for v in host.operands]
    host_outputs = [v for host in hosts for v in host.outputs]
    params = pltpu.CompilerParams(vmem_limit_bytes=VMEM_BYTES)
    if hosts:
        params = pltpu.CompilerParams(vmem_limit_bytes=VMEM_BYTES, collective_id=unique, has_side_effects=True)
    results = pl.pallas_call(
        body,
        out_shape=tuple(shape for shape, _ in outs) + tuple(host_outputs),
        grid=grid,
        in_specs=[spec for _, spec in ins] + [ANY] * (len(host_operands) + len(before)),
        out_specs=tuple(spec for _, spec in outs) + (ANY,) * len(host_outputs),
        scratch_shapes=list(scratch) + [v for host in hosts for v in host.scratch],
        input_output_aliases=aliases or {},
        compiler_params=params,
        cost_estimate=cost(us),
        name=name,
    )(*[array for array, _ in ins], *host_operands, *before)
    own, rest = results[:nouts], results[nouts:]
    found = []
    for host in hosts:
        found.append(host.result(rest[: len(host.outputs)]))
        rest = rest[len(host.outputs) :]
    return own, found


def cost(us):
    return pl.CostEstimate(flops=int(us * COST_SCALE * 1.15e9), bytes_accessed=1 << 16, transcendentals=0)


def whole(array):
    zeros = (0,) * array.ndim
    return pl.BlockSpec(array.shape, lambda *_: zeros, pipeline_mode=pl.Buffered(1))


def layout_of(blocks, rows):
    if blocks != 4:
        return tuple((r, 0, rows) for r in range(blocks))
    return ((0, 0, rows), (1, 0, rows), (2, 0, rows), (3, 0, rows // 2), (3, rows // 2, rows - rows // 2))


def piece_outputs(layout, model):
    shapes = tuple(jax.ShapeDtypeStruct((count, model), bf16) for _, _, count in layout)
    specs = tuple(pl.BlockSpec(shape.shape, lambda *_: (0, 0)) for shape in shapes)
    return shapes, specs


def rec_forward(length, x, params, **more):
    blocks, (rows, model) = lax.axis_size("mp"), x[0].shape
    layout = layout_of(blocks, rows)
    width = params[0].shape[1] // 2

    def at(step):
        return (flip(step, lax.axis_index("mp"), blocks), 0, 0)

    wide = pl.BlockSpec((1, rows, width), at)
    out = jax.ShapeDtypeStruct((blocks, rows, width), f32)
    low = jax.ShapeDtypeStruct((blocks, rows, width), bf16)
    shapes, specs = piece_outputs(layout, model)
    final = (jax.ShapeDtypeStruct((SUB, width), f32), pl.BlockSpec((SUB, width), lambda step: (0, 0)))
    return call(
        functools.partial(rec_forward_kernel, layout),
        (blocks,),
        [(v, whole(v)) for v in (length,) + tuple(x) + tuple(params)],
        [(shape, wide) for shape in (low, out, out, low, out, out, out)] + [final] + list(zip(shapes, specs)),
        [
            pltpu.VMEM((rows, 2 * width), f32),
            pltpu.VMEM((SUB, width), f32),
            pltpu.VMEM((SUB, width), f32),
            pltpu.VMEM((rows, model), bf16),
        ],
        "rec_forward",
        37,
        **more,
    )


def rec_backward(length, seq, count, d_resid, x, params, saved, shared, **more):
    blocks, (rows, model) = lax.axis_size("mp"), x[0].shape
    layout = layout_of(blocks, rows)
    width = saved[0].shape[2]

    def at(step):
        return (flip(blocks - 1 - step, lax.axis_index("mp"), blocks), 0, 0)

    def placed(step):
        return (seq * blocks + flip(blocks - 1 - step, lax.axis_index("mp"), blocks), 0, 0)

    wide = pl.BlockSpec((1, rows, width), at)
    double = pl.BlockSpec((1, rows, 2 * width), placed)
    low = jax.ShapeDtypeStruct((count * blocks, rows, 2 * width), bf16)
    shapes, specs = piece_outputs(layout, model)
    sums = (jax.ShapeDtypeStruct((8, SUB, width), f32), pl.BlockSpec((8, SUB, width), lambda step: (0, 0, 0)))
    gain_sums = (jax.ShapeDtypeStruct((SUB, model), f32), pl.BlockSpec((SUB, model), lambda step: (0, 0)))
    inputs = [(v, whole(v)) for v in (length,) + tuple(d_resid) + tuple(x) + tuple(params)]
    inputs += [(v, wide) for v in saved] + [(v, ANY) for v in shared]
    return call(
        functools.partial(rec_backward_kernel, layout, len(shared)),
        (blocks,),
        inputs,
        [(low, double), (low, double), sums, gain_sums] + list(zip(shapes, specs)),
        [
            pltpu.VMEM((rows, width), f32),
            pltpu.VMEM((rows, width), f32),
            pltpu.VMEM((SUB, width), f32),
            pltpu.VMEM((SUB, width), f32),
            pltpu.VMEM((rows, model), bf16),
            pltpu.VMEM((rows, model), bf16),
        ],
        "rec_backward",
        43,
        aliases={len(inputs) - len(shared) + at: at for at in range(len(shared))},
        **more,
    )


def largest_tile(total, limit, unit=LANES):
    return max(t for t in range(unit, limit + 1, unit) if total % t == 0)


def mlp_core(seq, count, x, cot, w_gate, w_up, w_down, shared, **more):
    blocks, (rows, model) = lax.axis_size("mp"), x[0].shape
    layout = layout_of(blocks, rows)
    units = w_gate.shape[1]
    low = jax.ShapeDtypeStruct((count * blocks, rows, units), bf16)
    part = pl.BlockSpec((1, rows, units), lambda r: (seq * blocks + r, 0, 0))
    long = pl.BlockSpec((1, rows, model), lambda r: (flip(r, lax.axis_index("mp"), blocks), 0, 0))
    shapes, specs = piece_outputs(layout, model)
    inputs = [(v, whole(v)) for v in tuple(x) + tuple(cot) + (w_gate, w_up, w_down)] + [(v, ANY) for v in shared]
    return call(
        functools.partial(mlp_kernel, layout),
        (blocks,),
        inputs,
        [(low, part)] * 3 + [(jax.ShapeDtypeStruct((blocks, rows, model), bf16), long)] + list(zip(shapes, specs)),
        [pltpu.VMEM((rows, model), bf16)] * 3,
        "mlp_core",
        54,
        aliases={len(inputs) - len(shared) + at: at for at in range(len(shared))},
        **more,
    )


def flat(array):
    return array.reshape(-1, array.shape[-1])


def core_index():
    return lax.axis_index("dp") % 2 if lax.axis_size("dp") == 8 else 0


def weight_grad(lefts, rights, by_rows=True, limit=512, **more):
    lefts, rights = [flat(v) for v in lefts], [flat(v) for v in rights]
    rows, columns = lefts[0].shape[1], rights[0].shape[1]
    tokens = sum(v.shape[0] for v in lefts)
    half = (rows if by_rows else columns) // 2
    tile = largest_tile(half, limit)
    steps = half // tile

    def cut(array, tiled):
        if not tiled:
            return whole(array)
        return pl.BlockSpec((array.shape[0], tile), lambda h, i: (0, (h + core_index()) % 2 * steps + i))

    def kept(h, i):
        at = i + h * (steps - 1 - i)
        return (at, 0) if by_rows else (0, at)

    def given(h, i):
        at = h * i
        return (at, 0) if by_rows else (0, at)

    shape = jax.ShapeDtypeStruct((half, columns) if by_rows else (rows, half), bf16)
    block = (tile, columns) if by_rows else (rows, tile)
    return call(
        functools.partial(weight_grad_kernel, by_rows, len(lefts), len(rights)),
        (2, steps),
        [(v, cut(v, by_rows)) for v in lefts] + [(v, cut(v, not by_rows)) for v in rights],
        [(shape, pl.BlockSpec(block, kept)), (shape, pl.BlockSpec(block, given))],
        [
            pltpu.VMEM((tokens if len(lefts) > 1 else 16, tile if by_rows else rows), bf16),
            pltpu.VMEM((tokens if len(rights) > 1 else 16, columns if by_rows else tile), bf16),
        ],
        "weight_grad",
        20 if columns > 1000 and by_rows else 13,
        **more,
    )


def join_quarters(where, quarters, by_rows, ways):
    rows, columns = quarters[0].shape
    tile = max(t for t in range(16, 256 + 1, 16) if rows % t == 0)
    steps = rows // tile

    def source(at):
        def index(p, i, where):
            return (jnp.where(p == at, i, jnp.where(p < at, 0, steps - 1)), 0)

        return pl.BlockSpec((tile, columns), index)

    def target(p, i, where):
        half, quarter = where[0] ^ (p // 2), where[1] ^ (p % 2)
        if by_rows:
            return ((half * 2 + quarter) * steps + i, 0)
        return (quarter * steps + i, half)

    shape = (4 * rows, columns // ways) if by_rows else (2 * rows, 2 * columns)
    out = jax.ShapeDtypeStruct(shape, f32)
    return pl.pallas_call(
        join_kernel,
        out_shape=(out,) * ways,
        grid_spec=pltpu.PrefetchScalarGridSpec(
            num_scalar_prefetch=1,
            grid=(4, steps),
            in_specs=[source(at) for at in range(4)],
            out_specs=(pl.BlockSpec((tile, columns // ways), target),) * ways,
        ),
        compiler_params=PARAMS,
        cost_estimate=cost(10),
        name="join_quarters",
    )(where, *quarters)


def swap(value, axis, bit):
    size = lax.axis_size(axis)
    return lax.ppermute(value, axis, [(i, i ^ bit) for i in range(size)])


def gather(shard):
    size = lax.axis_size("mp")
    if size != 4:
        return (shard,) + tuple(swap(shard, "mp", r) for r in range(1, size))
    half = shard.shape[0] // 2
    by_x = swap(shard, "mp", 1)
    by_y = swap(shard, "mp", 2)
    return (shard, by_x, by_y, swap(by_x[:half], "mp", 2), swap(by_y[half:], "mp", 1))


def scatter(parts):
    size = lax.axis_size("mp")
    if size != 4:
        total = parts[0].astype(f32)
        for r in range(1, size):
            total = total + swap(parts[r], "mp", r).astype(f32)
        return total
    half = parts[3].shape[0]
    from_x = swap(parts[3], "mp", 1)
    from_y = swap(parts[4], "mp", 2)
    for_y = jnp.concatenate([add_low(parts[2][:half], from_x), parts[2][half:]], axis=0)
    for_x = jnp.concatenate([parts[1][:half], add_low(parts[1][half:], from_y)], axis=0)
    return parts[0].astype(f32) + swap(for_y, "mp", 2).astype(f32) + swap(for_x, "mp", 1).astype(f32)


def add_low(left, right):
    return (left.astype(f32) + right.astype(f32)).astype(bf16)


def split_half(value, mine):
    half = value.shape[0] // 2
    keep = lax.dynamic_slice_in_dim(value, mine * half, half, 0)
    give = lax.dynamic_slice_in_dim(value, (1 - mine) * half, half, 0)
    return keep, give


class SumOverDp:
    def __init__(self, core, keep, give, by_rows=True, ways=1):
        if lax.axis_size("dp") != 8:
            part = jnp.concatenate([keep, give], axis=0 if by_rows else 1)
            self.totals = jnp.split(lax.psum(part, "dp").astype(f32), ways, axis=1)
            self.total = self.totals[0]
            self.pair = self.quad = self.every = part
            return
        chip = lax.axis_index("dp") // 2
        outer = jnp.where((chip == 0) | (chip == 3), 0, 1)
        self.pair = add_low(keep, swap(give, "dp", 1))
        keep, give = split_half(self.pair, outer)
        self.quad = add_low(keep, swap(give, "dp", 2))
        mirrored = lax.ppermute(self.quad, "dp", [(i, (3 - i // 2) * 2 + i % 2) for i in range(8)])
        self.every = add_low(self.quad, mirrored)
        self.paired = swap(self.every, "dp", 2)
        quarters = (self.every, self.paired, swap(self.every, "dp", 1), swap(self.paired, "dp", 1))
        where = jnp.stack([core[0], outer.astype(jnp.int32)])
        self.totals = join_quarters(where, quarters, by_rows, ways)
        self.total = self.totals[0]


def normalize(values, gain):
    return values * lax.rsqrt(jnp.mean(values * values, axis=-1, keepdims=True) + EPS) * gain


def normalize_back(values, gain, grad):
    inverse = lax.rsqrt(jnp.mean(values * values, axis=-1, keepdims=True) + EPS)
    scaled = grad * gain
    unit = values * inverse
    return inverse * (scaled - unit * jnp.mean(scaled * unit, axis=-1, keepdims=True)), unit


def dense_blocks(weight):
    blocks, inner, outer = weight.shape
    rows = [
        jnp.pad(weight[n], ((0, 0), (n * outer, (blocks - 1 - n) * outer))) for n in range(blocks)
    ]
    return jnp.concatenate(rows, axis=0)


def diagonal_blocks(full, blocks, width):
    inner = width // blocks
    return jnp.stack([full[n * inner : (n + 1) * inner, n * inner : (n + 1) * inner] for n in range(blocks)])


def per_device(
    block_in,
    norm1_gain,
    w_branch,
    w_input,
    conv_weight,
    conv_bias,
    gate_a_weight,
    gate_a_bias,
    gate_i_weight,
    gate_i_bias,
    decay_param,
    w_out,
    norm2_gain,
    w_gate,
    w_up,
    w_down,
    lengths,
    cotangent,
):
    count = block_in.shape[0]
    nblocks = gate_a_weight.shape[0]
    true_width = w_branch.shape[1]
    extra = -true_width % LANES
    me = lax.axis_index("mp")

    def pad_last(value):
        return jnp.pad(value, [(0, 0)] * (value.ndim - 1) + [(0, extra)]) if extra else value

    def line(value):
        return pad_last(value)[None, :]

    wb, wi = pad_last(w_branch), pad_last(w_input)
    wo = jnp.pad(w_out, ((0, extra), (0, 0))) if extra else w_out
    w_ga, w_gi = dense_blocks(gate_a_weight), dense_blocks(gate_i_weight)
    if extra:
        w_ga, w_gi = (jnp.pad(v, ((0, extra), (0, extra))) for v in (w_ga, w_gi))
    taps = pad_last(conv_weight)
    decay_line = line(decay_param)
    w_both = jnp.concatenate([wb, wi], axis=1)
    w_gates = jnp.concatenate([w_ga, w_gi], axis=1)
    forward_params = (
        w_both, taps, line(conv_bias), w_gates, line(gate_a_bias), line(gate_i_bias), decay_line, wo
    )
    backward_params = (wo, w_both, taps, w_gates, decay_line)
    seqs = range(count)
    limits = [jnp.full((SUB, LANES), lengths[s], jnp.int32) for s in seqs]
    core = jnp.int32(core_index()).reshape(1)
    blocks = lax.axis_size("mp")
    hosted = blocks == 4 and count == 2
    ids = iter(range(1, 100))

    def tied(value, *deps):
        return lax.optimization_barrier((value,) + deps)[0]

    def run(function, *args, hosts=(), middle=0, **more):
        if hosted and hosts:
            return function(*args, hosts=hosts, middle=middle, unique=next(ids), **more)
        out, _ = function(*args, **more)
        return out, [
            gather(host.operands[0]) if isinstance(host, GatherHost) else scatter((host.first, *host.operands))
            for host in hosts
        ]

    resid = [block_in[s].astype(f32) for s in seqs]
    starts = [normalize(resid[s], norm1_gain).astype(bf16) for s in seqs]
    piece, model = starts[0].shape
    seq_in = [gather(starts[0])]
    out, (second,) = run(rec_forward, limits[0], seq_in[0], forward_params, hosts=[GatherHost(starts[1])], middle=3)
    seq_in.append(second)
    forward = [out]
    out, (branch,) = run(
        rec_forward, limits[1], seq_in[1], forward_params, hosts=[ScatterHost(out[8:])], middle=2, before=(out[7],)
    )
    forward.append(out)
    mixed = [out[0] for out in forward]
    saved = [out[1:7] for out in forward]
    finals = [out[7][:1, :true_width] for out in forward]
    resid_mid = [resid[0] + branch]
    mids = [normalize(resid_mid[0], norm2_gain).astype(bf16)]
    seq_mid = [gather(mids[0])]
    resid_mid.append(resid[1] + scatter(forward[1][8:]))
    mids.append(normalize(resid_mid[1], norm2_gain).astype(bf16))
    cot_seq = [gather(tied(cotangent[0], forward[1][7]))]

    gathers = [GatherHost(mids[1]), GatherHost(cotangent[1])]
    out, found = run(
        mlp_core, 0, count, seq_mid[0], cot_seq[0], w_gate, w_up, w_down, (), hosts=gathers, middle=3, before=(mids[1],)
    )
    seq_mid.append(found[0])
    cot_seq.append(found[1])
    mlp_part = [out[3]]
    out, (d_mid,) = run(
        mlp_core, 1, count, seq_mid[1], cot_seq[1], w_gate, w_up, w_down, out[:3],
        hosts=[ScatterHost(out[4:])], middle=2,
    )
    mlp_part.append(out[3])
    hidden, d_gate, d_up = out[:3]
    last_parts = out[4:]

    def middle_grad(s, d_mid):
        back, unit = normalize_back(resid_mid[s], norm2_gain, d_mid)
        return cotangent[s].astype(f32) + back, jnp.sum(d_mid * unit, axis=0)

    mlp_total = [lax.psum_scatter(flat(v), "mp", scatter_dimension=0, tiled=True) for v in mlp_part]
    first, gain2 = middle_grad(0, d_mid)
    flat_mid = [p for pieces in seq_mid for p in pieces]
    flat_cot = [p for pieces in cot_seq for p in pieces]
    halves, (first_seq,) = run(weight_grad, [hidden], flat_cot, hosts=[GatherHost(first.astype(bf16))], middle=3)
    down = SumOverDp(core, *halves)
    halves, (d_mid,) = run(
        weight_grad, flat_mid, [d_gate], hosts=[ScatterHost(last_parts)], middle=2, before=(halves[0],)
    )
    gate = SumOverDp(core, *halves)
    halves, _ = run(weight_grad, flat_mid, [d_up], before=(halves[0], down.pair))
    up = SumOverDp(core, *halves)
    second, more_gain2 = middle_grad(1, d_mid)
    gain2 = gain2 + more_gain2
    d_resid = [first, second]

    out, (second_seq,) = run(
        rec_backward, limits[0], 0, count, first_seq, seq_in[0], backward_params, saved[0], (),
        hosts=[GatherHost(second.astype(bf16))], middle=3, before=(halves[0], gate.pair),
    )
    d_resid_seq = [first_seq, second_seq]
    sums, gain1 = out[2], jnp.sum(out[3], axis=0)
    out, (d_in,) = run(
        rec_backward, limits[1], 1, count, second_seq, seq_in[1], backward_params, saved[1], out[:2],
        hosts=[ScatterHost(out[4:])], middle=2, before=(down.quad, gate.quad, up.pair),
    )
    sums, gain1 = sums + out[2], gain1 + jnp.sum(out[3], axis=0)
    d_both, d_gates = out[:2]
    input_grad = [(first + normalize_back(resid[0], norm1_gain, d_in)[0]).astype(bf16)]

    flat_in = [p for pieces in seq_in for p in pieces]
    flat_resid = [p for pieces in d_resid_seq for p in pieces]
    halves, (d_in,) = run(
        weight_grad, flat_in, [d_both], hosts=[ScatterHost(out[4:])], middle=3, before=(up.quad,)
    )
    inward = SumOverDp(core, *halves, ways=2)
    halves, _ = run(weight_grad, mixed, flat_resid, False, before=(halves[0],))
    grad_w_out = SumOverDp(core, *halves, by_rows=False).total[:true_width]
    grad_w_branch, grad_w_input = (v[:, :true_width] for v in inward.totals)
    input_grad.append((second + normalize_back(resid[1], norm1_gain, d_in)[0]).astype(bf16))
    input_grad = jnp.stack(input_grad)
    block_out = jnp.stack([(resid_mid[s] + mlp_total[s].astype(f32)).astype(bf16) for s in seqs])

    gains = jnp.stack([gain1 / norm1_gain, gain2])
    for bit in range(blocks.bit_length() - 1):
        gains = gains + swap(gains, "mp", 1 << bit)
    conv = [part[2] for part in saved]
    d_gates = d_gates.reshape(count, blocks, piece, -1)
    width = d_gates.shape[-1] // 2
    full = sum(jnp.einsum("rtd,rtc->dc", conv[s], d_gates[s], preferred_element_type=f32) for s in seqs)
    full_ga = diagonal_blocks(full[:, :width], nblocks, true_width)
    full_gi = diagonal_blocks(full[:, width:], nblocks, true_width)
    vectors = jnp.sum(sums, axis=1)[:, :true_width]
    decay_grad = vectors[0] * DECAY_EXP * jax.nn.sigmoid(-decay_param)
    vectors = jnp.concatenate([decay_grad[None, :], vectors[1:]], axis=0)
    small = jnp.concatenate(
        [full_ga.reshape(-1), full_gi.reshape(-1), vectors.reshape(-1), gains.reshape(-1)]
    ).astype(bf16)
    used = small.shape[0]
    columns = 640
    padded = -(-used // (64 * columns)) * 64 * columns
    small = jnp.pad(small, (0, padded - used)).reshape(-1, columns)
    small = SumOverDp(core, *split_half(small, core[0])).total.reshape(-1)
    many, few = full_ga.size, vectors.size
    grad_gate_a_weight = small[:many].reshape(full_ga.shape)
    grad_gate_i_weight = small[many : 2 * many].reshape(full_gi.shape)
    vectors = small[2 * many : 2 * many + few].reshape(8, true_width)
    gains = small[2 * many + few : used].reshape(2, model)

    return (
        block_out,
        input_grad,
        gains[0],
        grad_w_branch,
        grad_w_input,
        vectors[4:8],
        vectors[3],
        grad_gate_a_weight,
        vectors[1],
        grad_gate_i_weight,
        vectors[2],
        vectors[0],
        grad_w_out,
        gains[1],
        gate.total,
        up.total,
        down.total,
        jnp.concatenate(finals, axis=0),
    )


def solution(mesh):
    placed = (
        P("dp", "mp", None),
        P(),
        P(None, "mp"),
        P(None, "mp"),
        P(None, "mp"),
        P("mp"),
        P("mp", None, None),
        P("mp"),
        P("mp", None, None),
        P("mp"),
        P("mp"),
        P("mp", None),
        P(),
        P(None, "mp"),
        P(None, "mp"),
        P("mp", None),
        P("dp"),
        P("dp", "mp", None),
    )
    return jax.shard_map(
        per_device,
        mesh=mesh,
        in_specs=placed,
        out_specs=(
            P("dp", "mp", None),
            P("dp", "mp", None),
            P(),
            P(None, "mp"),
            P(None, "mp"),
            P(None, "mp"),
            P("mp"),
            P("mp", None, None),
            P("mp"),
            P("mp", None, None),
            P("mp"),
            P("mp"),
            P("mp", None),
            P(),
            P(None, "mp"),
            P(None, "mp"),
            P("mp", None),
            P("dp", "mp"),
        ),
        check_vma=False,
    )
```

time: 1420 us -> 1160 us (0.82)
  Pallas kernels: 211 us -> 544 us
  waiting for transfers between devices: 588 us -> 353 us
  matrix products: 186 us -> 5.85 us
  other arithmetic: 171 us -> 71.6 us
  starting transfers between devices: 186 us -> 124 us
  local copies, waits for them, and re-layouts: 61.8 us -> 36 us
    pallas_call x6 -> x17, Pallas kernels: 211 us -> 544 us  [the longest x11 493 us: call(): pl.pallas_call(body, out_shape=tuple((shape for shape, _ in outs)) + tupl...]
    dot_general x24 -> x2, matrix products: 186 us -> 5.85 us  [per_device(): jnp.einsum('rtd,rtc->dc', conv[s], d_gates[s], preferred_element_type=f32)]
    ppermute x94 -> x48, waiting for transfers between devices: 407 us -> 261 us  [swap(): return lax.ppermute(value, axis, [(i, i ^ bit) for i in range(size)])]
    ppermute x7 -> x6, waiting for transfers between devices: 181 us -> 83.6 us  [__init__(): lax.ppermute(self.quad, 'dp', [(i, (3 - i // 2) * 2 + i % 2) for i in ran...]
    ppermute x94 -> x48, starting transfers between devices: 173 us -> 118 us  [swap(): return lax.ppermute(value, axis, [(i, i ^ bit) for i in range(size)])]
    another operation x21 -> x4, other arithmetic: 33.5 us -> 3.87 us  [the longest x1 3.2 us: per_device(): jnp.stack([(resid_mid[s] + mlp_total[s].astype(f32)).astype(bf16) for s i...]
    select_n x14 -> x0, other arithmetic: 18.8 us -> none  [join(): jnp.where(mine == 0, kept, other)]
    convert_element_type x15 -> x4, other arithmetic: 31.1 us -> 13.7 us  [the longest x1 5.41 us: per_device(): second.astype(bf16)]
  transfers between devices with their start and end apart: 101 -> 56, of which waited for: 41 -> 25; matrix products, arithmetic and copies ran while one was open for 29% -> 8% of each run, Pallas kernels for 15% -> 33%
where the time goes in v2:
time: 1160 us; the launch traced here: 1150 us
  Pallas kernels  544 us (47%)
  waiting for transfers between devices  353 us (30%)
  starting transfers between devices  124 us (11%)
  other arithmetic  71.6 us (6%)
  local copies, waits for them, and re-layouts  36 us (3%)
  between operations  15.8 us (1%)
    pallas_call x11, Pallas kernels, call(): pl.pallas_call(body, out_shape=tuple((shape for shape, _ in outs)) + tupl...  493 us
    ppermute x48, waiting for transfers between devices, swap(): return lax.ppermute(value, axis, [(i, i ^ bit) for i in range(size)])  261 us
    ppermute x48, starting transfers between devices, swap(): return lax.ppermute(value, axis, [(i, i ^ bit) for i in range(size)])  118 us
    ppermute x6, waiting for transfers between devices, __init__(): lax.ppermute(self.quad, 'dp', [(i, (3 - i // 2) * 2 + i % 2) for i in ran...  83.6 us
    pallas_call x6, Pallas kernels, join_quarters(): pl.pallas_call(join_kernel, out_shape=(out,) * ways, grid_spec=pltpu.Pref...  51.5 us
    convert_element_type x20, other arithmetic, add_low(): return (left.astype(f32) + right.astype(f32)).astype(bf16)  27.5 us
  transfers between devices with their start and end apart: 56, of which 25 were waited for; matrix products, arithmetic and copies ran while one was open for 8% of the time, Pallas kernels for 33%

profile of v2, /device:TPU:9, one launch (start us, length us, event | category | flops | bytes accessed | tf_op | source)
XLA Modules:
  0.0 1149.9 jit_solution(17818092629840815832)
XLA Ops:
  7.3 2.2 fusion.44
  13.6 8.5 fusion.48.refs_9_.refs_14_
  24.9 10.1 collective-permute-done.1.refs_3_.refs_8_.refs_2_
  39.0 2.3 copy-done.38
  41.4 5.7 collective-permute-done.3.refs_5_.refs_10_.refs_4_
  49.4 41.4 %rec_forward.2 = (bf16[4,256,640]{2,1,0:T(8,128)(2,1)}, f32[4,256,640]{2,1,0:T(8,128)}, f32[4,256,640]{2,1,0:T(8,128)}, bf16[4,256,640]{2,1,0:T(8,128)(2,1)}, f3...) custom-call(s32[8,128]{1,0:T(8,128)} %broadcast_in_dim.15.refs_0_, ...), custom_call_target="tpu_custom_call" | custom-call | flops 21275000832 | bytes 65536 | tf_op jit(solution)/shard_map/rec_forward/pallas_call | solution.py:565
  92.0 42.4 %rec_forward.3 = (bf16[4,256,640]{2,1,0:T(8,128)(2,1)}, f32[4,256,640]{2,1,0:T(8,128)}, f32[4,256,640]{2,1,0:T(8,128)}, bf16[4,256,640]{2,1,0:T(8,128)(2,1)}, f3...) custom-call(s32[8,128]{1,0:T(8,128)} %broadcast_in_dim.20.refs_0_, ...), custom_call_target="tpu_custom_call" | custom-call | flops 21275000832 | bytes 65536 | tf_op jit(solution)/shard_map/rec_forward/pallas_call | solution.py:565
  134.4 1.8 collective-permute-start.14
  138.6 5.5 collective-permute-done.14
  150.4 19.4 %collective-permute-done.15 = bf16[256,2048]{1,0:T(8,128)(2,1)S(1)} collective-permute-done((bf16[256,2048]{1,0:T(8,128)(2,1)S(1)}, bf16[256,2048]{1,0:T(8,128)(2,1)S(1)}, u32[]{:S(2)}, u32[]{:S(2)}) %collective-permute-start.15) | collective-permute-done | bytes 1048608 | tf_op jit(solution)/shard_map/ppermute | solution.py:783
  175.4 8.8 collective-permute-done.9.refs_7_.refs_3_
  184.9 7.4 collective-permute-done.8.refs_6_.refs_2_
  193.7 13.0 %collective-permute-done.5.refs_2_ = bf16[256,2048]{1,0:T(8,128)(2,1)S(1)} collective-permute-done((bf16[256,2048]{1,0:T(8,128)(2,1)S(1)}, bf16[256,2048]{1,0:T(8,128)(2,1)S(1)}, u32[]{:S(2)}, u32[]{:S(2)}) %collective-permute-start.5) | collective-permute-done | bytes 1048608 | tf_op jit(solution)/shard_map/ppermute | solution.py:783
  207.3 7.4 collective-permute-done.4.refs_1_
  216.2 9.8 collective-permute-done.11.refs_9_.refs_5_
  226.0 11.2 collective-permute-done.7.refs_4_
  238.3 77.0 %mlp_core.2 = (bf16[8,256,1536]{2,1,0:T(8,128)(2,1)}, bf16[8,256,1536]{2,1,0:T(8,128)(2,1)}, bf16[8,256,1536]{2,1,0:T(8,128)(2,1)}, bf16[4,256,2048]{2,1,0:T(8,1...) custom-call(bf16[256,2048]{1,0:T(8,128)(2,1)} %copy-done.44, ...), custom_call_target="tpu_custom_call" | custom-call | flops 31050000384 | bytes 65536 | tf_op jit(solution)/shard_map/mlp_core/pallas_call | solution.py:565
  315.3 69.9 %mlp_core.3 = (bf16[8,256,1536]{2,1,0:T(8,128)(2,1)}, bf16[8,256,1536]{2,1,0:T(8,128)(2,1)}, bf16[8,256,1536]{2,1,0:T(8,128)(2,1)}, bf16[4,256,2048]{2,1,0:T(8,1...) custom-call(bf16[256,2048]{1,0:T(8,128)(2,1)} %get-tuple-element.279, ...), custom_call_target="tpu_custom_call", output_to_operand_aliasing={{0}: (13, {}), {1}: (14, {}), {2}: (15, {})} | custom-call | flops 31050000384 | bytes 65536 | tf_op jit(solution)/shard_map/mlp_core/pallas_call | solution.py:565
  387.1 2.5 multiply_reduce_fusion.1
  389.6 7.5 reduce-scatter.3.cloned.1.call-done
  397.0 5.3 fusion.72
  402.3 69.7 %weight_grad.5 = (bf16[768,2048]{1,0:T(8,128)(2,1)}, bf16[768,2048]{1,0:T(8,128)(2,1)}, bf16[256,2048]{1,0:T(8,128)(2,1)}, bf16[256,2048]{1,0:T(8,128)(2,1)}, bf...) custom-call(bf16[2048,1536]{1,0:T(8,128)(2,1)} %bitcast.102, bf16[256,2048]{1,0:T(8,128)(2,1)} %copy-done.45, ...), custom_call_target="tpu_custom_call" | custom-call | flops 11500000256 | bytes 65536 | tf_op jit(solution)/shard_map/weight_grad/pallas_call | solution.py:565
  472.1 4.0 collective-permute-start.16
  476.1 42.4 %weight_grad.6 = (bf16[1024,1536]{1,0:T(8,128)(2,1)}, bf16[1024,1536]{1,0:T(8,128)(2,1)}, bf16[256,2048]{1,0:T(8,128)(2,1)}, bf16[256,2048]{1,0:T(8,128)(2,1)}) custom-call(bf16[256,2048]{1,0:T(8,128)(2,1)} %copy-done.44, bf16[256,2048]{1,0:T(8,128)(2,1)} %copy-done.56, bf16[256,2048]{1,0:T(8,128)(2,1)} %copy-done.55, bf16[128,2048]{1,0:T(8,128)(2,1)} %copy-done.84, ...), custom_call_target="tpu_custom_call" | custom-call | flops 11500000256 | bytes 65536 | tf_op jit(solution)/shard_map/weight_grad/pallas_call | solution.py:565
  519.5 2.4 multiply_reduce_fusion
  522.0 5.4 fusion.71
  527.4 3.2 add_convert_fusion.2.refs_12_
  532.8 20.7 %weight_grad.7 = (bf16[1024,1536]{1,0:T(8,128)(2,1)}, bf16[1024,1536]{1,0:T(8,128)(2,1)}) custom-call(bf16[256,2048]{1,0:T(8,128)(2,1)} %copy-done.44, bf16[256,2048]{1,0:T(8,128)(2,1)} %copy-done.56, bf16[256,2048]{1,0:T(8,128)(2,1)} %copy-done.55, bf16[128,2048]{1,0:T(8,128)(2,1)} %copy-done.84, bf16[128,2048]{1,0:T(8,128)(2,1)} %copy-done.83, ...), custom_call_target="tpu_custom_call" | custom-call | flops 11500000256 | bytes 65536 | tf_op jit(solution)/shard_map/weight_grad/pallas_call | solution.py:565
  553.6 2.7 add_convert_fusion.1.refs_24_
  558.9 48.1 %rec_backward.2 = (bf16[8,256,1280]{2,1,0:T(8,128)(2,1)}, bf16[8,256,1280]{2,1,0:T(8,128)(2,1)}, f32[8,8,640]{2,1,0:T(8,128)}, f32[8,2048]{1,0:T(8,128)}, bf16[2...) custom-call(s32[8,128]{1,0:T(8,128)} %broadcast_in_dim.15.refs_0_, ...), custom_call_target="tpu_custom_call" | custom-call | flops 24725000192 | bytes 65536 | tf_op jit(solution)/shard_map/rec_backward/pallas_call | solution.py:565
  607.9 3.3 add_convert_fusion.9.refs_28_
  611.2 3.1 add_convert_fusion.8.refs_29_
  614.3 2.7 add_convert_fusion.refs_30_
  619.4 45.0 %rec_backward.3 = (bf16[8,256,1280]{2,1,0:T(8,128)(2,1)}, bf16[8,256,1280]{2,1,0:T(8,128)(2,1)}, f32[8,8,640]{2,1,0:T(8,128)}, f32[8,2048]{1,0:T(8,128)}, bf16[2...) custom-call(s32[8,128]{1,0:T(8,128)} %broadcast_in_dim.20.refs_0_, ...), custom_call_target="tpu_custom_call", output_to_operand_aliasing={{0}: (22, {}), {1}: (23, {})} | custom-call | flops 24725000192 | bytes 65536 | tf_op jit(solution)/shard_map/rec_backward/pallas_call | solution.py:565
  666.5 3.8 convolution_bitcast_fusion
  670.4 2.0 fusion.23
  676.0 3.9 collective-permute-start.24
  689.5 3.2 pad_maximum_fusion
  694.2 3.5 collective-permute-start.27
  697.7 2.9 add_convert_fusion.7.refs_15_
  700.7 24.8 %weight_grad.8 = (bf16[1024,1280]{1,0:T(8,128)(2,1)}, bf16[1024,1280]{1,0:T(8,128)(2,1)}, bf16[256,2048]{1,0:T(8,128)(2,1)}, bf16[256,2048]{1,0:T(8,128)(2,1)}) custom-call(bf16[256,2048]{1,0:T(8,128)(2,1)} %copy-done.43, bf16[256,2048]{1,0:T(8,128)(2,1)} %copy-done.54, bf16[256,2048]{1,0:T(8,128)(2,1)} %copy-done.53, bf16[128,2048]{1,0:T(8,128)(2,1)} %copy-done.82, ...), custom_call_target="tpu_custom_call" | custom-call | flops 11500000256 | bytes 65536 | tf_op jit(solution)/shard_map/weight_grad/pallas_call | solution.py:565
  725.4 65.8 %collective-permute-start.30 = (bf16[1024,1280]{1,0:T(8,128)(2,1)}, bf16[1024,1280]{1,0:T(8,128)(2,1)}, u32[]{:S(2)}, u32[]{:S(2)}) collective-permute-start(bf16[1024,1280]{1,0:T(8,128)(2,1)} %get-tuple-element.221), channel_id=1, source_target_pairs={{0,4},{4,0},{8,12},{12,8},{16,20},{20,16},{24,28},{28,24},{1,5},{5... | collective-permute-start | bytes 7864328 | tf_op jit(solution)/shard_map/ppermute | solution.py:783
  791.2 4.5 collective-permute-done.50
  795.7 1.7 add_convert_fusion.4.first
  797.5 3.2 collective-permute-start.52
  800.7 28.9 %collective-permute-done.42 = bf16[512,1536]{1,0:T(8,128)(2,1)S(1)} collective-permute-done((bf16[512,1536]{1,0:T(8,128)(2,1)S(1)}, bf16[512,1536]{1,0:T(8,128)(2,1)S(1)}, u32[]{:S(2)}, u32[]{:S(2)}) %collective-permute-start.42) | collective-permute-done | bytes 1572896 | tf_op jit(solution)/shard_map/ppermute | solution.py:835
  834.1 3.5 join_quarters.6
  843.3 11.4 weight_grad.9
  855.2 2.5 add_convert_fusion.3
  862.3 2.4 collective-permute-start.37
  864.7 23.6 %collective-permute-done.31 = bf16[512,1280]{1,0:T(8,128)(2,1)S(1)} collective-permute-done((bf16[512,1280]{1,0:T(8,128)(2,1)S(1)}, bf16[512,1280]{1,0:T(8,128)(2,1)S(1)}, u32[]{:S(2)}, u32[]{:S(2)}) %collective-permute-start.31) | collective-permute-done | bytes 1310752 | tf_op jit(solution)/shard_map/ppermute | solution.py:783
  888.8 47.2 %collective-permute-done.37 = bf16[320,1024]{1,0:T(8,128)(2,1)S(1)} collective-permute-done((bf16[320,1024]{1,0:T(8,128)(2,1)S(1)}, bf16[320,1024]{1,0:T(8,128)(2,1)S(1)}, u32[]{:S(2)}, u32[]{:S(2)}) %collective-permute-start.37) | collective-permute-done | bytes 655392 | tf_op jit(solution)/shard_map/ppermute | solution.py:783
  939.9 29.9 %collective-permute-done.43.second = bf16[512,1536]{1,0:T(8,128)(2,1)S(1)} collective-permute-done((bf16[512,1536]{1,0:T(8,128)(2,1)S(1)}, bf16[512,1536]{1,0:T(8,128)(2,1)S(1)}, u32[]{:S(2)}, u32[]{:S(2)}) %collective-permute-start.43) | collective-permute-done | bytes 1572896 | tf_op jit(solution)/shard_map/ppermute | solution.py:783
  971.1 50.2 %collective-permute-done.38 = bf16[320,1024]{1,0:T(8,128)(2,1)S(1)} collective-permute-done((bf16[320,1024]{1,0:T(8,128)(2,1)S(1)}, bf16[320,1024]{1,0:T(8,128)(2,1)S(1)}, u32[]{:S(2)}, u32[]{:S(2)}) %collective-permute-start.38) | collective-permute-done | bytes 655392 | tf_op jit(solution)/shard_map/ppermute | solution.py:835
  1021.3 2.2 collective-permute-start.45
  1026.9 2.6 fusion.59
  1032.0 28.0 %collective-permute-done.47.second = bf16[512,1536]{1,0:T(8,128)(2,1)} collective-permute-done((bf16[512,1536]{1,0:T(8,128)(2,1)S(1)}, bf16[512,1536]{1,0:T(8,128)(2,1)}, u32[]{:S(2)}, u32[]{:S(2)}) %collective-permute-start.47) | collective-permute-done | bytes 1572896 | tf_op jit(solution)/shard_map/ppermute | solution.py:783
  1061.1 12.9 %collective-permute-done.39.second = bf16[320,1024]{1,0:T(8,128)(2,1)} collective-permute-done((bf16[320,1024]{1,0:T(8,128)(2,1)S(1)}, bf16[320,1024]{1,0:T(8,128)(2,1)}, u32[]{:S(2)}, u32[]{:S(2)}) %collective-permute-start.39) | collective-permute-done | bytes 655392 | tf_op jit(solution)/shard_map/ppermute | solution.py:783
  1075.2 10.5 join_quarters.9
  1085.7 16.3 %collective-permute-done.33.second = bf16[512,1280]{1,0:T(8,128)(2,1)S(1)} collective-permute-done((bf16[512,1280]{1,0:T(8,128)(2,1)S(1)}, bf16[512,1280]{1,0:T(8,128)(2,1)S(1)}, u32[]{:S(2)}, u32[]{:S(2)}) %collective-permute-start.33) | collective-permute-done | bytes 1310752 | tf_op jit(solution)/shard_map/ppermute | solution.py:783
  1102.8 10.3 join_quarters.11
  1113.1 7.5 join_quarters.8
  1122.8 10.3 join_quarters.10
  1133.1 9.5 join_quarters.7
  (354 shorter events, 93.1 us)
Async XLA Ops:
  7.2 389.8 %reduce-scatter.3.cloned.1.call-start = ((), (), s32[]{:S(2)}) async-start(), calls=%async_computation.2 | async-start | bytes 5242880 | tf_op jit(solution)/shard_map/reduce_scatter | solution.py:972
  11.0 24.1 %collective-permute-start.1 = (bf16[256,2048]{1,0:T(8,128)(2,1)S(1)}, bf16[256,2048]{1,0:T(8,128)(2,1)S(1)}, u32[]{:S(2)}, u32[]{:S(2)}) collective-permute-start(bf16[256,2048]{1,0:T(8,128)(2,1)S(1)} %get-tuple-element.250.refs_1_.refs_6_.refs_0_), channel_id=1, source_target_pairs={{0,2},{1,3},{2,0},{3,1},{4,6},{5,7},{6,4},{7,5},{8,10},{9,11},{10,... | collective-permute-start | bytes 3145736 | tf_op jit(solution)/shard_map/ppermute | solution.py:783
  12.3 24.1 %collective-permute-start = (bf16[256,2048]{1,0:T(8,128)(2,1)S(1)}, bf16[256,2048]{1,0:T(8,128)(2,1)S(1)}, u32[]{:S(2)}, u32[]{:S(2)}) collective-permute-start(bf16[256,2048]{1,0:T(8,128)(2,1)S(1)} %get-tuple-element.250.refs_1_.refs_6_.refs_0_), channel_id=1, source_target_pairs={{0,1},{1,0},{2,3},{3,2},{4,5},{5,4},{6,7},{7,6},{8,9},{9,8},{10,11... | collective-permute-start | bytes 3145736 | tf_op jit(solution)/shard_map/ppermute | solution.py:783
  35.1 11.9 %collective-permute-start.3 = (bf16[128,2048]{1,0:T(8,128)(2,1)S(1)}, bf16[128,2048]{1,0:T(8,128)(2,1)S(1)}, u32[]{:S(2)}, u32[]{:S(2)}) collective-permute-start(bf16[128,2048]{1,0:T(8,128)(2,1)S(1)} %slice.227), channel_id=1, source_target_pairs={{0,1},{1,0},{2,3},{3,2},{4,5},{5,4},{6,7},{7,6},{8,9},{9,8},{10,11... | collective-permute-start | bytes 1572872 | tf_op jit(solution)/shard_map/ppermute | solution.py:783
  36.5 11.7 %collective-permute-start.2 = (bf16[128,2048]{1,0:T(8,128)(2,1)S(1)}, bf16[128,2048]{1,0:T(8,128)(2,1)S(1)}, u32[]{:S(2)}, u32[]{:S(2)}) collective-permute-start(bf16[128,2048]{1,0:T(8,128)(2,1)S(1)} %slice.226), channel_id=1, source_target_pairs={{0,2},{1,3},{2,0},{3,1},{4,6},{5,7},{6,4},{7,5},{8,10},{9,11},{10,... | collective-permute-start | bytes 1572872 | tf_op jit(solution)/shard_map/ppermute | solution.py:783
  134.4 9.7 collective-permute-start.14
  138.4 8.9 collective-permute-start.12
  144.4 25.4 %collective-permute-start.15 = (bf16[256,2048]{1,0:T(8,128)(2,1)S(1)}, bf16[256,2048]{1,0:T(8,128)(2,1)S(1)}, u32[]{:S(2)}, u32[]{:S(2)}) collective-permute-start(bf16[256,2048]{1,0:T(8,128)(2,1)S(1)} %pad_maximum_fusion.3), channel_id=1, source_target_pairs={{0,1},{1,0},{2,3},{3,2},{4,5},{5,4},{6,7},{7,6},{8,9},{9,8},{10,11... | collective-permute-start | bytes 3145736 | tf_op jit(solution)/shard_map/ppermute | solution.py:783
  147.6 22.2 %collective-permute-start.13 = (bf16[256,2048]{1,0:T(8,128)(2,1)S(1)}, bf16[256,2048]{1,0:T(8,128)(2,1)S(1)}, u32[]{:S(2)}, u32[]{:S(2)}) collective-permute-start(bf16[256,2048]{1,0:T(8,128)(2,1)S(1)} %pad_maximum_fusion.2), channel_id=1, source_target_pairs={{0,2},{1,3},{2,0},{3,1},{4,6},{5,7},{6,4},{7,5},{8,10},{9,11},{10,... | collective-permute-start | bytes 3145736 | tf_op jit(solution)/shard_map/ppermute | solution.py:783
  148.9 35.3 %collective-permute-start.9 = (bf16[256,2048]{1,0:T(8,128)(2,1)S(1)}, bf16[256,2048]{1,0:T(8,128)(2,1)S(1)}, u32[]{:S(2)}, u32[]{:S(2)}) collective-permute-start(bf16[256,2048]{1,0:T(8,128)(2,1)S(1)} %get-tuple-element.136.refs_5_.refs_1_), channel_id=1, source_target_pairs={{0,2},{1,3},{2,0},{3,1},{4,6},{5,7},{6,4},{7,5},{8,10},{9,11},{10,... | collective-permute-start | bytes 3145736 | tf_op jit(solution)/shard_map/ppermute | solution.py:783
  150.3 42.0 %collective-permute-start.8 = (bf16[256,2048]{1,0:T(8,128)(2,1)S(1)}, bf16[256,2048]{1,0:T(8,128)(2,1)S(1)}, u32[]{:S(2)}, u32[]{:S(2)}) collective-permute-start(bf16[256,2048]{1,0:T(8,128)(2,1)S(1)} %get-tuple-element.136.refs_5_.refs_1_), channel_id=1, source_target_pairs={{0,1},{1,0},{2,3},{3,2},{4,5},{5,4},{6,7},{7,6},{8,9},{9,8},{10,11... | collective-permute-start | bytes 3145736 | tf_op jit(solution)/shard_map/ppermute | solution.py:783
  173.9 32.8 %collective-permute-start.5 = (bf16[256,2048]{1,0:T(8,128)(2,1)S(1)}, bf16[256,2048]{1,0:T(8,128)(2,1)S(1)}, u32[]{:S(2)}, u32[]{:S(2)}) collective-permute-start(bf16[256,2048]{1,0:T(8,128)(2,1)S(1)} %get-tuple-element.278.refs_0_), channel_id=1, source_target_pairs={{0,2},{1,3},{2,0},{3,1},{4,6},{5,7},{6,4},{7,5},{8,10},{9,11},{10,... | collective-permute-start | bytes 3145736 | tf_op jit(solution)/shard_map/ppermute | solution.py:783
  175.2 39.6 %collective-permute-start.4 = (bf16[256,2048]{1,0:T(8,128)(2,1)S(1)}, bf16[256,2048]{1,0:T(8,128)(2,1)S(1)}, u32[]{:S(2)}, u32[]{:S(2)}) collective-permute-start(bf16[256,2048]{1,0:T(8,128)(2,1)S(1)} %get-tuple-element.278.refs_0_), channel_id=1, source_target_pairs={{0,1},{1,0},{2,3},{3,2},{4,5},{5,4},{6,7},{7,6},{8,9},{9,8},{10,11... | collective-permute-start | bytes 3145736 | tf_op jit(solution)/shard_map/ppermute | solution.py:783
  184.3 41.7 %collective-permute-start.11 = (bf16[128,2048]{1,0:T(8,128)(2,1)S(1)}, bf16[128,2048]{1,0:T(8,128)(2,1)S(1)}, u32[]{:S(2)}, u32[]{:S(2)}) collective-permute-start(bf16[128,2048]{1,0:T(8,128)(2,1)S(1)} %slice.231), channel_id=1, source_target_pairs={{0,1},{1,0},{2,3},{3,2},{4,5},{5,4},{6,7},{7,6},{8,9},{9,8},{10,11... | collective-permute-start | bytes 1572872 | tf_op jit(solution)/shard_map/ppermute | solution.py:783
  192.3 33.7 %collective-permute-start.10 = (bf16[128,2048]{1,0:T(8,128)(2,1)S(1)}, bf16[128,2048]{1,0:T(8,128)(2,1)S(1)}, u32[]{:S(2)}, u32[]{:S(2)}) collective-permute-start(bf16[128,2048]{1,0:T(8,128)(2,1)S(1)} %slice.230), channel_id=1, source_target_pairs={{0,2},{1,3},{2,0},{3,1},{4,6},{5,7},{6,4},{7,5},{8,10},{9,11},{10,... | collective-permute-start | bytes 1572872 | tf_op jit(solution)/shard_map/ppermute | solution.py:783
  206.7 30.5 %collective-permute-start.7 = (bf16[128,2048]{1,0:T(8,128)(2,1)S(1)}, bf16[128,2048]{1,0:T(8,128)(2,1)S(1)}, u32[]{:S(2)}, u32[]{:S(2)}) collective-permute-start(bf16[128,2048]{1,0:T(8,128)(2,1)S(1)} %slice.229), channel_id=1, source_target_pairs={{0,1},{1,0},{2,3},{3,2},{4,5},{5,4},{6,7},{7,6},{8,9},{9,8},{10,11... | collective-permute-start | bytes 1572872 | tf_op jit(solution)/shard_map/ppermute | solution.py:783
  214.8 22.4 %collective-permute-start.6 = (bf16[128,2048]{1,0:T(8,128)(2,1)S(1)}, bf16[128,2048]{1,0:T(8,128)(2,1)S(1)}, u32[]{:S(2)}, u32[]{:S(2)}) collective-permute-start(bf16[128,2048]{1,0:T(8,128)(2,1)S(1)} %slice.228), channel_id=1, source_target_pairs={{0,2},{1,3},{2,0},{3,1},{4,6},{5,7},{6,4},{7,5},{8,10},{9,11},{10,... | collective-permute-start | bytes 1572872 | tf_op jit(solution)/shard_map/ppermute | solution.py:783
  315.3 206.7 %reduce-scatter.5.cloned.1.call-start = ((), (), s32[]{:S(2)}) async-start(), calls=%async_computation.3 | async-start | bytes 5242880 | tf_op jit(solution)/shard_map/reduce_scatter | solution.py:972
  472.1 55.3 %collective-permute-start.16 = (bf16[768,2048]{1,0:T(8,128)(2,1)}, bf16[768,2048]{1,0:T(8,128)(2,1)}, u32[]{:S(2)}, u32[]{:S(2)}) collective-permute-start(bf16[768,2048]{1,0:T(8,128)(2,1)} %get-tuple-element.184), channel_id=1, source_target_pairs={{0,4},{4,0},{8,12},{12,8},{16,20},{20,16},{24,28},{28,24},{1,5},{5... | collective-permute-start | bytes 9437192 | tf_op jit(solution)/shard_map/ppermute | solution.py:783
  518.6 35.1 %collective-permute-start.17 = (bf16[1024,1536]{1,0:T(8,128)(2,1)}, bf16[1024,1536]{1,0:T(8,128)(2,1)}, u32[]{:S(2)}, u32[]{:S(2)}) collective-permute-start(bf16[1024,1536]{1,0:T(8,128)(2,1)} %get-tuple-element.186), channel_id=1, source_target_pairs={{0,4},{4,0},{8,12},{12,8},{16,20},{20,16},{24,28},{28,24},{1,5},{5... | collective-permute-start | bytes 9437192 | tf_op jit(solution)/shard_map/ppermute | solution.py:783
  532.2 75.7 %collective-permute-start.18 = (bf16[384,2048]{1,0:T(8,128)(2,1)}, bf16[384,2048]{1,0:T(8,128)(2,1)}, u32[]{:S(2)}, u32[]{:S(2)}) collective-permute-start(bf16[384,2048]{1,0:T(8,128)(2,1)} %constant_dynamic-slice_fusion.6), channel_id=1, source_target_pairs={{0,8},{4,12},{8,0},{12,4},{16,24},{20,28},{24,16},{28,20},{1,9},{5... | collective-permute-start | bytes 4718600 | tf_op jit(solution)/shard_map/ppermute | solution.py:783
  553.5 60.8 %collective-permute-start.20 = (bf16[1024,1536]{1,0:T(8,128)(2,1)}, bf16[1024,1536]{1,0:T(8,128)(2,1)}, u32[]{:S(2)}, u32[]{:S(2)}) collective-permute-start(bf16[1024,1536]{1,0:T(8,128)(2,1)} %get-tuple-element.204), channel_id=1, source_target_pairs={{0,4},{4,0},{8,12},{12,8},{16,20},{20,16},{24,28},{28,24},{1,5},{5... | collective-permute-start | bytes 9437192 | tf_op jit(solution)/shard_map/ppermute | solution.py:783
  557.8 53.4 %collective-permute-start.19 = (bf16[512,1536]{1,0:T(8,128)(2,1)}, bf16[512,1536]{1,0:T(8,128)(2,1)}, u32[]{:S(2)}, u32[]{:S(2)}) collective-permute-start(bf16[512,1536]{1,0:T(8,128)(2,1)} %constant_dynamic-slice_fusion.5), channel_id=1, source_target_pairs={{0,8},{4,12},{8,0},{12,4},{16,24},{20,28},{24,16},{28,20},{1,9},{5... | collective-permute-start | bytes 4718600 | tf_op jit(solution)/shard_map/ppermute | solution.py:783
  558.9 49.0 %copy-start.9 = (bf16[768,2048]{1,0:T(8,128)(2,1)S(1)}, bf16[768,2048]{1,0:T(8,128)(2,1)}, u32[]{:S(2)}) copy-start(bf16[768,2048]{1,0:T(8,128)(2,1)} %copy-done.8) | copy-start | bytes 9437188
  618.5 79.3 %collective-permute-start.21 = (bf16[512,1536]{1,0:T(8,128)(2,1)}, bf16[512,1536]{1,0:T(8,128)(2,1)}, u32[]{:S(2)}, u32[]{:S(2)}) collective-permute-start(bf16[512,1536]{1,0:T(8,128)(2,1)} %constant_dynamic-slice_fusion.4), channel_id=1, source_target_pairs={{0,8},{4,12},{8,0},{12,4},{16,24},{20,28},{24,16},{28,20},{1,9},{5... | collective-permute-start | bytes 4718600 | tf_op jit(solution)/shard_map/ppermute | solution.py:783
  619.4 46.1 %copy-start.65 = (f32[640]{0:T(1024)S(1)}, f32[640]{0:T(1024)}, u32[]{:S(2)}) copy-start(f32[640]{0:T(1024)} %param.28) | copy-start | bytes 7684
  619.4 46.9 %copy-start.62 = (f32[2048]{0:T(1024)S(1)}, f32[2048]{0:T(1024)}, u32[]{:S(2)}) copy-start(f32[2048]{0:T(1024)} %param.19) | copy-start | bytes 24580
  619.4 47.1 %copy-start.37 = (bf16[4,256,640]{2,1,0:T(8,128)(2,1)S(1)}, bf16[4,256,640]{2,1,0:T(8,128)(2,1)}, u32[]{:S(2)}) copy-start(bf16[4,256,640]{2,1,0:T(8,128)(2,1)} %get-tuple-element.194.refs_18_) | copy-start | bytes 3932164
  666.4 6.4 collective-permute-start.22
  672.9 2.7 collective-permute-start.23
  676.0 5.1 collective-permute-start.24
  683.1 4.7 collective-permute-start.25
  687.9 6.3 collective-permute-start.26
  692.7 103.0 %collective-permute-start.50 = (bf16[384,2048]{1,0:T(8,128)(2,1)S(1)}, bf16[384,2048]{1,0:T(8,128)(2,1)S(1)}, u32[]{:S(2)}, u32[]{:S(2)}) collective-permute-start(bf16[384,2048]{1,0:T(8,128)(2,1)S(1)} %copy-done.16), channel_id=1, source_target_pairs={{0,24},{4,28},{8,16},{12,20},{16,8},{20,12},{24,0},{28,4},{1,25},{... | collective-permute-start | bytes 4718600 | tf_op jit(solution)/shard_map/ppermute | solution.py:835
  692.7 136.8 %collective-permute-start.42 = (bf16[512,1536]{1,0:T(8,128)(2,1)S(1)}, bf16[512,1536]{1,0:T(8,128)(2,1)S(1)}, u32[]{:S(2)}, u32[]{:S(2)}) collective-permute-start(bf16[512,1536]{1,0:T(8,128)(2,1)S(1)} %copy-done.15), channel_id=1, source_target_pairs={{0,24},{4,28},{8,16},{12,20},{16,8},{20,12},{24,0},{28,4},{1,25},{... | collective-permute-start | bytes 4718600 | tf_op jit(solution)/shard_map/ppermute | solution.py:835
  694.2 135.3 %copy-start.63 = (bf16[96,640]{1,0:T(8,128)(2,1)}, bf16[96,640]{1,0:T(8,128)(2,1)S(1)}, u32[]{:S(2)}) copy-start(bf16[96,640]{1,0:T(8,128)(2,1)S(1)} %add_convert_fusion.20.first) | copy-start | bytes 368644
  694.2 137.0 %collective-permute-start.27 = (bf16[96,640]{1,0:T(8,128)(2,1)S(1)}, bf16[96,640]{1,0:T(8,128)(2,1)S(1)}, u32[]{:S(2)}, u32[]{:S(2)}) collective-permute-start(bf16[96,640]{1,0:T(8,128)(2,1)S(1)} %add_convert_fusion.20.first), channel_id=1, source_target_pairs={{0,8},{4,12},{8,0},{12,4},{16,24},{20,28},{24,16},{28,20},{1,9},{5... | collective-permute-start | bytes 368648 | tf_op jit(solution)/shard_map/ppermute | solution.py:783
  725.4 129.7 %collective-permute-start.30 = (bf16[1024,1280]{1,0:T(8,128)(2,1)}, bf16[1024,1280]{1,0:T(8,128)(2,1)}, u32[]{:S(2)}, u32[]{:S(2)}) collective-permute-start(bf16[1024,1280]{1,0:T(8,128)(2,1)} %get-tuple-element.221), channel_id=1, source_target_pairs={{0,4},{4,0},{8,12},{12,8},{16,20},{20,16},{24,28},{28,24},{1,5},{5... | collective-permute-start | bytes 7864328 | tf_op jit(solution)/shard_map/ppermute | solution.py:783
  797.5 226.7 %collective-permute-start.52 = (bf16[384,2048]{1,0:T(8,128)(2,1)}, bf16[384,2048]{1,0:T(8,128)(2,1)}, u32[]{:S(2)}, u32[]{:S(2)}) collective-permute-start(bf16[384,2048]{1,0:T(8,128)(2,1)} %add_convert_fusion.4.first), channel_id=1, source_target_pairs={{0,4},{4,0},{8,12},{12,8},{16,20},{20,16},{24,28},{28,24},{1,5},{5... | collective-permute-start | bytes 4718600 | tf_op jit(solution)/shard_map/ppermute | solution.py:783
  800.7 137.2 %collective-permute-start.51 = (bf16[384,2048]{1,0:T(8,128)(2,1)}, bf16[384,2048]{1,0:T(8,128)(2,1)}, u32[]{:S(2)}, u32[]{:S(2)}) collective-permute-start(bf16[384,2048]{1,0:T(8,128)(2,1)} %add_convert_fusion.4.first), channel_id=1, source_target_pairs={{0,8},{4,12},{8,0},{12,4},{16,24},{20,28},{24,16},{28,20},{1,9},{5... | collective-permute-start | bytes 4718600 | tf_op jit(solution)/shard_map/ppermute | solution.py:783
  829.5 3.3 collective-permute-start.28
  831.2 1.6 collective-permute-start.29
  854.6 7.0 collective-permute-start.36
  857.9 30.4 %collective-permute-start.31 = (bf16[512,1280]{1,0:T(8,128)(2,1)S(1)}, bf16[512,1280]{1,0:T(8,128)(2,1)S(1)}, u32[]{:S(2)}, u32[]{:S(2)}) collective-permute-start(bf16[512,1280]{1,0:T(8,128)(2,1)S(1)} %constant_dynamic-slice_fusion.1), channel_id=1, source_target_pairs={{0,8},{4,12},{8,0},{12,4},{16,24},{20,28},{24,16},{28,20},{1,9},{5... | collective-permute-start | bytes 3932168 | tf_op jit(solution)/shard_map/ppermute | solution.py:783
  858.6 80.9 %collective-permute-start.46 = (bf16[512,1536]{1,0:T(8,128)(2,1)S(1)}, bf16[512,1536]{1,0:T(8,128)(2,1)S(1)}, u32[]{:S(2)}, u32[]{:S(2)}) collective-permute-start(bf16[512,1536]{1,0:T(8,128)(2,1)S(1)} %copy-done.17), channel_id=1, source_target_pairs={{0,24},{4,28},{8,16},{12,20},{16,8},{20,12},{24,0},{28,4},{1,25},{... | collective-permute-start | bytes 4718600 | tf_op jit(solution)/shard_map/ppermute | solution.py:835
  862.3 73.8 %collective-permute-start.37 = (bf16[320,1024]{1,0:T(8,128)(2,1)S(1)}, bf16[320,1024]{1,0:T(8,128)(2,1)S(1)}, u32[]{:S(2)}, u32[]{:S(2)}) collective-permute-start(bf16[320,1024]{1,0:T(8,128)(2,1)S(1)} %constant_dynamic-slice_fusion), channel_id=1, source_target_pairs={{0,8},{4,12},{8,0},{12,4},{16,24},{20,28},{24,16},{28,20},{1,9},{5... | collective-permute-start | bytes 1966088 | tf_op jit(solution)/shard_map/ppermute | solution.py:783
  888.3 81.5 %collective-permute-start.43 = (bf16[512,1536]{1,0:T(8,128)(2,1)S(1)}, bf16[512,1536]{1,0:T(8,128)(2,1)S(1)}, u32[]{:S(2)}, u32[]{:S(2)}) collective-permute-start(bf16[512,1536]{1,0:T(8,128)(2,1)S(1)} %copy-done.34), channel_id=1, source_target_pairs={{0,8},{4,12},{8,0},{12,4},{16,24},{20,28},{24,16},{28,20},{1,9},{5... | collective-permute-start | bytes 4718600 | tf_op jit(solution)/shard_map/ppermute | solution.py:783
  936.1 87.7 %collective-permute-start.32 = (bf16[512,1280]{1,0:T(8,128)(2,1)S(1)}, bf16[512,1280]{1,0:T(8,128)(2,1)S(1)}, u32[]{:S(2)}, u32[]{:S(2)}) collective-permute-start(bf16[512,1280]{1,0:T(8,128)(2,1)S(1)} %add_convert_fusion.12), channel_id=1, source_target_pairs={{0,24},{4,28},{8,16},{12,20},{16,8},{20,12},{24,0},{28,4},{1,25},{... | collective-permute-start | bytes 3932168 | tf_op jit(solution)/shard_map/ppermute | solution.py:835
  937.8 87.9 %collective-permute-start.44 = (bf16[512,1536]{1,0:T(8,128)(2,1)S(1)}, bf16[512,1536]{1,0:T(8,128)(2,1)S(1)}, u32[]{:S(2)}, u32[]{:S(2)}) collective-permute-start(bf16[512,1536]{1,0:T(8,128)(2,1)S(1)} %copy-done.34), channel_id=1, source_target_pairs={{0,4},{4,0},{8,12},{12,8},{16,20},{20,16},{24,28},{28,24},{1,5},{5... | collective-permute-start | bytes 4718600 | tf_op jit(solution)/shard_map/ppermute | solution.py:783
  939.5 81.8 %collective-permute-start.38 = (bf16[320,1024]{1,0:T(8,128)(2,1)S(1)}, bf16[320,1024]{1,0:T(8,128)(2,1)S(1)}, u32[]{:S(2)}, u32[]{:S(2)}) collective-permute-start(bf16[320,1024]{1,0:T(8,128)(2,1)S(1)} %add_convert_fusion.16), channel_id=1, source_target_pairs={{0,24},{4,28},{8,16},{12,20},{16,8},{20,12},{24,0},{28,4},{1,25},{... | collective-permute-start | bytes 1966088 | tf_op jit(solution)/shard_map/ppermute | solution.py:835
  939.9 91.7 %copy-start.35 = (bf16[512,1536]{1,0:T(8,128)(2,1)}, bf16[512,1536]{1,0:T(8,128)(2,1)S(1)}, u32[]{:S(2)}) copy-start(bf16[512,1536]{1,0:T(8,128)(2,1)S(1)} %add_convert_fusion.5.first) | copy-start | bytes 4718596
  969.8 54.4 %copy-start.74 = (bf16[512,1536]{1,0:T(8,128)(2,1)}, bf16[512,1536]{1,0:T(8,128)(2,1)S(1)}, u32[]{:S(2)}) copy-start(bf16[512,1536]{1,0:T(8,128)(2,1)S(1)} %collective-permute-done.43.second) | copy-start | bytes 4718596
  969.8 59.7 %collective-permute-start.53 = (bf16[384,2048]{1,0:T(8,128)(2,1)}, bf16[384,2048]{1,0:T(8,128)(2,1)S(1)}, u32[]{:S(2)}, u32[]{:S(2)}) collective-permute-start(bf16[384,2048]{1,0:T(8,128)(2,1)} %collective-permute-done.51.second), channel_id=1, source_target_pairs={{0,4},{4,0},{8,12},{12,8},{16,20},{20,16},{24,28},{28,24},{1,5},{5... | collective-permute-start | bytes 4718600 | tf_op jit(solution)/shard_map/ppermute | solution.py:783
  1021.3 10.3 collective-permute-start.45
  1023.8 36.2 %collective-permute-start.47 = (bf16[512,1536]{1,0:T(8,128)(2,1)S(1)}, bf16[512,1536]{1,0:T(8,128)(2,1)}, u32[]{:S(2)}, u32[]{:S(2)}) collective-permute-start(bf16[512,1536]{1,0:T(8,128)(2,1)S(1)} %add_convert_fusion.5.first), channel_id=1, source_target_pairs={{0,8},{4,12},{8,0},{12,4},{16,24},{20,28},{24,16},{28,20},{1,9},{5... | collective-permute-start | bytes 4718600 | tf_op jit(solution)/shard_map/ppermute | solution.py:783
  1024.2 61.5 %copy-start.39 = (bf16[512,1280]{1,0:T(8,128)(2,1)}, bf16[512,1280]{1,0:T(8,128)(2,1)S(1)}, u32[]{:S(2)}) copy-start(bf16[512,1280]{1,0:T(8,128)(2,1)S(1)} %add_convert_fusion.11.first) | copy-start | bytes 3932164
  1024.2 49.8 %collective-permute-start.39 = (bf16[320,1024]{1,0:T(8,128)(2,1)S(1)}, bf16[320,1024]{1,0:T(8,128)(2,1)}, u32[]{:S(2)}, u32[]{:S(2)}) collective-permute-start(bf16[320,1024]{1,0:T(8,128)(2,1)S(1)} %add_convert_fusion.15.first), channel_id=1, source_target_pairs={{0,8},{4,12},{8,0},{12,4},{16,24},{20,28},{24,16},{28,20},{1,9},{5... | collective-permute-start | bytes 1966088 | tf_op jit(solution)/shard_map/ppermute | solution.py:783
  1025.7 76.3 %collective-permute-start.33 = (bf16[512,1280]{1,0:T(8,128)(2,1)S(1)}, bf16[512,1280]{1,0:T(8,128)(2,1)S(1)}, u32[]{:S(2)}, u32[]{:S(2)}) collective-permute-start(bf16[512,1280]{1,0:T(8,128)(2,1)S(1)} %add_convert_fusion.11.first), channel_id=1, source_target_pairs={{0,8},{4,12},{8,0},{12,4},{16,24},{20,28},{24,16},{28,20},{1,9},{5... | collective-permute-start | bytes 3932168 | tf_op jit(solution)/shard_map/ppermute | solution.py:783
  1029.5 56.2 %collective-permute-start.40 = (bf16[320,1024]{1,0:T(8,128)(2,1)S(1)}, bf16[320,1024]{1,0:T(8,128)(2,1)}, u32[]{:S(2)}, u32[]{:S(2)}) collective-permute-start(bf16[320,1024]{1,0:T(8,128)(2,1)S(1)} %add_convert_fusion.15.first), channel_id=1, source_target_pairs={{0,4},{4,0},{8,12},{12,8},{16,20},{20,16},{24,28},{28,24},{1,5},{5... | collective-permute-start | bytes 1966088 | tf_op jit(solution)/shard_map/ppermute | solution.py:783
  1031.6 88.9 %collective-permute-start.48 = (bf16[512,1536]{1,0:T(8,128)(2,1)S(1)}, bf16[512,1536]{1,0:T(8,128)(2,1)S(1)}, u32[]{:S(2)}, u32[]{:S(2)}) collective-permute-start(bf16[512,1536]{1,0:T(8,128)(2,1)S(1)} %add_convert_fusion.5.first), channel_id=1, source_target_pairs={{0,4},{4,0},{8,12},{12,8},{16,20},{20,16},{24,28},{28,24},{1,5},{5... | collective-permute-start | bytes 4718600 | tf_op jit(solution)/shard_map/ppermute | solution.py:783
  1060.0 60.6 %collective-permute-start.49 = (bf16[512,1536]{1,0:T(8,128)(2,1)}, bf16[512,1536]{1,0:T(8,128)(2,1)S(1)}, u32[]{:S(2)}, u32[]{:S(2)}) collective-permute-start(bf16[512,1536]{1,0:T(8,128)(2,1)} %collective-permute-done.47.second), channel_id=1, source_target_pairs={{0,4},{4,0},{8,12},{12,8},{16,20},{20,16},{24,28},{28,24},{1,5},{5... | collective-permute-start | bytes 4718600 | tf_op jit(solution)/shard_map/ppermute | solution.py:783
  1074.0 39.0 %collective-permute-start.41 = (bf16[320,1024]{1,0:T(8,128)(2,1)}, bf16[320,1024]{1,0:T(8,128)(2,1)}, u32[]{:S(2)}, u32[]{:S(2)}) collective-permute-start(bf16[320,1024]{1,0:T(8,128)(2,1)} %collective-permute-done.39.second), channel_id=1, source_target_pairs={{0,4},{4,0},{8,12},{12,8},{16,20},{20,16},{24,28},{28,24},{1,5},{5... | collective-permute-start | bytes 1966088 | tf_op jit(solution)/shard_map/ppermute | solution.py:783
  1085.7 47.5 %collective-permute-start.34 = (bf16[512,1280]{1,0:T(8,128)(2,1)S(1)}, bf16[512,1280]{1,0:T(8,128)(2,1)}, u32[]{:S(2)}, u32[]{:S(2)}) collective-permute-start(bf16[512,1280]{1,0:T(8,128)(2,1)S(1)} %add_convert_fusion.11.first), channel_id=1, source_target_pairs={{0,4},{4,0},{8,12},{12,8},{16,20},{20,16},{24,28},{28,24},{1,5},{5... | collective-permute-start | bytes 3932168 | tf_op jit(solution)/shard_map/ppermute | solution.py:783
  1102.0 31.1 %collective-permute-start.35 = (bf16[512,1280]{1,0:T(8,128)(2,1)S(1)}, bf16[512,1280]{1,0:T(8,128)(2,1)}, u32[]{:S(2)}, u32[]{:S(2)}) collective-permute-start(bf16[512,1280]{1,0:T(8,128)(2,1)S(1)} %collective-permute-done.33.second), channel_id=1, source_target_pairs={{0,4},{4,0},{8,12},{12,8},{16,20},{20,16},{24,28},{28,24},{1,5},{5... | collective-permute-start | bytes 3932168 | tf_op jit(solution)/shard_map/ppermute | solution.py:783
  (84 other events, 855.2 us)
Sparse Core Ops, SparseCore 0:
  315.4 81.5 reduce-scatter.2
  400.3 80.1 reduce-scatter.4

commit v3 on v2

--- a/solution.py
+++ b/solution.py
@@ -285,35 +285,52 @@
     store_block(parts, layout, block, slice(None), d_resid[...])
 
 
-def mlp_kernel(layout, *refs):
+def mlp_forward_kernel(layout, *refs):
     many = len(layout)
-    x_pieces, cot_pieces, (w_gate, w_up, w_down) = refs[:many], refs[many : 2 * many], refs[2 * many : 2 * many + 3]
-    x, cot, mid = refs[-3:]
-    hidden, d_gate, d_up, mlp_part = refs[-3 - many - 4 : -3 - many]
-    parts = refs[-3 - many : -3]
-    r = pl.program_id(0)
-    load_block(x_pieces, layout, r, x)
-    load_block(cot_pieces, layout, r, cot)
+    x_pieces, (w_gate, w_up, w_down) = refs[:many], refs[many : many + 3]
+    hidden, gate, up, mlp_part, x = refs[-5:]
+    load_block(x_pieces, layout, pl.program_id(0), x)
     for at in range(0, hidden.shape[2], UNIT_TILE):
         column = pl.ds(at, UNIT_TILE)
-        up = dot_nn(x[...], w_up[:, column])
+        up_pre = dot_nn(x[...], w_up[:, column])
+        gate_pre = dot_nn(x[...], w_gate[:, column])
+        value, _ = gelu_parts(gate_pre)
+        hidden[0, :, column] = (value * up_pre).astype(bf16)
+        gate[0, :, column] = gate_pre.astype(bf16)
+        up[0, :, column] = up_pre.astype(bf16)
+    for at in range(0, x.shape[1], MODEL_TILE):
+        column = pl.ds(at, MODEL_TILE)
+        mlp_part[0, :, column] = dot_nn(hidden[0], w_down[:, column]).astype(bf16)
+
+
+def mlp_backward_kernel(layout, *refs):
+    many = len(layout)
+    cot_pieces, (gate, up, w_gate, w_up, w_down) = refs[:many], refs[many : many + 5]
+    cot, mid = refs[-2:]
+    d_gate, d_up = refs[-2 - many - 2 : -2 - many]
+    parts = refs[-2 - many : -2]
+    r = pl.program_id(0)
+    load_block(cot_pieces, layout, r, cot)
+    for at in range(0, d_gate.shape[2], UNIT_TILE):
+        column = pl.ds(at, UNIT_TILE)
         back = dot_nt(cot[...], w_down[column, :])
-        value, slope = gelu_parts(dot_nn(x[...], w_gate[:, column]))
-        hidden[0, :, column] = (value * up).astype(bf16)
-        d_gate[0, :, column] = (back * up * slope).astype(bf16)
+        value, slope = gelu_parts(gate[0, :, column].astype(f32))
+        d_gate[0, :, column] = (back * up[0, :, column].astype(f32) * slope).astype(bf16)
         d_up[0, :, column] = (back * value).astype(bf16)
     for at in range(0, cot.shape[1], MODEL_TILE):
         column = pl.ds(at, MODEL_TILE)
-        mlp_part[0, :, column] = dot_nn(hidden[0], w_down[:, column]).astype(bf16)
         total = dot_nt(d_gate[0], w_gate[column, :]) + dot_nt(d_up[0], w_up[column, :])
         mid[:, column] = total.astype(bf16)
     store_block(parts, layout, r, slice(None), mid[...])
 
 
-def weight_grad_kernel(by_rows, nlefts, nrights, *refs):
+def weight_grad_kernel(by_rows, nlefts, nrights, exchange, *refs):
     lefts, rights = refs[:nlefts], refs[nlefts : nlefts + nrights]
-    keep, give, left, right = refs[-4:]
-    start = (pl.program_id(0) == 0) & (pl.program_id(1) == 0)
+    if exchange:
+        first, second, left, right, sent, got, send, recv = refs[-8:]
+    else:
+        out, left, right = refs[-3:]
+    step = pl.program_id(0)
 
     def assemble(target, sources):
         at = 0
@@ -326,27 +343,38 @@
     elif by_rows:
         assemble(left, lefts)
     else:
-        pl.when(start)(functools.partial(assemble, left, lefts))
+        pl.when(step == 0)(functools.partial(assemble, left, lefts))
     if nrights == 1:
         right = rights[0]
     elif not by_rows:
         assemble(right, rights)
     else:
-        pl.when(start)(functools.partial(assemble, right, rights))
-    total = lax.dot_general(
-        left[...], right[...], (((0,), (0,)), ((), ())), preferred_element_type=f32
-    ).astype(bf16)
-
-    @pl.when(pl.program_id(0) == 0)
-    def _():
-        keep[...] = total
-
-    @pl.when(pl.program_id(0) == 1)
-    def _():
-        give[...] = total
-
-
-def join_kernel(info, first, second, third, fourth, *outs):
+        pl.when(step == 0)(functools.partial(assemble, right, rights))
+    total = lax.dot_general(left[...], right[...], (((0,), (0,)), ((), ())), preferred_element_type=f32)
+    if not exchange:
+        out[...] = total.astype(bf16)
+        return
+
+    def copy(at):
+        return remote(sent.at[at], got.at[at], send, recv, at, other_core())
+
+    for at in range(2):
+
+        @pl.when(step == at)
+        def _(at=at):
+            sent[at] = total.astype(bf16)
+            copy(at).start()
+
+    for at, target in ((0, first), (1, second)):
+
+        @pl.when(step == 2 + at)
+        def _(at=at, target=target):
+            copy(at).wait_recv()
+            target[...] = (total + got[at].astype(f32)).astype(bf16)
+            copy(at).wait_send()
+
+
+def join_kernel(ways, first, second, third, fourth, *outs):
     for at, ref in enumerate((first, second, third, fourth)):
 
         @pl.when(pl.program_id(0) == at)
@@ -373,6 +401,10 @@
 def neighbours():
     me = lax.axis_index("mp")
     return {"mp": flip(me, 1, 4)}, {"mp": flip(me, 2, 4)}
+
+
+def other_core():
+    return {"dp": flip(lax.axis_index("dp"), 1, 8)}
 
 
 def remote(source, target, send, recv, at, device):
@@ -398,29 +430,32 @@
         half = far_a.shape[0]
         x, y = neighbours()
         return (
-            remote(shard, by_x, send, recv, 0, x),
-            remote(shard, by_y, send, recv, 1, y),
-            remote(by_x.at[pl.ds(0, half)], far_a, send, recv, 2, y),
-            remote(by_y.at[pl.ds(half, half)], far_b, send, recv, 3, x),
+            lambda: remote(shard, by_x, send, recv, 0, x),
+            lambda: remote(shard, by_y, send, recv, 1, y),
+            lambda: remote(by_x.at[pl.ds(0, half)], far_a, send, recv, 2, y),
+            lambda: remote(by_y.at[pl.ds(half, half)], far_b, send, recv, 3, x),
         )
 
     def begin(self, *refs):
         for copy in self.copies(*refs)[:2]:
-            copy.start()
+            copy().start()
 
     def middle(self, *refs):
         copies = self.copies(*refs)
-        copies[0].wait_recv()
-        copies[1].wait_recv()
-        copies[2].start()
-        copies[3].start()
+        copies[0]().wait_recv()
+        copies[1]().wait_recv()
+        copies[2]().start()
+        copies[3]().start()
 
     def end(self, *refs):
         copies = self.copies(*refs)
-        copies[0].wait_send()
-        copies[1].wait_send()
-        copies[2].wait()
-        copies[3].wait()
+        copies[0]().wait_send()
+        copies[1]().wait_send()
+        copies[2]().wait()
+        copies[3]().wait()
+
+    def devices(self):
+        return neighbours()
 
     def result(self, outs):
         return (self.operands[0],) + tuple(outs)
@@ -443,75 +478,255 @@
         low, high = pl.ds(0, half), pl.ds(half, half)
         x, y = neighbours()
         return (
-            remote(far_a, got_x, send, recv, 0, x),
-            remote(far_b, got_y, send, recv, 1, y),
-            remote(one.at[low], from_x.at[low], send, recv, 2, x),
-            remote(two.at[high], from_y.at[high], send, recv, 3, y),
-            remote(own_x, from_x.at[high], send, recv, 4, x),
-            remote(own_y, from_y.at[low], send, recv, 5, y),
-        ), (
-            pltpu.make_async_copy(one.at[high], own_x, local.at[0]),
-            pltpu.make_async_copy(two.at[low], own_y, local.at[1]),
+            lambda: remote(far_a, got_x, send, recv, 0, x),
+            lambda: remote(far_b, got_y, send, recv, 1, y),
+            lambda: remote(one.at[low], from_x.at[low], send, recv, 2, x),
+            lambda: remote(two.at[high], from_y.at[high], send, recv, 3, y),
+            lambda: remote(own_x, from_x.at[high], send, recv, 4, x),
+            lambda: remote(own_y, from_y.at[low], send, recv, 5, y),
+            lambda: pltpu.make_async_copy(one.at[high], own_x, local.at[0]),
+            lambda: pltpu.make_async_copy(two.at[low], own_y, local.at[1]),
         )
 
     def begin(self, *refs):
-        copies, locals_ = self.copies(*refs)
-        for copy in copies[:4] + locals_:
-            copy.start()
+        copies = self.copies(*refs)
+        for at in (0, 1, 2, 3, 6, 7):
+            copies[at]().start()
 
     def middle(self, ins, outs, scratch):
-        copies, locals_ = self.copies(ins, outs, scratch)
+        copies = self.copies(ins, outs, scratch)
         got_x, got_y, own_x, own_y = scratch[:4]
-        for copy in locals_:
-            copy.wait()
-        copies[0].wait_recv()
-        copies[1].wait_recv()
+        copies[6]().wait()
+        copies[7]().wait()
+        copies[0]().wait_recv()
+        copies[1]().wait_recv()
         own_x[...] = (own_x[...].astype(f32) + got_y[...].astype(f32)).astype(bf16)
         own_y[...] = (own_y[...].astype(f32) + got_x[...].astype(f32)).astype(bf16)
-        copies[4].start()
-        copies[5].start()
+        copies[4]().start()
+        copies[5]().start()
 
     def end(self, *refs):
-        copies, _ = self.copies(*refs)
-        copies[0].wait_send()
-        copies[1].wait_send()
-        for copy in copies[2:]:
-            copy.wait()
+        copies = self.copies(*refs)
+        copies[0]().wait_send()
+        copies[1]().wait_send()
+        for at in (2, 3, 4, 5):
+            copies[at]().wait()
+
+    def devices(self):
+        return neighbours()
 
     def result(self, outs):
         return self.first.astype(f32) + outs[0].astype(f32) + outs[1].astype(f32)
 
 
-class SendHost:
-    def __init__(self, pairs):
-        self.operands = [array for array, _ in pairs]
-        self.which = [which for _, which in pairs]
-        self.outputs = [jax.ShapeDtypeStruct(array.shape, array.dtype) for array in self.operands]
-        self.scratch = [pltpu.SemaphoreType.DMA((len(pairs),))] * 2
-
-    def copies(self, ins, outs, scratch):
-        to = neighbours()
-        return [
-            remote(source, target, scratch[0], scratch[1], at, to[self.which[at]])
-            for at, (source, target) in enumerate(zip(ins, outs))
-        ]
+class PipeHost:
+    def __init__(self, inward, between, outward):
+        self.counts = len(inward), len(between), len(outward)
+        self.operands = [chunk for _, chunk in inward + between + outward]
+        self.names = [name for name, _ in inward + between + outward]
+        self.outputs = [jax.ShapeDtypeStruct(chunk.shape, bf16) for chunk in self.operands]
+        adding = len(inward) + len(between)
+        self.scratch = [pltpu.VMEM(chunk.shape, bf16) for chunk in self.operands[:adding] for _ in range(2)]
+        self.scratch += [pltpu.VMEM(chunk.shape, bf16) for chunk in self.operands[adding:]]
+        self.scratch += [pltpu.SemaphoreType.DMA((len(self.operands),))] * 4
+
+    def devices(self):
+        dp = lax.axis_index("dp")
+        return {"dp": flip(dp, 2, 8)}, {"dp": (3 - dp // 2) * 2 + dp % 2}
+
+    def parts(self, ins, outs, scratch):
+        pair, mirror = self.devices()
+        send, recv, local, back = scratch[-4:]
+        inward, between, _ = self.counts
+        for at, (chunk, out) in enumerate(zip(ins, outs)):
+            if at < inward + between:
+                own, got = scratch[2 * at], scratch[2 * at + 1]
+                way, device = ("in", pair) if at < inward else ("mid", mirror)
+                yield (
+                    way,
+                    lambda chunk=chunk, got=got, at=at, device=device: remote(chunk, got, send, recv, at, device),
+                    lambda chunk=chunk, own=own, at=at: pltpu.make_async_copy(chunk, own, local.at[at]),
+                    lambda own=own, out=out, at=at: pltpu.make_async_copy(own, out, back.at[at]),
+                    own,
+                    got,
+                )
+            else:
+                own = scratch[at + inward + between]
+                yield (
+                    "out",
+                    lambda chunk=chunk, out=out, at=at: remote(chunk, out, send, recv, at, pair),
+                    lambda chunk=chunk, own=own, at=at: pltpu.make_async_copy(chunk, own, local.at[at]),
+                    lambda own=own, out=out, at=at: pltpu.make_async_copy(own, out, back.at[at]),
+                    None,
+                    None,
+                )
+
+    def inner(self):
+        chip = lax.axis_index("dp") // 2
+        return (chip + 1) // 2 % 2 == 1
 
     def begin(self, *refs):
-        for copy in self.copies(*refs):
-            copy.start()
+        inner = self.inner()
+        for way, there, here, _, _, _ in self.parts(*refs):
+
+            @pl.when(inner)
+            def _(way=way, there=there, here=here):
+                here().start()
+                if way != "in":
+                    there().start()
+
+            if way == "in":
+
+                @pl.when(jnp.logical_not(inner))
+                def _(there=there):
+                    there().start()
 
     def middle(self, *refs):
         pass
 
     def end(self, *refs):
-        for copy in self.copies(*refs):
-            copy.wait()
+        inner = self.inner()
+        parts = list(self.parts(*refs))
+        for way, there, here, back, own, got in parts:
+
+            @pl.when(inner)
+            def _(way=way, there=there, here=here, back=back, own=own, got=got):
+                here().wait()
+                if way != "out":
+                    there().wait_recv()
+                    own[...] = (own[...].astype(f32) + got[...].astype(f32)).astype(bf16)
+                back().start()
+                if way != "in":
+                    there().wait_send()
+
+            if way != "mid":
+
+                @pl.when(jnp.logical_not(inner))
+                def _(way=way, there=there):
+                    if way == "in":
+                        there().wait_send()
+                    else:
+                        there().wait_recv()
+
+        for _, _, _, back, _, _ in parts:
+
+            @pl.when(inner)
+            def _(back=back):
+                back().wait()
 
     def result(self, outs):
-        return tuple(outs)
-
-
-def call(kernel, grid, ins, outs, scratch, name, us, hosts=(), before=(), aliases=None, middle=0, unique=None):
+        return dict(zip(self.names, outs))
+
+
+class TailHost(PipeHost):
+    def __init__(self, inward, between, outward):
+        chunks = [(chunk, stage) for stage, group in enumerate((inward, between, outward)) for _, chunk in group]
+        self.names = [name for name, _ in inward + between + outward]
+        self.operands = [chunk for chunk, _ in chunks]
+        self.outputs = [jax.ShapeDtypeStruct(chunk.shape, bf16) for chunk in self.operands]
+        self.scratch = [pltpu.VMEM(chunk.shape, bf16) for chunk, stage in chunks for _ in range(3 - stage)]
+        self.pieces = []
+        for at, (chunk, stage) in enumerate(chunks):
+            rows = chunk.shape[0]
+            first = rows if stage == 2 else (rows // 32 + 1) // 2 * 32
+            for start, count in ((0, first), (first, rows - first)):
+                if count > 0:
+                    self.pieces.append((at, stage, start, count))
+        self.scratch += [pltpu.SemaphoreType.DMA((len(self.pieces),))] * 8
+
+    def begin(self, ins, outs, scratch):
+        pair, mirror = self.devices()
+        p_send, p_recv, q_send, q_recv, f_send, f_recv, local, back = scratch[-8:]
+        buffers, given = {}, 0
+        for at, stage, start, _ in self.pieces:
+            if start == 0:
+                buffers[at] = scratch[given : given + 3 - stage]
+                given += 3 - stage
+
+        def part(ref, number):
+            _, _, start, count = self.pieces[number]
+            return ref.at[pl.ds(start, count)]
+
+        def transfers(number):
+            at, stage, _, _ = self.pieces[number]
+            own, from_pair, from_mirror = (buffers[at] + [None, None])[:3]
+            if stage == 1:
+                from_mirror = from_pair
+            chunk, out = part(ins[at], number), part(outs[at], number)
+            done = own if stage == 2 else from_mirror
+            return {
+                "inward": lambda: remote(chunk, part(from_pair, number), p_send, p_recv, number, pair),
+                "load": lambda: pltpu.make_async_copy(chunk, part(own, number), local.at[number]),
+                "between": lambda: remote(part(own, number), part(from_mirror, number), q_send, q_recv, number, mirror),
+                "outward": lambda: remote(part(done, number), out, f_send, f_recv, number, pair),
+                "keep": lambda: pltpu.make_async_copy(part(done, number), out, back.at[number]),
+            }
+
+        def add(number, target, other):
+            at, _, start, count = self.pieces[number]
+            rows = pl.ds(start, count)
+            target[rows, :] = (target[rows, :].astype(f32) + other[rows, :].astype(f32)).astype(bf16)
+
+        numbers = range(len(self.pieces))
+        moves = [transfers(number) for number in numbers]
+        stages = [stage for _, stage, _, _ in self.pieces]
+        inner = self.inner()
+
+        def finish(number):
+            if stages[number] < 2:
+                moves[number]["between"]().wait_recv()
+                own, other = buffers[self.pieces[number][0]][0], buffers[self.pieces[number][0]][-1]
+                add(number, other, own)
+            moves[number]["outward"]().start()
+            moves[number]["keep"]().start()
+
+        @pl.when(inner)
+        def _():
+            for move in moves:
+                move["load"]().start()
+            for number in numbers:
+                if stages[number] == 2:
+                    moves[number]["load"]().wait()
+                    finish(number)
+            for number in numbers:
+                if stages[number] == 1:
+                    moves[number]["load"]().wait()
+                    moves[number]["between"]().start()
+            waiting = [number for number in numbers if stages[number] == 1]
+            for number in numbers:
+                if stages[number] == 0:
+                    moves[number]["load"]().wait()
+                    moves[number]["inward"]().wait_recv()
+                    own, other = buffers[self.pieces[number][0]][:2]
+                    add(number, own, other)
+                    moves[number]["between"]().start()
+                    waiting.append(number)
+                    finish(waiting.pop(0))
+            for number in waiting:
+                finish(number)
+            for number in numbers:
+                if stages[number] < 2:
+                    moves[number]["between"]().wait_send()
+                moves[number]["outward"]().wait_send()
+                moves[number]["keep"]().wait()
+
+        @pl.when(jnp.logical_not(inner))
+        def _():
+            for number in numbers:
+                if stages[number] == 0:
+                    moves[number]["inward"]().start()
+            for number in numbers:
+                if stages[number] == 0:
+                    moves[number]["inward"]().wait_send()
+                moves[number]["outward"]().wait_recv()
+
+    def end(self, *refs):
+        pass
+
+
+def call(
+    kernel, grid, ins, outs, scratch, name, us, hosts=(), before=(), aliases=None, middle=0, unique=None, pair=False
+):
     nins, nouts, nscratch = len(ins), len(outs), len(scratch)
     steps = math.prod(grid)
 
@@ -533,16 +748,23 @@
         step = pl.program_id(0)
         if len(grid) == 2:
             step = step * grid[1] + pl.program_id(1)
-        if hosts:
+        if hosts or pair:
 
             @pl.when(step == 0)
             def _():
+                devices = (other_core(),) if pair else ()
+                for kind in (GatherHost, ScatterHost, PipeHost):
+                    kinds = [host for host in hosts if isinstance(host, kind)]
+                    if kinds and not (kind is ScatterHost and any(isinstance(host, GatherHost) for host in hosts)):
+                        devices += tuple(kinds[0].devices())
                 barrier = pltpu.get_barrier_semaphore()
-                for device in neighbours():
+                for device in devices:
                     pl.semaphore_signal(barrier, inc=1, device_id=device, device_id_type=MESH)
-                pl.semaphore_wait(barrier, 2)
+                pl.semaphore_wait(barrier, len(devices))
                 for host, there in zip(hosts, host_refs):
                     host.begin(*there)
+
+        if hosts:
 
             @pl.when(step == middle)
             def _():
@@ -560,7 +782,7 @@
     host_operands = [v for host in hosts for v in host.operands]
     host_outputs = [v for host in hosts for v in host.outputs]
     params = pltpu.CompilerParams(vmem_limit_bytes=VMEM_BYTES)
-    if hosts:
+    if hosts or pair:
         params = pltpu.CompilerParams(vmem_limit_bytes=VMEM_BYTES, collective_id=unique, has_side_effects=True)
     results = pl.pallas_call(
         body,
@@ -676,23 +898,43 @@
     return max(t for t in range(unit, limit + 1, unit) if total % t == 0)
 
 
-def mlp_core(seq, count, x, cot, w_gate, w_up, w_down, shared, **more):
+def mlp_forward(seq, count, x, w_gate, w_up, w_down, shared, **more):
     blocks, (rows, model) = lax.axis_size("mp"), x[0].shape
+    units = w_gate.shape[1]
+    low = jax.ShapeDtypeStruct((count * blocks, rows, units), bf16)
+    part = pl.BlockSpec((1, rows, units), lambda r: (seq * blocks + r, 0, 0))
+    long = pl.BlockSpec((1, rows, model), lambda r: (flip(r, lax.axis_index("mp"), blocks), 0, 0))
+    inputs = [(v, whole(v)) for v in tuple(x) + (w_gate, w_up, w_down)] + [(v, ANY) for v in shared]
+    return call(
+        functools.partial(mlp_forward_kernel, layout_of(blocks, rows)),
+        (blocks,),
+        inputs,
+        [(low, part)] * 3 + [(jax.ShapeDtypeStruct((blocks, rows, model), bf16), long)],
+        [pltpu.VMEM((rows, model), bf16)],
+        "mlp_forward",
+        30,
+        aliases={len(inputs) - len(shared) + at: at for at in range(len(shared))},
+        **more,
+    )
+
+
+def mlp_backward(seq, count, cot, gate, up, w_gate, w_up, w_down, shared, **more):
+    blocks, (rows, model) = lax.axis_size("mp"), cot[0].shape
     layout = layout_of(blocks, rows)
     units = w_gate.shape[1]
     low = jax.ShapeDtypeStruct((count * blocks, rows, units), bf16)
     part = pl.BlockSpec((1, rows, units), lambda r: (seq * blocks + r, 0, 0))
-    long = pl.BlockSpec((1, rows, model), lambda r: (flip(r, lax.axis_index("mp"), blocks), 0, 0))
     shapes, specs = piece_outputs(layout, model)
-    inputs = [(v, whole(v)) for v in tuple(x) + tuple(cot) + (w_gate, w_up, w_down)] + [(v, ANY) for v in shared]
+    inputs = [(v, whole(v)) for v in cot] + [(gate, part), (up, part)]
+    inputs += [(v, whole(v)) for v in (w_gate, w_up, w_down)] + [(v, ANY) for v in shared]
     return call(
-        functools.partial(mlp_kernel, layout),
+        functools.partial(mlp_backward_kernel, layout),
         (blocks,),
         inputs,
-        [(low, part)] * 3 + [(jax.ShapeDtypeStruct((blocks, rows, model), bf16), long)] + list(zip(shapes, specs)),
-        [pltpu.VMEM((rows, model), bf16)] * 3,
-        "mlp_core",
-        54,
+        [(low, part)] * 2 + list(zip(shapes, specs)),
+        [pltpu.VMEM((rows, model), bf16)] * 2,
+        "mlp_backward",
+        32,
         aliases={len(inputs) - len(shared) + at: at for at in range(len(shared))},
         **more,
     )
@@ -706,76 +948,75 @@
     return lax.axis_index("dp") % 2 if lax.axis_size("dp") == 8 else 0
 
 
-def weight_grad(lefts, rights, by_rows=True, limit=512, **more):
+def weight_grad(lefts, rights, by_rows=True, **more):
     lefts, rights = [flat(v) for v in lefts], [flat(v) for v in rights]
     rows, columns = lefts[0].shape[1], rights[0].shape[1]
     tokens = sum(v.shape[0] for v in lefts)
-    half = (rows if by_rows else columns) // 2
-    tile = largest_tile(half, limit)
-    steps = half // tile
-
-    def cut(array, tiled):
-        if not tiled:
+    exchange = lax.axis_size("dp") == 8
+    tiled = rows if by_rows else columns
+    tile = tiled // 4 if exchange else largest_tile(tiled, 512)
+
+    def place(step):
+        if not exchange:
+            return step
+        return (core_index() + 1 + step // 2) % 2 * 2 + step % 2
+
+    def cut(array, in_tiles):
+        if not in_tiles:
             return whole(array)
-        return pl.BlockSpec((array.shape[0], tile), lambda h, i: (0, (h + core_index()) % 2 * steps + i))
-
-    def kept(h, i):
-        at = i + h * (steps - 1 - i)
-        return (at, 0) if by_rows else (0, at)
-
-    def given(h, i):
-        at = h * i
-        return (at, 0) if by_rows else (0, at)
-
-    shape = jax.ShapeDtypeStruct((half, columns) if by_rows else (rows, half), bf16)
+        return pl.BlockSpec((array.shape[0], tile), lambda step: (0, place(step)))
+
+    scratch = [
+        pltpu.VMEM((tokens if len(lefts) > 1 else 16, tile if by_rows else rows), bf16),
+        pltpu.VMEM((tokens if len(rights) > 1 else 16, columns if by_rows else tile), bf16),
+    ]
     block = (tile, columns) if by_rows else (rows, tile)
+    if exchange:
+        outs = [(jax.ShapeDtypeStruct(block, bf16), pl.BlockSpec(block, lambda step: (0, 0)))] * 2
+        scratch += [pltpu.VMEM((2,) + block, bf16)] * 2 + [pltpu.SemaphoreType.DMA((2,))] * 2
+    else:
+        whole_out = jax.ShapeDtypeStruct((rows, columns), bf16)
+        outs = [(whole_out, pl.BlockSpec(block, lambda step: (step, 0) if by_rows else (0, step)))]
     return call(
-        functools.partial(weight_grad_kernel, by_rows, len(lefts), len(rights)),
-        (2, steps),
+        functools.partial(weight_grad_kernel, by_rows, len(lefts), len(rights), exchange),
+        (tiled // tile,),
         [(v, cut(v, by_rows)) for v in lefts] + [(v, cut(v, not by_rows)) for v in rights],
-        [(shape, pl.BlockSpec(block, kept)), (shape, pl.BlockSpec(block, given))],
-        [
-            pltpu.VMEM((tokens if len(lefts) > 1 else 16, tile if by_rows else rows), bf16),
-            pltpu.VMEM((tokens if len(rights) > 1 else 16, columns if by_rows else tile), bf16),
-        ],
+        outs,
+        scratch,
         "weight_grad",
         20 if columns > 1000 and by_rows else 13,
+        pair=exchange,
         **more,
     )
 
 
-def join_quarters(where, quarters, by_rows, ways):
-    rows, columns = quarters[0].shape
+def join_quarters(quarters, by_rows, ways, rows, **more):
+    columns = quarters[0].shape[1]
     tile = max(t for t in range(16, 256 + 1, 16) if rows % t == 0)
     steps = rows // tile
 
     def source(at):
-        def index(p, i, where):
+        def index(p, i):
             return (jnp.where(p == at, i, jnp.where(p < at, 0, steps - 1)), 0)
 
         return pl.BlockSpec((tile, columns), index)
 
-    def target(p, i, where):
-        half, quarter = where[0] ^ (p // 2), where[1] ^ (p % 2)
-        if by_rows:
-            return ((half * 2 + quarter) * steps + i, 0)
-        return (quarter * steps + i, half)
-
-    shape = (4 * rows, columns // ways) if by_rows else (2 * rows, 2 * columns)
-    out = jax.ShapeDtypeStruct(shape, f32)
-    return pl.pallas_call(
-        join_kernel,
-        out_shape=(out,) * ways,
-        grid_spec=pltpu.PrefetchScalarGridSpec(
-            num_scalar_prefetch=1,
-            grid=(4, steps),
-            in_specs=[source(at) for at in range(4)],
-            out_specs=(pl.BlockSpec((tile, columns // ways), target),) * ways,
-        ),
-        compiler_params=PARAMS,
-        cost_estimate=cost(10),
-        name="join_quarters",
-    )(where, *quarters)
+    def target(p, i):
+        at = (core_index() + p // 2) % 2 * 2 + p % 2
+        return (at * steps + i, 0) if by_rows else (i, at)
+
+    shape = (4 * rows, columns // ways) if by_rows else (rows, 4 * columns)
+    out = (jax.ShapeDtypeStruct(shape, f32), pl.BlockSpec((tile, columns // ways), target))
+    return call(
+        functools.partial(join_kernel, ways),
+        (4, steps),
+        [(quarter, source(at)) for at, quarter in enumerate(quarters)],
+        [out] * ways,
+        [],
+        "join_quarters",
+        10,
+        **more,
+    )
 
 
 def swap(value, axis, bit):
@@ -812,33 +1053,36 @@
     return (left.astype(f32) + right.astype(f32)).astype(bf16)
 
 
-def split_half(value, mine):
-    half = value.shape[0] // 2
-    keep = lax.dynamic_slice_in_dim(value, mine * half, half, 0)
-    give = lax.dynamic_slice_in_dim(value, (1 - mine) * half, half, 0)
-    return keep, give
-
-
-class SumOverDp:
-    def __init__(self, core, keep, give, by_rows=True, ways=1):
-        if lax.axis_size("dp") != 8:
-            part = jnp.concatenate([keep, give], axis=0 if by_rows else 1)
-            self.totals = jnp.split(lax.psum(part, "dp").astype(f32), ways, axis=1)
-            self.total = self.totals[0]
-            self.pair = self.quad = self.every = part
-            return
-        chip = lax.axis_index("dp") // 2
-        outer = jnp.where((chip == 0) | (chip == 3), 0, 1)
-        self.pair = add_low(keep, swap(give, "dp", 1))
-        keep, give = split_half(self.pair, outer)
-        self.quad = add_low(keep, swap(give, "dp", 2))
-        mirrored = lax.ppermute(self.quad, "dp", [(i, (3 - i // 2) * 2 + i % 2) for i in range(8)])
-        self.every = add_low(self.quad, mirrored)
-        self.paired = swap(self.every, "dp", 2)
-        quarters = (self.every, self.paired, swap(self.every, "dp", 1), swap(self.paired, "dp", 1))
-        where = jnp.stack([core[0], outer.astype(jnp.int32)])
-        self.totals = join_quarters(where, quarters, by_rows, ways)
-        self.total = self.totals[0]
+class Pipe:
+    def __init__(self):
+        self.stages = [{}, {}, {}]
+        self.done = {}
+
+    def add(self, **chunks):
+        self.stages[0].update(chunks)
+
+    def host(self):
+        return PipeHost(*[list(stage.items()) for stage in self.stages])
+
+    def took(self, results):
+        inward, between, outward = self.stages
+        self.done.update({name: results[name] for name in outward})
+        self.stages = [{}, {name: results[name] for name in inward}, {name: results[name] for name in between}]
+
+
+def add_small(quarters, small):
+    columns = quarters[0].shape[1]
+    small = add_low(small, swap(small, "dp", 1)).reshape(4, -1, columns)
+    return [
+        jnp.concatenate([quarter, lax.dynamic_index_in_dim(small, core_index() * 2 + at, 0, False)], axis=0)
+        for at, quarter in enumerate(quarters)
+    ]
+
+
+def take_small(quarters, start):
+    parts = jnp.stack([quarter[start:] for quarter in quarters])
+    order = [((half + core_index()) % 2) * 2 + at for half in range(2) for at in range(2)]
+    return jnp.concatenate([lax.dynamic_index_in_dim(parts, pick, 0, False) for pick in order], axis=0).astype(f32)
 
 
 def normalize(values, gain):
@@ -912,17 +1156,29 @@
     backward_params = (wo, w_both, taps, w_gates, decay_line)
     seqs = range(count)
     limits = [jnp.full((SUB, LANES), lengths[s], jnp.int32) for s in seqs]
-    core = jnp.int32(core_index()).reshape(1)
     blocks = lax.axis_size("mp")
     hosted = blocks == 4 and count == 2
     ids = iter(range(1, 100))
 
+    piped = hosted and lax.axis_size("dp") == 8
+    pipe = Pipe()
+
+    def enter(**chunks):
+        if piped:
+            pipe.add(**chunks)
+
     def tied(value, *deps):
         return lax.optimization_barrier((value,) + deps)[0]
 
     def run(function, *args, hosts=(), middle=0, **more):
-        if hosted and hosts:
-            return function(*args, hosts=hosts, middle=middle, unique=next(ids), **more)
+        if hosted:
+            moving = piped and any(pipe.stages)
+            out, found = function(
+                *args, hosts=list(hosts) + ([pipe.host()] if moving else []), middle=middle, unique=next(ids), **more
+            )
+            if moving:
+                pipe.took(found[-1])
+            return out, found[: len(hosts)]
         out, _ = function(*args, **more)
         return out, [
             gather(host.operands[0]) if isinstance(host, GatherHost) else scatter((host.first, *host.operands))
@@ -944,73 +1200,75 @@
     saved = [out[1:7] for out in forward]
     finals = [out[7][:1, :true_width] for out in forward]
     resid_mid = [resid[0] + branch]
-    mids = [normalize(resid_mid[0], norm2_gain).astype(bf16)]
-    seq_mid = [gather(mids[0])]
-    resid_mid.append(resid[1] + scatter(forward[1][8:]))
-    mids.append(normalize(resid_mid[1], norm2_gain).astype(bf16))
-    cot_seq = [gather(tied(cotangent[0], forward[1][7]))]
-
-    gathers = [GatherHost(mids[1]), GatherHost(cotangent[1])]
-    out, found = run(
-        mlp_core, 0, count, seq_mid[0], cot_seq[0], w_gate, w_up, w_down, (), hosts=gathers, middle=3, before=(mids[1],)
-    )
-    seq_mid.append(found[0])
-    cot_seq.append(found[1])
-    mlp_part = [out[3]]
-    out, (d_mid,) = run(
-        mlp_core, 1, count, seq_mid[1], cot_seq[1], w_gate, w_up, w_down, out[:3],
-        hosts=[ScatterHost(out[4:])], middle=2,
-    )
-    mlp_part.append(out[3])
-    hidden, d_gate, d_up = out[:3]
-    last_parts = out[4:]
+    mid = normalize(resid_mid[0], norm2_gain).astype(bf16)
+    seq_mid = [gather(mid)]
+    forward_shared, (branch,) = run(
+        mlp_forward, 0, count, seq_mid[0], w_gate, w_up, w_down, (), hosts=[ScatterHost(forward[1][8:])], middle=2
+    )
+    mlp_part = [forward_shared[3]]
+    resid_mid.append(resid[1] + branch)
+    mid = normalize(resid_mid[1], norm2_gain).astype(bf16)
+    seq_mid.append(gather(mid))
+    forward_shared, (found,) = run(
+        mlp_forward, 1, count, seq_mid[1], w_gate, w_up, w_down, forward_shared[:3],
+        hosts=[GatherHost(cotangent[0])], middle=3,
+    )
+    mlp_part.append(forward_shared[3])
+    cot_seq = [found]
+    hidden, gate_low, up_low = forward_shared[:3]
+    backward, (found,) = run(
+        mlp_backward, 0, count, cot_seq[0], gate_low, up_low, w_gate, w_up, w_down, (),
+        hosts=[GatherHost(cotangent[1])], middle=3,
+    )
+    cot_seq.append(found)
 
     def middle_grad(s, d_mid):
         back, unit = normalize_back(resid_mid[s], norm2_gain, d_mid)
         return cotangent[s].astype(f32) + back, jnp.sum(d_mid * unit, axis=0)
 
-    mlp_total = [lax.psum_scatter(flat(v), "mp", scatter_dimension=0, tiled=True) for v in mlp_part]
-    first, gain2 = middle_grad(0, d_mid)
     flat_mid = [p for pieces in seq_mid for p in pieces]
     flat_cot = [p for pieces in cot_seq for p in pieces]
-    halves, (first_seq,) = run(weight_grad, [hidden], flat_cot, hosts=[GatherHost(first.astype(bf16))], middle=3)
-    down = SumOverDp(core, *halves)
-    halves, (d_mid,) = run(
-        weight_grad, flat_mid, [d_gate], hosts=[ScatterHost(last_parts)], middle=2, before=(halves[0],)
-    )
-    gate = SumOverDp(core, *halves)
-    halves, _ = run(weight_grad, flat_mid, [d_up], before=(halves[0], down.pair))
-    up = SumOverDp(core, *halves)
+    grad_down, _ = run(weight_grad, [hidden], flat_cot)
+    enter(down0=grad_down[0])
+    backward, (d_mid,) = run(
+        mlp_backward, 1, count, cot_seq[1], gate_low, up_low, w_gate, w_up, w_down, backward[:2],
+        hosts=[ScatterHost(backward[2:])], middle=2, before=(grad_down[0],),
+    )
+    d_gate, d_up = backward[:2]
+    first, gain2 = middle_grad(0, d_mid)
+    enter(down1=grad_down[-1])
+    grad_gate, (first_seq,) = run(weight_grad, flat_mid, [d_gate], hosts=[GatherHost(first.astype(bf16))], middle=3)
+    enter(gate0=grad_gate[0])
+    grad_up, (d_mid,) = run(
+        weight_grad, flat_mid, [d_up], hosts=[ScatterHost(backward[2:])], middle=2, before=(grad_gate[0],)
+    )
     second, more_gain2 = middle_grad(1, d_mid)
     gain2 = gain2 + more_gain2
-    d_resid = [first, second]
-
+    enter(gate1=grad_gate[-1])
     out, (second_seq,) = run(
         rec_backward, limits[0], 0, count, first_seq, seq_in[0], backward_params, saved[0], (),
-        hosts=[GatherHost(second.astype(bf16))], middle=3, before=(halves[0], gate.pair),
-    )
-    d_resid_seq = [first_seq, second_seq]
+        hosts=[GatherHost(second.astype(bf16))], middle=3, before=(grad_up[0],),
+    )
     sums, gain1 = out[2], jnp.sum(out[3], axis=0)
+    enter(up0=grad_up[0])
     out, (d_in,) = run(
         rec_backward, limits[1], 1, count, second_seq, seq_in[1], backward_params, saved[1], out[:2],
-        hosts=[ScatterHost(out[4:])], middle=2, before=(down.quad, gate.quad, up.pair),
+        hosts=[ScatterHost(out[4:])], middle=2,
     )
     sums, gain1 = sums + out[2], gain1 + jnp.sum(out[3], axis=0)
     d_both, d_gates = out[:2]
     input_grad = [(first + normalize_back(resid[0], norm1_gain, d_in)[0]).astype(bf16)]
+    enter(up1=grad_up[-1])
 
     flat_in = [p for pieces in seq_in for p in pieces]
-    flat_resid = [p for pieces in d_resid_seq for p in pieces]
-    halves, (d_in,) = run(
-        weight_grad, flat_in, [d_both], hosts=[ScatterHost(out[4:])], middle=3, before=(up.quad,)
-    )
-    inward = SumOverDp(core, *halves, ways=2)
-    halves, _ = run(weight_grad, mixed, flat_resid, False, before=(halves[0],))
-    grad_w_out = SumOverDp(core, *halves, by_rows=False).total[:true_width]
-    grad_w_branch, grad_w_input = (v[:, :true_width] for v in inward.totals)
+    flat_resid = [p for pieces in (first_seq, second_seq) for p in pieces]
+    grad_in, _ = run(weight_grad, flat_in, [d_both])
+    enter(in0=grad_in[0])
+    grad_out, (d_in,) = run(
+        weight_grad, mixed, flat_resid, False, hosts=[ScatterHost(out[4:])], middle=2, before=(grad_in[0],)
+    )
     input_grad.append((second + normalize_back(resid[1], norm1_gain, d_in)[0]).astype(bf16))
     input_grad = jnp.stack(input_grad)
-    block_out = jnp.stack([(resid_mid[s] + mlp_total[s].astype(f32)).astype(bf16) for s in seqs])
 
     gains = jnp.stack([gain1 / norm1_gain, gain2])
     for bit in range(blocks.bit_length() - 1):
@@ -1028,10 +1286,42 @@
         [full_ga.reshape(-1), full_gi.reshape(-1), vectors.reshape(-1), gains.reshape(-1)]
     ).astype(bf16)
     used = small.shape[0]
-    columns = 640
-    padded = -(-used // (64 * columns)) * 64 * columns
-    small = jnp.pad(small, (0, padded - used)).reshape(-1, columns)
-    small = SumOverDp(core, *split_half(small, core[0])).total.reshape(-1)
+    unit = 4 * 16 * model // 4
+    small = jnp.pad(small, (0, -used % unit)).reshape(4, -1, model // 4)
+    if piped:
+
+        def join(name, grad, before=(), by_rows=True, ways=1):
+            first, second = (pipe.done[name + at] for at in "01")
+            quarters = (first, second, swap(first, "dp", 1), swap(second, "dp", 1))
+            return join_quarters(quarters, by_rows, ways, grad[0].shape[0], before=before)[0], quarters
+
+        with_small = add_small(grad_out, small)
+        enter(in1=grad_in[-1], out0=with_small[0], out1=with_small[1])
+        last = TailHost(*[list(stage.items()) for stage in pipe.stages])
+        _, (found,) = call(
+            lambda: None, (1,), [], [], [], "sum_tail", 90, hosts=[last], before=(grad_out[0],), unique=next(ids)
+        )
+        pipe.done.update(found)
+        totals_down, _ = join("down", grad_down)
+        totals_gate, _ = join("gate", grad_gate)
+        totals_up, _ = join("up", grad_up)
+        totals_in, _ = join("in", grad_in, ways=2)
+        totals_out, quarters = join("out", grad_out, by_rows=False)
+        small = take_small(quarters, grad_out[0].shape[0])
+    else:
+        small = lax.psum(small, "dp").astype(f32)
+        totals_down, totals_gate, totals_up, totals_in, totals_out = (
+            jnp.split(lax.psum(v[0], "dp").astype(f32), ways, axis=1)
+            for v, ways in ((grad_down, 1), (grad_gate, 1), (grad_up, 1), (grad_in, 2), (grad_out, 1))
+        )
+    grad_w_out = totals_out[0][:true_width]
+    grad_w_branch, grad_w_input = (v[:, :true_width] for v in totals_in)
+    mlp_total = [
+        lax.psum_scatter(flat(tied(v, grad_out[0])), "mp", scatter_dimension=0, tiled=True) for v in mlp_part
+    ]
+    block_out = jnp.stack([(resid_mid[s] + mlp_total[s].astype(f32)).astype(bf16) for s in seqs])
+
+    small = small.reshape(-1)
     many, few = full_ga.size, vectors.size
     grad_gate_a_weight = small[:many].reshape(full_ga.shape)
     grad_gate_i_weight = small[many : 2 * many].reshape(full_gi.shape)
@@ -1053,9 +1343,9 @@
         vectors[0],
         grad_w_out,
         gains[1],
-        gate.total,
-        up.total,
-        down.total,
+        totals_gate[0],
+        totals_up[0],
+        totals_down[0],
         jnp.concatenate(finals, axis=0),
     )
 

time: 1160 us -> 948 us (0.82)
  waiting for transfers between devices: 353 us -> 75.1 us
  Pallas kernels: 544 us -> 741 us
  starting transfers between devices: 124 us -> 18.8 us
  other arithmetic: 71.6 us -> 48.5 us
    pallas_call x11 -> x19, Pallas kernels: 493 us -> 741 us  [call(): pl.pallas_call(body, out_shape=tuple((shape for shape, _ in outs)) + tupl...]
    ppermute x48 -> x25, waiting for transfers between devices: 261 us -> 75.1 us  [swap(): return lax.ppermute(value, axis, [(i, i ^ bit) for i in range(size)])]
    ppermute x48 -> x25, starting transfers between devices: 118 us -> 18.5 us  [swap(): return lax.ppermute(value, axis, [(i, i ^ bit) for i in range(size)])]
    ppermute x6 -> x0, waiting for transfers between devices: 83.6 us -> none  [__init__(): lax.ppermute(self.quad, 'dp', [(i, (3 - i // 2) * 2 + i % 2) for i in ran...]
    pallas_call x6 -> x0, Pallas kernels: 51.5 us -> none  [join_quarters(): pl.pallas_call(join_kernel, out_shape=(out,) * ways, grid_spec=pltpu.Pref...]
    convert_element_type x20 -> x1, other arithmetic: 27.5 us -> 0.12 us  [add_low(): return (left.astype(f32) + right.astype(f32)).astype(bf16)]
  transfers between devices with their start and end apart: 56 -> 27, of which waited for: 25 -> 8; matrix products, arithmetic and copies ran while one was open for 8% -> 5% of each run, Pallas kernels for 33% -> 19%
where the time goes in v3:
time: 948 us; the launch traced here: 935 us
  Pallas kernels  741 us (78%)
  waiting for transfers between devices  75.1 us (8%)
  other arithmetic  48.5 us (5%)
  local copies, waits for them, and re-layouts  29.6 us (3%)
  starting transfers between devices  18.8 us (2%)
  between operations  15.7 us (2%)
    pallas_call x19, Pallas kernels, call(): pl.pallas_call(body, out_shape=tuple((shape for shape, _ in outs)) + tupl...  741 us
    ppermute x25, waiting for transfers between devices, swap(): return lax.ppermute(value, axis, [(i, i ^ bit) for i in range(size)])  75.1 us
  transfers between devices with their start and end apart: 27, of which 8 were waited for; matrix products, arithmetic and copies ran while one was open for 5% of the time, Pallas kernels for 19%

profile of v3, /device:TPU:9, one launch (start us, length us, event | category | flops | bytes accessed | tf_op | source)
XLA Modules:
  0.0 935.3 jit_solution(9807451546242328932)
XLA Ops:
  7.3 2.2 fusion.44
  9.5 1.4 fusion.38
  10.9 1.3 collective-permute-start.1
  12.2 1.2 collective-permute-start
  13.5 8.4 fusion.48.refs_9_.refs_14_
  24.9 10.2 %collective-permute-done.1.refs_3_.refs_8_.refs_2_ = bf16[256,2048]{1,0:T(8,128)(2,1)S(1)} collective-permute-done((bf16[256,2048]{1,0:T(8,128)(2,1)S(1)}, bf16[256,2048]{1,0:T(8,128)(2,1)S(1)}, u32[]{:S(2)}, u32[]{:S(2)}) %collective-permute-start.1) | collective-permute-done | bytes 1048608 | tf_op jit(solution)/shard_map/ppermute | solution.py:1024
  35.1 1.3 collective-permute-start.3
  36.4 1.3 collective-permute-start.2
  39.0 2.3 copy-done.20
  41.3 5.7 collective-permute-done.3.refs_5_.refs_10_.refs_4_
  47.0 1.1 collective-permute-done.2.refs_4_.refs_9_.refs_3_
  48.1 1.2 broadcast_in_dim.15.refs_0_
  49.3 41.5 %rec_forward.2 = (bf16[4,256,640]{2,1,0:T(8,128)(2,1)}, f32[4,256,640]{2,1,0:T(8,128)}, f32[4,256,640]{2,1,0:T(8,128)}, bf16[4,256,640]{2,1,0:T(8,128)(2,1)}, f3...) custom-call(s32[8,128]{1,0:T(8,128)} %broadcast_in_dim.15.refs_0_, ...), custom_call_target="tpu_custom_call" | custom-call | flops 21275000832 | bytes 65536 | tf_op jit(solution)/shard_map/rec_forward/pallas_call | solution.py:787
  90.9 1.2 broadcast_in_dim.20.refs_0_
  92.1 42.1 %rec_forward.3 = (bf16[4,256,640]{2,1,0:T(8,128)(2,1)}, f32[4,256,640]{2,1,0:T(8,128)}, f32[4,256,640]{2,1,0:T(8,128)}, bf16[4,256,640]{2,1,0:T(8,128)(2,1)}, f3...) custom-call(s32[8,128]{1,0:T(8,128)} %broadcast_in_dim.20.refs_0_, ...), custom_call_target="tpu_custom_call" | custom-call | flops 21275000832 | bytes 65536 | tf_op jit(solution)/shard_map/rec_forward/pallas_call | solution.py:787
  134.2 2.2 multiply_reduce_fusion.5
  136.7 1.8 collective-permute-start.5
  138.7 18.7 %collective-permute-done.5.refs_2_ = bf16[256,2048]{1,0:T(8,128)(2,1)S(1)} collective-permute-done((bf16[256,2048]{1,0:T(8,128)(2,1)S(1)}, bf16[256,2048]{1,0:T(8,128)(2,1)S(1)}, u32[]{:S(2)}, u32[]{:S(2)}) %collective-permute-start.5) | collective-permute-done | bytes 1048608 | tf_op jit(solution)/shard_map/ppermute | solution.py:1024
  157.4 1.6 collective-permute-start.7
  159.2 11.9 %collective-permute-done.7.refs_4_ = bf16[128,2048]{1,0:T(8,128)(2,1)S(1)} collective-permute-done((bf16[128,2048]{1,0:T(8,128)(2,1)S(1)}, bf16[128,2048]{1,0:T(8,128)(2,1)S(1)}, u32[]{:S(2)}, u32[]{:S(2)}) %collective-permute-start.7) | collective-permute-done | bytes 524320 | tf_op jit(solution)/shard_map/ppermute | solution.py:1024
  172.2 40.8 %mlp_forward.2 = (bf16[8,256,1536]{2,1,0:T(8,128)(2,1)}, bf16[8,256,1536]{2,1,0:T(8,128)(2,1)}, bf16[8,256,1536]{2,1,0:T(8,128)(2,1)}, bf16[4,256,2048]{2,1,0:T(...) custom-call(bf16[256,2048]{1,0:T(8,128)(2,1)} %copy-done.21, bf16[256,2048]{1,0:T(8,128)(2,1)} %copy-done.34, ...), custom_call_target="tpu_custom_call" | custom-call | flops 17250000896 | bytes 65536 | tf_op jit(solution)/shard_map/mlp_forward/pallas_call | solution.py:787
  213.0 2.2 multiply_reduce_fusion.4
  215.9 1.1 collective-permute-start.8
  217.0 17.0 %collective-permute-done.9.refs_2_.refs_7_ = bf16[256,2048]{1,0:T(8,128)(2,1)S(1)} collective-permute-done((bf16[256,2048]{1,0:T(8,128)(2,1)S(1)}, bf16[256,2048]{1,0:T(8,128)(2,1)S(1)}, u32[]{:S(2)}, u32[]{:S(2)}) %collective-permute-start.9) | collective-permute-done | bytes 1048608 | tf_op jit(solution)/shard_map/ppermute | solution.py:1024
  236.6 1.6 slice_bitcast_fusion
  238.2 8.7 collective-permute-done.11.refs_4_.refs_9_
  247.9 41.3 %mlp_forward.3 = (bf16[8,256,1536]{2,1,0:T(8,128)(2,1)}, bf16[8,256,1536]{2,1,0:T(8,128)(2,1)}, bf16[8,256,1536]{2,1,0:T(8,128)(2,1)}, bf16[4,256,2048]{2,1,0:T(...) custom-call(bf16[256,2048]{1,0:T(8,128)(2,1)} %copy-done.22, ...), custom_call_target="tpu_custom_call", output_to_operand_aliasing={{0}: (8, {}), {1}: (9, {}), {2}: (10, {})} | custom-call | flops 17250000896 | bytes 65536 | tf_op jit(solution)/shard_map/mlp_forward/pallas_call | solution.py:787
  289.2 41.6 %mlp_backward.2 = (bf16[8,256,1536]{2,1,0:T(8,128)(2,1)}, bf16[8,256,1536]{2,1,0:T(8,128)(2,1)}, bf16[256,2048]{1,0:T(8,128)(2,1)}, bf16[256,2048]{1,0:T(8,128)(...) custom-call(bf16[256,2048]{1,0:T(8,128)(2,1)} %get-tuple-element.313, ...), custom_call_target="tpu_custom_call" | custom-call | flops 18400000000 | bytes 65536 | tf_op jit(solution)/shard_map/mlp_backward/pallas_call | solution.py:787
  330.8 31.1 %weight_grad.5 = (bf16[384,2048]{1,0:T(8,128)(2,1)}, bf16[384,2048]{1,0:T(8,128)(2,1)}) custom-call(bf16[2048,1536]{1,0:T(8,128)(2,1)} %bitcast.128, bf16[256,2048]{1,0:T(8,128)(2,1)} %get-tuple-element.313.refs_11_.refs_0_.refs_1_, bf16[256,2048]{1,0:T(8,128)(2,1)} %get-tuple-element.178.refs_1_.refs_2_, ...), custom_call_target="tpu_custom_call" | custom-call | flops 11500000256 | bytes 65536 | tf_op jit(solution)/shard_map/weight_grad/pallas_call | solution.py:787
  362.0 50.8 %mlp_backward.3 = (bf16[8,256,1536]{2,1,0:T(8,128)(2,1)}, bf16[8,256,1536]{2,1,0:T(8,128)(2,1)}, bf16[256,2048]{1,0:T(8,128)(2,1)}, bf16[256,2048]{1,0:T(8,128)(...) custom-call(bf16[256,2048]{1,0:T(8,128)(2,1)} %get-tuple-element.312, ...), custom_call_target="tpu_custom_call", output_to_operand_aliasing={{0}: (10, {}), {1}: (11, {})} | custom-call | flops 18400000000 | bytes 65536 | tf_op jit(solution)/shard_map/mlp_backward/pallas_call | solution.py:787
  412.8 2.6 multiply_reduce_fusion.1
  415.4 2.8 fusion.72
  418.2 45.3 %weight_grad.6 = (bf16[512,1536]{1,0:T(8,128)(2,1)}, bf16[512,1536]{1,0:T(8,128)(2,1)}, bf16[256,2048]{1,0:T(8,128)(2,1)}, bf16[256,2048]{1,0:T(8,128)(2,1)}, bf...) custom-call(bf16[256,2048]{1,0:T(8,128)(2,1)} %copy-done.21, ...), custom_call_target="tpu_custom_call" | custom-call | flops 11500000256 | bytes 65536 | tf_op jit(solution)/shard_map/weight_grad/pallas_call | solution.py:787
  463.6 43.8 %weight_grad.7 = (bf16[512,1536]{1,0:T(8,128)(2,1)}, bf16[512,1536]{1,0:T(8,128)(2,1)}, bf16[256,2048]{1,0:T(8,128)(2,1)}, bf16[256,2048]{1,0:T(8,128)(2,1)}, bf...) custom-call(bf16[256,2048]{1,0:T(8,128)(2,1)} %copy-done.21, ...), custom_call_target="tpu_custom_call" | custom-call | flops 11500000256 | bytes 65536 | tf_op jit(solution)/shard_map/weight_grad/pallas_call | solution.py:787
  507.4 2.6 multiply_reduce_fusion
  510.0 2.8 fusion.71
  512.8 51.2 %rec_backward.2 = (bf16[8,256,1280]{2,1,0:T(8,128)(2,1)}, bf16[8,256,1280]{2,1,0:T(8,128)(2,1)}, f32[8,8,640]{2,1,0:T(8,128)}, f32[8,2048]{1,0:T(8,128)}, bf16[2...) custom-call(s32[8,128]{1,0:T(8,128)} %broadcast_in_dim.15.refs_0_, ...), custom_call_target="tpu_custom_call" | custom-call | flops 24725000192 | bytes 65536 | tf_op jit(solution)/shard_map/rec_backward/pallas_call | solution.py:787
  564.0 47.7 %rec_backward.3 = (bf16[8,256,1280]{2,1,0:T(8,128)(2,1)}, bf16[8,256,1280]{2,1,0:T(8,128)(2,1)}, f32[8,8,640]{2,1,0:T(8,128)}, f32[8,2048]{1,0:T(8,128)}, bf16[2...) custom-call(s32[8,128]{1,0:T(8,128)} %broadcast_in_dim.20.refs_0_, ...), custom_call_target="tpu_custom_call", output_to_operand_aliasing={{0}: (22, {}), {1}: (23, {})} | custom-call | flops 24725000192 | bytes 65536 | tf_op jit(solution)/shard_map/rec_backward/pallas_call | solution.py:787
  611.8 46.0 %weight_grad.8 = (bf16[512,1280]{1,0:T(8,128)(2,1)}, bf16[512,1280]{1,0:T(8,128)(2,1)}, bf16[512,1536]{1,0:T(8,128)(2,1)}, bf16[512,1536]{1,0:T(8,128)(2,1)}, bf16[512,1536]{1,0:T(8,128)(2,1)}) custom-call(bf16[256,2048]{1,0:T(8,128)(2,1)} %copy-done.23, bf16[256,2048]{1,0:T(8,128)(2,1)} %copy-done.32, bf16[256,2048]{1,0:T(8,128)(2,1)} %copy-done.31, ...), custom_call_target="tpu_custom_call" | custom-call | flops 11500000256 | bytes 65536 | tf_op jit(solution)/shard_map/weight_grad/pallas_call | solution.py:787
  657.8 41.9 %weight_grad.9 = (bf16[640,512]{1,0:T(8,128)(2,1)}, bf16[640,512]{1,0:T(8,128)(2,1)}, bf16[256,2048]{1,0:T(8,128)(2,1)}, bf16[256,2048]{1,0:T(8,128)(2,1)}, bf16...) custom-call(bf16[1024,640]{1,0:T(8,128)(2,1)} %bitcast.132, ...), custom_call_target="tpu_custom_call" | custom-call | flops 7474999808 | bytes 65536 | tf_op jit(solution)/shard_map/weight_grad/pallas_call | solution.py:787
  700.2 0.9 slice.227
  702.5 1.7 collective-permute-start.23
  705.8 4.5 convolution_bitcast_fusion
  710.3 2.0 fusion.23
  715.7 1.8 collective-permute-done.13
  718.3 1.5 fusion.67
  719.8 2.1 reshape.188
  721.8 1.2 collective-permute-start.14
  723.0 4.1 fusion.39
  730.0 127.6 %sum_tail.1 = (bf16[512,1280]{1,0:T(8,128)(2,1)}, bf16[752,512]{1,0:T(8,128)(2,1)}, bf16[752,512]{1,0:T(8,128)(2,1)}, bf16[512,1280]{1,0:T(8,128)(2,1)}, bf16[512,1536]{1,0:T(8,128)(2,1)}) custom-call(bf16[512,1280]{1,0:T(8,128)(2,1)} %get-tuple-element.266.refs_0_, bf16[752,512]{1,0:T(8,128)(2,1)} %pad_maximum_fusion.2.refs_1_, ...), custom_call_target="tpu_custom_call" | custom-call | flops 51749998592 | bytes 65536 | tf_op jit(solution)/shard_map/sum_tail/pallas_call | solution.py:787
  858.6 4.1 fusion.59
  862.7 1.5 pad_maximum_fusion.1
  866.6 10.5 %join_quarters.6 = f32[640,2048]{1,0:T(8,128)} custom-call(bf16[752,512]{1,0:T(8,128)(2,1)} %get-tuple-element.275.refs_0_, bf16[752,512]{1,0:T(8,128)(2,1)} %get-tuple-element.276.refs_1_, bf16[752,512]{1,0:T(8,128)(2,1)} %copy-done.48, bf16[752,512]{1,0:T(8,128)(2,1)} %copy-done.49), custom_call_target="tpu_custom_call" | custom-call | flops 5750000128 | bytes 65536 | tf_op jit(solution)/shard_map/join_quarters/pallas_call | solution.py:787
  879.1 1.2 reshape.191
  880.3 1.2 reshape.190
  882.7 9.6 %join_quarters.9 = f32[1536,2048]{1,0:T(8,128)} custom-call(bf16[384,2048]{1,0:T(8,128)(2,1)} %get-tuple-element.285.refs_0_, bf16[384,2048]{1,0:T(8,128)(2,1)} %get-tuple-element.286.refs_1_, bf16[384,2048]{1,0:T(8,128)(2,1)} %collective-permute-done.23.refs_2_, bf16[384,2048]{1,0:T(8,128)(2,1)} %collective-permute-done.24.refs_3_), custom_call_target="tpu_custom_call" | custom-call | flops 5750000128 | bytes 65536 | tf_op jit(solution)/shard_map/join_quarters/pallas_call | solution.py:787
  892.3 9.6 %join_quarters.7 = f32[2048,1536]{1,0:T(8,128)} custom-call(bf16[512,1536]{1,0:T(8,128)(2,1)} %get-tuple-element.281.refs_0_, bf16[512,1536]{1,0:T(8,128)(2,1)} %get-tuple-element.282.refs_1_, bf16[512,1536]{1,0:T(8,128)(2,1)} %collective-permute-done.19.refs_2_, bf16[512,1536]{1,0:T(8,128)(2,1)} %collective-permute-done.20.refs_3_), custom_call_target="tpu_custom_call" | custom-call | flops 5750000128 | bytes 65536 | tf_op jit(solution)/shard_map/join_quarters/pallas_call | solution.py:787
  901.9 8.9 join_quarters.5
  910.9 1.1 copy-done.61
  912.0 1.2 copy-done.62
  913.2 9.6 %join_quarters.8 = f32[2048,1536]{1,0:T(8,128)} custom-call(bf16[512,1536]{1,0:T(8,128)(2,1)} %get-tuple-element.283.refs_0_, bf16[512,1536]{1,0:T(8,128)(2,1)} %get-tuple-element.284.refs_1_, bf16[512,1536]{1,0:T(8,128)(2,1)} %copy-done.61, bf16[512,1536]{1,0:T(8,128)(2,1)} %copy-done.62), custom_call_target="tpu_custom_call" | custom-call | flops 5750000128 | bytes 65536 | tf_op jit(solution)/shard_map/join_quarters/pallas_call | solution.py:787
  922.8 1.5 fusion.57
  924.3 2.1 fusion.58
  926.5 1.5 pad_maximum_fusion
  (241 shorter events, 26.8 us)
Async XLA Ops:
  7.2 915.6 %reduce-scatter.3.cloned.1.call-start = ((), (), s32[]{:S(2)}) async-start(), calls=%async_computation.2 | async-start | bytes 5242880 | tf_op jit(solution)/shard_map/reduce_scatter | solution.py:1320
  10.9 24.2 %copy-start.23 = (bf16[256,2048]{1,0:T(8,128)(2,1)}, bf16[256,2048]{1,0:T(8,128)(2,1)S(1)}, u32[]{:S(2)}) copy-start(bf16[256,2048]{1,0:T(8,128)(2,1)S(1)} %get-tuple-element.310.refs_1_.refs_6_.refs_0_) | copy-start | bytes 3145732
  10.9 11.1 %copy-start.50 = (f32[640]{0:T(1024)S(1)}, f32[640]{0:T(1024)}, u32[]{:S(2)}) copy-start(f32[640]{0:T(1024)} %param.28) | copy-start | bytes 7684
  10.9 11.7 %copy-start.56 = (f32[640]{0:T(1024)S(1)}, f32[640]{0:T(1024)}, u32[]{:S(2)}) copy-start(f32[640]{0:T(1024)} %param.23) | copy-start | bytes 7684
  10.9 12.2 %copy-start.57 = (f32[640]{0:T(1024)S(1)}, f32[640]{0:T(1024)}, u32[]{:S(2)}) copy-start(f32[640]{0:T(1024)} %param.25) | copy-start | bytes 7684
  10.9 12.8 %copy-start.58 = (f32[640]{0:T(1024)S(1)}, f32[640]{0:T(1024)}, u32[]{:S(2)}) copy-start(f32[640]{0:T(1024)} %param.27) | copy-start | bytes 7684
  10.9 13.4 %copy-start.59 = (s32[2]{0:T(128)S(1)}, s32[2]{0:T(128)}, u32[]{:S(2)}) copy-start(s32[2]{0:T(128)} %param.34) | copy-start | bytes 28
  10.9 24.1 %collective-permute-start.1 = (bf16[256,2048]{1,0:T(8,128)(2,1)S(1)}, bf16[256,2048]{1,0:T(8,128)(2,1)S(1)}, u32[]{:S(2)}, u32[]{:S(2)}) collective-permute-start(bf16[256,2048]{1,0:T(8,128)(2,1)S(1)} %get-tuple-element.310.refs_1_.refs_6_.refs_0_), channel_id=1, source_target_pairs={{0,2},{1,3},{2,0},{3,1},{4,6},{5,7},{6,4},{7,5},{8,10},{9,11},{10,... | collective-permute-start | bytes 3145736 | tf_op jit(solution)/shard_map/ppermute | solution.py:1024
  12.2 24.1 %collective-permute-start = (bf16[256,2048]{1,0:T(8,128)(2,1)S(1)}, bf16[256,2048]{1,0:T(8,128)(2,1)S(1)}, u32[]{:S(2)}, u32[]{:S(2)}) collective-permute-start(bf16[256,2048]{1,0:T(8,128)(2,1)S(1)} %get-tuple-element.310.refs_1_.refs_6_.refs_0_), channel_id=1, source_target_pairs={{0,1},{1,0},{2,3},{3,2},{4,5},{5,4},{6,7},{7,6},{8,9},{9,8},{10,11... | collective-permute-start | bytes 3145736 | tf_op jit(solution)/shard_map/ppermute | solution.py:1024
  13.5 24.2 %copy-start.15 = (bf16[2048,640]{1,0:T(8,128)(2,1)S(1)}, bf16[2048,640]{1,0:T(8,128)(2,1)}, u32[]{:S(2)}) copy-start(bf16[2048,640]{1,0:T(8,128)(2,1)} %param.20) | copy-start | bytes 7864324
  35.1 11.9 %collective-permute-start.3 = (bf16[128,2048]{1,0:T(8,128)(2,1)S(1)}, bf16[128,2048]{1,0:T(8,128)(2,1)S(1)}, u32[]{:S(2)}, u32[]{:S(2)}) collective-permute-start(bf16[128,2048]{1,0:T(8,128)(2,1)S(1)} %slice.230), channel_id=1, source_target_pairs={{0,1},{1,0},{2,3},{3,2},{4,5},{5,4},{6,7},{7,6},{8,9},{9,8},{10,11... | collective-permute-start | bytes 1572872 | tf_op jit(solution)/shard_map/ppermute | solution.py:1024
  36.4 11.7 %collective-permute-start.2 = (bf16[128,2048]{1,0:T(8,128)(2,1)S(1)}, bf16[128,2048]{1,0:T(8,128)(2,1)S(1)}, u32[]{:S(2)}, u32[]{:S(2)}) collective-permute-start(bf16[128,2048]{1,0:T(8,128)(2,1)S(1)} %slice.229), channel_id=1, source_target_pairs={{0,2},{1,3},{2,0},{3,1},{4,6},{5,7},{6,4},{7,5},{8,10},{9,11},{10,... | collective-permute-start | bytes 1572872 | tf_op jit(solution)/shard_map/ppermute | solution.py:1024
  92.1 42.1 %copy-start.25 = (bf16[256,2048]{1,0:T(8,128)(2,1)S(1)}, bf16[256,2048]{1,0:T(8,128)(2,1)}, u32[]{:S(2)}) copy-start(bf16[256,2048]{1,0:T(8,128)(2,1)} %get-tuple-element.153) | copy-start | bytes 3145732
  136.4 278.9 %copy-start = (f32[256,2048]{1,0:T(8,128)}, f32[256,2048]{1,0:T(8,128)S(1)}, u32[]{:S(2)}) copy-start(f32[256,2048]{1,0:T(8,128)S(1)} %get-tuple-element.307) | copy-start | bytes 6291460
  136.7 35.3 %copy-start.21 = (bf16[256,2048]{1,0:T(8,128)(2,1)}, bf16[256,2048]{1,0:T(8,128)(2,1)S(1)}, u32[]{:S(2)}) copy-start(bf16[256,2048]{1,0:T(8,128)(2,1)S(1)} %multiply_convert_fusion.1.refs_0_) | copy-start | bytes 3145732
  136.7 20.6 %collective-permute-start.5 = (bf16[256,2048]{1,0:T(8,128)(2,1)S(1)}, bf16[256,2048]{1,0:T(8,128)(2,1)S(1)}, u32[]{:S(2)}, u32[]{:S(2)}) collective-permute-start(bf16[256,2048]{1,0:T(8,128)(2,1)S(1)} %multiply_convert_fusion.1.refs_0_), channel_id=1, source_target_pairs={{0,2},{1,3},{2,0},{3,1},{4,6},{5,7},{6,4},{7,5},{8,10},{9,11},{10,... | collective-permute-start | bytes 3145736 | tf_op jit(solution)/shard_map/ppermute | solution.py:1024
  138.5 20.5 %collective-permute-start.4 = (bf16[256,2048]{1,0:T(8,128)(2,1)S(1)}, bf16[256,2048]{1,0:T(8,128)(2,1)S(1)}, u32[]{:S(2)}, u32[]{:S(2)}) collective-permute-start(bf16[256,2048]{1,0:T(8,128)(2,1)S(1)} %multiply_convert_fusion.1.refs_0_), channel_id=1, source_target_pairs={{0,1},{1,0},{2,3},{3,2},{4,5},{5,4},{6,7},{7,6},{8,9},{9,8},{10,11... | collective-permute-start | bytes 3145736 | tf_op jit(solution)/shard_map/ppermute | solution.py:1024
  157.4 13.8 %copy-start.33 = (bf16[256,2048]{1,0:T(8,128)(2,1)}, bf16[256,2048]{1,0:T(8,128)(2,1)S(1)}, u32[]{:S(2)}) copy-start(bf16[256,2048]{1,0:T(8,128)(2,1)S(1)} %collective-permute-done.5.refs_2_) | copy-start | bytes 3145732
  157.4 13.7 %collective-permute-start.7 = (bf16[128,2048]{1,0:T(8,128)(2,1)S(1)}, bf16[128,2048]{1,0:T(8,128)(2,1)S(1)}, u32[]{:S(2)}, u32[]{:S(2)}) collective-permute-start(bf16[128,2048]{1,0:T(8,128)(2,1)S(1)} %slice.232), channel_id=1, source_target_pairs={{0,1},{1,0},{2,3},{3,2},{4,5},{5,4},{6,7},{7,6},{8,9},{9,8},{10,11... | collective-permute-start | bytes 1572872 | tf_op jit(solution)/shard_map/ppermute | solution.py:1024
  159.0 12.1 %copy-start.34 = (bf16[256,2048]{1,0:T(8,128)(2,1)}, bf16[256,2048]{1,0:T(8,128)(2,1)S(1)}, u32[]{:S(2)}) copy-start(bf16[256,2048]{1,0:T(8,128)(2,1)S(1)} %collective-permute-done.4.refs_1_) | copy-start | bytes 3145732
  159.1 12.0 %collective-permute-start.6 = (bf16[128,2048]{1,0:T(8,128)(2,1)S(1)}, bf16[128,2048]{1,0:T(8,128)(2,1)S(1)}, u32[]{:S(2)}, u32[]{:S(2)}) collective-permute-start(bf16[128,2048]{1,0:T(8,128)(2,1)S(1)} %slice.231), channel_id=1, source_target_pairs={{0,2},{1,3},{2,0},{3,1},{4,6},{5,7},{6,4},{7,5},{8,10},{9,11},{10,... | collective-permute-start | bytes 1572872 | tf_op jit(solution)/shard_map/ppermute | solution.py:1024
  172.2 40.8 %copy-start.24 = (bf16[256,2048]{1,0:T(8,128)(2,1)S(1)}, bf16[256,2048]{1,0:T(8,128)(2,1)}, u32[]{:S(2)}) copy-start(bf16[256,2048]{1,0:T(8,128)(2,1)} %get-tuple-element.172) | copy-start | bytes 3145732
  215.2 294.8 %copy-start.2 = (f32[256,2048]{1,0:T(8,128)}, f32[256,2048]{1,0:T(8,128)S(1)}, u32[]{:S(2)}) copy-start(f32[256,2048]{1,0:T(8,128)S(1)} %get-tuple-element.305) | copy-start | bytes 6291460
  215.2 21.4 %copy-start.5 = (bf16[2,256,2048]{2,1,0:T(8,128)(2,1)S(1)}, bf16[2,256,2048]{2,1,0:T(8,128)(2,1)}, u32[]{:S(2)}) copy-start(bf16[2,256,2048]{2,1,0:T(8,128)(2,1)} %param.35) | copy-start | bytes 6291460
  215.5 22.7 %copy-start.22 = (bf16[256,2048]{1,0:T(8,128)(2,1)}, bf16[256,2048]{1,0:T(8,128)(2,1)S(1)}, u32[]{:S(2)}) copy-start(bf16[256,2048]{1,0:T(8,128)(2,1)S(1)} %multiply_convert_fusion.refs_0_.refs_5_) | copy-start | bytes 3145732
  215.5 18.5 %collective-permute-start.9 = (bf16[256,2048]{1,0:T(8,128)(2,1)S(1)}, bf16[256,2048]{1,0:T(8,128)(2,1)S(1)}, u32[]{:S(2)}, u32[]{:S(2)}) collective-permute-start(bf16[256,2048]{1,0:T(8,128)(2,1)S(1)} %multiply_convert_fusion.refs_0_.refs_5_), channel_id=1, source_target_pairs={{0,2},{1,3},{2,0},{3,1},{4,6},{5,7},{6,4},{7,5},{8,10},{9,11},{10,... | collective-permute-start | bytes 3145736 | tf_op jit(solution)/shard_map/ppermute | solution.py:1024
  215.9 18.9 %collective-permute-start.8 = (bf16[256,2048]{1,0:T(8,128)(2,1)S(1)}, bf16[256,2048]{1,0:T(8,128)(2,1)S(1)}, u32[]{:S(2)}, u32[]{:S(2)}) collective-permute-start(bf16[256,2048]{1,0:T(8,128)(2,1)S(1)} %multiply_convert_fusion.refs_0_.refs_5_), channel_id=1, source_target_pairs={{0,1},{1,0},{2,3},{3,2},{4,5},{5,4},{6,7},{7,6},{8,9},{9,8},{10,11... | collective-permute-start | bytes 3145736 | tf_op jit(solution)/shard_map/ppermute | solution.py:1024
  234.1 12.8 %collective-permute-start.11 = (bf16[128,2048]{1,0:T(8,128)(2,1)S(1)}, bf16[128,2048]{1,0:T(8,128)(2,1)S(1)}, u32[]{:S(2)}, u32[]{:S(2)}) collective-permute-start(bf16[128,2048]{1,0:T(8,128)(2,1)S(1)} %slice.234), channel_id=1, source_target_pairs={{0,1},{1,0},{2,3},{3,2},{4,5},{5,4},{6,7},{7,6},{8,9},{9,8},{10,11... | collective-permute-start | bytes 1572872 | tf_op jit(solution)/shard_map/ppermute | solution.py:1024
  236.0 10.9 %collective-permute-start.10 = (bf16[128,2048]{1,0:T(8,128)(2,1)S(1)}, bf16[128,2048]{1,0:T(8,128)(2,1)S(1)}, u32[]{:S(2)}, u32[]{:S(2)}) collective-permute-start(bf16[128,2048]{1,0:T(8,128)(2,1)S(1)} %slice.233), channel_id=1, source_target_pairs={{0,2},{1,3},{2,0},{3,1},{4,6},{5,7},{6,4},{7,5},{8,10},{9,11},{10,... | collective-permute-start | bytes 1572872 | tf_op jit(solution)/shard_map/ppermute | solution.py:1024
  362.0 50.8 %copy-start.9 = (bf16[256,2048]{1,0:T(8,128)(2,1)S(1)}, bf16[256,2048]{1,0:T(8,128)(2,1)}, u32[]{:S(2)}) copy-start(bf16[256,2048]{1,0:T(8,128)(2,1)} %get-tuple-element.184) | copy-start | bytes 3145732
  463.6 43.8 %copy-start.8 = (bf16[256,2048]{1,0:T(8,128)(2,1)S(1)}, bf16[256,2048]{1,0:T(8,128)(2,1)}, u32[]{:S(2)}) copy-start(bf16[256,2048]{1,0:T(8,128)(2,1)} %get-tuple-element.206) | copy-start | bytes 3145732
  699.8 4.4 copy-start.37
  699.8 4.4 copy-start.38
  699.8 4.5 copy-start.51
  699.8 4.5 copy-start.46
  699.8 4.5 copy-start.45
  699.8 4.5 copy-start.40
  699.8 6.0 copy-start.19
  699.9 224.5 %reduce-scatter.5.cloned.1.call-start = ((), (), s32[]{:S(2)}) async-start(), calls=%async_computation.3 | async-start | bytes 5242880 | tf_op jit(solution)/shard_map/reduce_scatter | solution.py:1320
  702.5 174.7 %collective-permute-start.23 = (bf16[384,2048]{1,0:T(8,128)(2,1)}, bf16[384,2048]{1,0:T(8,128)(2,1)}, u32[]{:S(2)}, u32[]{:S(2)}) collective-permute-start(bf16[384,2048]{1,0:T(8,128)(2,1)} %get-tuple-element.285.refs_0_), channel_id=1, source_target_pairs={{0,4},{4,0},{8,12},{12,8},{16,20},{20,16},{24,28},{28,24},{1,5},{5... | collective-permute-start | bytes 4718600 | tf_op jit(solution)/shard_map/ppermute | solution.py:1024
  704.4 8.9 copy-start.42
  704.4 8.9 copy-start.43
  704.4 8.8 collective-permute-start.12
  705.3 176.9 %collective-permute-start.20 = (bf16[512,1536]{1,0:T(8,128)(2,1)}, bf16[512,1536]{1,0:T(8,128)(2,1)}, u32[]{:S(2)}, u32[]{:S(2)}) collective-permute-start(bf16[512,1536]{1,0:T(8,128)(2,1)} %get-tuple-element.282.refs_1_), channel_id=1, source_target_pairs={{0,4},{4,0},{8,12},{12,8},{16,20},{20,16},{24,28},{28,24},{1,5},{5... | collective-permute-start | bytes 4718600 | tf_op jit(solution)/shard_map/ppermute | solution.py:1024
  705.5 186.7 %collective-permute-start.19 = (bf16[512,1536]{1,0:T(8,128)(2,1)}, bf16[512,1536]{1,0:T(8,128)(2,1)}, u32[]{:S(2)}, u32[]{:S(2)}) collective-permute-start(bf16[512,1536]{1,0:T(8,128)(2,1)} %get-tuple-element.281.refs_0_), channel_id=1, source_target_pairs={{0,4},{4,0},{8,12},{12,8},{16,20},{20,16},{24,28},{28,24},{1,5},{5... | collective-permute-start | bytes 4718600 | tf_op jit(solution)/shard_map/ppermute | solution.py:1024
  705.8 4.5 copy-start.18
  705.8 4.5 copy-start.69
  713.9 3.5 collective-permute-start.13
  715.6 7.4 copy-start.4
  715.6 7.3 copy-start.14
  721.8 5.3 collective-permute-start.14
  730.0 128.5 %copy-start.6 = (f32[256,2048]{1,0:T(8,128)S(1)}, f32[256,2048]{1,0:T(8,128)}, u32[]{:S(2)}) copy-start(f32[256,2048]{1,0:T(8,128)} %get-tuple-element.303) | copy-start | bytes 6291460
  730.0 128.5 %copy-start.7 = (f32[256,2048]{1,0:T(8,128)S(1)}, f32[256,2048]{1,0:T(8,128)}, u32[]{:S(2)}) copy-start(f32[256,2048]{1,0:T(8,128)} %get-tuple-element.301) | copy-start | bytes 6291460
  730.0 128.5 %copy-start.41 = (f32[2048]{0:T(1024)S(1)}, f32[2048]{0:T(1024)}, u32[]{:S(2)}) copy-start(f32[2048]{0:T(1024)} %param.19) | copy-start | bytes 24580
  730.0 128.5 %copy-start.53 = (f32[256]{0:T(256)S(1)}, f32[256]{0:T(256)}, u32[]{:S(2)}) copy-start(f32[256]{0:T(256)} %copy-done.52) | copy-start | bytes 3076
  730.0 128.5 %copy-start.55 = (f32[256]{0:T(256)S(1)}, f32[256]{0:T(256)}, u32[]{:S(2)}) copy-start(f32[256]{0:T(256)} %copy-done.54) | copy-start | bytes 3076
  857.7 7.5 collective-permute-start.15
  862.6 3.1 collective-permute-start.16
  865.2 17.3 %collective-permute-start.24 = (bf16[384,2048]{1,0:T(8,128)(2,1)S(1)}, bf16[384,2048]{1,0:T(8,128)(2,1)}, u32[]{:S(2)}, u32[]{:S(2)}) collective-permute-start(bf16[384,2048]{1,0:T(8,128)(2,1)S(1)} %copy-done.60), channel_id=1, source_target_pairs={{0,4},{4,0},{8,12},{12,8},{16,20},{20,16},{24,28},{28,24},{1,5},{5... | collective-permute-start | bytes 4718600 | tf_op jit(solution)/shard_map/ppermute | solution.py:1024
  865.8 36.2 %collective-permute-start.17 = (bf16[512,1280]{1,0:T(8,128)(2,1)}, bf16[512,1280]{1,0:T(8,128)(2,1)}, u32[]{:S(2)}, u32[]{:S(2)}) collective-permute-start(bf16[512,1280]{1,0:T(8,128)(2,1)} %get-tuple-element.277.refs_0_), channel_id=1, source_target_pairs={{0,4},{4,0},{8,12},{12,8},{16,20},{20,16},{24,28},{28,24},{1,5},{5... | collective-permute-start | bytes 3932168 | tf_op jit(solution)/shard_map/ppermute | solution.py:1024
  877.1 24.8 %collective-permute-start.18 = (bf16[512,1280]{1,0:T(8,128)(2,1)}, bf16[512,1280]{1,0:T(8,128)(2,1)}, u32[]{:S(2)}, u32[]{:S(2)}) collective-permute-start(bf16[512,1280]{1,0:T(8,128)(2,1)} %get-tuple-element.278.refs_1_), channel_id=1, source_target_pairs={{0,4},{4,0},{8,12},{12,8},{16,20},{20,16},{24,28},{28,24},{1,5},{5... | collective-permute-start | bytes 3932168 | tf_op jit(solution)/shard_map/ppermute | solution.py:1024
  882.2 28.7 %collective-permute-start.21 = (bf16[512,1536]{1,0:T(8,128)(2,1)}, bf16[512,1536]{1,0:T(8,128)(2,1)S(1)}, u32[]{:S(2)}, u32[]{:S(2)}) collective-permute-start(bf16[512,1536]{1,0:T(8,128)(2,1)} %get-tuple-element.283.refs_0_), channel_id=1, source_target_pairs={{0,4},{4,0},{8,12},{12,8},{16,20},{20,16},{24,28},{28,24},{1,5},{5... | collective-permute-start | bytes 4718600 | tf_op jit(solution)/shard_map/ppermute | solution.py:1024
  882.5 28.4 %collective-permute-start.22 = (bf16[512,1536]{1,0:T(8,128)(2,1)}, bf16[512,1536]{1,0:T(8,128)(2,1)S(1)}, u32[]{:S(2)}, u32[]{:S(2)}) collective-permute-start(bf16[512,1536]{1,0:T(8,128)(2,1)} %get-tuple-element.284.refs_1_), channel_id=1, source_target_pairs={{0,4},{4,0},{8,12},{12,8},{16,20},{20,16},{24,28},{28,24},{1,5},{5... | collective-permute-start | bytes 4718600 | tf_op jit(solution)/shard_map/ppermute | solution.py:1024
  910.9 11.9 %copy-start.1 = (f32[256,2048]{1,0:T(8,128)S(1)}, f32[256,2048]{1,0:T(8,128)}, u32[]{:S(2)}) copy-start(f32[256,2048]{1,0:T(8,128)} %copy-done) | copy-start | bytes 6291460
  (33 other events, 66.7 us)
Sparse Core Ops, SparseCore 0:
  700.0 52.5 reduce-scatter.2
  755.8 52.6 reduce-scatter.4

commit v4 on v3

--- a/solution.py
+++ b/solution.py
@@ -374,10 +374,12 @@
             copy(at).wait_send()
 
 
-def join_kernel(ways, first, second, third, fourth, *outs):
-    for at, ref in enumerate((first, second, third, fourth)):
-
-        @pl.when(pl.program_id(0) == at)
+def join_kernel(starts, *refs):
+    step = pl.program_id(0)
+    outs = refs[len(starts) - 1 :]
+    for ref, first, after in zip(refs, starts, starts[1:]):
+
+        @pl.when((step >= first) & (step < after))
         def _(ref=ref):
             start = 0
             for out in outs:
@@ -519,216 +521,245 @@
         return self.first.astype(f32) + outs[0].astype(f32) + outs[1].astype(f32)
 
 
+def chip_partners():
+    dp = lax.axis_index("dp")
+    return {"dp": flip(dp, 2, 8)}, {"dp": (3 - dp // 2) * 2 + dp % 2}
+
+
+def chip_is_inner():
+    return (lax.axis_index("dp") // 2 + 1) // 2 % 2 == 1
+
+
 class PipeHost:
-    def __init__(self, inward, between, outward):
-        self.counts = len(inward), len(between), len(outward)
-        self.operands = [chunk for _, chunk in inward + between + outward]
-        self.names = [name for name, _ in inward + between + outward]
-        self.outputs = [jax.ShapeDtypeStruct(chunk.shape, bf16) for chunk in self.operands]
-        adding = len(inward) + len(between)
-        self.scratch = [pltpu.VMEM(chunk.shape, bf16) for chunk in self.operands[:adding] for _ in range(2)]
-        self.scratch += [pltpu.VMEM(chunk.shape, bf16) for chunk in self.operands[adding:]]
-        self.scratch += [pltpu.SemaphoreType.DMA((len(self.operands),))] * 4
+    def __init__(self, pieces):
+        self.pieces = pieces
+        self.names = [piece[0] for piece in pieces]
+        self.operands = [piece[1] for piece in pieces]
+        self.outputs = [jax.ShapeDtypeStruct((piece[3], piece[1].shape[1]), bf16) for piece in pieces]
+        self.scratch = []
+        for (_, _, _, _, stage, hops), out in zip(pieces, self.outputs):
+            self.scratch += [pltpu.VMEM(out.shape, bf16)] * (1 + min(hops, 2 - stage))
+        self.scratch += [pltpu.SemaphoreType.DMA((len(pieces),))] * 6
 
     def devices(self):
-        dp = lax.axis_index("dp")
-        return {"dp": flip(dp, 2, 8)}, {"dp": (3 - dp // 2) * 2 + dp % 2}
+        return chip_partners()
 
     def parts(self, ins, outs, scratch):
-        pair, mirror = self.devices()
-        send, recv, local, back = scratch[-4:]
-        inward, between, _ = self.counts
-        for at, (chunk, out) in enumerate(zip(ins, outs)):
-            if at < inward + between:
-                own, got = scratch[2 * at], scratch[2 * at + 1]
-                way, device = ("in", pair) if at < inward else ("mid", mirror)
-                yield (
-                    way,
-                    lambda chunk=chunk, got=got, at=at, device=device: remote(chunk, got, send, recv, at, device),
-                    lambda chunk=chunk, own=own, at=at: pltpu.make_async_copy(chunk, own, local.at[at]),
-                    lambda own=own, out=out, at=at: pltpu.make_async_copy(own, out, back.at[at]),
-                    own,
-                    got,
-                )
-            else:
-                own = scratch[at + inward + between]
-                yield (
-                    "out",
-                    lambda chunk=chunk, out=out, at=at: remote(chunk, out, send, recv, at, pair),
-                    lambda chunk=chunk, own=own, at=at: pltpu.make_async_copy(chunk, own, local.at[at]),
-                    lambda own=own, out=out, at=at: pltpu.make_async_copy(own, out, back.at[at]),
-                    None,
-                    None,
-                )
-
-    def inner(self):
-        chip = lax.axis_index("dp") // 2
-        return (chip + 1) // 2 % 2 == 1
+        pair, mirror = chip_partners()
+        send, recv, send_on, recv_on, local, back = scratch[-6:]
+        given = 0
+        for at, ((_, _, start, count, stage, hops), array, out) in enumerate(zip(self.pieces, ins, outs)):
+            many = 1 + min(hops, 2 - stage)
+            buffers = list(scratch[given : given + many])
+            given += many
+            source = array.at[pl.ds(start, count)]
+
+            def hop(number, at=at, stage=stage, source=source, buffers=buffers, out=out):
+                way = stage + number
+                target = out if way == 2 else buffers[number + 1]
+                sems = (send, recv) if number == 0 else (send_on, recv_on)
+                return remote(source if number == 0 else buffers[number], target, *sems, at, mirror if way == 1 else pair)
+
+            def load(at=at, source=source, buffers=buffers):
+                return pltpu.make_async_copy(source, buffers[0], local.at[at])
+
+            def keep(at=at, buffers=buffers, out=out):
+                return pltpu.make_async_copy(buffers[-1], out, back.at[at])
+
+            yield stage, hops, buffers, hop, load, keep
+
+    def add(self, target, other):
+        target[...] = (target[...].astype(f32) + other[...].astype(f32)).astype(bf16)
 
     def begin(self, *refs):
-        inner = self.inner()
-        for way, there, here, _, _, _ in self.parts(*refs):
+        inner = chip_is_inner()
+        for stage, _, _, hop, load, _ in self.parts(*refs):
 
             @pl.when(inner)
-            def _(way=way, there=there, here=here):
-                here().start()
-                if way != "in":
-                    there().start()
-
-            if way == "in":
+            def _(stage=stage, hop=hop, load=load):
+                load().start()
+                if stage > 0:
+                    hop(0).start()
+
+            if stage == 0:
 
                 @pl.when(jnp.logical_not(inner))
-                def _(there=there):
-                    there().start()
+                def _(hop=hop):
+                    hop(0).start()
 
     def middle(self, *refs):
-        pass
+        inner = chip_is_inner()
+        for stage, hops, buffers, hop, load, keep in self.parts(*refs):
+
+            @pl.when(inner)
+            def _(stage=stage, hops=hops, buffers=buffers, hop=hop, load=load, keep=keep):
+                load().wait()
+                if stage == 2:
+                    keep().start()
+                elif hops == 2:
+                    hop(0).wait_recv()
+                    self.add(buffers[1], buffers[0])
+                    hop(1).start()
+                    if stage == 1:
+                        keep().start()
 
     def end(self, *refs):
-        inner = self.inner()
+        inner = chip_is_inner()
         parts = list(self.parts(*refs))
-        for way, there, here, back, own, got in parts:
+        for stage, hops, buffers, hop, load, keep in parts:
 
             @pl.when(inner)
-            def _(way=way, there=there, here=here, back=back, own=own, got=got):
-                here().wait()
-                if way != "out":
-                    there().wait_recv()
-                    own[...] = (own[...].astype(f32) + got[...].astype(f32)).astype(bf16)
-                back().start()
-                if way != "in":
-                    there().wait_send()
-
-            if way != "mid":
-
-                @pl.when(jnp.logical_not(inner))
-                def _(way=way, there=there):
-                    if way == "in":
-                        there().wait_send()
-                    else:
-                        there().wait_recv()
-
-        for _, _, _, back, _, _ in parts:
+            def _(stage=stage, hops=hops, buffers=buffers, hop=hop, load=load, keep=keep):
+                if stage > 0:
+                    hop(0).wait_send()
+                if hops == 2:
+                    hop(1).wait_send()
+                if stage + hops < 3:
+                    hop(hops - 1).wait_recv()
+                    self.add(buffers[-1], buffers[-2])
+                    keep().start()
+
+            @pl.when(jnp.logical_not(inner))
+            def _(stage=stage, hops=hops, hop=hop):
+                if stage == 0:
+                    hop(0).wait_send()
+                if stage + hops == 3:
+                    hop(hops - 1).wait_recv()
+
+        for _, _, _, _, _, keep in parts:
 
             @pl.when(inner)
-            def _(back=back):
-                back().wait()
+            def _(keep=keep):
+                keep().wait()
 
     def result(self, outs):
         return dict(zip(self.names, outs))
 
 
-class TailHost(PipeHost):
-    def __init__(self, inward, between, outward):
-        chunks = [(chunk, stage) for stage, group in enumerate((inward, between, outward)) for _, chunk in group]
-        self.names = [name for name, _ in inward + between + outward]
-        self.operands = [chunk for chunk, _ in chunks]
-        self.outputs = [jax.ShapeDtypeStruct(chunk.shape, bf16) for chunk in self.operands]
-        self.scratch = [pltpu.VMEM(chunk.shape, bf16) for chunk, stage in chunks for _ in range(3 - stage)]
+class Tail:
+    def __init__(self, chunks):
+        self.chunks = chunks
         self.pieces = []
-        for at, (chunk, stage) in enumerate(chunks):
-            rows = chunk.shape[0]
-            first = rows if stage == 2 else (rows // 32 + 1) // 2 * 32
-            for start, count in ((0, first), (first, rows - first)):
-                if count > 0:
-                    self.pieces.append((at, stage, start, count))
+        for at, (shape, stage, _, _) in enumerate(chunks):
+            rows = shape[0]
+            first = rows if stage == 2 or rows < 64 else (rows // 32 + 1) // 2 * 32
+            self.pieces += [(at, start, count) for start, count in ((0, first), (first, rows - first)) if count > 0]
+        self.scratch = []
+        for shape, stage, late, _ in chunks:
+            self.scratch += [pltpu.VMEM(shape, bf16)] * (3 - stage - (1 if late else 0))
         self.scratch += [pltpu.SemaphoreType.DMA((len(self.pieces),))] * 8
 
-    def begin(self, ins, outs, scratch):
-        pair, mirror = self.devices()
+    def setup(self, refs, outs, scratch):
+        pair, mirror = chip_partners()
         p_send, p_recv, q_send, q_recv, f_send, f_recv, local, back = scratch[-8:]
-        buffers, given = {}, 0
-        for at, stage, start, _ in self.pieces:
-            if start == 0:
-                buffers[at] = scratch[given : given + 3 - stage]
-                given += 3 - stage
-
-        def part(ref, number):
-            _, _, start, count = self.pieces[number]
-            return ref.at[pl.ds(start, count)]
+        buffers, given = [], 0
+        for ref, (_, stage, late, _) in zip(refs, self.chunks):
+            count = 3 - stage - (1 if late else 0)
+            mine = ([ref] if late else []) + list(scratch[given : given + count])
+            given += count
+            buffers.append(mine if stage == 0 else [mine[0], None, mine[-1]])
 
         def transfers(number):
-            at, stage, _, _ = self.pieces[number]
-            own, from_pair, from_mirror = (buffers[at] + [None, None])[:3]
-            if stage == 1:
-                from_mirror = from_pair
-            chunk, out = part(ins[at], number), part(outs[at], number)
-            done = own if stage == 2 else from_mirror
+            at, start, count = self.pieces[number]
+            rows = pl.ds(start, count)
+            own, from_pair, from_mirror = buffers[at]
+            early = self.chunks[at][1]
+            source, out = refs[at].at[rows], outs[at].at[rows]
+            sent = source if early == 1 else own.at[rows]
+            done = own if early == 2 else from_mirror
+            given_out = source if early == 2 else done.at[rows]
             return {
-                "inward": lambda: remote(chunk, part(from_pair, number), p_send, p_recv, number, pair),
-                "load": lambda: pltpu.make_async_copy(chunk, part(own, number), local.at[number]),
-                "between": lambda: remote(part(own, number), part(from_mirror, number), q_send, q_recv, number, mirror),
-                "outward": lambda: remote(part(done, number), out, f_send, f_recv, number, pair),
-                "keep": lambda: pltpu.make_async_copy(part(done, number), out, back.at[number]),
+                "inward": lambda: remote(source, from_pair.at[rows], p_send, p_recv, number, pair),
+                "load": lambda: pltpu.make_async_copy(source, own.at[rows], local.at[number]),
+                "between": lambda: remote(sent, from_mirror.at[rows], q_send, q_recv, number, mirror),
+                "outward": lambda: remote(given_out, out, f_send, f_recv, number, pair),
+                "keep": lambda: pltpu.make_async_copy(done.at[rows], out, back.at[number]),
             }
 
-        def add(number, target, other):
-            at, _, start, count = self.pieces[number]
-            rows = pl.ds(start, count)
-            target[rows, :] = (target[rows, :].astype(f32) + other[rows, :].astype(f32)).astype(bf16)
-
+        self.buffers = buffers
+        self.moves = [transfers(number) for number in range(len(self.pieces))]
+        self.stages = [self.chunks[at][1] for at, _, _ in self.pieces]
+        self.late = [self.chunks[at][2] for at, _, _ in self.pieces]
+        self.out = [self.chunks[at][3] for at, _, _ in self.pieces]
+        self.inner = chip_is_inner()
+
+    def start(self):
+        @pl.when(self.inner)
+        def _():
+            for move, stage, late in zip(self.moves, self.stages, self.late):
+                if stage == 2:
+                    move["outward"]().start()
+                if stage == 1:
+                    move["between"]().start()
+                if not late:
+                    move["load"]().start()
+
+        @pl.when(jnp.logical_not(self.inner))
+        def _():
+            for move, stage, late in zip(self.moves, self.stages, self.late):
+                if stage == 0 and not late:
+                    move["inward"]().start()
+
+    def add(self, number, target, other):
+        _, start, count = self.pieces[number]
+        rows = pl.ds(start, count)
+        target[rows, :] = (target[rows, :].astype(f32) + other[rows, :].astype(f32)).astype(bf16)
+
+    def finish(self):
         numbers = range(len(self.pieces))
-        moves = [transfers(number) for number in numbers]
-        stages = [stage for _, stage, _, _ in self.pieces]
-        inner = self.inner()
-
-        def finish(number):
-            if stages[number] < 2:
-                moves[number]["between"]().wait_recv()
-                own, other = buffers[self.pieces[number][0]][0], buffers[self.pieces[number][0]][-1]
-                add(number, other, own)
-            moves[number]["outward"]().start()
-            moves[number]["keep"]().start()
-
-        @pl.when(inner)
-        def _():
-            for move in moves:
-                move["load"]().start()
-            for number in numbers:
-                if stages[number] == 2:
-                    moves[number]["load"]().wait()
-                    finish(number)
-            for number in numbers:
-                if stages[number] == 1:
-                    moves[number]["load"]().wait()
-                    moves[number]["between"]().start()
-            waiting = [number for number in numbers if stages[number] == 1]
-            for number in numbers:
-                if stages[number] == 0:
-                    moves[number]["load"]().wait()
-                    moves[number]["inward"]().wait_recv()
-                    own, other = buffers[self.pieces[number][0]][:2]
-                    add(number, own, other)
-                    moves[number]["between"]().start()
-                    waiting.append(number)
-                    finish(waiting.pop(0))
-            for number in waiting:
-                finish(number)
-            for number in numbers:
-                if stages[number] < 2:
-                    moves[number]["between"]().wait_send()
-                moves[number]["outward"]().wait_send()
-                moves[number]["keep"]().wait()
-
-        @pl.when(jnp.logical_not(inner))
+
+        def on(number):
+            self.moves[number]["between"]().wait_recv()
+            own, _, other = self.buffers[self.pieces[number][0]]
+            self.add(number, other, own)
+            if self.out[number]:
+                self.moves[number]["outward"]().start()
+            self.moves[number]["keep"]().start()
+
+        @pl.when(self.inner)
         def _():
             for number in numbers:
-                if stages[number] == 0:
-                    moves[number]["inward"]().start()
+                if not self.late[number]:
+                    self.moves[number]["load"]().wait()
+                if self.stages[number] == 2:
+                    self.moves[number]["keep"]().start()
+            waiting = [number for number in numbers if self.stages[number] == 1]
             for number in numbers:
-                if stages[number] == 0:
-                    moves[number]["inward"]().wait_send()
-                moves[number]["outward"]().wait_recv()
-
-    def end(self, *refs):
-        pass
+                if self.stages[number] == 0:
+                    self.moves[number]["inward"]().wait_recv()
+                    own, other, _ = self.buffers[self.pieces[number][0]]
+                    self.add(number, own, other)
+                    self.moves[number]["between"]().start()
+                    waiting.append(number)
+                    on(waiting.pop(0))
+            for number in waiting:
+                on(number)
+            for number in numbers:
+                if self.stages[number] < 2:
+                    self.moves[number]["between"]().wait_send()
+                if self.out[number]:
+                    self.moves[number]["outward"]().wait_send()
+                self.moves[number]["keep"]().wait()
+
+        @pl.when(jnp.logical_not(self.inner))
+        def _():
+            for number in numbers:
+                if self.stages[number] == 0 and self.late[number]:
+                    self.moves[number]["inward"]().start()
+            for number in numbers:
+                if self.stages[number] == 0:
+                    self.moves[number]["inward"]().wait_send()
+                if self.out[number]:
+                    self.moves[number]["outward"]().wait_recv()
 
 
 def call(
-    kernel, grid, ins, outs, scratch, name, us, hosts=(), before=(), aliases=None, middle=0, unique=None, pair=False
+    kernel, grid, ins, outs, scratch, name, us, hosts=(), before=(), aliases=None, middle=0, unique=None, pair=False, chips=False,
+    pipe_middle=0
 ):
     nins, nouts, nscratch = len(ins), len(outs), len(scratch)
     steps = math.prod(grid)
+    loaded = [at for at, (_, spec) in enumerate(ins) if spec is WHOLE]
 
     def body(*refs):
         refs = list(refs)
@@ -745,6 +776,7 @@
         host_outs = [take(len(host.outputs)) for host in hosts]
         own_scratch = take(nscratch)
         host_refs = [(i, o, take(len(host.scratch))) for host, i, o in zip(hosts, host_ins, host_outs)]
+        buffers = take(len(loaded))
         step = pl.program_id(0)
         if len(grid) == 2:
             step = step * grid[1] + pl.program_id(1)
@@ -757,6 +789,8 @@
                     kinds = [host for host in hosts if isinstance(host, kind)]
                     if kinds and not (kind is ScatterHost and any(isinstance(host, GatherHost) for host in hosts)):
                         devices += tuple(kinds[0].devices())
+                if chips:
+                    devices += tuple(chip_partners())
                 barrier = pltpu.get_barrier_semaphore()
                 for device in devices:
                     pl.semaphore_signal(barrier, inc=1, device_id=device, device_id_type=MESH)
@@ -764,11 +798,26 @@
                 for host, there in zip(hosts, host_refs):
                     host.begin(*there)
 
+        if loaded:
+            arrived = take(1)[0]
+            loads = [(own_ins[at], buffer, arrived.at[k]) for k, (at, buffer) in enumerate(zip(loaded, buffers))]
+
+            @pl.when(step == 0)
+            def _():
+                for load in loads:
+                    pltpu.make_async_copy(*load).start()
+                for load in loads:
+                    pltpu.make_async_copy(*load).wait()
+
+            for at, buffer in zip(loaded, buffers):
+                own_ins[at] = buffer
         if hosts:
 
-            @pl.when(step == middle)
-            def _():
-                for host, there in zip(hosts, host_refs):
+            for host, there in list(zip(hosts, host_refs))[::-1]:
+                at = pipe_middle if isinstance(host, PipeHost) else middle
+
+                @pl.when(step == at)
+                def _(host=host, there=there):
                     host.middle(*there)
 
         kernel(*own_ins, *own_outs, *own_scratch)
@@ -788,9 +837,12 @@
         body,
         out_shape=tuple(shape for shape, _ in outs) + tuple(host_outputs),
         grid=grid,
-        in_specs=[spec for _, spec in ins] + [ANY] * (len(host_operands) + len(before)),
+        in_specs=[ANY if spec is WHOLE else spec for _, spec in ins] + [ANY] * (len(host_operands) + len(before)),
         out_specs=tuple(spec for _, spec in outs) + (ANY,) * len(host_outputs),
-        scratch_shapes=list(scratch) + [v for host in hosts for v in host.scratch],
+        scratch_shapes=list(scratch)
+        + [v for host in hosts for v in host.scratch]
+        + [pltpu.VMEM(ins[at][0].shape, ins[at][0].dtype) for at in loaded]
+        + ([pltpu.SemaphoreType.DMA((len(loaded),))] if loaded else []),
         input_output_aliases=aliases or {},
         compiler_params=params,
         cost_estimate=cost(us),
@@ -808,9 +860,11 @@
     return pl.CostEstimate(flops=int(us * COST_SCALE * 1.15e9), bytes_accessed=1 << 16, transcendentals=0)
 
 
+WHOLE = "whole"
+
+
 def whole(array):
-    zeros = (0,) * array.ndim
-    return pl.BlockSpec(array.shape, lambda *_: zeros, pipeline_mode=pl.Buffered(1))
+    return WHOLE
 
 
 def layout_of(blocks, rows):
@@ -990,31 +1044,168 @@
     )
 
 
-def join_quarters(quarters, by_rows, ways, rows, **more):
-    columns = quarters[0].shape[1]
-    tile = max(t for t in range(16, 256 + 1, 16) if rows % t == 0)
-    steps = rows // tile
+def last_kernel(nlefts, nrights, nchunks, nblocks, tail, *refs):
+    lefts, refs = refs[:nlefts], refs[nlefts:]
+    rights, refs = refs[:nrights], refs[nrights:]
+    convs, refs = refs[:nlefts], refs[nlefts:]
+    d_gates, sums_a, sums_b, gain_a, gain_b, gain_c, gain_d = refs[:7]
+    chunks, refs = refs[7 : 7 + nchunks], refs[7 + nchunks :]
+    outs, scratch = refs[: nchunks + 4], refs[nchunks + 4 :]
+    pack, gains, first, second, whole_pack, got_pack, left, right, dense, sent, got, send, recv = scratch[:13]
+    step = pl.program_id(0)
+    tail.setup(list(chunks) + [pack, gains, first, second], outs, scratch[13:])
+    pl.when(step == 0)(tail.start)
+
+    def copy(at):
+        return remote(sent.at[at], got.at[at], send, recv, at, other_core())
+
+    def pack_copy():
+        return remote(whole_pack, got_pack, send, recv, 2, other_core())
+
+    @pl.when(step < 4)
+    def _():
+        at = 0
+        for ref in rights:
+            right[at : at + ref.shape[0], :] = ref[...]
+            at += ref.shape[0]
+
+    @pl.when(step == 0)
+    def _():
+        at = 0
+        for ref in lefts:
+            left[at : at + ref.shape[0], :] = ref[...]
+            at += ref.shape[0]
+
+    for at in range(4):
+
+        @pl.when(step == at)
+        def _(at=at):
+            total = lax.dot_general(left[...], right[...], (((0,), (0,)), ((), ())), preferred_element_type=f32)
+            if at < 2:
+                sent[at] = total.astype(bf16)
+                copy(at).start()
+            else:
+                copy(at - 2).wait_recv()
+                (first, second)[at - 2][...] = (total + got[at - 2].astype(f32)).astype(bf16)
+                copy(at - 2).wait_send()
+
+    @pl.when(step == 3)
+    def _():
+        at = 0
+        for ref in convs:
+            rows = ref.shape[0]
+            term = lax.dot_general(
+                ref[...], d_gates[at : at + rows, :], (((0,), (0,)), ((), ())), preferred_element_type=f32
+            )
+            dense[...] = term if at == 0 else dense[...] + term
+            at += rows
+        width = dense.shape[0]
+        inner = width // nblocks
+        lane = lax.broadcasted_iota(jnp.int32, (inner, width), 1)
+        for gate in range(2):
+            total = jnp.zeros((inner, width), f32)
+            for n in range(nblocks):
+                here = (lane >= n * inner) & (lane < (n + 1) * inner)
+                block = dense[n * inner : (n + 1) * inner, gate * width : (gate + 1) * width]
+                total = total + jnp.where(here, block, 0.0)
+            whole_pack[gate * inner : (gate + 1) * inner, :] = total.astype(bf16)
+        vectors = jnp.sum(sums_a[...] + sums_b[...], axis=1)
+        rest = whole_pack.shape[0] - 2 * inner
+        vectors = jnp.concatenate([vectors, jnp.zeros((rest - 8, width), f32)], axis=0)
+        whole_pack[2 * inner :, :] = vectors.astype(bf16)
+        pack_copy().start()
+        one = jnp.sum(gain_a[...] + gain_b[...], axis=0, keepdims=True)
+        two = gain_c[...] + gain_d[...]
+        row = lax.broadcasted_iota(jnp.int32, (16, one.shape[1]), 0)
+        gains[...] = jnp.where(row == 0, one, jnp.where(row == 1, two, 0.0)).astype(bf16)
+
+    @pl.when(step == 4)
+    def _():
+        pack_copy().wait()
+        mine = pl.ds(pl.multiple_of(core_index() * pack.shape[0], 16), pack.shape[0])
+        pack[...] = (whole_pack[mine, :].astype(f32) + got_pack[mine, :].astype(f32)).astype(bf16)
+        tail.finish()
+
+
+def last_grad(lefts, rights, convs, d_gates, vectors, moving, nblocks, **more):
+    lefts, rights, convs = ([flat(v) for v in group] for group in (lefts, rights, convs))
+    rows, columns = lefts[0].shape[1], rights[0].shape[1]
+    tokens = sum(v.shape[0] for v in lefts)
+    tile = columns // 4
+
+    def place(step):
+        step = step - step // 4
+        return (core_index() + 1 + step // 2) % 2 * 2 + step % 2
+
+    chunks = [(chunk, stage) for stage, group in enumerate(moving) for _, chunk in group.items()]
+    names = [name for group in moving for name in group]
+    block = (rows, tile)
+    packed = -(-(2 * rows // nblocks + 16) // 32) * 32
+    made = [((packed // 2, rows), True), ((16, columns), True), (block, False), (block, False)]
+    tail = Tail(
+        [(chunk.shape, stage, False, True) for chunk, stage in chunks] + [(shape, 0, True, out) for shape, out in made]
+    )
+    outs = [jax.ShapeDtypeStruct(chunk[0], bf16) for chunk in tail.chunks]
+    out, found = call(
+        functools.partial(last_kernel, len(lefts), len(rights), len(chunks), nblocks, tail),
+        (5,),
+        [(v, whole(v)) for v in lefts]
+        + [(v, pl.BlockSpec((v.shape[0], tile), lambda step: (0, place(step)))) for v in rights]
+        + [(v, whole(v)) for v in convs + [flat(d_gates)] + list(vectors)]
+        + [(chunk, ANY) for chunk, _ in chunks],
+        [(shape, ANY) for shape in outs],
+        [pltpu.VMEM(shape, bf16) for shape, _ in made]
+        + [
+            pltpu.VMEM((packed, rows), bf16),
+            pltpu.VMEM((packed, rows), bf16),
+            pltpu.VMEM((tokens, rows), bf16),
+            pltpu.VMEM((tokens, tile), bf16),
+            pltpu.VMEM((rows, 2 * rows), f32),
+            pltpu.VMEM((2,) + block, bf16),
+            pltpu.VMEM((2,) + block, bf16),
+            pltpu.SemaphoreType.DMA((3,)),
+            pltpu.SemaphoreType.DMA((3,)),
+        ]
+        + tail.scratch,
+        "last_grad",
+        120,
+        pair=True,
+        chips=True,
+        **more,
+    )
+    return dict(zip(names + ["pack", "gains", "out0", "out1"], out)), found
+
+
+def join_pieces(pieces, by_rows, ways, **more):
+    columns = pieces[0].shape[1]
+    half = len(pieces) // 2
+    rows = pieces[0].shape[0] if not by_rows else sum(piece.shape[0] for piece in pieces[:half])
+    unit = math.gcd(*[piece.shape[0] for piece in pieces])
+    tile = max(t for t in range(16, 256 + 1, 16) if unit % t == 0)
+    counts = [piece.shape[0] // tile for piece in pieces]
+    starts = [sum(counts[:at]) for at in range(len(counts))]
+    steps = sum(counts)
 
     def source(at):
-        def index(p, i):
-            return (jnp.where(p == at, i, jnp.where(p < at, 0, steps - 1)), 0)
+        def index(i):
+            return (jnp.clip(i - starts[at], 0, counts[at] - 1), 0)
 
         return pl.BlockSpec((tile, columns), index)
 
-    def target(p, i):
-        at = (core_index() + p // 2) % 2 * 2 + p % 2
-        return (at * steps + i, 0) if by_rows else (i, at)
-
-    shape = (4 * rows, columns // ways) if by_rows else (rows, 4 * columns)
+    def target(i):
+        at = (i + core_index() * (steps // 2)) % steps
+        return (at, 0) if by_rows else (at % counts[0], at // counts[0])
+
+    shape = (2 * rows, columns // ways) if by_rows else (rows, len(pieces) * columns)
     out = (jax.ShapeDtypeStruct(shape, f32), pl.BlockSpec((tile, columns // ways), target))
     return call(
-        functools.partial(join_kernel, ways),
-        (4, steps),
-        [(quarter, source(at)) for at, quarter in enumerate(quarters)],
+        functools.partial(join_kernel, tuple(starts) + (steps,)),
+        (steps,),
+        [(piece, source(at)) for at, piece in enumerate(pieces)],
         [out] * ways,
         [],
-        "join_quarters",
-        10,
+        "join_pieces",
+        0.05,
         **more,
     )
 
@@ -1055,34 +1246,48 @@
 
 class Pipe:
     def __init__(self):
-        self.stages = [{}, {}, {}]
-        self.done = {}
-
-    def add(self, **chunks):
-        self.stages[0].update(chunks)
-
-    def host(self):
-        return PipeHost(*[list(stage.items()) for stage in self.stages])
-
-    def took(self, results):
-        inward, between, outward = self.stages
-        self.done.update({name: results[name] for name in outward})
-        self.stages = [{}, {name: results[name] for name in inward}, {name: results[name] for name in between}]
-
-
-def add_small(quarters, small):
-    columns = quarters[0].shape[1]
-    small = add_low(small, swap(small, "dp", 1)).reshape(4, -1, columns)
-    return [
-        jnp.concatenate([quarter, lax.dynamic_index_in_dim(small, core_index() * 2 + at, 0, False)], axis=0)
-        for at, quarter in enumerate(quarters)
-    ]
-
-
-def take_small(quarters, start):
-    parts = jnp.stack([quarter[start:] for quarter in quarters])
-    order = [((half + core_index()) % 2) * 2 + at for half in range(2) for at in range(2)]
-    return jnp.concatenate([lax.dynamic_index_in_dim(parts, pick, 0, False) for pick in order], axis=0).astype(f32)
+        self.queue, self.moving, self.done = [], [], {}
+
+    def enter(self, name, quarters):
+        self.queue += [[name + str(at), quarter, 0] for at, quarter in enumerate(quarters)]
+
+    def host(self, budget):
+        pieces = [(name, array, 0, array.shape[0], stage, 3 - stage) for name, array, stage in self.moving]
+        cuts, left = [], budget
+        while self.queue and left > 0:
+            name, array, start = self.queue[0]
+            unit = array.shape[0] // 4
+            units = min((array.shape[0] - start) // unit, left)
+            cuts.append((name, array, start, units))
+            left -= units
+            self.queue[0][2] += units * unit
+            if self.queue[0][2] == array.shape[0]:
+                self.queue.pop(0)
+        early = sum(units for _, _, _, units in cuts) // 2
+        for name, array, start, units in cuts:
+            unit = array.shape[0] // 4
+            first = min(units, early)
+            early -= first
+            for at, count, hops in ((start, first * unit, 2), (start + first * unit, (units - first) * unit, 1)):
+                if count > 0:
+                    pieces.append((name + "_" + str(at).zfill(4), array, at, count, 0, hops))
+        return PipeHost(pieces) if pieces else None
+
+    def took(self, host, results):
+        self.moving = []
+        for name, _, _, _, stage, hops in host.pieces:
+            if stage + hops == 3:
+                self.done[name] = results[name]
+            else:
+                self.moving.append((name, results[name], stage + hops))
+
+    def left(self):
+        groups = ({}, {}, {})
+        for name, array, stage in self.moving:
+            groups[stage][name] = array
+        for name, array, start in self.queue:
+            groups[0][name + "_" + str(start).zfill(4)] = array[start:]
+        return groups
 
 
 def normalize(values, gain):
@@ -1160,24 +1365,25 @@
     hosted = blocks == 4 and count == 2
     ids = iter(range(1, 100))
 
-    piped = hosted and lax.axis_size("dp") == 8
+    piped = hosted and lax.axis_size("dp") == 8 and not extra
     pipe = Pipe()
 
-    def enter(**chunks):
+    def enter(name, quarters):
         if piped:
-            pipe.add(**chunks)
+            pipe.enter(name, quarters)
 
     def tied(value, *deps):
         return lax.optimization_barrier((value,) + deps)[0]
 
-    def run(function, *args, hosts=(), middle=0, **more):
+    def run(function, *args, hosts=(), middle=0, budget=4, **more):
         if hosted:
-            moving = piped and any(pipe.stages)
+            window = pipe.host(budget) if piped else None
             out, found = function(
-                *args, hosts=list(hosts) + ([pipe.host()] if moving else []), middle=middle, unique=next(ids), **more
+                *args, hosts=list(hosts) + ([window] if window else []), middle=middle, unique=next(ids),
+                pipe_middle=3 if function is weight_grad else 2, **more
             )
-            if moving:
-                pipe.took(found[-1])
+            if window:
+                pipe.took(window, found[-1])
             return out, found[: len(hosts)]
         out, _ = function(*args, **more)
         return out, [
@@ -1224,109 +1430,111 @@
 
     def middle_grad(s, d_mid):
         back, unit = normalize_back(resid_mid[s], norm2_gain, d_mid)
-        return cotangent[s].astype(f32) + back, jnp.sum(d_mid * unit, axis=0)
+        return cotangent[s].astype(f32) + back, jnp.sum(d_mid * unit, axis=0, keepdims=True)
 
     flat_mid = [p for pieces in seq_mid for p in pieces]
     flat_cot = [p for pieces in cot_seq for p in pieces]
     grad_down, _ = run(weight_grad, [hidden], flat_cot)
-    enter(down0=grad_down[0])
+    enter("down", grad_down)
     backward, (d_mid,) = run(
         mlp_backward, 1, count, cot_seq[1], gate_low, up_low, w_gate, w_up, w_down, backward[:2],
         hosts=[ScatterHost(backward[2:])], middle=2, before=(grad_down[0],),
     )
     d_gate, d_up = backward[:2]
     first, gain2 = middle_grad(0, d_mid)
-    enter(down1=grad_down[-1])
     grad_gate, (first_seq,) = run(weight_grad, flat_mid, [d_gate], hosts=[GatherHost(first.astype(bf16))], middle=3)
-    enter(gate0=grad_gate[0])
+    enter("gate", grad_gate)
     grad_up, (d_mid,) = run(
         weight_grad, flat_mid, [d_up], hosts=[ScatterHost(backward[2:])], middle=2, before=(grad_gate[0],)
     )
     second, more_gain2 = middle_grad(1, d_mid)
-    gain2 = gain2 + more_gain2
-    enter(gate1=grad_gate[-1])
+    enter("up", grad_up)
     out, (second_seq,) = run(
         rec_backward, limits[0], 0, count, first_seq, seq_in[0], backward_params, saved[0], (),
-        hosts=[GatherHost(second.astype(bf16))], middle=3, before=(grad_up[0],),
-    )
-    sums, gain1 = out[2], jnp.sum(out[3], axis=0)
-    enter(up0=grad_up[0])
+        hosts=[GatherHost(second.astype(bf16))], middle=3, before=(grad_up[0],), budget=4,
+    )
+    sums, gain1 = out[2], out[3]
     out, (d_in,) = run(
         rec_backward, limits[1], 1, count, second_seq, seq_in[1], backward_params, saved[1], out[:2],
-        hosts=[ScatterHost(out[4:])], middle=2,
-    )
-    sums, gain1 = sums + out[2], gain1 + jnp.sum(out[3], axis=0)
+        hosts=[ScatterHost(out[4:])], middle=2, budget=4,
+    )
     d_both, d_gates = out[:2]
     input_grad = [(first + normalize_back(resid[0], norm1_gain, d_in)[0]).astype(bf16)]
-    enter(up1=grad_up[-1])
 
     flat_in = [p for pieces in seq_in for p in pieces]
     flat_resid = [p for pieces in (first_seq, second_seq) for p in pieces]
     grad_in, _ = run(weight_grad, flat_in, [d_both])
-    enter(in0=grad_in[0])
-    grad_out, (d_in,) = run(
-        weight_grad, mixed, flat_resid, False, hosts=[ScatterHost(out[4:])], middle=2, before=(grad_in[0],)
-    )
-    input_grad.append((second + normalize_back(resid[1], norm1_gain, d_in)[0]).astype(bf16))
-    input_grad = jnp.stack(input_grad)
-
-    gains = jnp.stack([gain1 / norm1_gain, gain2])
-    for bit in range(blocks.bit_length() - 1):
-        gains = gains + swap(gains, "mp", 1 << bit)
     conv = [part[2] for part in saved]
-    d_gates = d_gates.reshape(count, blocks, piece, -1)
-    width = d_gates.shape[-1] // 2
-    full = sum(jnp.einsum("rtd,rtc->dc", conv[s], d_gates[s], preferred_element_type=f32) for s in seqs)
-    full_ga = diagonal_blocks(full[:, :width], nblocks, true_width)
-    full_gi = diagonal_blocks(full[:, width:], nblocks, true_width)
-    vectors = jnp.sum(sums, axis=1)[:, :true_width]
-    decay_grad = vectors[0] * DECAY_EXP * jax.nn.sigmoid(-decay_param)
-    vectors = jnp.concatenate([decay_grad[None, :], vectors[1:]], axis=0)
-    small = jnp.concatenate(
-        [full_ga.reshape(-1), full_gi.reshape(-1), vectors.reshape(-1), gains.reshape(-1)]
-    ).astype(bf16)
-    used = small.shape[0]
-    unit = 4 * 16 * model // 4
-    small = jnp.pad(small, (0, -used % unit)).reshape(4, -1, model // 4)
     if piped:
 
-        def join(name, grad, before=(), by_rows=True, ways=1):
-            first, second = (pipe.done[name + at] for at in "01")
-            quarters = (first, second, swap(first, "dp", 1), swap(second, "dp", 1))
-            return join_quarters(quarters, by_rows, ways, grad[0].shape[0], before=before)[0], quarters
-
-        with_small = add_small(grad_out, small)
-        enter(in1=grad_in[-1], out0=with_small[0], out1=with_small[1])
-        last = TailHost(*[list(stage.items()) for stage in pipe.stages])
-        _, (found,) = call(
-            lambda: None, (1,), [], [], [], "sum_tail", 90, hosts=[last], before=(grad_out[0],), unique=next(ids)
+        def join(prefix, by_rows=True, ways=1):
+            mine = [pipe.done[name] for name in sorted(pipe.done) if name.startswith(prefix)]
+            return join_pieces(mine + [swap(piece, "dp", 1) for piece in mine], by_rows, ways)[0]
+
+        moving = pipe.left()
+        moving[0].update(in0=grad_in[0], in1=grad_in[1])
+        found, (d_in,) = last_grad(
+            mixed, flat_resid, conv, d_gates, (sums, out[2], gain1, out[3], gain2, more_gain2), moving, nblocks,
+            hosts=[ScatterHost(out[4:])], middle=4, unique=next(ids), before=(grad_in[0],),
         )
-        pipe.done.update(found)
-        totals_down, _ = join("down", grad_down)
-        totals_gate, _ = join("gate", grad_gate)
-        totals_up, _ = join("up", grad_up)
-        totals_in, _ = join("in", grad_in, ways=2)
-        totals_out, quarters = join("out", grad_out, by_rows=False)
-        small = take_small(quarters, grad_out[0].shape[0])
+        pipe.done.update({name: found[name] for name in found if name not in ("out0", "out1")})
+        pairs = [(2 * a + core, 2 * b + core) for a, b in ((1, 0), (2, 3)) for core in range(2)]
+        came = {name: lax.ppermute(found[name], "dp", pairs) for name in ("out0", "out1")}
+        totals_down, totals_gate, totals_up = (join(name) for name in ("down", "gate", "up"))
+        totals_in = join("in", ways=2)
+        came = dict(zip(came, lax.optimization_barrier((*came.values(), totals_gate, totals_up, totals_in[0]))))
+        for name in came:
+            found[name] = jnp.where(chip_is_inner(), found[name], came[name])
+        pipe.done.update(out0=found["out0"], out1=found["out1"])
+        totals_out = join("out", by_rows=False)
+        pack, other = found["pack"].astype(f32), swap(found["pack"], "dp", 1).astype(f32)
+        mine = core_index() == 0
+        pack = jnp.concatenate([jnp.where(mine, pack, other), jnp.where(mine, other, pack)], axis=0)
+        inner = true_width // nblocks
+        full_ga, full_gi = (
+            jnp.transpose(pack[at * inner : (at + 1) * inner].reshape(inner, nblocks, inner), (1, 0, 2)) for at in range(2)
+        )
+        vectors = pack[2 * inner : 2 * inner + 8]
+        gains = found["gains"][:2].astype(f32)
+        gains = gains + swap(gains, "dp", 1)
+        for bit in (1, 2):
+            gains = gains + swap(gains, "mp", bit)
     else:
-        small = lax.psum(small, "dp").astype(f32)
+        grad_out, _ = run(weight_grad, mixed, flat_resid, False, before=(grad_in[0],))
+        d_in = scatter(out[4:])
         totals_down, totals_gate, totals_up, totals_in, totals_out = (
             jnp.split(lax.psum(v[0], "dp").astype(f32), ways, axis=1)
             for v, ways in ((grad_down, 1), (grad_gate, 1), (grad_up, 1), (grad_in, 2), (grad_out, 1))
         )
+        d_gates = d_gates.reshape(count, blocks, piece, -1)
+        width = d_gates.shape[-1] // 2
+        full = sum(jnp.einsum("rtd,rtc->dc", conv[s], d_gates[s], preferred_element_type=f32) for s in seqs)
+        gains = jnp.stack([jnp.sum(gain1 + out[3], axis=0), (gain2 + more_gain2)[0]])
+        vectors = jnp.sum(sums + out[2], axis=1)[:, :true_width]
+        full_ga, full_gi, vectors, gains = lax.psum(
+            (
+                diagonal_blocks(full[:, :width], nblocks, true_width).astype(bf16),
+                diagonal_blocks(full[:, width:], nblocks, true_width).astype(bf16),
+                vectors.astype(bf16),
+                lax.psum(gains, "mp").astype(bf16),
+            ),
+            "dp",
+        )
+    input_grad.append((second + normalize_back(resid[1], norm1_gain, d_in)[0]).astype(bf16))
+    input_grad = jnp.stack(input_grad)
+    grad_gate_a_weight, grad_gate_i_weight, vectors, gains = (
+        v.astype(f32) for v in (full_ga, full_gi, vectors, gains)
+    )
+    gains = jnp.stack([gains[0] / norm1_gain, gains[1]])
+    vectors = jnp.concatenate(
+        [(vectors[0] * DECAY_EXP * jax.nn.sigmoid(-decay_param))[None, :], vectors[1:]], axis=0
+    )
     grad_w_out = totals_out[0][:true_width]
     grad_w_branch, grad_w_input = (v[:, :true_width] for v in totals_in)
     mlp_total = [
-        lax.psum_scatter(flat(tied(v, grad_out[0])), "mp", scatter_dimension=0, tiled=True) for v in mlp_part
+        lax.psum_scatter(flat(tied(v, grad_in[0])), "mp", scatter_dimension=0, tiled=True) for v in mlp_part
     ]
     block_out = jnp.stack([(resid_mid[s] + mlp_total[s].astype(f32)).astype(bf16) for s in seqs])
-
-    small = small.reshape(-1)
-    many, few = full_ga.size, vectors.size
-    grad_gate_a_weight = small[:many].reshape(full_ga.shape)
-    grad_gate_i_weight = small[many : 2 * many].reshape(full_gi.shape)
-    vectors = small[2 * many : 2 * many + few].reshape(8, true_width)
-    gains = small[2 * many + few : used].reshape(2, model)
 
     return (
         block_out,

time: 948 us -> 856 us (0.903)
  Pallas kernels: 741 us -> 653 us
    pallas_call x19 -> x18, Pallas kernels: 741 us -> 653 us  [call(): pl.pallas_call(body, out_shape=tuple((shape for shape, _ in outs)) + tupl...]
    ppermute x25 -> x32, starting transfers between devices: 18.5 us -> 25.4 us  [swap(): return lax.ppermute(value, axis, [(i, i ^ bit) for i in range(size)])]
    ppermute x25 -> x32, waiting for transfers between devices: 75.1 us -> 76.9 us  [swap(): return lax.ppermute(value, axis, [(i, i ^ bit) for i in range(size)])]
  transfers between devices with their start and end apart: 27 -> 36, of which waited for: 8 -> 9; matrix products, arithmetic and copies ran while one was open for 5% -> 4% of each run, Pallas kernels for 19% -> 19%
where the time goes in v4:
time: 856 us; the launch traced here: 846 us
  Pallas kernels  653 us (76%)
  waiting for transfers between devices  77.6 us (9%)
  other arithmetic  49.9 us (6%)
  starting transfers between devices  28.2 us (3%)
  local copies, waits for them, and re-layouts  22.2 us (3%)
  between operations  15.2 us (2%)
    pallas_call x18, Pallas kernels, call(): pl.pallas_call(body, out_shape=tuple((shape for shape, _ in outs)) + tupl...  653 us
    ppermute x32, waiting for transfers between devices, swap(): return lax.ppermute(value, axis, [(i, i ^ bit) for i in range(size)])  76.9 us
    ppermute x32, starting transfers between devices, swap(): return lax.ppermute(value, axis, [(i, i ^ bit) for i in range(size)])  25.4 us
  transfers between devices with their start and end apart: 36, of which 9 were waited for; matrix products, arithmetic and copies ran while one was open for 4% of the time, Pallas kernels for 19%

profile of v4, /device:TPU:9, one launch (start us, length us, event | category | flops | bytes accessed | tf_op | source)
XLA Modules:
  0.0 845.8 jit_solution(16806499416435330411)
XLA Ops:
  7.3 2.2 fusion.40
  9.5 1.4 fusion.34
  10.9 1.3 collective-permute-start.1
  12.2 1.2 collective-permute-start
  13.5 8.4 fusion.44.refs_9_.refs_14_
  24.9 10.2 %collective-permute-done.1.refs_3_.refs_8_.refs_2_ = bf16[256,2048]{1,0:T(8,128)(2,1)S(1)} collective-permute-done((bf16[256,2048]{1,0:T(8,128)(2,1)S(1)}, bf16[256,2048]{1,0:T(8,128)(2,1)S(1)}, u32[]{:S(2)}, u32[]{:S(2)}) %collective-permute-start.1) | collective-permute-done | bytes 1048608 | tf_op jit(solution)/shard_map/ppermute | solution.py:1215
  35.1 1.3 collective-permute-start.3
  36.4 1.3 collective-permute-start.2
  39.0 2.3 copy-done.25
  41.3 5.7 collective-permute-done.3.refs_5_.refs_10_.refs_4_
  47.0 1.1 collective-permute-done.2.refs_4_.refs_9_.refs_3_
  48.1 1.2 broadcast_in_dim.16.refs_0_
  49.3 41.2 %rec_forward.2 = (bf16[4,256,640]{2,1,0:T(8,128)(2,1)}, f32[4,256,640]{2,1,0:T(8,128)}, f32[4,256,640]{2,1,0:T(8,128)}, bf16[4,256,640]{2,1,0:T(8,128)(2,1)}, f3...) custom-call(s32[8,128]{1,0:T(8,128)} %broadcast_in_dim.16.refs_0_, ...), custom_call_target="tpu_custom_call" | custom-call | flops 21275000832 | bytes 65536 | tf_op jit(solution)/shard_map/rec_forward/pallas_call | solution.py:836
  90.6 1.2 broadcast_in_dim.21.refs_0_
  91.8 39.1 %rec_forward.3 = (bf16[4,256,640]{2,1,0:T(8,128)(2,1)}, f32[4,256,640]{2,1,0:T(8,128)}, f32[4,256,640]{2,1,0:T(8,128)}, bf16[4,256,640]{2,1,0:T(8,128)(2,1)}, f3...) custom-call(s32[8,128]{1,0:T(8,128)} %broadcast_in_dim.21.refs_0_, ...), custom_call_target="tpu_custom_call" | custom-call | flops 21275000832 | bytes 65536 | tf_op jit(solution)/shard_map/rec_forward/pallas_call | solution.py:836
  131.0 2.2 multiply_reduce_fusion.5
  133.9 1.3 collective-permute-start.4
  135.2 19.1 %collective-permute-done.5.refs_2_ = bf16[256,2048]{1,0:T(8,128)(2,1)S(1)} collective-permute-done((bf16[256,2048]{1,0:T(8,128)(2,1)S(1)}, bf16[256,2048]{1,0:T(8,128)(2,1)S(1)}, u32[]{:S(2)}, u32[]{:S(2)}) %collective-permute-start.5) | collective-permute-done | bytes 1048608 | tf_op jit(solution)/shard_map/ppermute | solution.py:1215
  156.1 10.5 %collective-permute-done.7.refs_4_ = bf16[128,2048]{1,0:T(8,128)(2,1)S(1)} collective-permute-done((bf16[128,2048]{1,0:T(8,128)(2,1)S(1)}, bf16[128,2048]{1,0:T(8,128)(2,1)S(1)}, u32[]{:S(2)}, u32[]{:S(2)}) %collective-permute-start.7) | collective-permute-done | bytes 524320 | tf_op jit(solution)/shard_map/ppermute | solution.py:1215
  167.5 36.1 %mlp_forward.2 = (bf16[8,256,1536]{2,1,0:T(8,128)(2,1)}, bf16[8,256,1536]{2,1,0:T(8,128)(2,1)}, bf16[8,256,1536]{2,1,0:T(8,128)(2,1)}, bf16[4,256,2048]{2,1,0:T(...) custom-call(bf16[256,2048]{1,0:T(8,128)(2,1)} %copy-done.26, bf16[256,2048]{1,0:T(8,128)(2,1)} %copy-done.47, ...), custom_call_target="tpu_custom_call" | custom-call | flops 17250000896 | bytes 65536 | tf_op jit(solution)/shard_map/mlp_forward/pallas_call | solution.py:836
  203.6 2.2 multiply_reduce_fusion.4
  206.1 1.4 collective-permute-start.9
  207.6 19.4 %collective-permute-done.9.refs_2_.refs_7_ = bf16[256,2048]{1,0:T(8,128)(2,1)S(1)} collective-permute-done((bf16[256,2048]{1,0:T(8,128)(2,1)S(1)}, bf16[256,2048]{1,0:T(8,128)(2,1)S(1)}, u32[]{:S(2)}, u32[]{:S(2)}) %collective-permute-start.9) | collective-permute-done | bytes 1048608 | tf_op jit(solution)/shard_map/ppermute | solution.py:1215
  227.1 1.3 collective-permute-start.11
  228.5 0.9 copy-done.49
  230.3 1.6 slice_bitcast_fusion.1
  231.9 9.3 %collective-permute-done.11.refs_4_.refs_9_ = bf16[128,2048]{1,0:T(8,128)(2,1)S(1)} collective-permute-done((bf16[128,2048]{1,0:T(8,128)(2,1)S(1)}, bf16[128,2048]{1,0:T(8,128)(2,1)S(1)}, u32[]{:S(2)}, u32[]{:S(2)}) %collective-permute-start.11) | collective-permute-done | bytes 524320 | tf_op jit(solution)/shard_map/ppermute | solution.py:1215
  242.2 35.0 %mlp_forward.3 = (bf16[8,256,1536]{2,1,0:T(8,128)(2,1)}, bf16[8,256,1536]{2,1,0:T(8,128)(2,1)}, bf16[8,256,1536]{2,1,0:T(8,128)(2,1)}, bf16[4,256,2048]{2,1,0:T(...) custom-call(bf16[256,2048]{1,0:T(8,128)(2,1)} %copy-done.27, ...), custom_call_target="tpu_custom_call", output_to_operand_aliasing={{0}: (8, {}), {1}: (9, {}), {2}: (10, {})} | custom-call | flops 17250000896 | bytes 65536 | tf_op jit(solution)/shard_map/mlp_forward/pallas_call | solution.py:836
  277.2 36.9 %mlp_backward.2 = (bf16[8,256,1536]{2,1,0:T(8,128)(2,1)}, bf16[8,256,1536]{2,1,0:T(8,128)(2,1)}, bf16[256,2048]{1,0:T(8,128)(2,1)}, bf16[256,2048]{1,0:T(8,128)(...) custom-call(bf16[256,2048]{1,0:T(8,128)(2,1)} %get-tuple-element.327, ...), custom_call_target="tpu_custom_call" | custom-call | flops 18400000000 | bytes 65536 | tf_op jit(solution)/shard_map/mlp_backward/pallas_call | solution.py:836
  314.1 29.3 %weight_grad.4 = (bf16[384,2048]{1,0:T(8,128)(2,1)}, bf16[384,2048]{1,0:T(8,128)(2,1)}) custom-call(bf16[2048,1536]{1,0:T(8,128)(2,1)} %bitcast.81, bf16[256,2048]{1,0:T(8,128)(2,1)} %get-tuple-element.327.refs_11_.refs_0_.refs_1_, bf16[256,2048]{1,0:T(8,128)(2,1)} %get-tuple-element.183.refs_1_.refs_2_, ...), custom_call_target="tpu_custom_call" | custom-call | flops 11500000256 | bytes 65536 | tf_op jit(solution)/shard_map/weight_grad/pallas_call | solution.py:836
  343.4 45.4 %mlp_backward.3 = (bf16[8,256,1536]{2,1,0:T(8,128)(2,1)}, bf16[8,256,1536]{2,1,0:T(8,128)(2,1)}, bf16[256,2048]{1,0:T(8,128)(2,1)}, bf16[256,2048]{1,0:T(8,128)(...) custom-call(bf16[256,2048]{1,0:T(8,128)(2,1)} %get-tuple-element.326, ...), custom_call_target="tpu_custom_call", output_to_operand_aliasing={{0}: (10, {}), {1}: (11, {})} | custom-call | flops 18400000000 | bytes 65536 | tf_op jit(solution)/shard_map/mlp_backward/pallas_call | solution.py:836
  388.8 3.2 multiply_reduce_fusion.1
  392.0 2.8 fusion.60
  394.8 41.0 %weight_grad.5 = (bf16[512,1536]{1,0:T(8,128)(2,1)}, bf16[512,1536]{1,0:T(8,128)(2,1)}, bf16[256,2048]{1,0:T(8,128)(2,1)}, bf16[256,2048]{1,0:T(8,128)(2,1)}, bf...) custom-call(bf16[256,2048]{1,0:T(8,128)(2,1)} %copy-done.26, ...), custom_call_target="tpu_custom_call" | custom-call | flops 11500000256 | bytes 65536 | tf_op jit(solution)/shard_map/weight_grad/pallas_call | solution.py:836
  435.9 44.0 %weight_grad.6 = (bf16[512,1536]{1,0:T(8,128)(2,1)}, bf16[512,1536]{1,0:T(8,128)(2,1)}, bf16[256,2048]{1,0:T(8,128)(2,1)}, bf16[256,2048]{1,0:T(8,128)(2,1)}, bf...) custom-call(bf16[256,2048]{1,0:T(8,128)(2,1)} %copy-done.26, ...), custom_call_target="tpu_custom_call" | custom-call | flops 11500000256 | bytes 65536 | tf_op jit(solution)/shard_map/weight_grad/pallas_call | solution.py:836
  479.9 3.2 multiply_reduce_fusion
  483.1 2.8 fusion.59
  485.9 51.2 %rec_backward.2 = (bf16[8,256,1280]{2,1,0:T(8,128)(2,1)}, bf16[8,256,1280]{2,1,0:T(8,128)(2,1)}, f32[8,8,640]{2,1,0:T(8,128)}, f32[8,2048]{1,0:T(8,128)}, bf16[2...) custom-call(s32[8,128]{1,0:T(8,128)} %broadcast_in_dim.16.refs_0_, ...), custom_call_target="tpu_custom_call" | custom-call | flops 24725000192 | bytes 65536 | tf_op jit(solution)/shard_map/rec_backward/pallas_call | solution.py:836
  537.1 48.6 %rec_backward.3 = (bf16[8,256,1280]{2,1,0:T(8,128)(2,1)}, bf16[8,256,1280]{2,1,0:T(8,128)(2,1)}, f32[8,8,640]{2,1,0:T(8,128)}, f32[8,2048]{1,0:T(8,128)}, bf16[2...) custom-call(s32[8,128]{1,0:T(8,128)} %broadcast_in_dim.21.refs_0_, ...), custom_call_target="tpu_custom_call", output_to_operand_aliasing={{0}: (22, {}), {1}: (23, {})} | custom-call | flops 24725000192 | bytes 65536 | tf_op jit(solution)/shard_map/rec_backward/pallas_call | solution.py:836
  585.8 41.7 %weight_grad.7 = (bf16[512,1280]{1,0:T(8,128)(2,1)}, bf16[512,1280]{1,0:T(8,128)(2,1)}, bf16[256,1536]{1,0:T(8,128)(2,1)}, bf16[256,1536]{1,0:T(8,128)(2,1)}, bf...) custom-call(bf16[256,2048]{1,0:T(8,128)(2,1)} %copy-done.28, bf16[256,2048]{1,0:T(8,128)(2,1)} %copy-done.45, ...), custom_call_target="tpu_custom_call" | custom-call | flops 11500000256 | bytes 65536 | tf_op jit(solution)/shard_map/weight_grad/pallas_call | solution.py:836
  628.3 118.4 %last_grad.1 = (bf16[512,1280]{1,0:T(8,128)(2,1)}, bf16[512,1280]{1,0:T(8,128)(2,1)}, bf16[256,1536]{1,0:T(8,128)(2,1)}, bf16[256,1536]{1,0:T(8,128)(2,1)}, bf16...) custom-call(bf16[1024,640]{1,0:T(8,128)(2,1)} %bitcast.86, ...), custom_call_target="tpu_custom_call" | custom-call | flops 69000003584 | bytes 65536 | tf_op jit(solution)/shard_map/last_grad/pallas_call | solution.py:836
  747.4 5.0 collective-permute-start.12
  754.0 1.1 collective-permute-start.13
  757.3 1.1 collective-permute-start.14
  759.1 1.4 collective-permute-start.26
  760.9 1.3 collective-permute-start.22
  762.3 4.1 fusion.35
  767.5 0.9 copy-done.37
  768.6 3.6 fusion.55
  772.3 1.3 collective-permute-start.18
  773.7 1.3 collective-permute-start.19
  775.0 1.5 pad_maximum_fusion.1
  778.6 8.4 join_pieces.6
  787.1 8.4 join_pieces.7
  797.0 8.8 %join_pieces.5 = (f32[2048,640]{1,0:T(8,128)}, f32[2048,640]{1,0:T(8,128)}) custom-call(bf16[512,1280]{1,0:T(8,128)(2,1)} %get-tuple-element.280.refs_0_, bf16[512,1280]{1,0:T(8,128)(2,1)} %get-tuple-element.281.refs_1_, bf16[512,1280]{1,0:T(8,128)(2,1)} %copy-done.23, bf16[512,1280]{1,0:T(8,128)(2,1)} %copy-done.24), custom_call_target="tpu_custom_call" | custom-call | flops 28750000 | bytes 65536 | tf_op jit(solution)/shard_map/join_pieces/pallas_call | solution.py:836
  806.4 1.2 broadcast_select_fusion.1.refs_0_
  807.6 1.4 broadcast_select_fusion.refs_1_
  810.8 1.0 copy.47
  812.3 1.0 copy.48
  814.5 8.5 join_pieces.9
  822.9 10.7 %join_pieces.8 = f32[640,2048]{1,0:T(8,128)} custom-call(bf16[640,512]{1,0:T(8,128)(2,1)} %copy-done.21, bf16[640,512]{1,0:T(8,128)(2,1)} %copy-done.22, bf16[640,512]{1,0:T(8,128)(2,1)} %collective-permute-done.28.refs_2_, bf16[640,512]{1,0:T(8,128)(2,1)} %collective-permute-done.29.refs_3_), custom_call_target="tpu_custom_call" | custom-call | flops 28750000 | bytes 65536 | tf_op jit(solution)/shard_map/join_pieces/pallas_call | solution.py:836
  833.6 1.5 fusion.53
  835.1 2.1 fusion.54
  837.3 1.5 pad_maximum_fusion
  (227 shorter events, 25.6 us)
Async XLA Ops:
  7.2 826.4 %reduce-scatter.3.cloned.1.call-start = ((), (), s32[]{:S(2)}) async-start(), calls=%async_computation.2 | async-start | bytes 5242880 | tf_op jit(solution)/shard_map/reduce_scatter | solution.py:1535
  10.9 24.2 %copy-start.28 = (bf16[256,2048]{1,0:T(8,128)(2,1)}, bf16[256,2048]{1,0:T(8,128)(2,1)S(1)}, u32[]{:S(2)}) copy-start(bf16[256,2048]{1,0:T(8,128)(2,1)S(1)} %get-tuple-element.324.refs_1_.refs_6_.refs_0_) | copy-start | bytes 3145732
  10.9 11.1 %copy-start.53 = (f32[640]{0:T(1024)S(1)}, f32[640]{0:T(1024)}, u32[]{:S(2)}) copy-start(f32[640]{0:T(1024)} %param.28) | copy-start | bytes 7684
  10.9 11.7 %copy-start.59 = (f32[640]{0:T(1024)S(1)}, f32[640]{0:T(1024)}, u32[]{:S(2)}) copy-start(f32[640]{0:T(1024)} %param.23) | copy-start | bytes 7684
  10.9 12.2 %copy-start.60 = (f32[640]{0:T(1024)S(1)}, f32[640]{0:T(1024)}, u32[]{:S(2)}) copy-start(f32[640]{0:T(1024)} %param.25) | copy-start | bytes 7684
  10.9 12.8 %copy-start.61 = (f32[640]{0:T(1024)S(1)}, f32[640]{0:T(1024)}, u32[]{:S(2)}) copy-start(f32[640]{0:T(1024)} %param.27) | copy-start | bytes 7684
  10.9 13.4 %copy-start.62 = (s32[2]{0:T(128)S(1)}, s32[2]{0:T(128)}, u32[]{:S(2)}) copy-start(s32[2]{0:T(128)} %param.34) | copy-start | bytes 28
  10.9 24.1 %collective-permute-start.1 = (bf16[256,2048]{1,0:T(8,128)(2,1)S(1)}, bf16[256,2048]{1,0:T(8,128)(2,1)S(1)}, u32[]{:S(2)}, u32[]{:S(2)}) collective-permute-start(bf16[256,2048]{1,0:T(8,128)(2,1)S(1)} %get-tuple-element.324.refs_1_.refs_6_.refs_0_), channel_id=1, source_target_pairs={{0,2},{1,3},{2,0},{3,1},{4,6},{5,7},{6,4},{7,5},{8,10},{9,11},{10,... | collective-permute-start | bytes 3145736 | tf_op jit(solution)/shard_map/ppermute | solution.py:1215
  12.2 24.1 %collective-permute-start = (bf16[256,2048]{1,0:T(8,128)(2,1)S(1)}, bf16[256,2048]{1,0:T(8,128)(2,1)S(1)}, u32[]{:S(2)}, u32[]{:S(2)}) collective-permute-start(bf16[256,2048]{1,0:T(8,128)(2,1)S(1)} %get-tuple-element.324.refs_1_.refs_6_.refs_0_), channel_id=1, source_target_pairs={{0,1},{1,0},{2,3},{3,2},{4,5},{5,4},{6,7},{7,6},{8,9},{9,8},{10,11... | collective-permute-start | bytes 3145736 | tf_op jit(solution)/shard_map/ppermute | solution.py:1215
  13.5 24.2 %copy-start.19 = (bf16[2048,640]{1,0:T(8,128)(2,1)S(1)}, bf16[2048,640]{1,0:T(8,128)(2,1)}, u32[]{:S(2)}) copy-start(bf16[2048,640]{1,0:T(8,128)(2,1)} %param.20) | copy-start | bytes 7864324
  35.1 11.9 %collective-permute-start.3 = (bf16[128,2048]{1,0:T(8,128)(2,1)S(1)}, bf16[128,2048]{1,0:T(8,128)(2,1)S(1)}, u32[]{:S(2)}, u32[]{:S(2)}) collective-permute-start(bf16[128,2048]{1,0:T(8,128)(2,1)S(1)} %slice.139), channel_id=1, source_target_pairs={{0,1},{1,0},{2,3},{3,2},{4,5},{5,4},{6,7},{7,6},{8,9},{9,8},{10,11... | collective-permute-start | bytes 1572872 | tf_op jit(solution)/shard_map/ppermute | solution.py:1215
  36.4 11.7 %collective-permute-start.2 = (bf16[128,2048]{1,0:T(8,128)(2,1)S(1)}, bf16[128,2048]{1,0:T(8,128)(2,1)S(1)}, u32[]{:S(2)}, u32[]{:S(2)}) collective-permute-start(bf16[128,2048]{1,0:T(8,128)(2,1)S(1)} %slice.138), channel_id=1, source_target_pairs={{0,2},{1,3},{2,0},{3,1},{4,6},{5,7},{6,4},{7,5},{8,10},{9,11},{10,... | collective-permute-start | bytes 1572872 | tf_op jit(solution)/shard_map/ppermute | solution.py:1215
  91.8 39.2 %copy-start.30 = (bf16[256,2048]{1,0:T(8,128)(2,1)S(1)}, bf16[256,2048]{1,0:T(8,128)(2,1)}, u32[]{:S(2)}) copy-start(bf16[256,2048]{1,0:T(8,128)(2,1)} %get-tuple-element.160) | copy-start | bytes 3145732
  133.2 258.8 %copy-start = (f32[256,2048]{1,0:T(8,128)}, f32[256,2048]{1,0:T(8,128)S(1)}, u32[]{:S(2)}) copy-start(f32[256,2048]{1,0:T(8,128)S(1)} %get-tuple-element.321) | copy-start | bytes 6291460
  133.5 33.9 %copy-start.26 = (bf16[256,2048]{1,0:T(8,128)(2,1)}, bf16[256,2048]{1,0:T(8,128)(2,1)S(1)}, u32[]{:S(2)}) copy-start(bf16[256,2048]{1,0:T(8,128)(2,1)S(1)} %multiply_convert_fusion.1.refs_0_) | copy-start | bytes 3145732
  133.5 20.8 %collective-permute-start.5 = (bf16[256,2048]{1,0:T(8,128)(2,1)S(1)}, bf16[256,2048]{1,0:T(8,128)(2,1)S(1)}, u32[]{:S(2)}, u32[]{:S(2)}) collective-permute-start(bf16[256,2048]{1,0:T(8,128)(2,1)S(1)} %multiply_convert_fusion.1.refs_0_), channel_id=1, source_target_pairs={{0,2},{1,3},{2,0},{3,1},{4,6},{5,7},{6,4},{7,5},{8,10},{9,11},{10,... | collective-permute-start | bytes 3145736 | tf_op jit(solution)/shard_map/ppermute | solution.py:1215
  133.9 21.4 %collective-permute-start.4 = (bf16[256,2048]{1,0:T(8,128)(2,1)S(1)}, bf16[256,2048]{1,0:T(8,128)(2,1)S(1)}, u32[]{:S(2)}, u32[]{:S(2)}) collective-permute-start(bf16[256,2048]{1,0:T(8,128)(2,1)S(1)} %multiply_convert_fusion.1.refs_0_), channel_id=1, source_target_pairs={{0,1},{1,0},{2,3},{3,2},{4,5},{5,4},{6,7},{7,6},{8,9},{9,8},{10,11... | collective-permute-start | bytes 3145736 | tf_op jit(solution)/shard_map/ppermute | solution.py:1215
  154.3 12.2 %collective-permute-start.7 = (bf16[128,2048]{1,0:T(8,128)(2,1)S(1)}, bf16[128,2048]{1,0:T(8,128)(2,1)S(1)}, u32[]{:S(2)}, u32[]{:S(2)}) collective-permute-start(bf16[128,2048]{1,0:T(8,128)(2,1)S(1)} %slice.141), channel_id=1, source_target_pairs={{0,1},{1,0},{2,3},{3,2},{4,5},{5,4},{6,7},{7,6},{8,9},{9,8},{10,11... | collective-permute-start | bytes 1572872 | tf_op jit(solution)/shard_map/ppermute | solution.py:1215
  155.3 11.3 %copy-start.47 = (bf16[256,2048]{1,0:T(8,128)(2,1)}, bf16[256,2048]{1,0:T(8,128)(2,1)S(1)}, u32[]{:S(2)}) copy-start(bf16[256,2048]{1,0:T(8,128)(2,1)S(1)} %collective-permute-done.4.refs_1_) | copy-start | bytes 3145732
  155.3 11.3 %collective-permute-start.6 = (bf16[128,2048]{1,0:T(8,128)(2,1)S(1)}, bf16[128,2048]{1,0:T(8,128)(2,1)S(1)}, u32[]{:S(2)}, u32[]{:S(2)}) collective-permute-start(bf16[128,2048]{1,0:T(8,128)(2,1)S(1)} %slice.140), channel_id=1, source_target_pairs={{0,2},{1,3},{2,0},{3,1},{4,6},{5,7},{6,4},{7,5},{8,10},{9,11},{10,... | collective-permute-start | bytes 1572872 | tf_op jit(solution)/shard_map/ppermute | solution.py:1215
  167.5 36.1 %copy-start.29 = (bf16[256,2048]{1,0:T(8,128)(2,1)S(1)}, bf16[256,2048]{1,0:T(8,128)(2,1)}, u32[]{:S(2)}) copy-start(bf16[256,2048]{1,0:T(8,128)(2,1)} %get-tuple-element.177) | copy-start | bytes 3145732
  205.8 277.3 %copy-start.2 = (f32[256,2048]{1,0:T(8,128)}, f32[256,2048]{1,0:T(8,128)S(1)}, u32[]{:S(2)}) copy-start(f32[256,2048]{1,0:T(8,128)S(1)} %get-tuple-element.319) | copy-start | bytes 6291460
  205.9 24.4 %copy-start.5 = (bf16[2,256,2048]{2,1,0:T(8,128)(2,1)S(1)}, bf16[2,256,2048]{2,1,0:T(8,128)(2,1)}, u32[]{:S(2)}) copy-start(bf16[2,256,2048]{2,1,0:T(8,128)(2,1)} %param.35) | copy-start | bytes 6291460
  206.1 25.8 %copy-start.27 = (bf16[256,2048]{1,0:T(8,128)(2,1)}, bf16[256,2048]{1,0:T(8,128)(2,1)S(1)}, u32[]{:S(2)}) copy-start(bf16[256,2048]{1,0:T(8,128)(2,1)S(1)} %multiply_convert_fusion.refs_0_.refs_5_) | copy-start | bytes 3145732
  206.1 20.9 %collective-permute-start.9 = (bf16[256,2048]{1,0:T(8,128)(2,1)S(1)}, bf16[256,2048]{1,0:T(8,128)(2,1)S(1)}, u32[]{:S(2)}, u32[]{:S(2)}) collective-permute-start(bf16[256,2048]{1,0:T(8,128)(2,1)S(1)} %multiply_convert_fusion.refs_0_.refs_5_), channel_id=1, source_target_pairs={{0,2},{1,3},{2,0},{3,1},{4,6},{5,7},{6,4},{7,5},{8,10},{9,11},{10,... | collective-permute-start | bytes 3145736 | tf_op jit(solution)/shard_map/ppermute | solution.py:1215
  207.6 20.9 %collective-permute-start.8 = (bf16[256,2048]{1,0:T(8,128)(2,1)S(1)}, bf16[256,2048]{1,0:T(8,128)(2,1)S(1)}, u32[]{:S(2)}, u32[]{:S(2)}) collective-permute-start(bf16[256,2048]{1,0:T(8,128)(2,1)S(1)} %multiply_convert_fusion.refs_0_.refs_5_), channel_id=1, source_target_pairs={{0,1},{1,0},{2,3},{3,2},{4,5},{5,4},{6,7},{7,6},{8,9},{9,8},{10,11... | collective-permute-start | bytes 3145736 | tf_op jit(solution)/shard_map/ppermute | solution.py:1215
  227.1 14.1 %collective-permute-start.11 = (bf16[128,2048]{1,0:T(8,128)(2,1)S(1)}, bf16[128,2048]{1,0:T(8,128)(2,1)S(1)}, u32[]{:S(2)}, u32[]{:S(2)}) collective-permute-start(bf16[128,2048]{1,0:T(8,128)(2,1)S(1)} %slice.143), channel_id=1, source_target_pairs={{0,1},{1,0},{2,3},{3,2},{4,5},{5,4},{6,7},{7,6},{8,9},{9,8},{10,11... | collective-permute-start | bytes 1572872 | tf_op jit(solution)/shard_map/ppermute | solution.py:1215
  229.4 11.8 %collective-permute-start.10 = (bf16[128,2048]{1,0:T(8,128)(2,1)S(1)}, bf16[128,2048]{1,0:T(8,128)(2,1)S(1)}, u32[]{:S(2)}, u32[]{:S(2)}) collective-permute-start(bf16[128,2048]{1,0:T(8,128)(2,1)S(1)} %slice.142), channel_id=1, source_target_pairs={{0,2},{1,3},{2,0},{3,1},{4,6},{5,7},{6,4},{7,5},{8,10},{9,11},{10,... | collective-permute-start | bytes 1572872 | tf_op jit(solution)/shard_map/ppermute | solution.py:1215
  343.3 45.4 %copy-start.9 = (bf16[256,2048]{1,0:T(8,128)(2,1)S(1)}, bf16[256,2048]{1,0:T(8,128)(2,1)}, u32[]{:S(2)}) copy-start(bf16[256,2048]{1,0:T(8,128)(2,1)} %get-tuple-element.208) | copy-start | bytes 3145732
  435.9 44.0 %copy-start.8 = (bf16[256,2048]{1,0:T(8,128)(2,1)S(1)}, bf16[256,2048]{1,0:T(8,128)(2,1)}, u32[]{:S(2)}) copy-start(bf16[256,2048]{1,0:T(8,128)(2,1)} %get-tuple-element.201) | copy-start | bytes 3145732
  627.5 207.7 %reduce-scatter.5.cloned.1.call-start = ((), (), s32[]{:S(2)}) async-start(), calls=%async_computation.3 | async-start | bytes 5242880 | tf_op jit(solution)/shard_map/reduce_scatter | solution.py:1535
  628.2 134.0 %copy-start.4 = (bf16[2,256,2048]{2,1,0:T(8,128)(2,1)S(1)}, bf16[2,256,2048]{2,1,0:T(8,128)(2,1)}, u32[]{:S(2)}) copy-start(bf16[2,256,2048]{2,1,0:T(8,128)(2,1)} %param.18) | copy-start | bytes 6291460
  628.2 134.0 %copy-start.14 = (bf16[256,2048]{1,0:T(8,128)(2,1)S(1)}, bf16[256,2048]{1,0:T(8,128)(2,1)}, u32[]{:S(2)}) copy-start(bf16[256,2048]{1,0:T(8,128)(2,1)} %get-tuple-element.259) | copy-start | bytes 3145732
  628.2 134.0 %copy-start.52 = (f32[2048]{0:T(1024)S(1)}, f32[2048]{0:T(1024)}, u32[]{:S(2)}) copy-start(f32[2048]{0:T(1024)} %param.19) | copy-start | bytes 24580
  628.3 134.0 %copy-start.56 = (f32[256]{0:T(256)S(1)}, f32[256]{0:T(256)}, u32[]{:S(2)}) copy-start(f32[256]{0:T(256)} %copy-done.55) | copy-start | bytes 3076
  628.3 134.0 %copy-start.58 = (f32[256]{0:T(256)S(1)}, f32[256]{0:T(256)}, u32[]{:S(2)}) copy-start(f32[256]{0:T(256)} %copy-done.57) | copy-start | bytes 3076
  747.4 5.8 collective-permute-start.12
  754.0 3.3 collective-permute-start.13
  757.3 3.6 collective-permute-start.14
  759.1 7.3 collective-permute-start.26
  760.4 6.1 collective-permute-start.27
  760.4 6.6 collective-permute-start.24
  760.9 6.2 collective-permute-start.25
  760.9 6.6 collective-permute-start.22
  762.2 6.4 copy-start.6
  762.2 6.4 copy-start.7
  762.3 6.4 copy-start.15
  762.3 6.3 copy-start.16
  766.4 5.9 collective-permute-start.23
  766.5 7.1 collective-permute-start.20
  767.0 9.5 %collective-permute-start.21 = (bf16[256,1536]{1,0:T(8,128)(2,1)}, bf16[256,1536]{1,0:T(8,128)(2,1)S(1)}, u32[]{:S(2)}, u32[]{:S(2)}) collective-permute-start(bf16[256,1536]{1,0:T(8,128)(2,1)} %get-tuple-element.288.refs_1_), channel_id=1, source_target_pairs={{0,4},{4,0},{8,12},{12,8},{16,20},{20,16},{24,28},{28,24},{1,5},{5... | collective-permute-start | bytes 2359304 | tf_op jit(solution)/shard_map/ppermute | solution.py:1215
  767.1 28.4 %collective-permute-start.15 = (bf16[512,1280]{1,0:T(8,128)(2,1)}, bf16[512,1280]{1,0:T(8,128)(2,1)S(1)}, u32[]{:S(2)}, u32[]{:S(2)}) collective-permute-start(bf16[512,1280]{1,0:T(8,128)(2,1)} %get-tuple-element.280.refs_0_), channel_id=1, source_target_pairs={{0,4},{4,0},{8,12},{12,8},{16,20},{20,16},{24,28},{28,24},{1,5},{5... | collective-permute-start | bytes 3932168 | tf_op jit(solution)/shard_map/ppermute | solution.py:1215
  768.4 27.5 %collective-permute-start.16 = (bf16[512,1280]{1,0:T(8,128)(2,1)}, bf16[512,1280]{1,0:T(8,128)(2,1)S(1)}, u32[]{:S(2)}, u32[]{:S(2)}) collective-permute-start(bf16[512,1280]{1,0:T(8,128)(2,1)} %get-tuple-element.281.refs_1_), channel_id=1, source_target_pairs={{0,4},{4,0},{8,12},{12,8},{16,20},{20,16},{24,28},{28,24},{1,5},{5... | collective-permute-start | bytes 3932168 | tf_op jit(solution)/shard_map/ppermute | solution.py:1215
  772.3 33.5 %collective-permute-start.18 = (bf16[640,512]{1,0:T(8,128)(2,1)}, bf16[640,512]{1,0:T(8,128)(2,1)S(1)}, u32[]{:S(2)}, u32[]{:S(2)}) collective-permute-start(bf16[640,512]{1,0:T(8,128)(2,1)} %get-tuple-element.285), channel_id=1, source_target_pairs={{8,0},{12,4},{16,24},{20,28},{9,1},{13,5},{17,25},{21,29},{10,2},{... | collective-permute-start | bytes 1966088 | tf_op jit(solution)/shard_map/ppermute | solution.py:1482
  773.7 32.5 %collective-permute-start.19 = (bf16[640,512]{1,0:T(8,128)(2,1)}, bf16[640,512]{1,0:T(8,128)(2,1)S(1)}, u32[]{:S(2)}, u32[]{:S(2)}) collective-permute-start(bf16[640,512]{1,0:T(8,128)(2,1)} %get-tuple-element.286), channel_id=1, source_target_pairs={{8,0},{12,4},{16,24},{20,28},{9,1},{13,5},{17,25},{21,29},{10,2},{... | collective-permute-start | bytes 1966088 | tf_op jit(solution)/shard_map/ppermute | solution.py:1482
  776.6 32.8 %collective-permute-start.32 = (bf16[192,2048]{1,0:T(8,128)(2,1)S(1)}, bf16[192,2048]{1,0:T(8,128)(2,1)S(1)}, u32[]{:S(2)}, u32[]{:S(2)}) collective-permute-start(bf16[192,2048]{1,0:T(8,128)(2,1)S(1)} %copy-done.31), channel_id=1, source_target_pairs={{0,4},{4,0},{8,12},{12,8},{16,20},{20,16},{24,28},{28,24},{1,5},{5... | collective-permute-start | bytes 2359304 | tf_op jit(solution)/shard_map/ppermute | solution.py:1215
  795.5 18.9 %collective-permute-start.33 = (bf16[192,2048]{1,0:T(8,128)(2,1)}, bf16[192,2048]{1,0:T(8,128)(2,1)}, u32[]{:S(2)}, u32[]{:S(2)}) collective-permute-start(bf16[192,2048]{1,0:T(8,128)(2,1)} %get-tuple-element.300.refs_3_), channel_id=1, source_target_pairs={{0,4},{4,0},{8,12},{12,8},{16,20},{20,16},{24,28},{28,24},{1,5},{5... | collective-permute-start | bytes 2359304 | tf_op jit(solution)/shard_map/ppermute | solution.py:1215
  795.9 10.3 %copy-start.50 = (bf16[176,640]{1,0:T(8,128)(2,1)S(1)}, bf16[176,640]{1,0:T(8,128)(2,1)}, u32[]{:S(2)}) copy-start(bf16[176,640]{1,0:T(8,128)(2,1)} %get-tuple-element.284) | copy-start | bytes 675844
  795.9 18.5 %collective-permute-start.30 = (bf16[192,2048]{1,0:T(8,128)(2,1)}, bf16[192,2048]{1,0:T(8,128)(2,1)}, u32[]{:S(2)}, u32[]{:S(2)}) collective-permute-start(bf16[192,2048]{1,0:T(8,128)(2,1)} %get-tuple-element.297.refs_0_), channel_id=1, source_target_pairs={{0,4},{4,0},{8,12},{12,8},{16,20},{20,16},{24,28},{28,24},{1,5},{5... | collective-permute-start | bytes 2359304 | tf_op jit(solution)/shard_map/ppermute | solution.py:1215
  805.8 8.6 %collective-permute-start.31 = (bf16[192,2048]{1,0:T(8,128)(2,1)}, bf16[192,2048]{1,0:T(8,128)(2,1)}, u32[]{:S(2)}, u32[]{:S(2)}) collective-permute-start(bf16[192,2048]{1,0:T(8,128)(2,1)} %get-tuple-element.298.refs_1_), channel_id=1, source_target_pairs={{0,4},{4,0},{8,12},{12,8},{16,20},{20,16},{24,28},{28,24},{1,5},{5... | collective-permute-start | bytes 2359304 | tf_op jit(solution)/shard_map/ppermute | solution.py:1215
  806.2 2.8 collective-permute-start.17
  809.0 13.9 %collective-permute-start.29 = (bf16[640,512]{1,0:T(8,128)(2,1)S(1)}, bf16[640,512]{1,0:T(8,128)(2,1)}, u32[]{:S(2)}, u32[]{:S(2)}) collective-permute-start(bf16[640,512]{1,0:T(8,128)(2,1)S(1)} %broadcast_select_fusion.refs_1_), channel_id=1, source_target_pairs={{0,4},{4,0},{8,12},{12,8},{16,20},{20,16},{24,28},{28,24},{1,5},{5... | collective-permute-start | bytes 1966088 | tf_op jit(solution)/shard_map/ppermute | solution.py:1215
  809.4 13.6 %collective-permute-start.28 = (bf16[640,512]{1,0:T(8,128)(2,1)S(1)}, bf16[640,512]{1,0:T(8,128)(2,1)}, u32[]{:S(2)}, u32[]{:S(2)}) collective-permute-start(bf16[640,512]{1,0:T(8,128)(2,1)S(1)} %broadcast_select_fusion.1.refs_0_), channel_id=1, source_target_pairs={{0,4},{4,0},{8,12},{12,8},{16,20},{20,16},{24,28},{28,24},{1,5},{5... | collective-permute-start | bytes 1966088 | tf_op jit(solution)/shard_map/ppermute | solution.py:1215
  822.9 10.7 %copy-start.1 = (f32[256,2048]{1,0:T(8,128)S(1)}, f32[256,2048]{1,0:T(8,128)}, u32[]{:S(2)}) copy-start(f32[256,2048]{1,0:T(8,128)} %copy-done) | copy-start | bytes 6291460
  (41 other events, 104.2 us)
Sparse Core Ops, SparseCore 0:
  627.6 77.8 reduce-scatter.2
  708.7 51.9 reduce-scatter.4

commit v5 on v4

--- a/solution.py
+++ b/solution.py
@@ -79,10 +79,11 @@
 def rec_forward_kernel(layout, length, *refs):
     x_pieces, refs = refs[: len(layout)], refs[len(layout) :]
     w_both, taps, conv_bias, w_gates, ga_bias, gi_bias, decay_param, w_out = refs[:8]
-    gates_pre, tail, carry, x = refs[-4:]
-    outs = refs[-4 - 8 - len(layout) : -4]
-    mixed, pre, branch, conv, ga, gi, prev_state, final = outs[:8]
-    parts = outs[8:]
+    branch = refs[-1]
+    gates_pre, tail, carry, x = refs[-5:-1]
+    outs = refs[-5 - 10 - len(layout) : -5]
+    mixed, pre, value_out, slope_out, space_out, conv, ga, gi, prev_state, final = outs[:10]
+    parts = outs[10:]
     step = pl.program_id(0)
     block = flip(step, lax.axis_index("mp"), 4 if len(layout) == 5 else len(layout))
     rows, width = mixed.shape[1:]
@@ -97,7 +98,7 @@
         carry[...] = jnp.zeros_like(carry)
 
     both = dot_nn(x[...], w_both[...])
-    branch[0] = both[:, :width]
+    branch[...] = both[:, :width]
     pre[0] = both[:, width:]
 
     def conv_piece(i, _):
@@ -139,7 +140,9 @@
                 gi[0, at, lane] = gate_i
                 log_a = rate * gate_a
                 decay = jnp.exp(log_a)
-                scaled = jnp.sqrt(one_minus_square(log_a, decay)) * gate_i * conv_two[SUB * half : SUB * half + SUB]
+                space = one_minus_square(log_a, decay)
+                space_out[0, at, lane] = space
+                scaled = jnp.sqrt(space) * gate_i * conv_two[SUB * half : SUB * half + SUB]
                 mul = jnp.where(live, decay, 1.0)
                 add = jnp.where(live, scaled, 0.0)
                 for shift in (1, 2, 4):
@@ -149,7 +152,9 @@
                 states = mul * state + add
                 prev_state[0, at, lane] = jnp.where(row == 0, state, pltpu.roll(states, 1, 0))
                 state = jnp.broadcast_to(states[SUB - 1 : SUB], (SUB, LANES))
-                value, _ = gelu_parts(branch[0, at, lane])
+                value, slope = gelu_parts(branch[at, lane])
+                value_out[0, at, lane] = value
+                slope_out[0, at, lane] = slope
                 outs.append(states * value)
             carry[:, lane] = state
             mixed[0, pl.ds(base, 16), lane] = jnp.concatenate(outs, axis=0).astype(bf16)
@@ -163,11 +168,11 @@
     store_block(parts, layout, block, slice(None), x[...])
 
 
-def rec_backward_kernel(layout, nshared, length, *refs):
+def rec_backward_kernel(layout, nshared, wait_late, length, *refs):
     many = len(layout)
     d_resid_pieces, x_pieces, refs = refs[:many], refs[many : 2 * many], refs[2 * many :]
     w_out, w_both, taps, w_gates, decay_param = refs[:5]
-    pre, branch, conv, ga, gi, prev_state = refs[5:11]
+    pre, value_in, slope_in, space_in, conv, ga, gi, prev_state = refs[5:13]
     d_mixed, d_conv, flow, later, x, d_resid = refs[-6:]
     outs = refs[-6 - 4 - many : -6]
     d_both, d_gates, sums, gain_sums = outs[:4]
@@ -189,7 +194,6 @@
 
     block = flip(pl.num_programs(0) - 1 - step, lax.axis_index("mp"), 4 if len(layout) == 5 else len(layout))
     load_block(d_resid_pieces, layout, block, d_resid)
-    load_block(x_pieces, layout, block, x)
     d_mixed[...] = dot_nt(d_resid[...], w_out[...])
 
     def scan_piece(j, _):
@@ -210,15 +214,14 @@
                 d_mix = d_mixed[at, lane]
                 log_a = rate * gate_a
                 decay = jnp.exp(log_a)
-                space = one_minus_square(log_a, decay)
+                space = space_in[0, at, lane]
                 inverse = lax.rsqrt(jnp.maximum(space, 1e-37))
                 root = space * inverse
                 gated = gate_i * conv_val
                 mul = jnp.where(live, decay, 1.0)
                 states = mul * before + jnp.where(live, root * gated, 0.0)
-                value, slope = gelu_parts(branch[0, at, lane])
-                d_br = d_mix * states * slope
-                direct = d_mix * value
+                d_br = d_mix * states * slope_in[0, at, lane]
+                direct = d_mix * value_in[0, at, lane]
                 add = mul * direct
                 for shift in (1, 2, 4):
                     inside = row < SUB - shift
@@ -248,6 +251,8 @@
         return 0
 
     lax.fori_loop(0, pieces, scan_piece, 0)
+    wait_late()
+    load_block(x_pieces, layout, block, x)
     d_conv[...] += dot_nt(d_gates[0], w_gates[...])
 
     def conv_piece(j, _):
@@ -374,17 +379,39 @@
             copy(at).wait_send()
 
 
-def join_kernel(starts, *refs):
-    step = pl.program_id(0)
-    outs = refs[len(starts) - 1 :]
-    for ref, first, after in zip(refs, starts, starts[1:]):
-
-        @pl.when((step >= first) & (step < after))
-        def _(ref=ref):
-            start = 0
-            for out in outs:
-                out[...] = ref[:, start : start + out.shape[1]].astype(f32)
-                start += out.shape[1]
+def join_kernel(npieces, by_rows, ways, *refs):
+    pieces, outs = refs[:npieces], refs[npieces : npieces + ways]
+    held, wide = refs[npieces + ways : 2 * npieces + ways], refs[2 * npieces + ways : 3 * npieces + ways]
+    arrive, leave = refs[-2:]
+    half = npieces // 2
+    core = core_index()
+    loads = [pltpu.make_async_copy(piece, vmem, arrive.at[at]) for at, (piece, vmem) in enumerate(zip(pieces, held))]
+    for load in loads:
+        load.start()
+    stores, start = [], 0
+
+    def store(source, target):
+        stores.append(pltpu.make_async_copy(source, target, leave.at[len(stores)]))
+        stores[-1].start()
+
+    span = sum(piece.shape[0] for piece in pieces[:half])
+    for at, (load, vmem, big) in enumerate(zip(loads, held, wide)):
+        start = 0 if at == half else start
+        mine = core if at < half else 1 - core
+        load.wait()
+        big[...] = vmem[...].astype(f32)
+        if by_rows:
+            place = pl.ds(pl.multiple_of(mine * span + start, 16), vmem.shape[0])
+            start += vmem.shape[0]
+            for way, out in enumerate(outs):
+                store(big.at[:, pl.ds(way * out.shape[1], out.shape[1])], out.at[place, :])
+        else:
+            rows, columns = outs[0].shape[0], vmem.shape[1]
+            for block in range(2):
+                place = pl.ds(pl.multiple_of((mine * 2 + block) * columns, LANES), columns)
+                store(big.at[pl.ds(block * rows, rows), :], outs[0].at[:, place])
+    for store in stores:
+        store.wait()
 
 
 ANY = pl.BlockSpec(memory_space=pl.ANY)
@@ -537,7 +564,7 @@
         self.operands = [piece[1] for piece in pieces]
         self.outputs = [jax.ShapeDtypeStruct((piece[3], piece[1].shape[1]), bf16) for piece in pieces]
         self.scratch = []
-        for (_, _, _, _, stage, hops), out in zip(pieces, self.outputs):
+        for (_, _, _, _, stage, hops, _), out in zip(pieces, self.outputs):
             self.scratch += [pltpu.VMEM(out.shape, bf16)] * (1 + min(hops, 2 - stage))
         self.scratch += [pltpu.SemaphoreType.DMA((len(pieces),))] * 6
 
@@ -548,7 +575,7 @@
         pair, mirror = chip_partners()
         send, recv, send_on, recv_on, local, back = scratch[-6:]
         given = 0
-        for at, ((_, _, start, count, stage, hops), array, out) in enumerate(zip(self.pieces, ins, outs)):
+        for at, ((_, _, start, count, stage, hops, slot), array, out) in enumerate(zip(self.pieces, ins, outs)):
             many = 1 + min(hops, 2 - stage)
             buffers = list(scratch[given : given + many])
             given += many
@@ -566,14 +593,14 @@
             def keep(at=at, buffers=buffers, out=out):
                 return pltpu.make_async_copy(buffers[-1], out, back.at[at])
 
-            yield stage, hops, buffers, hop, load, keep
+            yield stage, hops, slot, buffers, hop, load, keep
 
     def add(self, target, other):
         target[...] = (target[...].astype(f32) + other[...].astype(f32)).astype(bf16)
 
     def begin(self, *refs):
         inner = chip_is_inner()
-        for stage, _, _, hop, load, _ in self.parts(*refs):
+        for stage, _, _, _, hop, load, _ in self.parts(*refs):
 
             @pl.when(inner)
             def _(stage=stage, hop=hop, load=load):
@@ -587,29 +614,34 @@
                 def _(hop=hop):
                     hop(0).start()
 
-    def middle(self, *refs):
+    def middle(self, at, *refs):
         inner = chip_is_inner()
-        for stage, hops, buffers, hop, load, keep in self.parts(*refs):
-
-            @pl.when(inner)
-            def _(stage=stage, hops=hops, buffers=buffers, hop=hop, load=load, keep=keep):
-                load().wait()
-                if stage == 2:
-                    keep().start()
-                elif hops == 2:
-                    hop(0).wait_recv()
-                    self.add(buffers[1], buffers[0])
-                    hop(1).start()
-                    if stage == 1:
+        for stage, hops, slot, buffers, hop, load, keep in self.parts(*refs):
+            if slot == at:
+
+                @pl.when(inner)
+                def _(stage=stage, hops=hops, buffers=buffers, hop=hop, load=load, keep=keep):
+                    load().wait()
+                    if hops == 2:
+                        hop(0).wait_recv()
+                        self.add(buffers[1], buffers[0])
+                        hop(1).start()
+                    if stage + hops == 3:
                         keep().start()
+
+    def slots(self):
+        return sorted(set(piece[6] for piece in self.pieces) - {END, None})
 
     def end(self, *refs):
         inner = chip_is_inner()
+        self.middle(END, *refs)
         parts = list(self.parts(*refs))
-        for stage, hops, buffers, hop, load, keep in parts:
+        for stage, hops, slot, buffers, hop, load, keep in parts:
 
             @pl.when(inner)
-            def _(stage=stage, hops=hops, buffers=buffers, hop=hop, load=load, keep=keep):
+            def _(stage=stage, hops=hops, slot=slot, buffers=buffers, hop=hop, load=load, keep=keep):
+                if slot is None:
+                    load().wait()
                 if stage > 0:
                     hop(0).wait_send()
                 if hops == 2:
@@ -626,7 +658,7 @@
                 if stage + hops == 3:
                     hop(hops - 1).wait_recv()
 
-        for _, _, _, _, _, keep in parts:
+        for _, _, _, _, _, _, keep in parts:
 
             @pl.when(inner)
             def _(keep=keep):
@@ -642,8 +674,9 @@
         self.pieces = []
         for at, (shape, stage, _, _) in enumerate(chunks):
             rows = shape[0]
-            first = rows if stage == 2 or rows < 64 else (rows // 32 + 1) // 2 * 32
-            self.pieces += [(at, start, count) for start, count in ((0, first), (first, rows - first)) if count > 0]
+            parts = 1 if stage == 2 or rows < 64 else 2 if rows < 256 else 4
+            size = -(-rows // parts // 16) * 16
+            self.pieces += [(at, start, min(size, rows - start)) for start in range(0, rows, size)]
         self.scratch = []
         for shape, stage, late, _ in chunks:
             self.scratch += [pltpu.VMEM(shape, bf16)] * (3 - stage - (1 if late else 0))
@@ -754,8 +787,7 @@
 
 
 def call(
-    kernel, grid, ins, outs, scratch, name, us, hosts=(), before=(), aliases=None, middle=0, unique=None, pair=False, chips=False,
-    pipe_middle=0
+    kernel, grid, ins, outs, scratch, name, us, hosts=(), before=(), aliases=None, middle=0, unique=None, pair=False, chips=False, late=()
 ):
     nins, nouts, nscratch = len(ins), len(outs), len(scratch)
     steps = math.prod(grid)
@@ -802,11 +834,14 @@
             arrived = take(1)[0]
             loads = [(own_ins[at], buffer, arrived.at[k]) for k, (at, buffer) in enumerate(zip(loaded, buffers))]
 
+            second = [load for load, at in zip(loads, loaded) if at in late]
+            first = [load for load, at in zip(loads, loaded) if at not in late]
+
             @pl.when(step == 0)
             def _():
-                for load in loads:
+                for load in first + second:
                     pltpu.make_async_copy(*load).start()
-                for load in loads:
+                for load in first:
                     pltpu.make_async_copy(*load).wait()
 
             for at, buffer in zip(loaded, buffers):
@@ -814,13 +849,19 @@
         if hosts:
 
             for host, there in list(zip(hosts, host_refs))[::-1]:
-                at = pipe_middle if isinstance(host, PipeHost) else middle
-
-                @pl.when(step == at)
-                def _(host=host, there=there):
-                    host.middle(*there)
-
-        kernel(*own_ins, *own_outs, *own_scratch)
+                for at in host.slots() if isinstance(host, PipeHost) else (middle,):
+
+                    @pl.when(step == at)
+                    def _(host=host, there=there, at=at):
+                        host.middle(*((at,) if isinstance(host, PipeHost) else ()), *there)
+
+        def wait_late():
+            @pl.when(step == 0)
+            def _():
+                for load in second:
+                    pltpu.make_async_copy(*load).wait()
+
+        kernel(*([wait_late] if late else []), *own_ins, *own_outs, *own_scratch)
         if hosts:
 
             @pl.when(step == steps - 1)
@@ -861,6 +902,7 @@
 
 
 WHOLE = "whole"
+END = 99
 
 
 def whole(array):
@@ -896,12 +938,13 @@
         functools.partial(rec_forward_kernel, layout),
         (blocks,),
         [(v, whole(v)) for v in (length,) + tuple(x) + tuple(params)],
-        [(shape, wide) for shape in (low, out, out, low, out, out, out)] + [final] + list(zip(shapes, specs)),
+        [(shape, wide) for shape in (low, out, out, out, out, low, out, out, out)] + [final] + list(zip(shapes, specs)),
         [
             pltpu.VMEM((rows, 2 * width), f32),
             pltpu.VMEM((SUB, width), f32),
             pltpu.VMEM((SUB, width), f32),
             pltpu.VMEM((rows, model), bf16),
+            pltpu.VMEM((rows, width), f32),
         ],
         "rec_forward",
         37,
@@ -927,6 +970,8 @@
     sums = (jax.ShapeDtypeStruct((8, SUB, width), f32), pl.BlockSpec((8, SUB, width), lambda step: (0, 0, 0)))
     gain_sums = (jax.ShapeDtypeStruct((SUB, model), f32), pl.BlockSpec((SUB, model), lambda step: (0, 0)))
     inputs = [(v, whole(v)) for v in (length,) + tuple(d_resid) + tuple(x) + tuple(params)]
+    before_x, before_params = 1 + len(d_resid), 1 + len(d_resid) + len(x)
+    late = tuple(range(before_x, before_params)) + tuple(before_params + at for at in (1, 2, 3))
     inputs += [(v, wide) for v in saved] + [(v, ANY) for v in shared]
     return call(
         functools.partial(rec_backward_kernel, layout, len(shared)),
@@ -944,6 +989,7 @@
         "rec_backward",
         43,
         aliases={len(inputs) - len(shared) + at: at for at in range(len(shared))},
+        late=late,
         **more,
     )
 
@@ -1044,17 +1090,39 @@
     )
 
 
-def last_kernel(nlefts, nrights, nchunks, nblocks, tail, *refs):
+def last_kernel(nlefts, nrights, nchunks, nblocks, nfinals, tail, *refs):
     lefts, refs = refs[:nlefts], refs[nlefts:]
     rights, refs = refs[:nrights], refs[nrights:]
     convs, refs = refs[:nlefts], refs[nlefts:]
     d_gates, sums_a, sums_b, gain_a, gain_b, gain_c, gain_d = refs[:7]
     chunks, refs = refs[7 : 7 + nchunks], refs[7 + nchunks :]
-    outs, scratch = refs[: nchunks + 4], refs[nchunks + 4 :]
-    pack, gains, first, second, whole_pack, got_pack, left, right, dense, sent, got, send, recv = scratch[:13]
+    finals, refs = refs[:nfinals], refs[nfinals:]
+    outs, refs = refs[: nchunks + 3], refs[nchunks + 3 :]
+    others, scratch = refs[:nfinals], refs[nfinals:]
+    pack, gains, both, whole_pack, got_pack, got_gains, left, right, dense, sent, got, send, recv = scratch[:13]
+    finals_send, finals_recv = scratch[13:15]
     step = pl.program_id(0)
-    tail.setup(list(chunks) + [pack, gains, first, second], outs, scratch[13:])
+    tail.setup(list(chunks) + [pack, gains, both], outs, scratch[15:])
     pl.when(step == 0)(tail.start)
+
+    def swap_final(at):
+        return remote(finals[at], others[at], finals_send, finals_recv, at, other_core())
+
+    def swap_gains():
+        return remote(gains, got_gains, send, recv, 3, other_core())
+
+    @pl.when(step == 0)
+    def _():
+        one = jnp.sum(gain_a[...] + gain_b[...], axis=0, keepdims=True)
+        two = gain_c[...] + gain_d[...]
+        row = lax.broadcasted_iota(jnp.int32, (16, one.shape[1]), 0)
+        gains[...] = jnp.where(row == 0, one, jnp.where(row == 1, two, 0.0)).astype(bf16)
+        swap_gains().start()
+
+    @pl.when(step == 1)
+    def _():
+        swap_gains().wait()
+        gains[...] = (gains[...].astype(f32) + got_gains[...].astype(f32)).astype(bf16)
 
     def copy(at):
         return remote(sent.at[at], got.at[at], send, recv, at, other_core())
@@ -1086,7 +1154,8 @@
                 copy(at).start()
             else:
                 copy(at - 2).wait_recv()
-                (first, second)[at - 2][...] = (total + got[at - 2].astype(f32)).astype(bf16)
+                rows = total.shape[0]
+                both[(at - 2) * rows : (at - 1) * rows, :] = (total + got[at - 2].astype(f32)).astype(bf16)
                 copy(at - 2).wait_send()
 
     @pl.when(step == 3)
@@ -1114,20 +1183,20 @@
         vectors = jnp.concatenate([vectors, jnp.zeros((rest - 8, width), f32)], axis=0)
         whole_pack[2 * inner :, :] = vectors.astype(bf16)
         pack_copy().start()
-        one = jnp.sum(gain_a[...] + gain_b[...], axis=0, keepdims=True)
-        two = gain_c[...] + gain_d[...]
-        row = lax.broadcasted_iota(jnp.int32, (16, one.shape[1]), 0)
-        gains[...] = jnp.where(row == 0, one, jnp.where(row == 1, two, 0.0)).astype(bf16)
 
     @pl.when(step == 4)
     def _():
         pack_copy().wait()
+        for at in range(nfinals):
+            swap_final(at).start()
         mine = pl.ds(pl.multiple_of(core_index() * pack.shape[0], 16), pack.shape[0])
         pack[...] = (whole_pack[mine, :].astype(f32) + got_pack[mine, :].astype(f32)).astype(bf16)
         tail.finish()
-
-
-def last_grad(lefts, rights, convs, d_gates, vectors, moving, nblocks, **more):
+        for at in range(nfinals):
+            swap_final(at).wait()
+
+
+def last_grad(lefts, rights, convs, d_gates, vectors, moving, finals, nblocks, **more):
     lefts, rights, convs = ([flat(v) for v in group] for group in (lefts, rights, convs))
     rows, columns = lefts[0].shape[1], rights[0].shape[1]
     tokens = sum(v.shape[0] for v in lefts)
@@ -1141,30 +1210,35 @@
     names = [name for group in moving for name in group]
     block = (rows, tile)
     packed = -(-(2 * rows // nblocks + 16) // 32) * 32
-    made = [((packed // 2, rows), True), ((16, columns), True), (block, False), (block, False)]
+    made = [((packed // 2, rows), True), ((16, columns), True), ((2 * rows, tile), False)]
     tail = Tail(
         [(chunk.shape, stage, False, True) for chunk, stage in chunks] + [(shape, 0, True, out) for shape, out in made]
     )
     outs = [jax.ShapeDtypeStruct(chunk[0], bf16) for chunk in tail.chunks]
     out, found = call(
-        functools.partial(last_kernel, len(lefts), len(rights), len(chunks), nblocks, tail),
+        functools.partial(last_kernel, len(lefts), len(rights), len(chunks), nblocks, len(finals), tail),
         (5,),
         [(v, whole(v)) for v in lefts]
         + [(v, pl.BlockSpec((v.shape[0], tile), lambda step: (0, place(step)))) for v in rights]
         + [(v, whole(v)) for v in convs + [flat(d_gates)] + list(vectors)]
-        + [(chunk, ANY) for chunk, _ in chunks],
-        [(shape, ANY) for shape in outs],
+        + [(chunk, ANY) for chunk, _ in chunks]
+        + [(piece, ANY) for piece in finals.values()],
+        [(shape, ANY) for shape in outs]
+        + [(jax.ShapeDtypeStruct(piece.shape, bf16), ANY) for piece in finals.values()],
         [pltpu.VMEM(shape, bf16) for shape, _ in made]
         + [
             pltpu.VMEM((packed, rows), bf16),
             pltpu.VMEM((packed, rows), bf16),
+            pltpu.VMEM((16, columns), bf16),
             pltpu.VMEM((tokens, rows), bf16),
             pltpu.VMEM((tokens, tile), bf16),
             pltpu.VMEM((rows, 2 * rows), f32),
             pltpu.VMEM((2,) + block, bf16),
             pltpu.VMEM((2,) + block, bf16),
-            pltpu.SemaphoreType.DMA((3,)),
-            pltpu.SemaphoreType.DMA((3,)),
+            pltpu.SemaphoreType.DMA((4,)),
+            pltpu.SemaphoreType.DMA((4,)),
+            pltpu.SemaphoreType.DMA((len(finals),)),
+            pltpu.SemaphoreType.DMA((len(finals),)),
         ]
         + tail.scratch,
         "last_grad",
@@ -1173,41 +1247,25 @@
         chips=True,
         **more,
     )
-    return dict(zip(names + ["pack", "gains", "out0", "out1"], out)), found
-
-
-def join_pieces(pieces, by_rows, ways, **more):
-    columns = pieces[0].shape[1]
-    half = len(pieces) // 2
-    rows = pieces[0].shape[0] if not by_rows else sum(piece.shape[0] for piece in pieces[:half])
-    unit = math.gcd(*[piece.shape[0] for piece in pieces])
-    tile = max(t for t in range(16, 256 + 1, 16) if unit % t == 0)
-    counts = [piece.shape[0] // tile for piece in pieces]
-    starts = [sum(counts[:at]) for at in range(len(counts))]
-    steps = sum(counts)
-
-    def source(at):
-        def index(i):
-            return (jnp.clip(i - starts[at], 0, counts[at] - 1), 0)
-
-        return pl.BlockSpec((tile, columns), index)
-
-    def target(i):
-        at = (i + core_index() * (steps // 2)) % steps
-        return (at, 0) if by_rows else (at % counts[0], at // counts[0])
-
-    shape = (2 * rows, columns // ways) if by_rows else (rows, len(pieces) * columns)
-    out = (jax.ShapeDtypeStruct(shape, f32), pl.BlockSpec((tile, columns // ways), target))
+    names += ["pack", "gains", "out"]
+    return dict(zip(names, out)), dict(zip(finals, out[len(names) :])), found
+
+
+def join_pieces(pieces, by_rows, ways):
+    rows, columns = sum(v.shape[0] for v in pieces), pieces[0].shape[1]
+    shape = (rows, columns // ways) if by_rows else (rows // 4, 4 * columns)
+    out = (jax.ShapeDtypeStruct(shape, f32), ANY)
     return call(
-        functools.partial(join_kernel, tuple(starts) + (steps,)),
-        (steps,),
-        [(piece, source(at)) for at, piece in enumerate(pieces)],
+        functools.partial(join_kernel, len(pieces), by_rows, ways),
+        (1,),
+        [(piece, ANY) for piece in pieces],
         [out] * ways,
-        [],
+        [pltpu.VMEM(piece.shape, bf16) for piece in pieces]
+        + [pltpu.VMEM(piece.shape, f32) for piece in pieces]
+        + [pltpu.SemaphoreType.DMA((len(pieces),)), pltpu.SemaphoreType.DMA((len(pieces) * max(2, ways),))],
         "join_pieces",
         0.05,
-        **more,
-    )
+    )[0]
 
 
 def swap(value, axis, bit):
@@ -1251,31 +1309,26 @@
     def enter(self, name, quarters):
         self.queue += [[name + str(at), quarter, 0] for at, quarter in enumerate(quarters)]
 
-    def host(self, budget):
-        pieces = [(name, array, 0, array.shape[0], stage, 3 - stage) for name, array, stage in self.moving]
-        cuts, left = [], budget
-        while self.queue and left > 0:
+    def host(self, budget, slots):
+        pieces, old = [], list(slots)
+        for name, array, stage in self.moving:
+            slot = slots[0] if stage == 2 else old.pop(0)
+            pieces.append((name, array, 0, array.shape[0], stage, 3 - stage, slot))
+        ahead = list(slots)
+        while self.queue and budget > 0:
             name, array, start = self.queue[0]
             unit = array.shape[0] // 4
-            units = min((array.shape[0] - start) // unit, left)
-            cuts.append((name, array, start, units))
-            left -= units
-            self.queue[0][2] += units * unit
+            slot = ahead.pop(0) if ahead else None
+            pieces.append((name + "_" + str(start).zfill(4), array, start, unit, 0, 2 if slot else 1, slot))
+            budget -= 1
+            self.queue[0][2] += unit
             if self.queue[0][2] == array.shape[0]:
                 self.queue.pop(0)
-        early = sum(units for _, _, _, units in cuts) // 2
-        for name, array, start, units in cuts:
-            unit = array.shape[0] // 4
-            first = min(units, early)
-            early -= first
-            for at, count, hops in ((start, first * unit, 2), (start + first * unit, (units - first) * unit, 1)):
-                if count > 0:
-                    pieces.append((name + "_" + str(at).zfill(4), array, at, count, 0, hops))
         return PipeHost(pieces) if pieces else None
 
     def took(self, host, results):
         self.moving = []
-        for name, _, _, _, stage, hops in host.pieces:
+        for name, _, _, _, stage, hops, _ in host.pieces:
             if stage + hops == 3:
                 self.done[name] = results[name]
             else:
@@ -1377,10 +1430,9 @@
 
     def run(function, *args, hosts=(), middle=0, budget=4, **more):
         if hosted:
-            window = pipe.host(budget) if piped else None
+            window = pipe.host(budget, (2, 3) if function is weight_grad else (1, 2)) if piped else None
             out, found = function(
-                *args, hosts=list(hosts) + ([window] if window else []), middle=middle, unique=next(ids),
-                pipe_middle=3 if function is weight_grad else 2, **more
+                *args, hosts=list(hosts) + ([window] if window else []), middle=middle, unique=next(ids), **more
             )
             if window:
                 pipe.took(window, found[-1])
@@ -1399,17 +1451,17 @@
     seq_in.append(second)
     forward = [out]
     out, (branch,) = run(
-        rec_forward, limits[1], seq_in[1], forward_params, hosts=[ScatterHost(out[8:])], middle=2, before=(out[7],)
+        rec_forward, limits[1], seq_in[1], forward_params, hosts=[ScatterHost(out[10:])], middle=2, before=(out[9],)
     )
     forward.append(out)
     mixed = [out[0] for out in forward]
-    saved = [out[1:7] for out in forward]
-    finals = [out[7][:1, :true_width] for out in forward]
+    saved = [out[1:9] for out in forward]
+    finals = [out[9][:1, :true_width] for out in forward]
     resid_mid = [resid[0] + branch]
     mid = normalize(resid_mid[0], norm2_gain).astype(bf16)
     seq_mid = [gather(mid)]
     forward_shared, (branch,) = run(
-        mlp_forward, 0, count, seq_mid[0], w_gate, w_up, w_down, (), hosts=[ScatterHost(forward[1][8:])], middle=2
+        mlp_forward, 0, count, seq_mid[0], w_gate, w_up, w_down, (), hosts=[ScatterHost(forward[1][10:])], middle=2
     )
     mlp_part = [forward_shared[3]]
     resid_mid.append(resid[1] + branch)
@@ -1464,28 +1516,29 @@
     flat_in = [p for pieces in seq_in for p in pieces]
     flat_resid = [p for pieces in (first_seq, second_seq) for p in pieces]
     grad_in, _ = run(weight_grad, flat_in, [d_both])
-    conv = [part[2] for part in saved]
+    conv = [part[4] for part in saved]
     if piped:
 
         def join(prefix, by_rows=True, ways=1):
-            mine = [pipe.done[name] for name in sorted(pipe.done) if name.startswith(prefix)]
-            return join_pieces(mine + [swap(piece, "dp", 1) for piece in mine], by_rows, ways)[0]
+            names = [name for name in sorted(pipe.done) if name.startswith(prefix)]
+            mine = [pipe.done[name] for name in names]
+            other = [others[name] if name in others else swap(pipe.done[name], "dp", 1) for name in names]
+            return join_pieces(mine + other, by_rows, ways)
 
         moving = pipe.left()
         moving[0].update(in0=grad_in[0], in1=grad_in[1])
-        found, (d_in,) = last_grad(
-            mixed, flat_resid, conv, d_gates, (sums, out[2], gain1, out[3], gain2, more_gain2), moving, nblocks,
+        found, others, (d_in,) = last_grad(
+            mixed, flat_resid, conv, d_gates, (sums, out[2], gain1, out[3], gain2, more_gain2), moving, dict(pipe.done),
+            nblocks,
             hosts=[ScatterHost(out[4:])], middle=4, unique=next(ids), before=(grad_in[0],),
         )
-        pipe.done.update({name: found[name] for name in found if name not in ("out0", "out1")})
+        pipe.done.update({name: found[name] for name in found if name != "out"})
         pairs = [(2 * a + core, 2 * b + core) for a, b in ((1, 0), (2, 3)) for core in range(2)]
-        came = {name: lax.ppermute(found[name], "dp", pairs) for name in ("out0", "out1")}
+        came = lax.ppermute(found["out"], "dp", pairs)
         totals_down, totals_gate, totals_up = (join(name) for name in ("down", "gate", "up"))
         totals_in = join("in", ways=2)
-        came = dict(zip(came, lax.optimization_barrier((*came.values(), totals_gate, totals_up, totals_in[0]))))
-        for name in came:
-            found[name] = jnp.where(chip_is_inner(), found[name], came[name])
-        pipe.done.update(out0=found["out0"], out1=found["out1"])
+        came = lax.optimization_barrier((came, totals_down, totals_gate, totals_up, totals_in[0]))[0]
+        pipe.done["out"] = jnp.where(chip_is_inner(), found["out"], came)
         totals_out = join("out", by_rows=False)
         pack, other = found["pack"].astype(f32), swap(found["pack"], "dp", 1).astype(f32)
         mine = core_index() == 0
@@ -1496,7 +1549,6 @@
         )
         vectors = pack[2 * inner : 2 * inner + 8]
         gains = found["gains"][:2].astype(f32)
-        gains = gains + swap(gains, "dp", 1)
         for bit in (1, 2):
             gains = gains + swap(gains, "mp", bit)
     else:

time: 856 us -> 820 us (0.958)
  Pallas kernels: 653 us -> 630 us
    pallas_call x18, Pallas kernels: 653 us -> 630 us  [call(): pl.pallas_call(body, out_shape=tuple((shape for shape, _ in outs)) + tupl...]
    ppermute x32 -> x22, starting transfers between devices: 25.4 us -> 18.4 us  [swap(): return lax.ppermute(value, axis, [(i, i ^ bit) for i in range(size)])]
    ppermute x32 -> x22, waiting for transfers between devices: 76.9 us -> 75.5 us  [swap(): return lax.ppermute(value, axis, [(i, i ^ bit) for i in range(size)])]
  transfers between devices with their start and end apart: 36 -> 25, of which waited for: 9 -> 9; matrix products, arithmetic and copies ran while one was open for 4% -> 4% of each run, Pallas kernels for 19% -> 19%
where the time goes in v5:
time: 820 us; the launch traced here: 810 us
  Pallas kernels  630 us (77%)
  waiting for transfers between devices  75.6 us (9%)
  other arithmetic  46.4 us (6%)
  local copies, waits for them, and re-layouts  21.6 us (3%)
  starting transfers between devices  20.8 us (3%)
  between operations  15.2 us (2%)
    pallas_call x18, Pallas kernels, call(): pl.pallas_call(body, out_shape=tuple((shape for shape, _ in outs)) + tupl...  630 us
    ppermute x22, waiting for transfers between devices, swap(): return lax.ppermute(value, axis, [(i, i ^ bit) for i in range(size)])  75.5 us
    ppermute x22, starting transfers between devices, swap(): return lax.ppermute(value, axis, [(i, i ^ bit) for i in range(size)])  18.4 us
  transfers between devices with their start and end apart: 25, of which 9 were waited for; matrix products, arithmetic and copies ran while one was open for 4% of the time, Pallas kernels for 19%

profile of v5, /device:TPU:9, one launch (start us, length us, event | category | flops | bytes accessed | tf_op | source)
XLA Modules:
  0.0 810.1 jit_solution(2164342062746966847)
XLA Ops:
  7.3 2.2 fusion.40
  9.5 1.4 fusion.34
  10.9 1.3 collective-permute-start.1
  12.2 1.2 collective-permute-start
  13.5 8.4 %fusion.44.refs_9_.refs_14_ = bf16[640,1280]{1,0:T(8,128)(2,1)} fusion(bf16[160,160]{1,0:T(8,128)(2,1)S(1)} %get-tuple-element.430, bf16[160,160]{1,0:T(8,128)(2,1)S(1)} %get-tuple-element.431, bf16[160,160]{1,0:T(8,128)(2,1)S(1)} %get-tuple-element.429, bf16[160,160]{1,0:T(8,128)(2,1)S(1)} %get-tuple-element.428, ...), kind=kLoop, calls=%fused_computation.76 | loop fusion | flops 40960000 | bytes 2048000 | tf_op jit(solution)/shard_map/concatenate | solution.py:1410
  24.9 10.2 %collective-permute-done.1.refs_3_.refs_8_.refs_2_ = bf16[256,2048]{1,0:T(8,128)(2,1)S(1)} collective-permute-done((bf16[256,2048]{1,0:T(8,128)(2,1)S(1)}, bf16[256,2048]{1,0:T(8,128)(2,1)S(1)}, u32[]{:S(2)}, u32[]{:S(2)}) %collective-permute-start.1) | collective-permute-done | bytes 1048608 | tf_op jit(solution)/shard_map/ppermute | solution.py:1273
  35.1 1.3 collective-permute-start.3
  36.4 1.3 collective-permute-start.2
  39.0 2.3 copy-done.26
  41.3 5.7 collective-permute-done.3.refs_5_.refs_10_.refs_4_
  47.0 1.1 collective-permute-done.2.refs_4_.refs_9_.refs_3_
  48.1 1.2 broadcast_in_dim.16.refs_0_
  49.3 42.2 %rec_forward.2 = (bf16[4,256,640]{2,1,0:T(8,128)(2,1)}, f32[4,256,640]{2,1,0:T(8,128)}, f32[4,256,640]{2,1,0:T(8,128)}, f32[4,256,640]{2,1,0:T(8,128)}, f32[4,25...) custom-call(s32[8,128]{1,0:T(8,128)} %broadcast_in_dim.16.refs_0_, ...), custom_call_target="tpu_custom_call" | custom-call | flops 21275000832 | bytes 65536 | tf_op jit(solution)/shard_map/rec_forward/pallas_call | solution.py:877
  91.6 1.2 broadcast_in_dim.21.refs_0_
  92.8 39.9 %rec_forward.3 = (bf16[4,256,640]{2,1,0:T(8,128)(2,1)}, f32[4,256,640]{2,1,0:T(8,128)}, f32[4,256,640]{2,1,0:T(8,128)}, f32[4,256,640]{2,1,0:T(8,128)}, f32[4,25...) custom-call(s32[8,128]{1,0:T(8,128)} %broadcast_in_dim.21.refs_0_, ...), custom_call_target="tpu_custom_call" | custom-call | flops 21275000832 | bytes 65536 | tf_op jit(solution)/shard_map/rec_forward/pallas_call | solution.py:877
  132.7 2.2 multiply_reduce_fusion.5
  135.8 1.1 collective-permute-start.4
  136.9 19.2 %collective-permute-done.5.refs_2_ = bf16[256,2048]{1,0:T(8,128)(2,1)S(1)} collective-permute-done((bf16[256,2048]{1,0:T(8,128)(2,1)S(1)}, bf16[256,2048]{1,0:T(8,128)(2,1)S(1)}, u32[]{:S(2)}, u32[]{:S(2)}) %collective-permute-start.5) | collective-permute-done | bytes 1048608 | tf_op jit(solution)/shard_map/ppermute | solution.py:1273
  156.7 1.0 collective-permute-start.6
  157.8 10.2 %collective-permute-done.7.refs_4_ = bf16[128,2048]{1,0:T(8,128)(2,1)S(1)} collective-permute-done((bf16[128,2048]{1,0:T(8,128)(2,1)S(1)}, bf16[128,2048]{1,0:T(8,128)(2,1)S(1)}, u32[]{:S(2)}, u32[]{:S(2)}) %collective-permute-start.7) | collective-permute-done | bytes 524320 | tf_op jit(solution)/shard_map/ppermute | solution.py:1273
  168.0 0.8 copy-done.63
  168.9 35.9 %mlp_forward.2 = (bf16[8,256,1536]{2,1,0:T(8,128)(2,1)}, bf16[8,256,1536]{2,1,0:T(8,128)(2,1)}, bf16[8,256,1536]{2,1,0:T(8,128)(2,1)}, bf16[4,256,2048]{2,1,0:T(...) custom-call(bf16[256,2048]{1,0:T(8,128)(2,1)} %copy-done.28, bf16[256,2048]{1,0:T(8,128)(2,1)} %copy-done.44, ...), custom_call_target="tpu_custom_call" | custom-call | flops 17250000896 | bytes 65536 | tf_op jit(solution)/shard_map/mlp_forward/pallas_call | solution.py:877
  204.9 2.2 multiply_reduce_fusion.4
  207.4 1.5 collective-permute-start.9
  209.0 19.3 %collective-permute-done.9.refs_2_.refs_7_ = bf16[256,2048]{1,0:T(8,128)(2,1)S(1)} collective-permute-done((bf16[256,2048]{1,0:T(8,128)(2,1)S(1)}, bf16[256,2048]{1,0:T(8,128)(2,1)S(1)}, u32[]{:S(2)}, u32[]{:S(2)}) %collective-permute-start.9) | collective-permute-done | bytes 1048608 | tf_op jit(solution)/shard_map/ppermute | solution.py:1273
  228.4 1.4 collective-permute-start.11
  229.9 0.9 copy-done.46
  230.8 0.8 collective-permute-start.10
  231.6 1.6 slice_bitcast_fusion.1
  233.2 9.2 %collective-permute-done.11.refs_4_.refs_9_ = bf16[128,2048]{1,0:T(8,128)(2,1)S(1)} collective-permute-done((bf16[128,2048]{1,0:T(8,128)(2,1)S(1)}, bf16[128,2048]{1,0:T(8,128)(2,1)S(1)}, u32[]{:S(2)}, u32[]{:S(2)}) %collective-permute-start.11) | collective-permute-done | bytes 524320 | tf_op jit(solution)/shard_map/ppermute | solution.py:1273
  242.5 0.8 copy-done.65
  243.4 34.7 %mlp_forward.3 = (bf16[8,256,1536]{2,1,0:T(8,128)(2,1)}, bf16[8,256,1536]{2,1,0:T(8,128)(2,1)}, bf16[8,256,1536]{2,1,0:T(8,128)(2,1)}, bf16[4,256,2048]{2,1,0:T(...) custom-call(bf16[256,2048]{1,0:T(8,128)(2,1)} %copy-done.29, ...), custom_call_target="tpu_custom_call", output_to_operand_aliasing={{0}: (8, {}), {1}: (9, {}), {2}: (10, {})} | custom-call | flops 17250000896 | bytes 65536 | tf_op jit(solution)/shard_map/mlp_forward/pallas_call | solution.py:877
  278.1 36.5 %mlp_backward.2 = (bf16[8,256,1536]{2,1,0:T(8,128)(2,1)}, bf16[8,256,1536]{2,1,0:T(8,128)(2,1)}, bf16[256,2048]{1,0:T(8,128)(2,1)}, bf16[256,2048]{1,0:T(8,128)(...) custom-call(bf16[256,2048]{1,0:T(8,128)(2,1)} %get-tuple-element.419, ...), custom_call_target="tpu_custom_call" | custom-call | flops 18400000000 | bytes 65536 | tf_op jit(solution)/shard_map/mlp_backward/pallas_call | solution.py:877
  314.6 29.9 %weight_grad.4 = (bf16[384,2048]{1,0:T(8,128)(2,1)}, bf16[384,2048]{1,0:T(8,128)(2,1)}) custom-call(bf16[2048,1536]{1,0:T(8,128)(2,1)} %bitcast.81, bf16[256,2048]{1,0:T(8,128)(2,1)} %get-tuple-element.419.refs_11_.refs_0_.refs_1_, bf16[256,2048]{1,0:T(8,128)(2,1)} %get-tuple-element.229.refs_1_.refs_2_, ...), custom_call_target="tpu_custom_call" | custom-call | flops 11500000256 | bytes 65536 | tf_op jit(solution)/shard_map/weight_grad/pallas_call | solution.py:877
  344.5 43.6 %mlp_backward.3 = (bf16[8,256,1536]{2,1,0:T(8,128)(2,1)}, bf16[8,256,1536]{2,1,0:T(8,128)(2,1)}, bf16[256,2048]{1,0:T(8,128)(2,1)}, bf16[256,2048]{1,0:T(8,128)(...) custom-call(bf16[256,2048]{1,0:T(8,128)(2,1)} %get-tuple-element.418, ...), custom_call_target="tpu_custom_call", output_to_operand_aliasing={{0}: (10, {}), {1}: (11, {})} | custom-call | flops 18400000000 | bytes 65536 | tf_op jit(solution)/shard_map/mlp_backward/pallas_call | solution.py:877
  388.2 3.2 multiply_reduce_fusion.1
  391.3 2.8 fusion.60
  394.1 43.6 %weight_grad.5 = (bf16[512,1536]{1,0:T(8,128)(2,1)}, bf16[512,1536]{1,0:T(8,128)(2,1)}, bf16[256,2048]{1,0:T(8,128)(2,1)}, bf16[256,2048]{1,0:T(8,128)(2,1)}, bf...) custom-call(bf16[256,2048]{1,0:T(8,128)(2,1)} %copy-done.28, ...), custom_call_target="tpu_custom_call" | custom-call | flops 11500000256 | bytes 65536 | tf_op jit(solution)/shard_map/weight_grad/pallas_call | solution.py:877
  437.7 40.9 %weight_grad.6 = (bf16[512,1536]{1,0:T(8,128)(2,1)}, bf16[512,1536]{1,0:T(8,128)(2,1)}, bf16[256,2048]{1,0:T(8,128)(2,1)}, bf16[256,2048]{1,0:T(8,128)(2,1)}, bf...) custom-call(bf16[256,2048]{1,0:T(8,128)(2,1)} %copy-done.28, ...), custom_call_target="tpu_custom_call" | custom-call | flops 11500000256 | bytes 65536 | tf_op jit(solution)/shard_map/weight_grad/pallas_call | solution.py:877
  478.7 3.2 multiply_reduce_fusion
  481.8 2.8 fusion.59
  484.6 46.5 %rec_backward.2 = (bf16[8,256,1280]{2,1,0:T(8,128)(2,1)}, bf16[8,256,1280]{2,1,0:T(8,128)(2,1)}, f32[8,8,640]{2,1,0:T(8,128)}, f32[8,2048]{1,0:T(8,128)}, bf16[2...) custom-call(s32[8,128]{1,0:T(8,128)} %broadcast_in_dim.16.refs_0_, ...), custom_call_target="tpu_custom_call" | custom-call | flops 24725000192 | bytes 65536 | tf_op jit(solution)/shard_map/rec_backward/pallas_call | solution.py:877
  531.2 41.8 %rec_backward.3 = (bf16[8,256,1280]{2,1,0:T(8,128)(2,1)}, bf16[8,256,1280]{2,1,0:T(8,128)(2,1)}, f32[8,8,640]{2,1,0:T(8,128)}, f32[8,2048]{1,0:T(8,128)}, bf16[2...) custom-call(s32[8,128]{1,0:T(8,128)} %broadcast_in_dim.21.refs_0_, ...), custom_call_target="tpu_custom_call", output_to_operand_aliasing={{0}: (24, {}), {1}: (25, {})} | custom-call | flops 24725000192 | bytes 65536 | tf_op jit(solution)/shard_map/rec_backward/pallas_call | solution.py:877
  573.0 42.8 %weight_grad.7 = (bf16[512,1280]{1,0:T(8,128)(2,1)}, bf16[512,1280]{1,0:T(8,128)(2,1)}, bf16[128,1536]{1,0:T(8,128)(2,1)}, bf16[128,1536]{1,0:T(8,128)(2,1)}, bf...) custom-call(bf16[256,2048]{1,0:T(8,128)(2,1)} %copy-done.30, ...), custom_call_target="tpu_custom_call" | custom-call | flops 11500000256 | bytes 65536 | tf_op jit(solution)/shard_map/weight_grad/pallas_call | solution.py:877
  618.2 123.0 %last_grad.1 = (bf16[512,1280]{1,0:T(8,128)(2,1)}, bf16[512,1280]{1,0:T(8,128)(2,1)}, bf16[128,1536]{1,0:T(8,128)(2,1)}, bf16[128,1536]{1,0:T(8,128)(2,1)}, bf16...) custom-call(bf16[1024,640]{1,0:T(8,128)(2,1)} %bitcast.86, ...), custom_call_target="tpu_custom_call" | custom-call | flops 69000003584 | bytes 65536 | tf_op jit(solution)/shard_map/last_grad/pallas_call | solution.py:877
  741.2 0.8 slice_convert_fusion
  742.0 2.8 collective-permute-start.14
  744.7 2.4 collective-permute-start.17
  747.2 3.2 fusion.35
  751.1 3.5 fusion.55
  754.6 6.4 join_pieces.6
  761.0 6.7 join_pieces.7
  768.3 0.8 fusion.58
  770.2 1.0 collective-permute-start.13
  771.2 6.4 join_pieces.8
  777.6 1.0 copy-done.25
  778.7 5.6 join_pieces.5
  786.2 1.5 pad_maximum_fusion.1
  790.2 1.0 copy.47
  791.6 1.0 copy.48
  793.8 4.0 join_pieces.9
  797.9 1.5 fusion.53
  799.4 2.1 fusion.54
  801.6 1.5 pad_maximum_fusion
  (197 shorter events, 17.3 us)
Async XLA Ops:
  7.2 790.7 %reduce-scatter.3.cloned.1.call-start = ((), (), s32[]{:S(2)}) async-start(), calls=%async_computation.2 | async-start | bytes 5242880 | tf_op jit(solution)/shard_map/reduce_scatter | solution.py:1587
  9.5 4.0 copy-start.38
  9.5 4.0 copy-start.39
  10.9 24.2 %copy-start.30 = (bf16[256,2048]{1,0:T(8,128)(2,1)}, bf16[256,2048]{1,0:T(8,128)(2,1)S(1)}, u32[]{:S(2)}) copy-start(bf16[256,2048]{1,0:T(8,128)(2,1)S(1)} %get-tuple-element.416.refs_1_.refs_6_.refs_0_) | copy-start | bytes 3145732
  10.9 11.1 %copy-start.50 = (f32[640]{0:T(1024)S(1)}, f32[640]{0:T(1024)}, u32[]{:S(2)}) copy-start(f32[640]{0:T(1024)} %param.28) | copy-start | bytes 7684
  10.9 11.7 %copy-start.56 = (f32[640]{0:T(1024)S(1)}, f32[640]{0:T(1024)}, u32[]{:S(2)}) copy-start(f32[640]{0:T(1024)} %param.23) | copy-start | bytes 7684
  10.9 12.2 %copy-start.57 = (f32[640]{0:T(1024)S(1)}, f32[640]{0:T(1024)}, u32[]{:S(2)}) copy-start(f32[640]{0:T(1024)} %param.25) | copy-start | bytes 7684
  10.9 12.8 %copy-start.58 = (f32[640]{0:T(1024)S(1)}, f32[640]{0:T(1024)}, u32[]{:S(2)}) copy-start(f32[640]{0:T(1024)} %param.27) | copy-start | bytes 7684
  10.9 13.4 %copy-start.59 = (s32[2]{0:T(128)S(1)}, s32[2]{0:T(128)}, u32[]{:S(2)}) copy-start(s32[2]{0:T(128)} %param.34) | copy-start | bytes 28
  10.9 24.1 %collective-permute-start.1 = (bf16[256,2048]{1,0:T(8,128)(2,1)S(1)}, bf16[256,2048]{1,0:T(8,128)(2,1)S(1)}, u32[]{:S(2)}, u32[]{:S(2)}) collective-permute-start(bf16[256,2048]{1,0:T(8,128)(2,1)S(1)} %get-tuple-element.416.refs_1_.refs_6_.refs_0_), channel_id=1, source_target_pairs={{0,2},{1,3},{2,0},{3,1},{4,6},{5,7},{6,4},{7,5},{8,10},{9,11},{10,... | collective-permute-start | bytes 3145736 | tf_op jit(solution)/shard_map/ppermute | solution.py:1273
  12.2 24.1 %collective-permute-start = (bf16[256,2048]{1,0:T(8,128)(2,1)S(1)}, bf16[256,2048]{1,0:T(8,128)(2,1)S(1)}, u32[]{:S(2)}, u32[]{:S(2)}) collective-permute-start(bf16[256,2048]{1,0:T(8,128)(2,1)S(1)} %get-tuple-element.416.refs_1_.refs_6_.refs_0_), channel_id=1, source_target_pairs={{0,1},{1,0},{2,3},{3,2},{4,5},{5,4},{6,7},{7,6},{8,9},{9,8},{10,11... | collective-permute-start | bytes 3145736 | tf_op jit(solution)/shard_map/ppermute | solution.py:1273
  13.5 24.2 %copy-start.23 = (bf16[2048,640]{1,0:T(8,128)(2,1)S(1)}, bf16[2048,640]{1,0:T(8,128)(2,1)}, u32[]{:S(2)}) copy-start(bf16[2048,640]{1,0:T(8,128)(2,1)} %param.20) | copy-start | bytes 7864324
  35.1 11.9 %collective-permute-start.3 = (bf16[128,2048]{1,0:T(8,128)(2,1)S(1)}, bf16[128,2048]{1,0:T(8,128)(2,1)S(1)}, u32[]{:S(2)}, u32[]{:S(2)}) collective-permute-start(bf16[128,2048]{1,0:T(8,128)(2,1)S(1)} %slice.139), channel_id=1, source_target_pairs={{0,1},{1,0},{2,3},{3,2},{4,5},{5,4},{6,7},{7,6},{8,9},{9,8},{10,11... | collective-permute-start | bytes 1572872 | tf_op jit(solution)/shard_map/ppermute | solution.py:1273
  36.4 11.7 %collective-permute-start.2 = (bf16[128,2048]{1,0:T(8,128)(2,1)S(1)}, bf16[128,2048]{1,0:T(8,128)(2,1)S(1)}, u32[]{:S(2)}, u32[]{:S(2)}) collective-permute-start(bf16[128,2048]{1,0:T(8,128)(2,1)S(1)} %slice.138), channel_id=1, source_target_pairs={{0,2},{1,3},{2,0},{3,1},{4,6},{5,7},{6,4},{7,5},{8,10},{9,11},{10,... | collective-permute-start | bytes 1572872 | tf_op jit(solution)/shard_map/ppermute | solution.py:1273
  92.8 39.9 %copy-start.32 = (bf16[256,2048]{1,0:T(8,128)(2,1)S(1)}, bf16[256,2048]{1,0:T(8,128)(2,1)}, u32[]{:S(2)}) copy-start(bf16[256,2048]{1,0:T(8,128)(2,1)} %get-tuple-element.206) | copy-start | bytes 3145732
  135.0 256.4 %copy-start = (f32[256,2048]{1,0:T(8,128)}, f32[256,2048]{1,0:T(8,128)S(1)}, u32[]{:S(2)}) copy-start(f32[256,2048]{1,0:T(8,128)S(1)} %get-tuple-element.413) | copy-start | bytes 6291460
  135.2 33.6 %copy-start.28 = (bf16[256,2048]{1,0:T(8,128)(2,1)}, bf16[256,2048]{1,0:T(8,128)(2,1)S(1)}, u32[]{:S(2)}) copy-start(bf16[256,2048]{1,0:T(8,128)(2,1)S(1)} %multiply_convert_fusion.1.refs_0_) | copy-start | bytes 3145732
  135.3 20.8 %collective-permute-start.5 = (bf16[256,2048]{1,0:T(8,128)(2,1)S(1)}, bf16[256,2048]{1,0:T(8,128)(2,1)S(1)}, u32[]{:S(2)}, u32[]{:S(2)}) collective-permute-start(bf16[256,2048]{1,0:T(8,128)(2,1)S(1)} %multiply_convert_fusion.1.refs_0_), channel_id=1, source_target_pairs={{0,2},{1,3},{2,0},{3,1},{4,6},{5,7},{6,4},{7,5},{8,10},{9,11},{10,... | collective-permute-start | bytes 3145736 | tf_op jit(solution)/shard_map/ppermute | solution.py:1273
  135.8 20.9 %collective-permute-start.4 = (bf16[256,2048]{1,0:T(8,128)(2,1)S(1)}, bf16[256,2048]{1,0:T(8,128)(2,1)S(1)}, u32[]{:S(2)}, u32[]{:S(2)}) collective-permute-start(bf16[256,2048]{1,0:T(8,128)(2,1)S(1)} %multiply_convert_fusion.1.refs_0_), channel_id=1, source_target_pairs={{0,1},{1,0},{2,3},{3,2},{4,5},{5,4},{6,7},{7,6},{8,9},{9,8},{10,11... | collective-permute-start | bytes 3145736 | tf_op jit(solution)/shard_map/ppermute | solution.py:1273
  156.0 12.0 %copy-start.43 = (bf16[256,2048]{1,0:T(8,128)(2,1)}, bf16[256,2048]{1,0:T(8,128)(2,1)S(1)}, u32[]{:S(2)}) copy-start(bf16[256,2048]{1,0:T(8,128)(2,1)S(1)} %collective-permute-done.5.refs_2_) | copy-start | bytes 3145732
  156.1 11.9 %collective-permute-start.7 = (bf16[128,2048]{1,0:T(8,128)(2,1)S(1)}, bf16[128,2048]{1,0:T(8,128)(2,1)S(1)}, u32[]{:S(2)}, u32[]{:S(2)}) collective-permute-start(bf16[128,2048]{1,0:T(8,128)(2,1)S(1)} %slice.141), channel_id=1, source_target_pairs={{0,1},{1,0},{2,3},{3,2},{4,5},{5,4},{6,7},{7,6},{8,9},{9,8},{10,11... | collective-permute-start | bytes 1572872 | tf_op jit(solution)/shard_map/ppermute | solution.py:1273
  156.7 11.3 %copy-start.44 = (bf16[256,2048]{1,0:T(8,128)(2,1)}, bf16[256,2048]{1,0:T(8,128)(2,1)S(1)}, u32[]{:S(2)}) copy-start(bf16[256,2048]{1,0:T(8,128)(2,1)S(1)} %collective-permute-done.4.refs_1_) | copy-start | bytes 3145732
  156.7 11.2 %collective-permute-start.6 = (bf16[128,2048]{1,0:T(8,128)(2,1)S(1)}, bf16[128,2048]{1,0:T(8,128)(2,1)S(1)}, u32[]{:S(2)}, u32[]{:S(2)}) collective-permute-start(bf16[128,2048]{1,0:T(8,128)(2,1)S(1)} %slice.140), channel_id=1, source_target_pairs={{0,2},{1,3},{2,0},{3,1},{4,6},{5,7},{6,4},{7,5},{8,10},{9,11},{10,... | collective-permute-start | bytes 1572872 | tf_op jit(solution)/shard_map/ppermute | solution.py:1273
  168.9 35.9 %copy-start.31 = (bf16[256,2048]{1,0:T(8,128)(2,1)S(1)}, bf16[256,2048]{1,0:T(8,128)(2,1)}, u32[]{:S(2)}) copy-start(bf16[256,2048]{1,0:T(8,128)(2,1)} %get-tuple-element.223) | copy-start | bytes 3145732
  207.1 274.7 %copy-start.2 = (f32[256,2048]{1,0:T(8,128)}, f32[256,2048]{1,0:T(8,128)S(1)}, u32[]{:S(2)}) copy-start(f32[256,2048]{1,0:T(8,128)S(1)} %get-tuple-element.411) | copy-start | bytes 6291460
  207.1 24.5 %copy-start.5 = (bf16[2,256,2048]{2,1,0:T(8,128)(2,1)S(1)}, bf16[2,256,2048]{2,1,0:T(8,128)(2,1)}, u32[]{:S(2)}) copy-start(bf16[2,256,2048]{2,1,0:T(8,128)(2,1)} %param.35) | copy-start | bytes 6291460
  207.4 25.9 %copy-start.29 = (bf16[256,2048]{1,0:T(8,128)(2,1)}, bf16[256,2048]{1,0:T(8,128)(2,1)S(1)}, u32[]{:S(2)}) copy-start(bf16[256,2048]{1,0:T(8,128)(2,1)S(1)} %multiply_convert_fusion.refs_0_.refs_5_) | copy-start | bytes 3145732
  207.4 20.9 %collective-permute-start.9 = (bf16[256,2048]{1,0:T(8,128)(2,1)S(1)}, bf16[256,2048]{1,0:T(8,128)(2,1)S(1)}, u32[]{:S(2)}, u32[]{:S(2)}) collective-permute-start(bf16[256,2048]{1,0:T(8,128)(2,1)S(1)} %multiply_convert_fusion.refs_0_.refs_5_), channel_id=1, source_target_pairs={{0,2},{1,3},{2,0},{3,1},{4,6},{5,7},{6,4},{7,5},{8,10},{9,11},{10,... | collective-permute-start | bytes 3145736 | tf_op jit(solution)/shard_map/ppermute | solution.py:1273
  208.9 20.9 %collective-permute-start.8 = (bf16[256,2048]{1,0:T(8,128)(2,1)S(1)}, bf16[256,2048]{1,0:T(8,128)(2,1)S(1)}, u32[]{:S(2)}, u32[]{:S(2)}) collective-permute-start(bf16[256,2048]{1,0:T(8,128)(2,1)S(1)} %multiply_convert_fusion.refs_0_.refs_5_), channel_id=1, source_target_pairs={{0,1},{1,0},{2,3},{3,2},{4,5},{5,4},{6,7},{7,6},{8,9},{9,8},{10,11... | collective-permute-start | bytes 3145736 | tf_op jit(solution)/shard_map/ppermute | solution.py:1273
  228.4 14.1 %collective-permute-start.11 = (bf16[128,2048]{1,0:T(8,128)(2,1)S(1)}, bf16[128,2048]{1,0:T(8,128)(2,1)S(1)}, u32[]{:S(2)}, u32[]{:S(2)}) collective-permute-start(bf16[128,2048]{1,0:T(8,128)(2,1)S(1)} %slice.143), channel_id=1, source_target_pairs={{0,1},{1,0},{2,3},{3,2},{4,5},{5,4},{6,7},{7,6},{8,9},{9,8},{10,11... | collective-permute-start | bytes 1572872 | tf_op jit(solution)/shard_map/ppermute | solution.py:1273
  230.8 11.7 %collective-permute-start.10 = (bf16[128,2048]{1,0:T(8,128)(2,1)S(1)}, bf16[128,2048]{1,0:T(8,128)(2,1)S(1)}, u32[]{:S(2)}, u32[]{:S(2)}) collective-permute-start(bf16[128,2048]{1,0:T(8,128)(2,1)S(1)} %slice.142), channel_id=1, source_target_pairs={{0,2},{1,3},{2,0},{3,1},{4,6},{5,7},{6,4},{7,5},{8,10},{9,11},{10,... | collective-permute-start | bytes 1572872 | tf_op jit(solution)/shard_map/ppermute | solution.py:1273
  344.5 43.6 %copy-start.10 = (bf16[256,2048]{1,0:T(8,128)(2,1)S(1)}, bf16[256,2048]{1,0:T(8,128)(2,1)}, u32[]{:S(2)}) copy-start(bf16[256,2048]{1,0:T(8,128)(2,1)} %get-tuple-element.254) | copy-start | bytes 3145732
  437.7 40.9 %copy-start.9 = (bf16[256,2048]{1,0:T(8,128)(2,1)S(1)}, bf16[256,2048]{1,0:T(8,128)(2,1)}, u32[]{:S(2)}) copy-start(bf16[256,2048]{1,0:T(8,128)(2,1)} %get-tuple-element.247) | copy-start | bytes 3145732
  615.9 183.5 %reduce-scatter.5.cloned.1.call-start = ((), (), s32[]{:S(2)}) async-start(), calls=%async_computation.3 | async-start | bytes 5242880 | tf_op jit(solution)/shard_map/reduce_scatter | solution.py:1587
  618.1 129.0 %copy-start.4 = (bf16[2,256,2048]{2,1,0:T(8,128)(2,1)S(1)}, bf16[2,256,2048]{2,1,0:T(8,128)(2,1)}, u32[]{:S(2)}) copy-start(bf16[2,256,2048]{2,1,0:T(8,128)(2,1)} %param.18) | copy-start | bytes 6291460
  618.1 129.0 %copy-start.15 = (bf16[256,2048]{1,0:T(8,128)(2,1)S(1)}, bf16[256,2048]{1,0:T(8,128)(2,1)}, u32[]{:S(2)}) copy-start(bf16[256,2048]{1,0:T(8,128)(2,1)} %get-tuple-element.319) | copy-start | bytes 3145732
  618.1 129.0 %copy-start.16 = (bf16[256,2048]{1,0:T(8,128)(2,1)S(1)}, bf16[256,2048]{1,0:T(8,128)(2,1)}, u32[]{:S(2)}) copy-start(bf16[256,2048]{1,0:T(8,128)(2,1)} %get-tuple-element.322) | copy-start | bytes 3145732
  618.1 129.0 %copy-start.17 = (bf16[256,2048]{1,0:T(8,128)(2,1)S(1)}, bf16[256,2048]{1,0:T(8,128)(2,1)}, u32[]{:S(2)}) copy-start(bf16[256,2048]{1,0:T(8,128)(2,1)} %get-tuple-element.320) | copy-start | bytes 3145732
  618.1 129.0 %copy-start.18 = (bf16[256,2048]{1,0:T(8,128)(2,1)S(1)}, bf16[256,2048]{1,0:T(8,128)(2,1)}, u32[]{:S(2)}) copy-start(bf16[256,2048]{1,0:T(8,128)(2,1)} %get-tuple-element.321) | copy-start | bytes 3145732
  618.1 129.0 %copy-start.49 = (f32[2048]{0:T(1024)S(1)}, f32[2048]{0:T(1024)}, u32[]{:S(2)}) copy-start(f32[2048]{0:T(1024)} %param.19) | copy-start | bytes 24580
  618.2 129.0 %copy-start.53 = (f32[256]{0:T(256)S(1)}, f32[256]{0:T(256)}, u32[]{:S(2)}) copy-start(f32[256]{0:T(256)} %copy-done.52) | copy-start | bytes 3076
  618.2 129.0 %copy-start.55 = (f32[256]{0:T(256)S(1)}, f32[256]{0:T(256)}, u32[]{:S(2)}) copy-start(f32[256]{0:T(256)} %copy-done.54) | copy-start | bytes 3076
  742.0 9.0 %collective-permute-start.12 = (f32[2,2048]{1,0:T(2,128)S(1)}, f32[2,2048]{1,0:T(2,128)S(1)}, u32[]{:S(2)}, u32[]{:S(2)}) collective-permute-start(f32[2,2048]{1,0:T(2,128)S(1)} %slice_convert_fusion), channel_id=1, source_target_pairs={{0,1},{1,0},{2,3},{3,2},{4,5},{5,4},{6,7},{7,6},{8,9},{9,8},{10,11... | collective-permute-start | bytes 49160 | tf_op jit(solution)/shard_map/ppermute | solution.py:1273
  742.0 35.6 %collective-permute-start.14 = (bf16[512,1280]{1,0:T(8,128)(2,1)}, bf16[512,1280]{1,0:T(8,128)(2,1)S(1)}, u32[]{:S(2)}, u32[]{:S(2)}) collective-permute-start(bf16[512,1280]{1,0:T(8,128)(2,1)} %get-tuple-element.362.refs_0_), channel_id=1, source_target_pairs={{0,4},{4,0},{8,12},{12,8},{16,20},{20,16},{24,28},{28,24},{1,5},{5... | collective-permute-start | bytes 3932168 | tf_op jit(solution)/shard_map/ppermute | solution.py:1273
  744.7 32.9 %collective-permute-start.15 = (bf16[512,1280]{1,0:T(8,128)(2,1)}, bf16[512,1280]{1,0:T(8,128)(2,1)}, u32[]{:S(2)}, u32[]{:S(2)}) collective-permute-start(bf16[512,1280]{1,0:T(8,128)(2,1)} %get-tuple-element.363.refs_1_), channel_id=1, source_target_pairs={{0,4},{4,0},{8,12},{12,8},{16,20},{20,16},{24,28},{28,24},{1,5},{5... | collective-permute-start | bytes 3932168 | tf_op jit(solution)/shard_map/ppermute | solution.py:1273
  744.7 39.5 %collective-permute-start.17 = (bf16[1280,512]{1,0:T(8,128)(2,1)}, bf16[1280,512]{1,0:T(8,128)(2,1)}, u32[]{:S(2)}, u32[]{:S(2)}) collective-permute-start(bf16[1280,512]{1,0:T(8,128)(2,1)} %get-tuple-element.367), channel_id=1, source_target_pairs={{8,0},{12,4},{16,24},{20,28},{9,1},{13,5},{17,25},{21,29},{10,2},{... | collective-permute-start | bytes 3932168 | tf_op jit(solution)/shard_map/ppermute | solution.py:1537
  747.1 3.2 copy-start.35
  747.2 3.9 copy-start.6
  747.2 3.9 copy-start.7
  747.2 3.9 copy-start.19
  747.2 3.9 copy-start.20
  750.4 17.3 %collective-permute-start.18 = (bf16[128,1536]{1,0:T(8,128)(2,1)S(1)}, bf16[128,1536]{1,0:T(8,128)(2,1)}, u32[]{:S(2)}, u32[]{:S(2)}) collective-permute-start(bf16[128,1536]{1,0:T(8,128)(2,1)S(1)} %copy-done.35), channel_id=1, source_target_pairs={{0,4},{4,0},{8,12},{12,8},{16,20},{20,16},{24,28},{28,24},{1,5},{5... | collective-permute-start | bytes 1179656 | tf_op jit(solution)/shard_map/ppermute | solution.py:1273
  751.0 17.3 %collective-permute-start.19 = (bf16[128,1536]{1,0:T(8,128)(2,1)}, bf16[128,1536]{1,0:T(8,128)(2,1)}, u32[]{:S(2)}, u32[]{:S(2)}) collective-permute-start(bf16[128,1536]{1,0:T(8,128)(2,1)} %get-tuple-element.385.refs_5_), channel_id=1, source_target_pairs={{0,4},{4,0},{8,12},{12,8},{16,20},{20,16},{24,28},{28,24},{1,5},{5... | collective-permute-start | bytes 1179656 | tf_op jit(solution)/shard_map/ppermute | solution.py:1273
  761.0 6.8 copy-start.33
  761.0 7.3 copy-start.34
  761.0 8.6 %copy-start.47 = (bf16[176,640]{1,0:T(8,128)(2,1)S(1)}, bf16[176,640]{1,0:T(8,128)(2,1)}, u32[]{:S(2)}) copy-start(bf16[176,640]{1,0:T(8,128)(2,1)} %get-tuple-element.366) | copy-start | bytes 675844
  767.7 1.8 collective-permute-start.20
  768.2 1.9 collective-permute-start.21
  769.6 19.4 %collective-permute-start.16 = (bf16[176,640]{1,0:T(8,128)(2,1)S(1)}, bf16[176,640]{1,0:T(8,128)(2,1)S(1)}, u32[]{:S(2)}, u32[]{:S(2)}) collective-permute-start(bf16[176,640]{1,0:T(8,128)(2,1)S(1)} %copy-done.47), channel_id=1, source_target_pairs={{0,4},{4,0},{8,12},{12,8},{16,20},{20,16},{24,28},{28,24},{1,5},{5... | collective-permute-start | bytes 675848 | tf_op jit(solution)/shard_map/ppermute | solution.py:1273
  770.2 17.6 %collective-permute-start.13 = (f32[2,2048]{1,0:T(2,128)S(1)}, f32[2,2048]{1,0:T(2,128)S(1)}, u32[]{:S(2)}, u32[]{:S(2)}) collective-permute-start(f32[2,2048]{1,0:T(2,128)S(1)} %fusion.58), channel_id=1, source_target_pairs={{0,2},{1,3},{2,0},{3,1},{4,6},{5,7},{6,4},{7,5},{8,10},{9,11},{10,... | collective-permute-start | bytes 49160 | tf_op jit(solution)/shard_map/ppermute | solution.py:1273
  777.6 6.7 copy-start.27
  784.4 3.3 copy-start.8
  784.4 9.4 %collective-permute-start.22 = (bf16[1280,512]{1,0:T(8,128)(2,1)S(1)}, bf16[1280,512]{1,0:T(8,128)(2,1)}, u32[]{:S(2)}, u32[]{:S(2)}) collective-permute-start(bf16[1280,512]{1,0:T(8,128)(2,1)S(1)} %broadcast_select_fusion.refs_0_), channel_id=1, source_target_pairs={{0,4},{4,0},{8,12},{12,8},{16,20},{20,16},{24,28},{28,24},{1,5},{5... | collective-permute-start | bytes 3932168 | tf_op jit(solution)/shard_map/ppermute | solution.py:1273
  793.8 4.1 copy-start.1
  (27 other events, 51.2 us)
Sparse Core Ops, SparseCore 0:
  616.0 76.9 reduce-scatter.2
  696.2 51.4 reduce-scatter.4

commit v6 on v5

--- a/solution.py
+++ b/solution.py
@@ -76,7 +76,7 @@
             ref[:, column] = value[start : start + count]
 
 
-def rec_forward_kernel(layout, length, *refs):
+def rec_forward_kernel(layout, wait_late, length, *refs):
     x_pieces, refs = refs[: len(layout)], refs[len(layout) :]
     w_both, taps, conv_bias, w_gates, ga_bias, gi_bias, decay_param, w_out = refs[:8]
     branch = refs[-1]
@@ -119,6 +119,7 @@
         return 0
 
     lax.fori_loop(0, pieces, conv_piece, 0)
+    wait_late()
     gates_pre[...] = dot_nn(conv[0], w_gates[...])
     limit = length[...]
 
@@ -331,6 +332,7 @@
 
 def weight_grad_kernel(by_rows, nlefts, nrights, exchange, *refs):
     lefts, rights = refs[:nlefts], refs[nlefts : nlefts + nrights]
+    arrived, refs = refs[-1], refs[:-1]
     if exchange:
         first, second, left, right, sent, got, send, recv = refs[-8:]
     else:
@@ -354,7 +356,18 @@
     elif not by_rows:
         assemble(right, rights)
     else:
-        pl.when(step == 0)(functools.partial(assemble, right, rights))
+
+        @pl.when(step == 0)
+        def _():
+            at, loads = 0, []
+            for ref in rights:
+                place = right.at[pl.ds(at, ref.shape[0])]
+                loads.append(pltpu.make_async_copy(ref, place, arrived.at[len(loads)]))
+                loads[-1].start()
+                at += ref.shape[0]
+            for load in loads:
+                load.wait()
+
     total = lax.dot_general(left[...], right[...], (((0,), (0,)), ((), ())), preferred_element_type=f32)
     if not exchange:
         out[...] = total.astype(bf16)
@@ -452,36 +465,39 @@
         rows, model = shard.shape
         self.operands = [shard]
         self.outputs = [jax.ShapeDtypeStruct((count, model), bf16) for count in (rows, rows, rows // 2, rows // 2)]
-        self.scratch = [pltpu.SemaphoreType.DMA((4,)), pltpu.SemaphoreType.DMA((4,))]
+        self.scratch = [pltpu.SemaphoreType.DMA((6,)), pltpu.SemaphoreType.DMA((6,))]
 
     def copies(self, ins, outs, scratch):
         (shard,), (by_x, by_y, far_a, far_b), (send, recv) = ins, outs, scratch
         half = far_a.shape[0]
+        low, high = pl.ds(0, half), pl.ds(half, half)
         x, y = neighbours()
         return (
-            lambda: remote(shard, by_x, send, recv, 0, x),
-            lambda: remote(shard, by_y, send, recv, 1, y),
-            lambda: remote(by_x.at[pl.ds(0, half)], far_a, send, recv, 2, y),
-            lambda: remote(by_y.at[pl.ds(half, half)], far_b, send, recv, 3, x),
+            lambda: remote(shard.at[low], by_x.at[low], send, recv, 0, x),
+            lambda: remote(shard.at[high], by_y.at[high], send, recv, 1, y),
+            lambda: remote(shard.at[high], by_x.at[high], send, recv, 2, x),
+            lambda: remote(shard.at[low], by_y.at[low], send, recv, 3, y),
+            lambda: remote(by_x.at[low], far_a, send, recv, 4, y),
+            lambda: remote(by_y.at[high], far_b, send, recv, 5, x),
         )
 
     def begin(self, *refs):
-        for copy in self.copies(*refs)[:2]:
+        for copy in self.copies(*refs)[:4]:
             copy().start()
 
     def middle(self, *refs):
         copies = self.copies(*refs)
         copies[0]().wait_recv()
         copies[1]().wait_recv()
-        copies[2]().start()
-        copies[3]().start()
+        copies[4]().start()
+        copies[5]().start()
 
     def end(self, *refs):
         copies = self.copies(*refs)
         copies[0]().wait_send()
         copies[1]().wait_send()
-        copies[2]().wait()
-        copies[3]().wait()
+        for at in (2, 3, 4, 5):
+            copies[at]().wait()
 
     def devices(self):
         return neighbours()
@@ -817,16 +833,26 @@
             @pl.when(step == 0)
             def _():
                 devices = (other_core(),) if pair else ()
-                for kind in (GatherHost, ScatterHost, PipeHost):
-                    kinds = [host for host in hosts if isinstance(host, kind)]
-                    if kinds and not (kind is ScatterHost and any(isinstance(host, GatherHost) for host in hosts)):
-                        devices += tuple(kinds[0].devices())
-                if chips:
-                    devices += tuple(chip_partners())
+                if any(isinstance(host, (GatherHost, ScatterHost)) for host in hosts):
+                    devices += tuple(neighbours())
+                between = chips or any(isinstance(host, PipeHost) for host in hosts)
+                if between:
+                    devices += chip_partners()[:1]
                 barrier = pltpu.get_barrier_semaphore()
                 for device in devices:
                     pl.semaphore_signal(barrier, inc=1, device_id=device, device_id_type=MESH)
-                pl.semaphore_wait(barrier, len(devices))
+                if between:
+
+                    @pl.when(chip_is_inner())
+                    def _():
+                        pl.semaphore_signal(barrier, inc=1, device_id=chip_partners()[1], device_id_type=MESH)
+                        pl.semaphore_wait(barrier, len(devices) + 1)
+
+                    @pl.when(jnp.logical_not(chip_is_inner()))
+                    def _():
+                        pl.semaphore_wait(barrier, len(devices))
+                else:
+                    pl.semaphore_wait(barrier, len(devices))
                 for host, there in zip(hosts, host_refs):
                     host.begin(*there)
 
@@ -849,6 +875,8 @@
         if hosts:
 
             for host, there in list(zip(hosts, host_refs))[::-1]:
+                if late and not isinstance(host, PipeHost):
+                    continue
                 for at in host.slots() if isinstance(host, PipeHost) else (middle,):
 
                     @pl.when(step == at)
@@ -860,6 +888,13 @@
             def _():
                 for load in second:
                     pltpu.make_async_copy(*load).wait()
+
+            for host, there in zip(hosts, host_refs):
+                if not isinstance(host, PipeHost):
+
+                    @pl.when(step == middle)
+                    def _(host=host, there=there):
+                        host.middle(*there)
 
         kernel(*([wait_late] if late else []), *own_ins, *own_outs, *own_scratch)
         if hosts:
@@ -948,6 +983,7 @@
         ],
         "rec_forward",
         37,
+        late=tuple(1 + len(x) + at for at in (3, 7)),
         **more,
     )
 
@@ -1074,13 +1110,16 @@
     if exchange:
         outs = [(jax.ShapeDtypeStruct(block, bf16), pl.BlockSpec(block, lambda step: (0, 0)))] * 2
         scratch += [pltpu.VMEM((2,) + block, bf16)] * 2 + [pltpu.SemaphoreType.DMA((2,))] * 2
+        scratch.append(pltpu.SemaphoreType.DMA((len(rights),)))
     else:
+        scratch.append(pltpu.SemaphoreType.DMA((len(rights),)))
         whole_out = jax.ShapeDtypeStruct((rows, columns), bf16)
         outs = [(whole_out, pl.BlockSpec(block, lambda step: (step, 0) if by_rows else (0, step)))]
     return call(
         functools.partial(weight_grad_kernel, by_rows, len(lefts), len(rights), exchange),
         (tiled // tile,),
-        [(v, cut(v, by_rows)) for v in lefts] + [(v, cut(v, not by_rows)) for v in rights],
+        [(v, cut(v, by_rows)) for v in lefts]
+        + [(v, ANY if by_rows and len(rights) > 1 else cut(v, not by_rows)) for v in rights],
         outs,
         scratch,
         "weight_grad",
@@ -1447,11 +1486,11 @@
     starts = [normalize(resid[s], norm1_gain).astype(bf16) for s in seqs]
     piece, model = starts[0].shape
     seq_in = [gather(starts[0])]
-    out, (second,) = run(rec_forward, limits[0], seq_in[0], forward_params, hosts=[GatherHost(starts[1])], middle=3)
+    out, (second,) = run(rec_forward, limits[0], seq_in[0], forward_params, hosts=[GatherHost(starts[1])], middle=1)
     seq_in.append(second)
     forward = [out]
     out, (branch,) = run(
-        rec_forward, limits[1], seq_in[1], forward_params, hosts=[ScatterHost(out[10:])], middle=2, before=(out[9],)
+        rec_forward, limits[1], seq_in[1], forward_params, hosts=[ScatterHost(out[10:])], middle=1, before=(out[9],)
     )
     forward.append(out)
     mixed = [out[0] for out in forward]
@@ -1469,14 +1508,14 @@
     seq_mid.append(gather(mid))
     forward_shared, (found,) = run(
         mlp_forward, 1, count, seq_mid[1], w_gate, w_up, w_down, forward_shared[:3],
-        hosts=[GatherHost(cotangent[0])], middle=3,
+        hosts=[GatherHost(cotangent[0])], middle=2,
     )
     mlp_part.append(forward_shared[3])
     cot_seq = [found]
     hidden, gate_low, up_low = forward_shared[:3]
     backward, (found,) = run(
         mlp_backward, 0, count, cot_seq[0], gate_low, up_low, w_gate, w_up, w_down, (),
-        hosts=[GatherHost(cotangent[1])], middle=3,
+        hosts=[GatherHost(cotangent[1])], middle=2,
     )
     cot_seq.append(found)
 
@@ -1503,12 +1542,12 @@
     enter("up", grad_up)
     out, (second_seq,) = run(
         rec_backward, limits[0], 0, count, first_seq, seq_in[0], backward_params, saved[0], (),
-        hosts=[GatherHost(second.astype(bf16))], middle=3, before=(grad_up[0],), budget=4,
+        hosts=[GatherHost(second.astype(bf16))], middle=1, before=(grad_up[0],), budget=4,
     )
     sums, gain1 = out[2], out[3]
     out, (d_in,) = run(
         rec_backward, limits[1], 1, count, second_seq, seq_in[1], backward_params, saved[1], out[:2],
-        hosts=[ScatterHost(out[4:])], middle=2, budget=4,
+        hosts=[ScatterHost(out[4:])], middle=1, budget=4,
     )
     d_both, d_gates = out[:2]
     input_grad = [(first + normalize_back(resid[0], norm1_gain, d_in)[0]).astype(bf16)]
@@ -1517,6 +1556,18 @@
     flat_resid = [p for pieces in (first_seq, second_seq) for p in pieces]
     grad_in, _ = run(weight_grad, flat_in, [d_both])
     conv = [part[4] for part in saved]
+    mlp_total = [
+        lax.psum_scatter(flat(tied(v, grad_in[0])), "mp", scatter_dimension=0, tiled=True) for v in mlp_part
+    ]
+
+    def finish_output(*after):
+        totals = lax.optimization_barrier((*mlp_total, *after))[:count]
+        return jnp.stack([(resid_mid[s] + totals[s].astype(f32)).astype(bf16) for s in seqs])
+
+    def finish_input(d_in):
+        last = (second + normalize_back(resid[1], norm1_gain, d_in)[0]).astype(bf16)
+        return jnp.stack(input_grad + [last])
+
     if piped:
 
         def join(prefix, by_rows=True, ways=1):
@@ -1537,8 +1588,10 @@
         came = lax.ppermute(found["out"], "dp", pairs)
         totals_down, totals_gate, totals_up = (join(name) for name in ("down", "gate", "up"))
         totals_in = join("in", ways=2)
+        input_grad = finish_input(d_in)
         came = lax.optimization_barrier((came, totals_down, totals_gate, totals_up, totals_in[0]))[0]
         pipe.done["out"] = jnp.where(chip_is_inner(), found["out"], came)
+        block_out = finish_output(pipe.done["out"])
         totals_out = join("out", by_rows=False)
         pack, other = found["pack"].astype(f32), swap(found["pack"], "dp", 1).astype(f32)
         mine = core_index() == 0
@@ -1553,7 +1606,7 @@
             gains = gains + swap(gains, "mp", bit)
     else:
         grad_out, _ = run(weight_grad, mixed, flat_resid, False, before=(grad_in[0],))
-        d_in = scatter(out[4:])
+        input_grad, block_out = finish_input(scatter(out[4:])), finish_output()
         totals_down, totals_gate, totals_up, totals_in, totals_out = (
             jnp.split(lax.psum(v[0], "dp").astype(f32), ways, axis=1)
             for v, ways in ((grad_down, 1), (grad_gate, 1), (grad_up, 1), (grad_in, 2), (grad_out, 1))
@@ -1572,8 +1625,6 @@
             ),
             "dp",
         )
-    input_grad.append((second + normalize_back(resid[1], norm1_gain, d_in)[0]).astype(bf16))
-    input_grad = jnp.stack(input_grad)
     grad_gate_a_weight, grad_gate_i_weight, vectors, gains = (
         v.astype(f32) for v in (full_ga, full_gi, vectors, gains)
     )
@@ -1583,11 +1634,6 @@
     )
     grad_w_out = totals_out[0][:true_width]
     grad_w_branch, grad_w_input = (v[:, :true_width] for v in totals_in)
-    mlp_total = [
-        lax.psum_scatter(flat(tied(v, grad_in[0])), "mp", scatter_dimension=0, tiled=True) for v in mlp_part
-    ]
-    block_out = jnp.stack([(resid_mid[s] + mlp_total[s].astype(f32)).astype(bf16) for s in seqs])
-
     return (
         block_out,
         input_grad,

time: 820 us -> 801 us (0.977)
  Pallas kernels: 630 us -> 616 us
    pallas_call x18, Pallas kernels: 630 us -> 616 us  [call(): pl.pallas_call(body, out_shape=tuple((shape for shape, _ in outs)) + tupl...]
where the time goes in v6:
time: 801 us; the launch traced here: 791 us
  Pallas kernels  616 us (77%)
  waiting for transfers between devices  75.1 us (9%)
  other arithmetic  45.2 us (6%)
  local copies, waits for them, and re-layouts  21.3 us (3%)
  starting transfers between devices  18.3 us (2%)
  between operations  15.3 us (2%)
    pallas_call x18, Pallas kernels, call(): pl.pallas_call(body, out_shape=tuple((shape for shape, _ in outs)) + tupl...  616 us
    ppermute x22, waiting for transfers between devices, swap(): return lax.ppermute(value, axis, [(i, i ^ bit) for i in range(size)])  75 us
  transfers between devices with their start and end apart: 25, of which 9 were waited for; matrix products, arithmetic and copies ran while one was open for 4% of the time, Pallas kernels for 19%

profile of v6, /device:TPU:9, one launch (start us, length us, event | category | flops | bytes accessed | tf_op | source)
XLA Modules:
  0.0 791.1 jit_solution(17833850379393110326)
XLA Ops:
  7.3 2.2 fusion.40
  9.5 1.4 fusion.34
  10.9 1.3 collective-permute-start.1
  12.2 1.2 collective-permute-start
  13.5 8.4 %fusion.44.refs_9_.refs_14_ = bf16[640,1280]{1,0:T(8,128)(2,1)} fusion(bf16[160,160]{1,0:T(8,128)(2,1)S(1)} %get-tuple-element.434, bf16[160,160]{1,0:T(8,128)(2,1)S(1)} %get-tuple-element.435, bf16[160,160]{1,0:T(8,128)(2,1)S(1)} %get-tuple-element.433, bf16[160,160]{1,0:T(8,128)(2,1)S(1)} %get-tuple-element.432, ...), kind=kLoop, calls=%fused_computation.76 | loop fusion | flops 40960000 | bytes 2048000 | tf_op jit(solution)/shard_map/concatenate | solution.py:1449
  24.9 10.2 %collective-permute-done.1.refs_3_.refs_8_.refs_2_ = bf16[256,2048]{1,0:T(8,128)(2,1)S(1)} collective-permute-done((bf16[256,2048]{1,0:T(8,128)(2,1)S(1)}, bf16[256,2048]{1,0:T(8,128)(2,1)S(1)}, u32[]{:S(2)}, u32[]{:S(2)}) %collective-permute-start.1) | collective-permute-done | bytes 1048608 | tf_op jit(solution)/shard_map/ppermute | solution.py:1312
  35.1 1.3 collective-permute-start.3
  36.4 1.3 collective-permute-start.2
  39.0 2.3 copy-done.24
  41.3 5.7 collective-permute-done.3.refs_5_.refs_10_.refs_4_
  47.0 1.1 collective-permute-done.2.refs_4_.refs_9_.refs_3_
  48.1 1.2 broadcast_in_dim.16.refs_0_
  49.3 38.2 %rec_forward.2 = (bf16[4,256,640]{2,1,0:T(8,128)(2,1)}, f32[4,256,640]{2,1,0:T(8,128)}, f32[4,256,640]{2,1,0:T(8,128)}, f32[4,256,640]{2,1,0:T(8,128)}, f32[4,25...) custom-call(s32[8,128]{1,0:T(8,128)} %broadcast_in_dim.16.refs_0_, ...), custom_call_target="tpu_custom_call" | custom-call | flops 21275000832 | bytes 65536 | tf_op jit(solution)/shard_map/rec_forward/pallas_call | solution.py:912
  87.5 1.2 broadcast_in_dim.21.refs_0_
  88.8 37.9 %rec_forward.3 = (bf16[4,256,640]{2,1,0:T(8,128)(2,1)}, f32[4,256,640]{2,1,0:T(8,128)}, f32[4,256,640]{2,1,0:T(8,128)}, f32[4,256,640]{2,1,0:T(8,128)}, f32[4,25...) custom-call(s32[8,128]{1,0:T(8,128)} %broadcast_in_dim.21.refs_0_, ...), custom_call_target="tpu_custom_call" | custom-call | flops 21275000832 | bytes 65536 | tf_op jit(solution)/shard_map/rec_forward/pallas_call | solution.py:912
  126.7 2.2 multiply_reduce_fusion.5
  129.3 0.9 collective-permute-start.5
  130.9 18.9 %collective-permute-done.5.refs_2_ = bf16[256,2048]{1,0:T(8,128)(2,1)S(1)} collective-permute-done((bf16[256,2048]{1,0:T(8,128)(2,1)S(1)}, bf16[256,2048]{1,0:T(8,128)(2,1)S(1)}, u32[]{:S(2)}, u32[]{:S(2)}) %collective-permute-start.5) | collective-permute-done | bytes 1048608 | tf_op jit(solution)/shard_map/ppermute | solution.py:1312
  149.8 0.9 collective-permute-start.7
  150.7 0.8 collective-permute-start.6
  151.5 11.3 %collective-permute-done.7.refs_4_ = bf16[128,2048]{1,0:T(8,128)(2,1)S(1)} collective-permute-done((bf16[128,2048]{1,0:T(8,128)(2,1)S(1)}, bf16[128,2048]{1,0:T(8,128)(2,1)S(1)}, u32[]{:S(2)}, u32[]{:S(2)}) %collective-permute-start.7) | collective-permute-done | bytes 524320 | tf_op jit(solution)/shard_map/ppermute | solution.py:1312
  162.8 0.8 copy-done.63
  163.7 35.2 %mlp_forward.2 = (bf16[8,256,1536]{2,1,0:T(8,128)(2,1)}, bf16[8,256,1536]{2,1,0:T(8,128)(2,1)}, bf16[8,256,1536]{2,1,0:T(8,128)(2,1)}, bf16[4,256,2048]{2,1,0:T(...) custom-call(bf16[256,2048]{1,0:T(8,128)(2,1)} %copy-done.26, bf16[256,2048]{1,0:T(8,128)(2,1)} %copy-done.44, ...), custom_call_target="tpu_custom_call" | custom-call | flops 17250000896 | bytes 65536 | tf_op jit(solution)/shard_map/mlp_forward/pallas_call | solution.py:912
  199.0 2.2 multiply_reduce_fusion.4
  201.9 1.2 collective-permute-start.8
  203.0 18.6 %collective-permute-done.9.refs_2_.refs_7_ = bf16[256,2048]{1,0:T(8,128)(2,1)S(1)} collective-permute-done((bf16[256,2048]{1,0:T(8,128)(2,1)S(1)}, bf16[256,2048]{1,0:T(8,128)(2,1)S(1)}, u32[]{:S(2)}, u32[]{:S(2)}) %collective-permute-start.9) | collective-permute-done | bytes 1048608 | tf_op jit(solution)/shard_map/ppermute | solution.py:1312
  221.8 0.8 copy-done.45
  222.6 0.9 copy-done.46
  224.1 1.6 slice_bitcast_fusion
  225.7 8.7 %collective-permute-done.11.refs_4_.refs_9_ = bf16[128,2048]{1,0:T(8,128)(2,1)S(1)} collective-permute-done((bf16[128,2048]{1,0:T(8,128)(2,1)S(1)}, bf16[128,2048]{1,0:T(8,128)(2,1)S(1)}, u32[]{:S(2)}, u32[]{:S(2)}) %collective-permute-start.11) | collective-permute-done | bytes 524320 | tf_op jit(solution)/shard_map/ppermute | solution.py:1312
  234.4 0.8 copy-done.65
  235.4 35.1 %mlp_forward.3 = (bf16[8,256,1536]{2,1,0:T(8,128)(2,1)}, bf16[8,256,1536]{2,1,0:T(8,128)(2,1)}, bf16[8,256,1536]{2,1,0:T(8,128)(2,1)}, bf16[4,256,2048]{2,1,0:T(...) custom-call(bf16[256,2048]{1,0:T(8,128)(2,1)} %copy-done.27, ...), custom_call_target="tpu_custom_call", output_to_operand_aliasing={{0}: (8, {}), {1}: (9, {}), {2}: (10, {})} | custom-call | flops 17250000896 | bytes 65536 | tf_op jit(solution)/shard_map/mlp_forward/pallas_call | solution.py:912
  270.6 37.2 %mlp_backward.2 = (bf16[8,256,1536]{2,1,0:T(8,128)(2,1)}, bf16[8,256,1536]{2,1,0:T(8,128)(2,1)}, bf16[256,2048]{1,0:T(8,128)(2,1)}, bf16[256,2048]{1,0:T(8,128)(...) custom-call(bf16[256,2048]{1,0:T(8,128)(2,1)} %get-tuple-element.422, ...), custom_call_target="tpu_custom_call" | custom-call | flops 18400000000 | bytes 65536 | tf_op jit(solution)/shard_map/mlp_backward/pallas_call | solution.py:912
  307.8 26.0 %weight_grad.4 = (bf16[384,2048]{1,0:T(8,128)(2,1)}, bf16[384,2048]{1,0:T(8,128)(2,1)}) custom-call(bf16[2048,1536]{1,0:T(8,128)(2,1)} %bitcast.81, bf16[256,2048]{1,0:T(8,128)(2,1)} %get-tuple-element.422.refs_11_.refs_0_.refs_1_, bf16[256,2048]{1,0:T(8,128)(2,1)} %get-tuple-element.231.refs_1_.refs_2_, ...), custom_call_target="tpu_custom_call" | custom-call | flops 11500000256 | bytes 65536 | tf_op jit(solution)/shard_map/weight_grad/pallas_call | solution.py:912
  333.8 43.1 %mlp_backward.3 = (bf16[8,256,1536]{2,1,0:T(8,128)(2,1)}, bf16[8,256,1536]{2,1,0:T(8,128)(2,1)}, bf16[256,2048]{1,0:T(8,128)(2,1)}, bf16[256,2048]{1,0:T(8,128)(...) custom-call(bf16[256,2048]{1,0:T(8,128)(2,1)} %get-tuple-element.423, ...), custom_call_target="tpu_custom_call", output_to_operand_aliasing={{0}: (10, {}), {1}: (11, {})} | custom-call | flops 18400000000 | bytes 65536 | tf_op jit(solution)/shard_map/mlp_backward/pallas_call | solution.py:912
  376.9 3.2 multiply_reduce_fusion.1
  380.1 2.8 fusion.60
  382.9 42.4 %weight_grad.5 = (bf16[512,1536]{1,0:T(8,128)(2,1)}, bf16[512,1536]{1,0:T(8,128)(2,1)}, bf16[256,2048]{1,0:T(8,128)(2,1)}, bf16[256,2048]{1,0:T(8,128)(2,1)}, bf...) custom-call(bf16[256,2048]{1,0:T(8,128)(2,1)} %copy-done.26, ...), custom_call_target="tpu_custom_call" | custom-call | flops 11500000256 | bytes 65536 | tf_op jit(solution)/shard_map/weight_grad/pallas_call | solution.py:912
  425.3 41.1 %weight_grad.6 = (bf16[512,1536]{1,0:T(8,128)(2,1)}, bf16[512,1536]{1,0:T(8,128)(2,1)}, bf16[256,2048]{1,0:T(8,128)(2,1)}, bf16[256,2048]{1,0:T(8,128)(2,1)}, bf...) custom-call(bf16[256,2048]{1,0:T(8,128)(2,1)} %copy-done.26, ...), custom_call_target="tpu_custom_call" | custom-call | flops 11500000256 | bytes 65536 | tf_op jit(solution)/shard_map/weight_grad/pallas_call | solution.py:912
  466.4 3.2 multiply_reduce_fusion
  469.5 2.8 fusion.59
  472.3 41.8 %rec_backward.2 = (bf16[8,256,1280]{2,1,0:T(8,128)(2,1)}, bf16[8,256,1280]{2,1,0:T(8,128)(2,1)}, f32[8,8,640]{2,1,0:T(8,128)}, f32[8,2048]{1,0:T(8,128)}, bf16[2...) custom-call(s32[8,128]{1,0:T(8,128)} %broadcast_in_dim.16.refs_0_, ...), custom_call_target="tpu_custom_call" | custom-call | flops 24725000192 | bytes 65536 | tf_op jit(solution)/shard_map/rec_backward/pallas_call | solution.py:912
  514.1 41.9 %rec_backward.3 = (bf16[8,256,1280]{2,1,0:T(8,128)(2,1)}, bf16[8,256,1280]{2,1,0:T(8,128)(2,1)}, f32[8,8,640]{2,1,0:T(8,128)}, f32[8,2048]{1,0:T(8,128)}, bf16[2...) custom-call(s32[8,128]{1,0:T(8,128)} %broadcast_in_dim.21.refs_0_, ...), custom_call_target="tpu_custom_call", output_to_operand_aliasing={{0}: (24, {}), {1}: (25, {})} | custom-call | flops 24725000192 | bytes 65536 | tf_op jit(solution)/shard_map/rec_backward/pallas_call | solution.py:912
  556.0 43.3 %weight_grad.7 = (bf16[512,1280]{1,0:T(8,128)(2,1)}, bf16[512,1280]{1,0:T(8,128)(2,1)}, bf16[128,1536]{1,0:T(8,128)(2,1)}, bf16[128,1536]{1,0:T(8,128)(2,1)}, bf...) custom-call(bf16[256,2048]{1,0:T(8,128)(2,1)} %copy-done.28, ...), custom_call_target="tpu_custom_call" | custom-call | flops 11500000256 | bytes 65536 | tf_op jit(solution)/shard_map/weight_grad/pallas_call | solution.py:912
  599.4 0.7 slice.136
  600.2 0.7 slice.137
  601.6 123.7 %last_grad.1 = (bf16[512,1280]{1,0:T(8,128)(2,1)}, bf16[512,1280]{1,0:T(8,128)(2,1)}, bf16[128,1536]{1,0:T(8,128)(2,1)}, bf16[128,1536]{1,0:T(8,128)(2,1)}, bf16...) custom-call(bf16[1024,640]{1,0:T(8,128)(2,1)} %bitcast.86, ...), custom_call_target="tpu_custom_call" | custom-call | flops 69000003584 | bytes 65536 | tf_op jit(solution)/shard_map/last_grad/pallas_call | solution.py:912
  725.3 0.8 slice_convert_fusion
  726.1 2.4 collective-permute-start.12
  728.4 1.4 collective-permute-start.17
  729.9 3.2 fusion.35
  733.9 3.3 fusion.55
  737.2 6.4 join_pieces.5
  743.6 6.7 join_pieces.6
  751.0 0.8 fusion.58
  752.8 1.6 collective-permute-start.20
  754.4 6.4 join_pieces.7
  760.8 5.7 join_pieces.8
  768.0 1.5 pad_maximum_fusion.1
  771.9 1.0 copy.47
  773.4 1.0 copy.48
  775.6 3.9 join_pieces.9
  779.5 2.3 fusion.54
  782.5 1.5 pad_maximum_fusion
  (197 shorter events, 16.5 us)
Async XLA Ops:
  7.2 772.3 %reduce-scatter.3.cloned.1.call-start = ((), (), s32[]{:S(2)}) async-start(), calls=%async_computation.2 | async-start | bytes 5242880 | tf_op jit(solution)/shard_map/reduce_scatter | solution.py:1560
  9.5 4.0 copy-start.38
  9.5 4.0 copy-start.39
  10.9 24.2 %copy-start.28 = (bf16[256,2048]{1,0:T(8,128)(2,1)}, bf16[256,2048]{1,0:T(8,128)(2,1)S(1)}, u32[]{:S(2)}) copy-start(bf16[256,2048]{1,0:T(8,128)(2,1)S(1)} %get-tuple-element.420.refs_1_.refs_6_.refs_0_) | copy-start | bytes 3145732
  10.9 11.1 %copy-start.50 = (f32[640]{0:T(1024)S(1)}, f32[640]{0:T(1024)}, u32[]{:S(2)}) copy-start(f32[640]{0:T(1024)} %param.28) | copy-start | bytes 7684
  10.9 11.7 %copy-start.56 = (f32[640]{0:T(1024)S(1)}, f32[640]{0:T(1024)}, u32[]{:S(2)}) copy-start(f32[640]{0:T(1024)} %param.23) | copy-start | bytes 7684
  10.9 12.2 %copy-start.57 = (f32[640]{0:T(1024)S(1)}, f32[640]{0:T(1024)}, u32[]{:S(2)}) copy-start(f32[640]{0:T(1024)} %param.25) | copy-start | bytes 7684
  10.9 12.8 %copy-start.58 = (f32[640]{0:T(1024)S(1)}, f32[640]{0:T(1024)}, u32[]{:S(2)}) copy-start(f32[640]{0:T(1024)} %param.27) | copy-start | bytes 7684
  10.9 13.4 %copy-start.59 = (s32[2]{0:T(128)S(1)}, s32[2]{0:T(128)}, u32[]{:S(2)}) copy-start(s32[2]{0:T(128)} %param.34) | copy-start | bytes 28
  10.9 24.1 %collective-permute-start.1 = (bf16[256,2048]{1,0:T(8,128)(2,1)S(1)}, bf16[256,2048]{1,0:T(8,128)(2,1)S(1)}, u32[]{:S(2)}, u32[]{:S(2)}) collective-permute-start(bf16[256,2048]{1,0:T(8,128)(2,1)S(1)} %get-tuple-element.420.refs_1_.refs_6_.refs_0_), channel_id=1, source_target_pairs={{0,2},{1,3},{2,0},{3,1},{4,6},{5,7},{6,4},{7,5},{8,10},{9,11},{10,... | collective-permute-start | bytes 3145736 | tf_op jit(solution)/shard_map/ppermute | solution.py:1312
  12.2 24.1 %collective-permute-start = (bf16[256,2048]{1,0:T(8,128)(2,1)S(1)}, bf16[256,2048]{1,0:T(8,128)(2,1)S(1)}, u32[]{:S(2)}, u32[]{:S(2)}) collective-permute-start(bf16[256,2048]{1,0:T(8,128)(2,1)S(1)} %get-tuple-element.420.refs_1_.refs_6_.refs_0_), channel_id=1, source_target_pairs={{0,1},{1,0},{2,3},{3,2},{4,5},{5,4},{6,7},{7,6},{8,9},{9,8},{10,11... | collective-permute-start | bytes 3145736 | tf_op jit(solution)/shard_map/ppermute | solution.py:1312
  13.5 24.2 %copy-start.22 = (bf16[2048,640]{1,0:T(8,128)(2,1)S(1)}, bf16[2048,640]{1,0:T(8,128)(2,1)}, u32[]{:S(2)}) copy-start(bf16[2048,640]{1,0:T(8,128)(2,1)} %param.20) | copy-start | bytes 7864324
  35.1 11.9 %collective-permute-start.3 = (bf16[128,2048]{1,0:T(8,128)(2,1)S(1)}, bf16[128,2048]{1,0:T(8,128)(2,1)S(1)}, u32[]{:S(2)}, u32[]{:S(2)}) collective-permute-start(bf16[128,2048]{1,0:T(8,128)(2,1)S(1)} %slice.139), channel_id=1, source_target_pairs={{0,1},{1,0},{2,3},{3,2},{4,5},{5,4},{6,7},{7,6},{8,9},{9,8},{10,11... | collective-permute-start | bytes 1572872 | tf_op jit(solution)/shard_map/ppermute | solution.py:1312
  36.4 11.7 %collective-permute-start.2 = (bf16[128,2048]{1,0:T(8,128)(2,1)S(1)}, bf16[128,2048]{1,0:T(8,128)(2,1)S(1)}, u32[]{:S(2)}, u32[]{:S(2)}) collective-permute-start(bf16[128,2048]{1,0:T(8,128)(2,1)S(1)} %slice.138), channel_id=1, source_target_pairs={{0,2},{1,3},{2,0},{3,1},{4,6},{5,7},{6,4},{7,5},{8,10},{9,11},{10,... | collective-permute-start | bytes 1572872 | tf_op jit(solution)/shard_map/ppermute | solution.py:1312
  88.8 37.9 %copy-start.31 = (bf16[256,2048]{1,0:T(8,128)(2,1)S(1)}, bf16[256,2048]{1,0:T(8,128)(2,1)}, u32[]{:S(2)}) copy-start(bf16[256,2048]{1,0:T(8,128)(2,1)} %get-tuple-element.208) | copy-start | bytes 3145732
  129.0 251.1 %copy-start = (f32[256,2048]{1,0:T(8,128)}, f32[256,2048]{1,0:T(8,128)S(1)}, u32[]{:S(2)}) copy-start(f32[256,2048]{1,0:T(8,128)S(1)} %get-tuple-element.417) | copy-start | bytes 6291460
  129.2 34.4 %copy-start.26 = (bf16[256,2048]{1,0:T(8,128)(2,1)}, bf16[256,2048]{1,0:T(8,128)(2,1)S(1)}, u32[]{:S(2)}) copy-start(bf16[256,2048]{1,0:T(8,128)(2,1)S(1)} %multiply_convert_fusion.1.refs_0_) | copy-start | bytes 3145732
  129.3 20.5 %collective-permute-start.5 = (bf16[256,2048]{1,0:T(8,128)(2,1)S(1)}, bf16[256,2048]{1,0:T(8,128)(2,1)S(1)}, u32[]{:S(2)}, u32[]{:S(2)}) collective-permute-start(bf16[256,2048]{1,0:T(8,128)(2,1)S(1)} %multiply_convert_fusion.1.refs_0_), channel_id=1, source_target_pairs={{0,2},{1,3},{2,0},{3,1},{4,6},{5,7},{6,4},{7,5},{8,10},{9,11},{10,... | collective-permute-start | bytes 3145736 | tf_op jit(solution)/shard_map/ppermute | solution.py:1312
  130.2 20.4 %collective-permute-start.4 = (bf16[256,2048]{1,0:T(8,128)(2,1)S(1)}, bf16[256,2048]{1,0:T(8,128)(2,1)S(1)}, u32[]{:S(2)}, u32[]{:S(2)}) collective-permute-start(bf16[256,2048]{1,0:T(8,128)(2,1)S(1)} %multiply_convert_fusion.1.refs_0_), channel_id=1, source_target_pairs={{0,1},{1,0},{2,3},{3,2},{4,5},{5,4},{6,7},{7,6},{8,9},{9,8},{10,11... | collective-permute-start | bytes 3145736 | tf_op jit(solution)/shard_map/ppermute | solution.py:1312
  149.7 13.0 %copy-start.43 = (bf16[256,2048]{1,0:T(8,128)(2,1)}, bf16[256,2048]{1,0:T(8,128)(2,1)S(1)}, u32[]{:S(2)}) copy-start(bf16[256,2048]{1,0:T(8,128)(2,1)S(1)} %collective-permute-done.5.refs_2_) | copy-start | bytes 3145732
  149.8 13.0 %collective-permute-start.7 = (bf16[128,2048]{1,0:T(8,128)(2,1)S(1)}, bf16[128,2048]{1,0:T(8,128)(2,1)S(1)}, u32[]{:S(2)}, u32[]{:S(2)}) collective-permute-start(bf16[128,2048]{1,0:T(8,128)(2,1)S(1)} %slice.141), channel_id=1, source_target_pairs={{0,1},{1,0},{2,3},{3,2},{4,5},{5,4},{6,7},{7,6},{8,9},{9,8},{10,11... | collective-permute-start | bytes 1572872 | tf_op jit(solution)/shard_map/ppermute | solution.py:1312
  150.6 12.2 %copy-start.44 = (bf16[256,2048]{1,0:T(8,128)(2,1)}, bf16[256,2048]{1,0:T(8,128)(2,1)S(1)}, u32[]{:S(2)}) copy-start(bf16[256,2048]{1,0:T(8,128)(2,1)S(1)} %collective-permute-done.4.refs_1_) | copy-start | bytes 3145732
  150.7 12.1 %collective-permute-start.6 = (bf16[128,2048]{1,0:T(8,128)(2,1)S(1)}, bf16[128,2048]{1,0:T(8,128)(2,1)S(1)}, u32[]{:S(2)}, u32[]{:S(2)}) collective-permute-start(bf16[128,2048]{1,0:T(8,128)(2,1)S(1)} %slice.140), channel_id=1, source_target_pairs={{0,2},{1,3},{2,0},{3,1},{4,6},{5,7},{6,4},{7,5},{8,10},{9,11},{10,... | collective-permute-start | bytes 1572872 | tf_op jit(solution)/shard_map/ppermute | solution.py:1312
  163.7 35.2 %copy-start.30 = (bf16[256,2048]{1,0:T(8,128)(2,1)S(1)}, bf16[256,2048]{1,0:T(8,128)(2,1)}, u32[]{:S(2)}) copy-start(bf16[256,2048]{1,0:T(8,128)(2,1)} %get-tuple-element.225) | copy-start | bytes 3145732
  201.2 268.3 %copy-start.2 = (f32[256,2048]{1,0:T(8,128)}, f32[256,2048]{1,0:T(8,128)S(1)}, u32[]{:S(2)}) copy-start(f32[256,2048]{1,0:T(8,128)S(1)} %get-tuple-element.415) | copy-start | bytes 6291460
  201.2 22.9 %copy-start.5 = (bf16[2,256,2048]{2,1,0:T(8,128)(2,1)S(1)}, bf16[2,256,2048]{2,1,0:T(8,128)(2,1)}, u32[]{:S(2)}) copy-start(bf16[2,256,2048]{2,1,0:T(8,128)(2,1)} %param.35) | copy-start | bytes 6291460
  201.5 24.2 %copy-start.27 = (bf16[256,2048]{1,0:T(8,128)(2,1)}, bf16[256,2048]{1,0:T(8,128)(2,1)S(1)}, u32[]{:S(2)}) copy-start(bf16[256,2048]{1,0:T(8,128)(2,1)S(1)} %multiply_convert_fusion.refs_0_.refs_5_) | copy-start | bytes 3145732
  201.5 20.1 %collective-permute-start.9 = (bf16[256,2048]{1,0:T(8,128)(2,1)S(1)}, bf16[256,2048]{1,0:T(8,128)(2,1)S(1)}, u32[]{:S(2)}, u32[]{:S(2)}) collective-permute-start(bf16[256,2048]{1,0:T(8,128)(2,1)S(1)} %multiply_convert_fusion.refs_0_.refs_5_), channel_id=1, source_target_pairs={{0,2},{1,3},{2,0},{3,1},{4,6},{5,7},{6,4},{7,5},{8,10},{9,11},{10,... | collective-permute-start | bytes 3145736 | tf_op jit(solution)/shard_map/ppermute | solution.py:1312
  201.9 19.9 %collective-permute-start.8 = (bf16[256,2048]{1,0:T(8,128)(2,1)S(1)}, bf16[256,2048]{1,0:T(8,128)(2,1)S(1)}, u32[]{:S(2)}, u32[]{:S(2)}) collective-permute-start(bf16[256,2048]{1,0:T(8,128)(2,1)S(1)} %multiply_convert_fusion.refs_0_.refs_5_), channel_id=1, source_target_pairs={{0,1},{1,0},{2,3},{3,2},{4,5},{5,4},{6,7},{7,6},{8,9},{9,8},{10,11... | collective-permute-start | bytes 3145736 | tf_op jit(solution)/shard_map/ppermute | solution.py:1312
  221.7 12.8 %collective-permute-start.11 = (bf16[128,2048]{1,0:T(8,128)(2,1)S(1)}, bf16[128,2048]{1,0:T(8,128)(2,1)S(1)}, u32[]{:S(2)}, u32[]{:S(2)}) collective-permute-start(bf16[128,2048]{1,0:T(8,128)(2,1)S(1)} %slice.143), channel_id=1, source_target_pairs={{0,1},{1,0},{2,3},{3,2},{4,5},{5,4},{6,7},{7,6},{8,9},{9,8},{10,11... | collective-permute-start | bytes 1572872 | tf_op jit(solution)/shard_map/ppermute | solution.py:1312
  223.6 10.9 %collective-permute-start.10 = (bf16[128,2048]{1,0:T(8,128)(2,1)S(1)}, bf16[128,2048]{1,0:T(8,128)(2,1)S(1)}, u32[]{:S(2)}, u32[]{:S(2)}) collective-permute-start(bf16[128,2048]{1,0:T(8,128)(2,1)S(1)} %slice.142), channel_id=1, source_target_pairs={{0,2},{1,3},{2,0},{3,1},{4,6},{5,7},{6,4},{7,5},{8,10},{9,11},{10,... | collective-permute-start | bytes 1572872 | tf_op jit(solution)/shard_map/ppermute | solution.py:1312
  333.8 43.1 %copy-start.10 = (bf16[256,2048]{1,0:T(8,128)(2,1)S(1)}, bf16[256,2048]{1,0:T(8,128)(2,1)}, u32[]{:S(2)}) copy-start(bf16[256,2048]{1,0:T(8,128)(2,1)} %get-tuple-element.256) | copy-start | bytes 3145732
  376.9 3.2 copy-start.13
  425.2 41.1 %copy-start.9 = (bf16[256,2048]{1,0:T(8,128)(2,1)S(1)}, bf16[256,2048]{1,0:T(8,128)(2,1)}, u32[]{:S(2)}) copy-start(bf16[256,2048]{1,0:T(8,128)(2,1)} %get-tuple-element.249) | copy-start | bytes 3145732
  599.3 180.2 %reduce-scatter.5.cloned.1.call-start = ((), (), s32[]{:S(2)}) async-start(), calls=%async_computation.3 | async-start | bytes 5242880 | tf_op jit(solution)/shard_map/reduce_scatter | solution.py:1560
  601.5 128.3 %copy-start.4 = (bf16[2,256,2048]{2,1,0:T(8,128)(2,1)S(1)}, bf16[2,256,2048]{2,1,0:T(8,128)(2,1)}, u32[]{:S(2)}) copy-start(bf16[2,256,2048]{2,1,0:T(8,128)(2,1)} %param.18) | copy-start | bytes 6291460
  601.5 128.3 %copy-start.15 = (bf16[256,2048]{1,0:T(8,128)(2,1)S(1)}, bf16[256,2048]{1,0:T(8,128)(2,1)}, u32[]{:S(2)}) copy-start(bf16[256,2048]{1,0:T(8,128)(2,1)} %get-tuple-element.388) | copy-start | bytes 3145732
  601.6 128.3 %copy-start.16 = (bf16[256,2048]{1,0:T(8,128)(2,1)S(1)}, bf16[256,2048]{1,0:T(8,128)(2,1)}, u32[]{:S(2)}) copy-start(bf16[256,2048]{1,0:T(8,128)(2,1)} %get-tuple-element.391) | copy-start | bytes 3145732
  601.6 128.3 %copy-start.17 = (bf16[256,2048]{1,0:T(8,128)(2,1)S(1)}, bf16[256,2048]{1,0:T(8,128)(2,1)}, u32[]{:S(2)}) copy-start(bf16[256,2048]{1,0:T(8,128)(2,1)} %get-tuple-element.389) | copy-start | bytes 3145732
  601.6 128.3 %copy-start.18 = (bf16[256,2048]{1,0:T(8,128)(2,1)S(1)}, bf16[256,2048]{1,0:T(8,128)(2,1)}, u32[]{:S(2)}) copy-start(bf16[256,2048]{1,0:T(8,128)(2,1)} %get-tuple-element.390) | copy-start | bytes 3145732
  601.6 128.3 %copy-start.49 = (f32[2048]{0:T(1024)S(1)}, f32[2048]{0:T(1024)}, u32[]{:S(2)}) copy-start(f32[2048]{0:T(1024)} %param.19) | copy-start | bytes 24580
  601.6 128.3 %copy-start.53 = (f32[256]{0:T(256)S(1)}, f32[256]{0:T(256)}, u32[]{:S(2)}) copy-start(f32[256]{0:T(256)} %copy-done.52) | copy-start | bytes 3076
  601.6 128.3 %copy-start.55 = (f32[256]{0:T(256)S(1)}, f32[256]{0:T(256)}, u32[]{:S(2)}) copy-start(f32[256]{0:T(256)} %copy-done.54) | copy-start | bytes 3076
  726.1 7.7 collective-permute-start.19
  726.1 40.4 %collective-permute-start.12 = (bf16[1280,512]{1,0:T(8,128)(2,1)}, bf16[1280,512]{1,0:T(8,128)(2,1)}, u32[]{:S(2)}, u32[]{:S(2)}) collective-permute-start(bf16[1280,512]{1,0:T(8,128)(2,1)} %get-tuple-element.357), channel_id=1, source_target_pairs={{8,0},{12,4},{16,24},{20,28},{9,1},{13,5},{17,25},{21,29},{10,2},{... | collective-permute-start | bytes 3932168 | tf_op jit(solution)/shard_map/ppermute | solution.py:1588
  728.4 32.3 %collective-permute-start.17 = (bf16[512,1280]{1,0:T(8,128)(2,1)}, bf16[512,1280]{1,0:T(8,128)(2,1)}, u32[]{:S(2)}, u32[]{:S(2)}) collective-permute-start(bf16[512,1280]{1,0:T(8,128)(2,1)} %get-tuple-element.382.refs_0_), channel_id=1, source_target_pairs={{0,4},{4,0},{8,12},{12,8},{16,20},{20,16},{24,28},{28,24},{1,5},{5... | collective-permute-start | bytes 3932168 | tf_op jit(solution)/shard_map/ppermute | solution.py:1312
  729.8 31.0 %collective-permute-start.18 = (bf16[512,1280]{1,0:T(8,128)(2,1)}, bf16[512,1280]{1,0:T(8,128)(2,1)}, u32[]{:S(2)}, u32[]{:S(2)}) collective-permute-start(bf16[512,1280]{1,0:T(8,128)(2,1)} %get-tuple-element.383.refs_1_), channel_id=1, source_target_pairs={{0,4},{4,0},{8,12},{12,8},{16,20},{20,16},{24,28},{28,24},{1,5},{5... | collective-permute-start | bytes 3932168 | tf_op jit(solution)/shard_map/ppermute | solution.py:1312
  729.9 3.3 copy-start.34
  729.9 3.9 copy-start.35
  729.9 4.0 copy-start.6
  729.9 3.9 copy-start.7
  729.9 3.9 copy-start.19
  729.9 3.9 copy-start.20
  733.2 17.2 %collective-permute-start.13 = (bf16[128,1536]{1,0:T(8,128)(2,1)S(1)}, bf16[128,1536]{1,0:T(8,128)(2,1)}, u32[]{:S(2)}, u32[]{:S(2)}) collective-permute-start(bf16[128,1536]{1,0:T(8,128)(2,1)S(1)} %copy-done.34), channel_id=1, source_target_pairs={{0,4},{4,0},{8,12},{12,8},{16,20},{20,16},{24,28},{28,24},{1,5},{5... | collective-permute-start | bytes 1179656 | tf_op jit(solution)/shard_map/ppermute | solution.py:1312
  733.8 17.1 %collective-permute-start.14 = (bf16[128,1536]{1,0:T(8,128)(2,1)S(1)}, bf16[128,1536]{1,0:T(8,128)(2,1)}, u32[]{:S(2)}, u32[]{:S(2)}) collective-permute-start(bf16[128,1536]{1,0:T(8,128)(2,1)S(1)} %copy-done.35), channel_id=1, source_target_pairs={{0,4},{4,0},{8,12},{12,8},{16,20},{20,16},{24,28},{28,24},{1,5},{5... | collective-permute-start | bytes 1179656 | tf_op jit(solution)/shard_map/ppermute | solution.py:1312
  743.6 6.8 copy-start.32
  743.6 7.3 copy-start.33
  743.6 8.6 %copy-start.47 = (bf16[176,640]{1,0:T(8,128)(2,1)S(1)}, bf16[176,640]{1,0:T(8,128)(2,1)}, u32[]{:S(2)}) copy-start(bf16[176,640]{1,0:T(8,128)(2,1)} %get-tuple-element.396) | copy-start | bytes 675844
  750.4 1.8 collective-permute-start.15
  750.9 1.9 collective-permute-start.16
  752.2 18.5 %collective-permute-start.21 = (bf16[176,640]{1,0:T(8,128)(2,1)S(1)}, bf16[176,640]{1,0:T(8,128)(2,1)S(1)}, u32[]{:S(2)}, u32[]{:S(2)}) collective-permute-start(bf16[176,640]{1,0:T(8,128)(2,1)S(1)} %copy-done.47), channel_id=1, source_target_pairs={{0,4},{4,0},{8,12},{12,8},{16,20},{20,16},{24,28},{28,24},{1,5},{5... | collective-permute-start | bytes 675848 | tf_op jit(solution)/shard_map/ppermute | solution.py:1312
  752.8 16.7 %collective-permute-start.20 = (f32[2,2048]{1,0:T(2,128)S(1)}, f32[2,2048]{1,0:T(2,128)S(1)}, u32[]{:S(2)}, u32[]{:S(2)}) collective-permute-start(f32[2,2048]{1,0:T(2,128)S(1)} %fusion.58), channel_id=1, source_target_pairs={{0,2},{1,3},{2,0},{3,1},{4,6},{5,7},{6,4},{7,5},{8,10},{9,11},{10,... | collective-permute-start | bytes 49160 | tf_op jit(solution)/shard_map/ppermute | solution.py:1312
  760.8 5.7 copy-start.25
  766.7 8.9 %collective-permute-start.22 = (bf16[1280,512]{1,0:T(8,128)(2,1)S(1)}, bf16[1280,512]{1,0:T(8,128)(2,1)}, u32[]{:S(2)}, u32[]{:S(2)}) collective-permute-start(bf16[1280,512]{1,0:T(8,128)(2,1)S(1)} %broadcast_select_fusion.refs_0_), channel_id=1, source_target_pairs={{0,4},{4,0},{8,12},{12,8},{16,20},{20,16},{24,28},{28,24},{1,5},{5... | collective-permute-start | bytes 3932168 | tf_op jit(solution)/shard_map/ppermute | solution.py:1312
  (27 other events, 53.7 us)
Sparse Core Ops, SparseCore 0:
  599.5 76.3 reduce-scatter.2
  679.0 51.7 reduce-scatter.4

commit v7 on v6

--- a/solution.py
+++ b/solution.py
@@ -76,7 +76,7 @@
             ref[:, column] = value[start : start + count]
 
 
-def rec_forward_kernel(layout, wait_late, length, *refs):
+def rec_forward_kernel(layout, seq, wait_late, length, *refs):
     x_pieces, refs = refs[: len(layout)], refs[len(layout) :]
     w_both, taps, conv_bias, w_gates, ga_bias, gi_bias, decay_param, w_out = refs[:8]
     branch = refs[-1]
@@ -121,7 +121,7 @@
     lax.fori_loop(0, pieces, conv_piece, 0)
     wait_late()
     gates_pre[...] = dot_nn(conv[0], w_gates[...])
-    limit = length[...]
+    limit = length[seq]
 
     def scan_piece(i, _):
         base = pl.multiple_of(i * 16, 16)
@@ -169,7 +169,7 @@
     store_block(parts, layout, block, slice(None), x[...])
 
 
-def rec_backward_kernel(layout, nshared, wait_late, length, *refs):
+def rec_backward_kernel(layout, seq, wait_late, length, *refs):
     many = len(layout)
     d_resid_pieces, x_pieces, refs = refs[:many], refs[many : 2 * many], refs[2 * many :]
     w_out, w_both, taps, w_gates, decay_param = refs[:5]
@@ -184,7 +184,7 @@
     lanes = [pl.ds(at, LANES) for at in range(0, width, LANES)]
     row = row_index((SUB, LANES))
     first = (pl.num_programs(0) - 1 - step) * rows
-    limit = length[...]
+    limit = length[seq]
 
     @pl.when(step == 0)
     def _():
@@ -901,7 +901,7 @@
 
             @pl.when(step == steps - 1)
             def _():
-                for host, there in zip(hosts, host_refs):
+                for host, there in list(zip(hosts, host_refs))[::-1]:
                     host.end(*there)
 
     host_operands = [v for host in hosts for v in host.operands]
@@ -956,7 +956,7 @@
     return shapes, specs
 
 
-def rec_forward(length, x, params, **more):
+def rec_forward(length, seq, x, params, **more):
     blocks, (rows, model) = lax.axis_size("mp"), x[0].shape
     layout = layout_of(blocks, rows)
     width = params[0].shape[1] // 2
@@ -970,7 +970,7 @@
     shapes, specs = piece_outputs(layout, model)
     final = (jax.ShapeDtypeStruct((SUB, width), f32), pl.BlockSpec((SUB, width), lambda step: (0, 0)))
     return call(
-        functools.partial(rec_forward_kernel, layout),
+        functools.partial(rec_forward_kernel, layout, seq),
         (blocks,),
         [(v, whole(v)) for v in (length,) + tuple(x) + tuple(params)],
         [(shape, wide) for shape in (low, out, out, out, out, low, out, out, out)] + [final] + list(zip(shapes, specs)),
@@ -1010,7 +1010,7 @@
     late = tuple(range(before_x, before_params)) + tuple(before_params + at for at in (1, 2, 3))
     inputs += [(v, wide) for v in saved] + [(v, ANY) for v in shared]
     return call(
-        functools.partial(rec_backward_kernel, layout, len(shared)),
+        functools.partial(rec_backward_kernel, layout, seq),
         (blocks,),
         inputs,
         [(low, double), (low, double), sums, gain_sums] + list(zip(shapes, specs)),
@@ -1452,7 +1452,7 @@
     )
     backward_params = (wo, w_both, taps, w_gates, decay_line)
     seqs = range(count)
-    limits = [jnp.full((SUB, LANES), lengths[s], jnp.int32) for s in seqs]
+    limits = jnp.broadcast_to(lengths[:, None, None], (count, SUB, LANES))
     blocks = lax.axis_size("mp")
     hosted = blocks == 4 and count == 2
     ids = iter(range(1, 100))
@@ -1486,11 +1486,11 @@
     starts = [normalize(resid[s], norm1_gain).astype(bf16) for s in seqs]
     piece, model = starts[0].shape
     seq_in = [gather(starts[0])]
-    out, (second,) = run(rec_forward, limits[0], seq_in[0], forward_params, hosts=[GatherHost(starts[1])], middle=1)
+    out, (second,) = run(rec_forward, limits, 0, seq_in[0], forward_params, hosts=[GatherHost(starts[1])], middle=1)
     seq_in.append(second)
     forward = [out]
     out, (branch,) = run(
-        rec_forward, limits[1], seq_in[1], forward_params, hosts=[ScatterHost(out[10:])], middle=1, before=(out[9],)
+        rec_forward, limits, 1, seq_in[1], forward_params, hosts=[ScatterHost(out[10:])], middle=1, before=(out[9],)
     )
     forward.append(out)
     mixed = [out[0] for out in forward]
@@ -1541,12 +1541,12 @@
     second, more_gain2 = middle_grad(1, d_mid)
     enter("up", grad_up)
     out, (second_seq,) = run(
-        rec_backward, limits[0], 0, count, first_seq, seq_in[0], backward_params, saved[0], (),
+        rec_backward, limits, 0, count, first_seq, seq_in[0], backward_params, saved[0], (),
         hosts=[GatherHost(second.astype(bf16))], middle=1, before=(grad_up[0],), budget=4,
     )
     sums, gain1 = out[2], out[3]
     out, (d_in,) = run(
-        rec_backward, limits[1], 1, count, second_seq, seq_in[1], backward_params, saved[1], out[:2],
+        rec_backward, limits, 1, count, second_seq, seq_in[1], backward_params, saved[1], out[:2],
         hosts=[ScatterHost(out[4:])], middle=1, budget=4,
     )
     d_both, d_gates = out[:2]

time: 801 us -> 799 us (level)
  no operation moved by 1% of the time
where the time goes in v7:
time: 799 us; the launch traced here: 789 us
  Pallas kernels  614 us (77%)
  waiting for transfers between devices  76 us (10%)
  other arithmetic  45.2 us (6%)
  starting transfers between devices  19.2 us (2%)
  local copies, waits for them, and re-layouts  18.7 us (2%)
  between operations  15.3 us (2%)
    pallas_call x18, Pallas kernels, call(): pl.pallas_call(body, out_shape=tuple((shape for shape, _ in outs)) + tupl...  614 us
    ppermute x22, waiting for transfers between devices, swap(): return lax.ppermute(value, axis, [(i, i ^ bit) for i in range(size)])  76 us
    ppermute x22, starting transfers between devices, swap(): return lax.ppermute(value, axis, [(i, i ^ bit) for i in range(size)])  16.8 us
  transfers between devices with their start and end apart: 25, of which 9 were waited for; matrix products, arithmetic and copies ran while one was open for 4% of the time, Pallas kernels for 19%

profile of v7, /device:TPU:9, one launch (start us, length us, event | category | flops | bytes accessed | tf_op | source)
XLA Modules:
  0.0 788.9 jit_solution(6196323891747679826)
XLA Ops:
  7.3 2.2 fusion.40
  9.5 1.4 fusion.34
  10.9 1.2 collective-permute-start.1
  12.2 1.2 collective-permute-start
  15.8 8.4 %fusion.44.refs_9_.refs_14_ = bf16[640,1280]{1,0:T(8,128)(2,1)} fusion(bf16[160,160]{1,0:T(8,128)(2,1)S(1)} %get-tuple-element.434, bf16[160,160]{1,0:T(8,128)(2,1)S(1)} %get-tuple-element.435, bf16[160,160]{1,0:T(8,128)(2,1)S(1)} %get-tuple-element.433, bf16[160,160]{1,0:T(8,128)(2,1)S(1)} %get-tuple-element.432, ...), kind=kLoop, calls=%fused_computation.76 | loop fusion | flops 40960000 | bytes 2048000 | tf_op jit(solution)/shard_map/concatenate | solution.py:1449
  24.2 10.7 %collective-permute-done.1.refs_3_.refs_8_.refs_2_ = bf16[256,2048]{1,0:T(8,128)(2,1)S(1)} collective-permute-done((bf16[256,2048]{1,0:T(8,128)(2,1)S(1)}, bf16[256,2048]{1,0:T(8,128)(2,1)S(1)}, u32[]{:S(2)}, u32[]{:S(2)}) %collective-permute-start.1) | collective-permute-done | bytes 1048608 | tf_op jit(solution)/shard_map/ppermute | solution.py:1312
  35.0 1.3 collective-permute-start.3
  36.4 1.3 collective-permute-start.2
  38.9 2.3 copy-done.24
  41.3 5.7 collective-permute-done.3.refs_5_.refs_10_.refs_4_
  47.0 1.1 collective-permute-done.2.refs_4_.refs_9_.refs_3_
  48.0 0.8 broadcast_in_dim.14.refs_0_
  48.8 38.3 %rec_forward.2 = (bf16[4,256,640]{2,1,0:T(8,128)(2,1)}, f32[4,256,640]{2,1,0:T(8,128)}, f32[4,256,640]{2,1,0:T(8,128)}, f32[4,256,640]{2,1,0:T(8,128)}, f32[4,25...) custom-call(s32[2,8,128]{2,1,0:T(8,128)} %broadcast_in_dim.14.refs_0, ...), custom_call_target="tpu_custom_call" | custom-call | flops 21275000832 | bytes 65536 | tf_op jit(solution)/shard_map/rec_forward/pallas_call | solution.py:912
  87.2 38.0 %rec_forward.3 = (bf16[4,256,640]{2,1,0:T(8,128)(2,1)}, f32[4,256,640]{2,1,0:T(8,128)}, f32[4,256,640]{2,1,0:T(8,128)}, f32[4,256,640]{2,1,0:T(8,128)}, f32[4,25...) custom-call(s32[2,8,128]{2,1,0:T(8,128)} %broadcast_in_dim.14.refs_0, ...), custom_call_target="tpu_custom_call" | custom-call | flops 21275000832 | bytes 65536 | tf_op jit(solution)/shard_map/rec_forward/pallas_call | solution.py:912
  125.2 2.2 multiply_reduce_fusion.5
  127.7 1.0 collective-permute-start.5
  129.3 18.8 %collective-permute-done.5.refs_2_ = bf16[256,2048]{1,0:T(8,128)(2,1)S(1)} collective-permute-done((bf16[256,2048]{1,0:T(8,128)(2,1)S(1)}, bf16[256,2048]{1,0:T(8,128)(2,1)S(1)}, u32[]{:S(2)}, u32[]{:S(2)}) %collective-permute-start.5) | collective-permute-done | bytes 1048608 | tf_op jit(solution)/shard_map/ppermute | solution.py:1312
  148.2 1.2 collective-permute-start.7
  149.8 11.7 %collective-permute-done.7.refs_4_ = bf16[128,2048]{1,0:T(8,128)(2,1)S(1)} collective-permute-done((bf16[128,2048]{1,0:T(8,128)(2,1)S(1)}, bf16[128,2048]{1,0:T(8,128)(2,1)S(1)}, u32[]{:S(2)}, u32[]{:S(2)}) %collective-permute-start.7) | collective-permute-done | bytes 524320 | tf_op jit(solution)/shard_map/ppermute | solution.py:1312
  161.6 0.8 copy-done.63
  162.6 35.3 %mlp_forward.2 = (bf16[8,256,1536]{2,1,0:T(8,128)(2,1)}, bf16[8,256,1536]{2,1,0:T(8,128)(2,1)}, bf16[8,256,1536]{2,1,0:T(8,128)(2,1)}, bf16[4,256,2048]{2,1,0:T(...) custom-call(bf16[256,2048]{1,0:T(8,128)(2,1)} %copy-done.26, bf16[256,2048]{1,0:T(8,128)(2,1)} %copy-done.44, ...), custom_call_target="tpu_custom_call" | custom-call | flops 17250000896 | bytes 65536 | tf_op jit(solution)/shard_map/mlp_forward/pallas_call | solution.py:912
  197.9 2.2 multiply_reduce_fusion.4
  200.6 1.4 collective-permute-start.8
  202.0 18.7 %collective-permute-done.9.refs_2_.refs_7_ = bf16[256,2048]{1,0:T(8,128)(2,1)S(1)} collective-permute-done((bf16[256,2048]{1,0:T(8,128)(2,1)S(1)}, bf16[256,2048]{1,0:T(8,128)(2,1)S(1)}, u32[]{:S(2)}, u32[]{:S(2)}) %collective-permute-start.9) | collective-permute-done | bytes 1048608 | tf_op jit(solution)/shard_map/ppermute | solution.py:1312
  221.8 0.9 copy-done.46
  223.1 1.6 slice_bitcast_fusion
  224.7 8.5 %collective-permute-done.11.refs_4_.refs_9_ = bf16[128,2048]{1,0:T(8,128)(2,1)S(1)} collective-permute-done((bf16[128,2048]{1,0:T(8,128)(2,1)S(1)}, bf16[128,2048]{1,0:T(8,128)(2,1)S(1)}, u32[]{:S(2)}, u32[]{:S(2)}) %collective-permute-start.11) | collective-permute-done | bytes 524320 | tf_op jit(solution)/shard_map/ppermute | solution.py:1312
  233.2 0.8 copy-done.65
  234.2 35.7 %mlp_forward.3 = (bf16[8,256,1536]{2,1,0:T(8,128)(2,1)}, bf16[8,256,1536]{2,1,0:T(8,128)(2,1)}, bf16[8,256,1536]{2,1,0:T(8,128)(2,1)}, bf16[4,256,2048]{2,1,0:T(...) custom-call(bf16[256,2048]{1,0:T(8,128)(2,1)} %copy-done.27, ...), custom_call_target="tpu_custom_call", output_to_operand_aliasing={{0}: (8, {}), {1}: (9, {}), {2}: (10, {})} | custom-call | flops 17250000896 | bytes 65536 | tf_op jit(solution)/shard_map/mlp_forward/pallas_call | solution.py:912
  269.9 37.2 %mlp_backward.2 = (bf16[8,256,1536]{2,1,0:T(8,128)(2,1)}, bf16[8,256,1536]{2,1,0:T(8,128)(2,1)}, bf16[256,2048]{1,0:T(8,128)(2,1)}, bf16[256,2048]{1,0:T(8,128)(...) custom-call(bf16[256,2048]{1,0:T(8,128)(2,1)} %get-tuple-element.422, ...), custom_call_target="tpu_custom_call" | custom-call | flops 18400000000 | bytes 65536 | tf_op jit(solution)/shard_map/mlp_backward/pallas_call | solution.py:912
  307.1 25.9 %weight_grad.4 = (bf16[384,2048]{1,0:T(8,128)(2,1)}, bf16[384,2048]{1,0:T(8,128)(2,1)}) custom-call(bf16[2048,1536]{1,0:T(8,128)(2,1)} %bitcast.79, bf16[256,2048]{1,0:T(8,128)(2,1)} %get-tuple-element.422.refs_11_.refs_0_.refs_1_, bf16[256,2048]{1,0:T(8,128)(2,1)} %get-tuple-element.231.refs_1_.refs_2_, ...), custom_call_target="tpu_custom_call" | custom-call | flops 11500000256 | bytes 65536 | tf_op jit(solution)/shard_map/weight_grad/pallas_call | solution.py:912
  333.0 41.9 %mlp_backward.3 = (bf16[8,256,1536]{2,1,0:T(8,128)(2,1)}, bf16[8,256,1536]{2,1,0:T(8,128)(2,1)}, bf16[256,2048]{1,0:T(8,128)(2,1)}, bf16[256,2048]{1,0:T(8,128)(...) custom-call(bf16[256,2048]{1,0:T(8,128)(2,1)} %get-tuple-element.423, ...), custom_call_target="tpu_custom_call", output_to_operand_aliasing={{0}: (10, {}), {1}: (11, {})} | custom-call | flops 18400000000 | bytes 65536 | tf_op jit(solution)/shard_map/mlp_backward/pallas_call | solution.py:912
  374.9 3.2 multiply_reduce_fusion.1
  378.1 2.8 fusion.60
  380.9 43.2 %weight_grad.5 = (bf16[512,1536]{1,0:T(8,128)(2,1)}, bf16[512,1536]{1,0:T(8,128)(2,1)}, bf16[256,2048]{1,0:T(8,128)(2,1)}, bf16[256,2048]{1,0:T(8,128)(2,1)}, bf...) custom-call(bf16[256,2048]{1,0:T(8,128)(2,1)} %copy-done.26, ...), custom_call_target="tpu_custom_call" | custom-call | flops 11500000256 | bytes 65536 | tf_op jit(solution)/shard_map/weight_grad/pallas_call | solution.py:912
  424.1 40.9 %weight_grad.6 = (bf16[512,1536]{1,0:T(8,128)(2,1)}, bf16[512,1536]{1,0:T(8,128)(2,1)}, bf16[256,2048]{1,0:T(8,128)(2,1)}, bf16[256,2048]{1,0:T(8,128)(2,1)}, bf...) custom-call(bf16[256,2048]{1,0:T(8,128)(2,1)} %copy-done.26, ...), custom_call_target="tpu_custom_call" | custom-call | flops 11500000256 | bytes 65536 | tf_op jit(solution)/shard_map/weight_grad/pallas_call | solution.py:912
  465.1 3.2 multiply_reduce_fusion
  468.3 2.8 fusion.59
  471.1 41.9 %rec_backward.2 = (bf16[8,256,1280]{2,1,0:T(8,128)(2,1)}, bf16[8,256,1280]{2,1,0:T(8,128)(2,1)}, f32[8,8,640]{2,1,0:T(8,128)}, f32[8,2048]{1,0:T(8,128)}, bf16[2...) custom-call(s32[2,8,128]{2,1,0:T(8,128)} %broadcast_in_dim.14.refs_0, ...), custom_call_target="tpu_custom_call" | custom-call | flops 24725000192 | bytes 65536 | tf_op jit(solution)/shard_map/rec_backward/pallas_call | solution.py:912
  513.0 41.1 %rec_backward.3 = (bf16[8,256,1280]{2,1,0:T(8,128)(2,1)}, bf16[8,256,1280]{2,1,0:T(8,128)(2,1)}, f32[8,8,640]{2,1,0:T(8,128)}, f32[8,2048]{1,0:T(8,128)}, bf16[2...) custom-call(s32[2,8,128]{2,1,0:T(8,128)} %broadcast_in_dim.14.refs_0, ...), custom_call_target="tpu_custom_call", output_to_operand_aliasing={{0}: (24, {}), {1}: (25, {})} | custom-call | flops 24725000192 | bytes 65536 | tf_op jit(solution)/shard_map/rec_backward/pallas_call | solution.py:912
  554.1 42.8 %weight_grad.7 = (bf16[512,1280]{1,0:T(8,128)(2,1)}, bf16[512,1280]{1,0:T(8,128)(2,1)}, bf16[128,1536]{1,0:T(8,128)(2,1)}, bf16[128,1536]{1,0:T(8,128)(2,1)}, bf...) custom-call(bf16[256,2048]{1,0:T(8,128)(2,1)} %copy-done.28, ...), custom_call_target="tpu_custom_call" | custom-call | flops 11500000256 | bytes 65536 | tf_op jit(solution)/shard_map/weight_grad/pallas_call | solution.py:912
  597.1 0.7 slice.128
  597.8 0.7 slice.129
  599.3 123.0 %last_grad.1 = (bf16[512,1280]{1,0:T(8,128)(2,1)}, bf16[512,1280]{1,0:T(8,128)(2,1)}, bf16[128,1536]{1,0:T(8,128)(2,1)}, bf16[128,1536]{1,0:T(8,128)(2,1)}, bf16...) custom-call(bf16[1024,640]{1,0:T(8,128)(2,1)} %bitcast.84, ...), custom_call_target="tpu_custom_call" | custom-call | flops 69000003584 | bytes 65536 | tf_op jit(solution)/shard_map/last_grad/pallas_call | solution.py:912
  722.3 0.8 slice_convert_fusion
  723.1 2.3 collective-permute-start.12
  725.5 2.8 collective-permute-start.17
  728.4 3.1 fusion.35
  732.3 3.3 fusion.55
  735.6 6.4 join_pieces.5
  742.1 6.7 join_pieces.6
  749.4 0.8 fusion.58
  751.2 1.0 collective-permute-start.20
  752.2 6.4 join_pieces.7
  758.6 5.7 join_pieces.8
  764.5 0.7 collective-permute-start.22
  765.8 1.5 pad_maximum_fusion.1
  767.3 0.6 fusion.61
  769.8 1.0 copy.47
  771.2 1.0 copy.48
  772.1 0.6 fusion.57
  773.4 3.9 join_pieces.9
  777.4 2.3 fusion.54
  780.4 1.5 pad_maximum_fusion
  (195 shorter events, 14.9 us)
Async XLA Ops:
  7.2 770.1 %reduce-scatter.3.cloned.1.call-start = ((), (), s32[]{:S(2)}) async-start(), calls=%async_computation.2 | async-start | bytes 5242880 | tf_op jit(solution)/shard_map/reduce_scatter | solution.py:1560
  9.5 3.9 copy-start.50
  9.5 4.5 copy-start.56
  9.5 5.1 copy-start.57
  9.5 5.6 copy-start.58
  9.5 6.2 copy-start.38
  9.5 6.2 copy-start.39
  10.9 24.1 %copy-start.28 = (bf16[256,2048]{1,0:T(8,128)(2,1)}, bf16[256,2048]{1,0:T(8,128)(2,1)S(1)}, u32[]{:S(2)}) copy-start(bf16[256,2048]{1,0:T(8,128)(2,1)S(1)} %get-tuple-element.420.refs_1_.refs_6_.refs_0_) | copy-start | bytes 3145732
  10.9 24.0 %collective-permute-start.1 = (bf16[256,2048]{1,0:T(8,128)(2,1)S(1)}, bf16[256,2048]{1,0:T(8,128)(2,1)S(1)}, u32[]{:S(2)}, u32[]{:S(2)}) collective-permute-start(bf16[256,2048]{1,0:T(8,128)(2,1)S(1)} %get-tuple-element.420.refs_1_.refs_6_.refs_0_), channel_id=1, source_target_pairs={{0,2},{1,3},{2,0},{3,1},{4,6},{5,7},{6,4},{7,5},{8,10},{9,11},{10,... | collective-permute-start | bytes 3145736 | tf_op jit(solution)/shard_map/ppermute | solution.py:1312
  12.2 24.1 %collective-permute-start = (bf16[256,2048]{1,0:T(8,128)(2,1)S(1)}, bf16[256,2048]{1,0:T(8,128)(2,1)S(1)}, u32[]{:S(2)}, u32[]{:S(2)}) collective-permute-start(bf16[256,2048]{1,0:T(8,128)(2,1)S(1)} %get-tuple-element.420.refs_1_.refs_6_.refs_0_), channel_id=1, source_target_pairs={{0,1},{1,0},{2,3},{3,2},{4,5},{5,4},{6,7},{7,6},{8,9},{9,8},{10,11... | collective-permute-start | bytes 3145736 | tf_op jit(solution)/shard_map/ppermute | solution.py:1312
  15.8 21.9 %copy-start.22 = (bf16[2048,640]{1,0:T(8,128)(2,1)S(1)}, bf16[2048,640]{1,0:T(8,128)(2,1)}, u32[]{:S(2)}) copy-start(bf16[2048,640]{1,0:T(8,128)(2,1)} %param.20) | copy-start | bytes 7864324
  35.0 11.9 %collective-permute-start.3 = (bf16[128,2048]{1,0:T(8,128)(2,1)S(1)}, bf16[128,2048]{1,0:T(8,128)(2,1)S(1)}, u32[]{:S(2)}, u32[]{:S(2)}) collective-permute-start(bf16[128,2048]{1,0:T(8,128)(2,1)S(1)} %slice.131), channel_id=1, source_target_pairs={{0,1},{1,0},{2,3},{3,2},{4,5},{5,4},{6,7},{7,6},{8,9},{9,8},{10,11... | collective-permute-start | bytes 1572872 | tf_op jit(solution)/shard_map/ppermute | solution.py:1312
  36.4 11.7 %collective-permute-start.2 = (bf16[128,2048]{1,0:T(8,128)(2,1)S(1)}, bf16[128,2048]{1,0:T(8,128)(2,1)S(1)}, u32[]{:S(2)}, u32[]{:S(2)}) collective-permute-start(bf16[128,2048]{1,0:T(8,128)(2,1)S(1)} %slice.130), channel_id=1, source_target_pairs={{0,2},{1,3},{2,0},{3,1},{4,6},{5,7},{6,4},{7,5},{8,10},{9,11},{10,... | collective-permute-start | bytes 1572872 | tf_op jit(solution)/shard_map/ppermute | solution.py:1312
  38.4 9.6 %copy-start.59 = (s32[2]{0:T(128)S(1)}, s32[2]{0:T(128)}, u32[]{:S(2)}) copy-start(s32[2]{0:T(128)} %param.34) | copy-start | bytes 28
  87.2 38.0 %copy-start.31 = (bf16[256,2048]{1,0:T(8,128)(2,1)S(1)}, bf16[256,2048]{1,0:T(8,128)(2,1)}, u32[]{:S(2)}) copy-start(bf16[256,2048]{1,0:T(8,128)(2,1)} %get-tuple-element.208) | copy-start | bytes 3145732
  127.4 250.7 %copy-start = (f32[256,2048]{1,0:T(8,128)}, f32[256,2048]{1,0:T(8,128)S(1)}, u32[]{:S(2)}) copy-start(f32[256,2048]{1,0:T(8,128)S(1)} %get-tuple-element.417) | copy-start | bytes 6291460
  127.7 34.7 %copy-start.26 = (bf16[256,2048]{1,0:T(8,128)(2,1)}, bf16[256,2048]{1,0:T(8,128)(2,1)S(1)}, u32[]{:S(2)}) copy-start(bf16[256,2048]{1,0:T(8,128)(2,1)S(1)} %multiply_convert_fusion.1.refs_0_) | copy-start | bytes 3145732
  127.7 20.4 %collective-permute-start.5 = (bf16[256,2048]{1,0:T(8,128)(2,1)S(1)}, bf16[256,2048]{1,0:T(8,128)(2,1)S(1)}, u32[]{:S(2)}, u32[]{:S(2)}) collective-permute-start(bf16[256,2048]{1,0:T(8,128)(2,1)S(1)} %multiply_convert_fusion.1.refs_0_), channel_id=1, source_target_pairs={{0,2},{1,3},{2,0},{3,1},{4,6},{5,7},{6,4},{7,5},{8,10},{9,11},{10,... | collective-permute-start | bytes 3145736 | tf_op jit(solution)/shard_map/ppermute | solution.py:1312
  128.7 20.6 %collective-permute-start.4 = (bf16[256,2048]{1,0:T(8,128)(2,1)S(1)}, bf16[256,2048]{1,0:T(8,128)(2,1)S(1)}, u32[]{:S(2)}, u32[]{:S(2)}) collective-permute-start(bf16[256,2048]{1,0:T(8,128)(2,1)S(1)} %multiply_convert_fusion.1.refs_0_), channel_id=1, source_target_pairs={{0,1},{1,0},{2,3},{3,2},{4,5},{5,4},{6,7},{7,6},{8,9},{9,8},{10,11... | collective-permute-start | bytes 3145736 | tf_op jit(solution)/shard_map/ppermute | solution.py:1312
  148.1 13.5 %copy-start.43 = (bf16[256,2048]{1,0:T(8,128)(2,1)}, bf16[256,2048]{1,0:T(8,128)(2,1)S(1)}, u32[]{:S(2)}) copy-start(bf16[256,2048]{1,0:T(8,128)(2,1)S(1)} %collective-permute-done.5.refs_2_) | copy-start | bytes 3145732
  148.2 13.4 %collective-permute-start.7 = (bf16[128,2048]{1,0:T(8,128)(2,1)S(1)}, bf16[128,2048]{1,0:T(8,128)(2,1)S(1)}, u32[]{:S(2)}, u32[]{:S(2)}) collective-permute-start(bf16[128,2048]{1,0:T(8,128)(2,1)S(1)} %slice.133), channel_id=1, source_target_pairs={{0,1},{1,0},{2,3},{3,2},{4,5},{5,4},{6,7},{7,6},{8,9},{9,8},{10,11... | collective-permute-start | bytes 1572872 | tf_op jit(solution)/shard_map/ppermute | solution.py:1312
  149.3 12.2 %copy-start.44 = (bf16[256,2048]{1,0:T(8,128)(2,1)}, bf16[256,2048]{1,0:T(8,128)(2,1)S(1)}, u32[]{:S(2)}) copy-start(bf16[256,2048]{1,0:T(8,128)(2,1)S(1)} %collective-permute-done.4.refs_1_) | copy-start | bytes 3145732
  149.4 12.2 %collective-permute-start.6 = (bf16[128,2048]{1,0:T(8,128)(2,1)S(1)}, bf16[128,2048]{1,0:T(8,128)(2,1)S(1)}, u32[]{:S(2)}, u32[]{:S(2)}) collective-permute-start(bf16[128,2048]{1,0:T(8,128)(2,1)S(1)} %slice.132), channel_id=1, source_target_pairs={{0,2},{1,3},{2,0},{3,1},{4,6},{5,7},{6,4},{7,5},{8,10},{9,11},{10,... | collective-permute-start | bytes 1572872 | tf_op jit(solution)/shard_map/ppermute | solution.py:1312
  162.6 35.3 %copy-start.30 = (bf16[256,2048]{1,0:T(8,128)(2,1)S(1)}, bf16[256,2048]{1,0:T(8,128)(2,1)}, u32[]{:S(2)}) copy-start(bf16[256,2048]{1,0:T(8,128)(2,1)} %get-tuple-element.225) | copy-start | bytes 3145732
  200.1 268.1 %copy-start.2 = (f32[256,2048]{1,0:T(8,128)}, f32[256,2048]{1,0:T(8,128)S(1)}, u32[]{:S(2)}) copy-start(f32[256,2048]{1,0:T(8,128)S(1)} %get-tuple-element.415) | copy-start | bytes 6291460
  200.2 23.0 %copy-start.5 = (bf16[2,256,2048]{2,1,0:T(8,128)(2,1)S(1)}, bf16[2,256,2048]{2,1,0:T(8,128)(2,1)}, u32[]{:S(2)}) copy-start(bf16[2,256,2048]{2,1,0:T(8,128)(2,1)} %param.35) | copy-start | bytes 6291460
  200.4 24.3 %copy-start.27 = (bf16[256,2048]{1,0:T(8,128)(2,1)}, bf16[256,2048]{1,0:T(8,128)(2,1)S(1)}, u32[]{:S(2)}) copy-start(bf16[256,2048]{1,0:T(8,128)(2,1)S(1)} %multiply_convert_fusion.refs_0_.refs_5_) | copy-start | bytes 3145732
  200.4 20.3 %collective-permute-start.9 = (bf16[256,2048]{1,0:T(8,128)(2,1)S(1)}, bf16[256,2048]{1,0:T(8,128)(2,1)S(1)}, u32[]{:S(2)}, u32[]{:S(2)}) collective-permute-start(bf16[256,2048]{1,0:T(8,128)(2,1)S(1)} %multiply_convert_fusion.refs_0_.refs_5_), channel_id=1, source_target_pairs={{0,2},{1,3},{2,0},{3,1},{4,6},{5,7},{6,4},{7,5},{8,10},{9,11},{10,... | collective-permute-start | bytes 3145736 | tf_op jit(solution)/shard_map/ppermute | solution.py:1312
  200.6 20.6 %collective-permute-start.8 = (bf16[256,2048]{1,0:T(8,128)(2,1)S(1)}, bf16[256,2048]{1,0:T(8,128)(2,1)S(1)}, u32[]{:S(2)}, u32[]{:S(2)}) collective-permute-start(bf16[256,2048]{1,0:T(8,128)(2,1)S(1)} %multiply_convert_fusion.refs_0_.refs_5_), channel_id=1, source_target_pairs={{0,1},{1,0},{2,3},{3,2},{4,5},{5,4},{6,7},{7,6},{8,9},{9,8},{10,11... | collective-permute-start | bytes 3145736 | tf_op jit(solution)/shard_map/ppermute | solution.py:1312
  220.8 12.4 %collective-permute-start.11 = (bf16[128,2048]{1,0:T(8,128)(2,1)S(1)}, bf16[128,2048]{1,0:T(8,128)(2,1)S(1)}, u32[]{:S(2)}, u32[]{:S(2)}) collective-permute-start(bf16[128,2048]{1,0:T(8,128)(2,1)S(1)} %slice.135), channel_id=1, source_target_pairs={{0,1},{1,0},{2,3},{3,2},{4,5},{5,4},{6,7},{7,6},{8,9},{9,8},{10,11... | collective-permute-start | bytes 1572872 | tf_op jit(solution)/shard_map/ppermute | solution.py:1312
  222.7 10.5 %collective-permute-start.10 = (bf16[128,2048]{1,0:T(8,128)(2,1)S(1)}, bf16[128,2048]{1,0:T(8,128)(2,1)S(1)}, u32[]{:S(2)}, u32[]{:S(2)}) collective-permute-start(bf16[128,2048]{1,0:T(8,128)(2,1)S(1)} %slice.134), channel_id=1, source_target_pairs={{0,2},{1,3},{2,0},{3,1},{4,6},{5,7},{6,4},{7,5},{8,10},{9,11},{10,... | collective-permute-start | bytes 1572872 | tf_op jit(solution)/shard_map/ppermute | solution.py:1312
  333.0 41.9 %copy-start.10 = (bf16[256,2048]{1,0:T(8,128)(2,1)S(1)}, bf16[256,2048]{1,0:T(8,128)(2,1)}, u32[]{:S(2)}) copy-start(bf16[256,2048]{1,0:T(8,128)(2,1)} %get-tuple-element.256) | copy-start | bytes 3145732
  374.9 3.2 copy-start.13
  424.1 41.0 %copy-start.9 = (bf16[256,2048]{1,0:T(8,128)(2,1)S(1)}, bf16[256,2048]{1,0:T(8,128)(2,1)}, u32[]{:S(2)}) copy-start(bf16[256,2048]{1,0:T(8,128)(2,1)} %get-tuple-element.249) | copy-start | bytes 3145732
  597.0 180.3 %reduce-scatter.5.cloned.1.call-start = ((), (), s32[]{:S(2)}) async-start(), calls=%async_computation.3 | async-start | bytes 5242880 | tf_op jit(solution)/shard_map/reduce_scatter | solution.py:1560
  599.2 129.1 %copy-start.4 = (bf16[2,256,2048]{2,1,0:T(8,128)(2,1)S(1)}, bf16[2,256,2048]{2,1,0:T(8,128)(2,1)}, u32[]{:S(2)}) copy-start(bf16[2,256,2048]{2,1,0:T(8,128)(2,1)} %param.18) | copy-start | bytes 6291460
  599.2 129.1 %copy-start.15 = (bf16[256,2048]{1,0:T(8,128)(2,1)S(1)}, bf16[256,2048]{1,0:T(8,128)(2,1)}, u32[]{:S(2)}) copy-start(bf16[256,2048]{1,0:T(8,128)(2,1)} %get-tuple-element.388) | copy-start | bytes 3145732
  599.2 129.1 %copy-start.16 = (bf16[256,2048]{1,0:T(8,128)(2,1)S(1)}, bf16[256,2048]{1,0:T(8,128)(2,1)}, u32[]{:S(2)}) copy-start(bf16[256,2048]{1,0:T(8,128)(2,1)} %get-tuple-element.391) | copy-start | bytes 3145732
  599.2 129.1 %copy-start.17 = (bf16[256,2048]{1,0:T(8,128)(2,1)S(1)}, bf16[256,2048]{1,0:T(8,128)(2,1)}, u32[]{:S(2)}) copy-start(bf16[256,2048]{1,0:T(8,128)(2,1)} %get-tuple-element.389) | copy-start | bytes 3145732
  599.2 129.1 %copy-start.18 = (bf16[256,2048]{1,0:T(8,128)(2,1)S(1)}, bf16[256,2048]{1,0:T(8,128)(2,1)}, u32[]{:S(2)}) copy-start(bf16[256,2048]{1,0:T(8,128)(2,1)} %get-tuple-element.390) | copy-start | bytes 3145732
  599.2 129.1 %copy-start.49 = (f32[2048]{0:T(1024)S(1)}, f32[2048]{0:T(1024)}, u32[]{:S(2)}) copy-start(f32[2048]{0:T(1024)} %param.19) | copy-start | bytes 24580
  599.3 129.1 %copy-start.53 = (f32[256]{0:T(256)S(1)}, f32[256]{0:T(256)}, u32[]{:S(2)}) copy-start(f32[256]{0:T(256)} %copy-done.52) | copy-start | bytes 3076
  599.3 129.1 %copy-start.55 = (f32[256]{0:T(256)S(1)}, f32[256]{0:T(256)}, u32[]{:S(2)}) copy-start(f32[256]{0:T(256)} %copy-done.54) | copy-start | bytes 3076
  723.1 9.1 %collective-permute-start.19 = (f32[2,2048]{1,0:T(2,128)S(1)}, f32[2,2048]{1,0:T(2,128)S(1)}, u32[]{:S(2)}, u32[]{:S(2)}) collective-permute-start(f32[2,2048]{1,0:T(2,128)S(1)} %slice_convert_fusion), channel_id=1, source_target_pairs={{0,1},{1,0},{2,3},{3,2},{4,5},{5,4},{6,7},{7,6},{8,9},{9,8},{10,11... | collective-permute-start | bytes 49160 | tf_op jit(solution)/shard_map/ppermute | solution.py:1312
  723.1 41.2 %collective-permute-start.12 = (bf16[1280,512]{1,0:T(8,128)(2,1)}, bf16[1280,512]{1,0:T(8,128)(2,1)}, u32[]{:S(2)}, u32[]{:S(2)}) collective-permute-start(bf16[1280,512]{1,0:T(8,128)(2,1)} %get-tuple-element.357), channel_id=1, source_target_pairs={{8,0},{12,4},{16,24},{20,28},{9,1},{13,5},{17,25},{21,29},{10,2},{... | collective-permute-start | bytes 3932168 | tf_op jit(solution)/shard_map/ppermute | solution.py:1588
  725.5 33.1 %collective-permute-start.17 = (bf16[512,1280]{1,0:T(8,128)(2,1)}, bf16[512,1280]{1,0:T(8,128)(2,1)}, u32[]{:S(2)}, u32[]{:S(2)}) collective-permute-start(bf16[512,1280]{1,0:T(8,128)(2,1)} %get-tuple-element.382.refs_0_), channel_id=1, source_target_pairs={{0,4},{4,0},{8,12},{12,8},{16,20},{20,16},{24,28},{28,24},{1,5},{5... | collective-permute-start | bytes 3932168 | tf_op jit(solution)/shard_map/ppermute | solution.py:1312
  728.3 30.3 %collective-permute-start.18 = (bf16[512,1280]{1,0:T(8,128)(2,1)}, bf16[512,1280]{1,0:T(8,128)(2,1)}, u32[]{:S(2)}, u32[]{:S(2)}) collective-permute-start(bf16[512,1280]{1,0:T(8,128)(2,1)} %get-tuple-element.383.refs_1_), channel_id=1, source_target_pairs={{0,4},{4,0},{8,12},{12,8},{16,20},{20,16},{24,28},{28,24},{1,5},{5... | collective-permute-start | bytes 3932168 | tf_op jit(solution)/shard_map/ppermute | solution.py:1312
  728.4 3.2 copy-start.34
  728.4 3.8 copy-start.35
  728.4 3.9 copy-start.6
  728.4 3.9 copy-start.7
  728.4 3.9 copy-start.19
  728.4 3.9 copy-start.20
  731.6 17.2 %collective-permute-start.13 = (bf16[128,1536]{1,0:T(8,128)(2,1)S(1)}, bf16[128,1536]{1,0:T(8,128)(2,1)}, u32[]{:S(2)}, u32[]{:S(2)}) collective-permute-start(bf16[128,1536]{1,0:T(8,128)(2,1)S(1)} %copy-done.34), channel_id=1, source_target_pairs={{0,4},{4,0},{8,12},{12,8},{16,20},{20,16},{24,28},{28,24},{1,5},{5... | collective-permute-start | bytes 1179656 | tf_op jit(solution)/shard_map/ppermute | solution.py:1312
  732.2 17.1 %collective-permute-start.14 = (bf16[128,1536]{1,0:T(8,128)(2,1)S(1)}, bf16[128,1536]{1,0:T(8,128)(2,1)}, u32[]{:S(2)}, u32[]{:S(2)}) collective-permute-start(bf16[128,1536]{1,0:T(8,128)(2,1)S(1)} %copy-done.35), channel_id=1, source_target_pairs={{0,4},{4,0},{8,12},{12,8},{16,20},{20,16},{24,28},{28,24},{1,5},{5... | collective-permute-start | bytes 1179656 | tf_op jit(solution)/shard_map/ppermute | solution.py:1312
  742.0 6.8 copy-start.32
  742.0 7.3 copy-start.33
  742.1 8.6 %copy-start.47 = (bf16[176,640]{1,0:T(8,128)(2,1)S(1)}, bf16[176,640]{1,0:T(8,128)(2,1)}, u32[]{:S(2)}) copy-start(bf16[176,640]{1,0:T(8,128)(2,1)} %get-tuple-element.396) | copy-start | bytes 675844
  748.8 1.8 collective-permute-start.15
  749.3 1.9 collective-permute-start.16
  750.6 17.9 %collective-permute-start.21 = (bf16[176,640]{1,0:T(8,128)(2,1)S(1)}, bf16[176,640]{1,0:T(8,128)(2,1)S(1)}, u32[]{:S(2)}, u32[]{:S(2)}) collective-permute-start(bf16[176,640]{1,0:T(8,128)(2,1)S(1)} %copy-done.47), channel_id=1, source_target_pairs={{0,4},{4,0},{8,12},{12,8},{16,20},{20,16},{24,28},{28,24},{1,5},{5... | collective-permute-start | bytes 675848 | tf_op jit(solution)/shard_map/ppermute | solution.py:1312
  751.2 16.1 %collective-permute-start.20 = (f32[2,2048]{1,0:T(2,128)S(1)}, f32[2,2048]{1,0:T(2,128)S(1)}, u32[]{:S(2)}, u32[]{:S(2)}) collective-permute-start(f32[2,2048]{1,0:T(2,128)S(1)} %fusion.58), channel_id=1, source_target_pairs={{0,2},{1,3},{2,0},{3,1},{4,6},{5,7},{6,4},{7,5},{8,10},{9,11},{10,... | collective-permute-start | bytes 49160 | tf_op jit(solution)/shard_map/ppermute | solution.py:1312
  758.6 5.7 copy-start.25
  764.5 8.9 %collective-permute-start.22 = (bf16[1280,512]{1,0:T(8,128)(2,1)S(1)}, bf16[1280,512]{1,0:T(8,128)(2,1)}, u32[]{:S(2)}, u32[]{:S(2)}) collective-permute-start(bf16[1280,512]{1,0:T(8,128)(2,1)S(1)} %broadcast_select_fusion.refs_0_), channel_id=1, source_target_pairs={{0,4},{4,0},{8,12},{12,8},{16,20},{20,16},{24,28},{28,24},{1,5},{5... | collective-permute-start | bytes 3932168 | tf_op jit(solution)/shard_map/ppermute | solution.py:1312
  (27 other events, 51.7 us)
Sparse Core Ops, SparseCore 0:
  597.1 77.0 reduce-scatter.2
  677.4 51.4 reduce-scatter.4
